TPU v7x, 32 devices: a whole 2x2x4 slice. The times are simulated.
32 devices in a mesh: dp: 8 (over z, core), chan: 4 (over y, x).
Axes of the slice: x: 2, y: 2, z: 4, core: 2. Of those that a mesh axis runs over, the one named last changes fastest.
Arguments:
- volume: bfloat16 [8, 512, 1024], P('dp', 'chan'), may hold values from -16 to 16
- w_first: bfloat16 [27, 512, 512], P(None, 'chan'), may hold values from -0.0546875 to 0.0546875
- gain: float32 [512], replicated, may hold values from 0.1 to 1.9
- w_second: bfloat16 [27, 512, 512], P(None, None, 'chan'), may hold values from -0.0546875 to 0.0546875
- cotangent: bfloat16 [8, 512, 1024], P('dp', 'chan'), may hold values from -8 to 8
Outputs:
- output: bfloat16 [8, 512, 1024], P('dp', 'chan')
- grad_volume: bfloat16 [8, 512, 1024], P('dp', 'chan')
- grad_w_first: float32 [27, 512, 512], P(None, 'chan')
- grad_gain: float32 [512], P('chan')
- grad_w_second: float32 [27, 512, 512], P(None, None, 'chan')
All inputs are finite; a program needn't handle non-finite values.
Results may differ from a plain program's by a relative error of at most 0.005.
Values may be sent and summed in bfloat16 or wider, within the bound.
No kernel may reach another device: no remote copies, remote signals or barrier semaphores. Data moves between devices by JAX's collectives and lax.ppermute only.
A program may use at most 128 MiB of HBM per device.

v0:
```python
import math

import jax
import jax.numpy as jnp
from jax import lax
from jax.sharding import PartitionSpec as P

DEPTH = 4
HEIGHT = 16
WIDTH = 16


TAP_OFFSETS = [
    (plane_off, row_off, col_off)
    for plane_off in (-1, 0, 1)
    for row_off in (-1, 0, 1)
    for col_off in (-1, 0, 1)
]
NORM_EPS = 1e-05


def moved_cells(field, plane_off, row_off, col_off):
    cell_count = field.shape[1]
    plane_cells = HEIGHT * WIDTH
    offset = plane_off * plane_cells + row_off * WIDTH + col_off
    margin = plane_cells + WIDTH + 1
    padded = jnp.pad(field, ((0, 0), (margin, margin)))
    sliced = lax.slice_in_dim(padded, margin + offset, margin + offset + cell_count, axis=1)
    cells = jnp.arange(cell_count, dtype=jnp.int32)
    depth_at = cells // plane_cells + plane_off
    row_at = cells // WIDTH % HEIGHT + row_off
    col_at = cells % WIDTH + col_off
    inside = (
        (depth_at >= 0)
        & (depth_at < DEPTH)
        & (row_at >= 0)
        & (row_at < HEIGHT)
        & (col_at >= 0)
        & (col_at < WIDTH)
    )
    return jnp.where(inside[None, :], sliced, jnp.zeros_like(sliced))


def stack_taps(field, sign):
    layers = [
        moved_cells(field, sign * offsets[0], sign * offsets[1], sign * offsets[2])
        for offsets in TAP_OFFSETS
    ]
    return jnp.concatenate(layers, axis=0).reshape(27, field.shape[0], field.shape[1])


def block_rows(count):
    chosen = 1
    for trial in range(1, 65):
        if count % trial == 0:
            chosen = trial
    return chosen


def normalize(pre, gain_rows):
    center = pre - jnp.mean(pre, axis=1, keepdims=True)
    inverse = lax.rsqrt(jnp.mean(center * center, axis=1, keepdims=True) + NORM_EPS)
    normed = center * inverse
    scaled = gain_rows[:, None] * normed
    return (normed, inverse, scaled, jax.nn.silu(scaled).astype(jnp.bfloat16))


def normalize_back(dact, normed, inverse, scaled, gain_rows):
    sigma = jax.nn.sigmoid(scaled)
    dscaled = dact * sigma * (1.0 + scaled * (1.0 - sigma))
    gain_part = jnp.sum(dscaled * normed, axis=1)
    dnormed = dscaled * gain_rows[:, None]
    dpre = (
        dnormed
        - jnp.mean(dnormed, axis=1, keepdims=True)
        - normed * jnp.mean(dnormed * normed, axis=1, keepdims=True)
    ) * inverse
    return (gain_part, dpre.astype(jnp.bfloat16))


def shards(volume, w_first, gain, w_second, cotangent):
    local_rows = volume.shape[1]
    channels_all = w_first.shape[2]
    cell_count = volume.shape[2]
    source = volume[0]
    target = cotangent[0]
    chan_index = lax.axis_index("chan")
    volume_cols = stack_taps(source, 1)
    target_cols = stack_taps(target, -1)
    contract_first = (((0, 1), (0, 1)), ((), ()))
    contract_second = (((0, 2), (0, 1)), ((), ()))
    contract_cells = (((2,), (1,)), ((), ()))
    second_init = (
        jnp.zeros((local_rows, cell_count), jnp.float32),
        jnp.zeros((27, channels_all, local_rows), jnp.float32),
    )
    first_init = (
        jnp.zeros((local_rows, cell_count), jnp.float32),
        jnp.zeros((27, local_rows, channels_all), jnp.float32),
    )
    own_gain = lax.dynamic_slice_in_dim(gain, chan_index * local_rows, local_rows, 0)
    weights = w_first
    pre_own = lax.psum_scatter(
        lax.dot_general(weights, volume_cols, contract_first, preferred_element_type=jnp.float32),
        "chan",
        scatter_dimension=0,
        tiled=True,
    )
    normed, inverse, scaled, act_own = normalize(pre_own, own_gain)
    act_rows = lax.all_gather(act_own, "chan", axis=0, tiled=True)
    count = act_rows.shape[0]
    step_rows = block_rows(count)

    def second_one_block(index, inner):
        out_now, grad_now = inner
        begin = index * step_rows
        rows = lax.dynamic_slice_in_dim(act_rows, begin, step_rows, 0)
        cols = stack_taps(rows, 1)
        weights = lax.dynamic_slice_in_dim(w_second, begin, step_rows, 1)
        out_now = out_now + lax.dot_general(
            weights, cols, contract_first, preferred_element_type=jnp.float32
        )
        grad_part = lax.dot_general(
            cols, target, contract_cells, preferred_element_type=jnp.float32
        )
        grad_now = lax.dynamic_update_slice_in_dim(grad_now, grad_part, begin, 1)
        return (out_now, grad_now)

    out_sum, second_grad = lax.fori_loop(0, count // step_rows, second_one_block, second_init)
    output = out_sum.astype(jnp.bfloat16)[None]
    factor = 1.0 / math.sqrt(lax.axis_size("dp") * cell_count)
    weights = w_second
    dact_own = lax.psum_scatter(
        lax.dot_general(weights, target_cols, contract_second, preferred_element_type=jnp.float32),
        "chan",
        scatter_dimension=0,
        tiled=True,
    )
    gain_part, dpre_own = normalize_back(dact_own, normed, inverse, scaled, own_gain)
    grad_rows = lax.all_gather(dpre_own, "chan", axis=0, tiled=True)
    count = grad_rows.shape[0]
    first_step_rows = block_rows(count)

    def first_one_block(index, inner):
        back_now, grad_now = inner
        begin = index * first_step_rows
        rows = lax.dynamic_slice_in_dim(grad_rows, begin, first_step_rows, 0)
        cols = stack_taps(rows, -1)
        weights = lax.dynamic_slice_in_dim(w_first, begin, first_step_rows, 2)
        back_now = back_now + lax.dot_general(
            weights, cols, contract_second, preferred_element_type=jnp.float32
        )
        grad_part = lax.dot_general(
            volume_cols, rows, contract_cells, preferred_element_type=jnp.float32
        )
        grad_now = lax.dynamic_update_slice_in_dim(grad_now, grad_part, begin, 2)
        return (back_now, grad_now)

    back_sum, first_grad = lax.fori_loop(0, count // first_step_rows, first_one_block, first_init)
    first_total, second_total, gain_total = lax.psum((first_grad, second_grad, gain_part), "dp")
    grad_volume = back_sum.astype(jnp.bfloat16)[None]
    return (output, grad_volume, first_total * factor, gain_total * factor, second_total * factor)


def solution(mesh):
    placed = (
        P("dp", "chan", None),
        P(None, "chan", None),
        P(),
        P(None, None, "chan"),
        P("dp", "chan", None),
    )
    return jax.shard_map(
        shards,
        mesh=mesh,
        in_specs=placed,
        out_specs=(
            P("dp", "chan", None),
            P("dp", "chan", None),
            P(None, "chan", None),
            P("chan"),
            P(None, None, "chan"),
        ),
        check_vma=False,
    )
```

profile of v0, /device:TPU:1, one launch (start us, length us, event | category | flops | bytes accessed | tf_op | source)
XLA Modules:
  0.0 671.9 jit_solution(6773029056736390060)
XLA Ops:
  40.3 3.0 copy-done.1
  43.2 5.3 convolution_bitcast_fusion.4
  48.6 7.7 %convolution_bitcast_fusion.3 = f32[512,1024]{0,1:T(8,128)} fusion(bf16[27,128,1024]{2,1,0:T(8,128)(2,1)} %bitcast.99, bf16[27,512,128]{2,1,0:T(8,128)(2,1)S(1)} %copy-done.9), kind=kOutput, calls=%fused_computation.337 | convolution fusion | flops 3623878656 | bytes 12713984 | tf_op jit(solution)/shard_map/dot_general | solution.py:134
  57.5 28.6 %reduce-scatter.3.cloned.1.call-done = f32[128,1024]{0,1:T(8,128)} async-done(((f32[512,1024]{0,1:T(8,128)}), f32[128,1024]{0,1:T(8,128)}) %reduce-scatter.3.cloned.1.call-update) | async-done | bytes 524304 | tf_op jit(solution)/shard_map/reduce_scatter | solution.py:103
  88.4 36.0 %reduce-scatter.5.cloned.1.call-done = f32[128,1024]{0,1:T(8,128)} async-done(((f32[512,1024]{0,1:T(8,128)}), f32[128,1024]{0,1:T(8,128)}) %reduce-scatter.5.cloned.1.call-update) | async-done | bytes 524304 | tf_op jit(solution)/shard_map/reduce_scatter | solution.py:133
  128.2 3.6 copy.18
  131.8 22.9 %all-gather.5.cloned.1.call-done = bf16[512,1024]{0,1:T(8,128)(2,1)} async-done(((bf16[128,1024]{0,1:T(8,128)(2,1)}), bf16[512,1024]{0,1:T(8,128)(2,1)}) %all-gather.5.cloned.1.call-update) | async-done | bytes 1048592 | tf_op jit(solution)/shard_map/all_gather | solution.py:140
  156.3 3.8 broadcast_in_dim.1619
  160.0 112.0 %while.39 = (s32[]{:T(128)}, f32[128,1024]{1,0:T(8,128)}, f32[27,128,512]{1,2,0:T(8,128)}, bf16[27,128,512]{1,2,0:T(8,128)(2,1)}, bf16[512,1024]{1,0:T(8,128)(2,...) while((s32[]{:T(128)}, f32[128,1024]{1,0:T(8,128)}, ...), condition=%wide.region_9.10_spmd.clone, body=%wide.region_8.9_spmd.clone.sunk | while | flops 909162496 | bytes 28908768 | solution.py:159
  167.6 6.3 fusion.437
  181.6 6.3 fusion.437
  195.6 6.3 fusion.437
  209.6 6.3 fusion.437
  223.6 6.3 fusion.437
  237.6 6.3 fusion.437
  251.6 6.3 fusion.437
  265.7 6.3 fusion.437
  272.0 8.0 %copy.20 = f32[27,128,512]{2,1,0:T(8,128)} copy(f32[27,128,512]{1,2,0:T(8,128)} %get-tuple-element.383) | data formatting | bytes 14155776 | tf_op jit(solution)/shard_map/while | solution.py:159
  282.2 3.8 broadcast_in_dim.1590
  286.0 83.8 %while.38 = (s32[]{:T(128)}, f32[128,1024]{1,0:T(8,128)}, f32[27,512,128]{2,1,0:T(8,128)}, bf16[27,512,128]{2,1,0:T(8,128)(2,1)}, bf16[512,1024]{1,0:T(8,128)(2,...) while((s32[]{:T(128)}, f32[128,1024]{1,0:T(8,128)}, ...), condition=%wide.region_4.5_spmd.clone, body=%wide.region_3.4_spmd.clone.sunk | while | flops 909162496 | bytes 17111212 | solution.py:129
  290.9 3.0 convolution_dynamic-update-slice_fusion.2
  301.2 3.0 convolution_dynamic-update-slice_fusion.2
  311.7 3.0 convolution_dynamic-update-slice_fusion.2
  322.2 3.0 convolution_dynamic-update-slice_fusion.2
  332.7 3.0 convolution_dynamic-update-slice_fusion.2
  343.2 3.0 convolution_dynamic-update-slice_fusion.2
  353.7 3.0 convolution_dynamic-update-slice_fusion.2
  364.2 3.0 convolution_dynamic-update-slice_fusion.2
  369.8 14.0 %psum.22 = f32[128]{0:T(128)S(1)} all-reduce(f32[128]{0:T(128)S(1)} %get-tuple-element.451), channel_id=1, replica_groups=mesh['dp'=8,'chan'=4] {'dp'}, use_global_device_ids=true, to_apply=%region_12.13 | all-reduce | flops 128 | bytes 1024 | tf_op jit(solution)/shard_map/psum | solution.py:160
  385.8 268.7 %all-reduce.7.cloned.1.call-done = (f32[27,128,512]{2,1,0:T(8,128)}, f32[27,512,128]{2,1,0:T(8,128)}) async-done(((f32[27,128,512]{2,1,0:T(8,128)}, f32[27,512,128]{2,1,0:T(8,128)}), (f32[27,128,512]{2,1,0:T(8,128)}, f32[27,512,128]{2,1,0:T(8,128)})) %all-reduce.7.cloned.1.call-update) | async-done | bytes 14155792 | tf_op jit(solution)/shard_map/psum | solution.py:160
  654.5 7.1 %broadcast_multiply_fusion = f32[27,512,128]{2,1,0:T(8,128)} fusion(f32[27,512,128]{2,1,0:T(8,128)} %get-tuple-element.479), kind=kLoop, calls=%fused_computation.335 | loop fusion | flops 1769472 | bytes 14155776 | tf_op jit(solution)/shard_map/mul | solution.py:162
  661.5 3.9 broadcast_multiply_fusion.1
  (1051 shorter events, 162.2 us)
Async XLA Ops:
  7.2 28.4 %copy-start = (bf16[1,128,1024]{2,1,0:T(8,128)(2,1)S(1)}, bf16[1,128,1024]{2,1,0:T(8,128)(2,1)}, u32[]{:S(2)}) copy-start(bf16[1,128,1024]{2,1,0:T(8,128)(2,1)} %param.9) | copy-start | bytes 786436
  7.2 78.9 %reduce-scatter.3.cloned.1.call-start = ((), (), s32[]{:S(2)}) async-start(), calls=%async_computation.2 | async-start | bytes 2621440 | tf_op jit(solution)/shard_map/reduce_scatter | solution.py:103
  36.7 3.6 copy-start.10
  36.7 6.5 copy-start.7
  40.3 3.0 copy-start.1
  43.2 5.4 copy-start.9
  48.6 75.9 %reduce-scatter.5.cloned.1.call-start = ((), (), s32[]{:S(2)}) async-start(), calls=%async_computation.4 | async-start | bytes 2621440 | tf_op jit(solution)/shard_map/reduce_scatter | solution.py:133
  56.3 71.9 %copy-start.8 = (bf16[27,128,512]{2,1,0:T(8,128)(2,1)S(1)}, bf16[27,128,512]{2,1,0:T(8,128)(2,1)}, u32[]{:S(2)}) copy-start(bf16[27,128,512]{2,1,0:T(8,128)(2,1)} %param.10) | copy-start | bytes 10616836
  56.3 98.4 %all-gather.5.cloned.1.call-start = ((), (), s32[]{:S(2)}) async-start(), calls=%async_computation.5 | async-start | bytes 1310720 | tf_op jit(solution)/shard_map/all_gather | solution.py:140
  128.1 151.8 %all-gather.3.cloned.1.call-start = ((), (), s32[]{:S(2)}) async-start(), calls=%async_computation.3 | async-start | bytes 1310720 | tf_op jit(solution)/shard_map/all_gather | solution.py:110
  131.8 522.7 %all-reduce.7.cloned.1.call-start = ((), (), s32[]{:S(2)}) async-start(), calls=%async_computation.6 | async-start | bytes 28311552 | tf_op jit(solution)/shard_map/psum | solution.py:160
  160.0 1.0 copy-start.4
  167.6 6.3 copy-start.5
  173.9 1.0 copy-start.4
  181.6 6.3 copy-start.5
  187.9 1.0 copy-start.4
  195.6 6.3 copy-start.5
  201.9 1.0 copy-start.4
  209.6 6.3 copy-start.5
  215.9 1.0 copy-start.4
  223.6 6.3 copy-start.5
  230.0 1.0 copy-start.4
  237.6 6.3 copy-start.5
  244.0 1.0 copy-start.4
  251.6 6.3 copy-start.5
  258.0 1.0 copy-start.4
  265.7 6.3 copy-start.5
  369.8 14.5 %copy-start.3 = (f32[128,1024]{1,0:T(8,128)S(1)}, f32[128,1024]{1,0:T(8,128)}, u32[]{:S(2)}) copy-start(f32[128,1024]{1,0:T(8,128)} %get-tuple-element.382) | copy-start | bytes 1572868
  369.8 15.3 %copy-start.2 = (f32[128,1024]{1,0:T(8,128)S(1)}, f32[128,1024]{1,0:T(8,128)}, u32[]{:S(2)}) copy-start(f32[128,1024]{1,0:T(8,128)} %get-tuple-element.381) | copy-start | bytes 1572868
  654.5 7.1 %copy-start.6 = (f32[27,128,512]{2,1,0:T(8,128)S(1)}, f32[27,128,512]{2,1,0:T(8,128)}, u32[]{:S(2)}) copy-start(f32[27,128,512]{2,1,0:T(8,128)} %get-tuple-element.478) | copy-start | bytes 21233668
Sparse Core Ops, SparseCore 0:
  48.7 37.2 reduce-scatter.2
  89.3 35.1 reduce-scatter.4
  128.3 26.4 all-gather.4
  157.0 26.6 all-gather.2
  369.9 284.5 all-reduce.6
where the time goes:
time: 675 us; the launch traced here: 672 us
  waiting for transfers between devices  356 us (53%)
  matrix products  129 us (19%)
  other arithmetic  110 us (16%)
  local copies, waits for them, and re-layouts  42.3 us (6%)
  between operations  14.4 us (2%)
  blocking collectives  14 us (2%)
    psum x1, waiting for transfers between devices, shards(): lax.psum((first_grad, second_grad, gain_part), 'dp')  269 us
    while x416, other arithmetic  52.8 us
    dot_general x8, matrix products, first_one_block(): lax.dot_general(volume_cols, rows, contract_cells, preferred_element_type...  50.6 us
    reduce_scatter x1, waiting for transfers between devices, shards(): lax.psum_scatter(lax.dot_general(weights, target_cols, contract_second, p...  36 us
    unnamed x53, other arithmetic  30.7 us
    reduce_scatter x1, waiting for transfers between devices, shards(): lax.psum_scatter(lax.dot_general(weights, volume_cols, contract_first, pr...  28.6 us
    dot_general x8, matrix products, second_one_block(): lax.dot_general(cols, target, contract_cells, preferred_element_type=jnp....  23.6 us
    all_gather x1, waiting for transfers between devices, shards(): grad_rows = lax.all_gather(dpre_own, 'chan', axis=0, tiled=True)  22.9 us
  transfers between devices with their start and end apart: 5, of which 4 were waited for; matrix products, arithmetic and copies ran while one was open for 20% of the time, Pallas kernels for 0%

commit v1 on v0

v1 whole, which is shorter than its diff:
```python
import functools
import math

import jax
import jax.numpy as jnp
from jax import lax
from jax.experimental import pallas as pl
from jax.experimental.pallas import tpu as pltpu
from jax.sharding import PartitionSpec as P

DEPTH, HEIGHT, WIDTH = 4, 16, 16
PLANE = HEIGHT * WIDTH
CELLS = DEPTH * PLANE
TAPS = [(a, b, c) for a in (-1, 0, 1) for b in (-1, 0, 1) for c in (-1, 0, 1)]
NORM_EPS = 1e-05
LIMIT = 56 * 1024 * 1024
F32, BF16 = jnp.float32, jnp.bfloat16
NT = (((1,), (1,)), ((), ()))


def params():
    return pltpu.CompilerParams(
        dimension_semantics=("arbitrary",), vmem_limit_bytes=LIMIT
    )


def whole(shape):
    return pl.BlockSpec(shape, lambda *_: (0,) * len(shape))


def smem():
    return pl.BlockSpec(memory_space=pltpu.SMEM)


def fill_padded(padded, rows_first, sign):
    padded[...] = jnp.zeros_like(padded)
    cells = rows_first.astype(F32).T
    width_at = lax.broadcasted_iota(jnp.int32, cells.shape, 0) % WIDTH
    for c in (-1, 0, 1):
        off = sign * c
        moved = cells if off == 0 else pltpu.roll(cells, (-off) % CELLS, 0)
        inside = (width_at + off >= 0) & (width_at + off < WIDTH)
        moved = jnp.where(inside, moved, 0.0).astype(BF16)
        padded[1 + c, 1 : 1 + DEPTH, 1 : 1 + HEIGHT] = moved.reshape(
            DEPTH, HEIGHT, WIDTH, cells.shape[1]
        )


def tap_cells(padded, plane, tap, sign):
    a, b, c = tap
    low = 1 + sign * b
    rows = padded[1 + c, plane + (1 + sign * a), low : low + HEIGHT]
    return rows.reshape(PLANE, rows.shape[-1])


def pre_kernel(n, idx, vol, w, *refs):
    outs, padded, shares = refs[:n], refs[n], refs[n + 1]
    rows = vol.shape[0]
    plane = pl.program_id(0)

    @pl.when(plane == 0)
    def _():
        fill_padded(padded, vol[...], 1)

    lhs = jnp.concatenate([tap_cells(padded, plane, tap, 1) for tap in TAPS], axis=1)
    sums = jnp.dot(lhs, w[...], preferred_element_type=F32).astype(BF16)
    for j in range(n):
        shares[j] = sums[:, j * rows : (j + 1) * rows]
    for m in range(n):
        outs[m][...] = shares[idx[0] ^ m]


def dact_kernel(n, idx, cot, w, *refs):
    outs, padded, shares, wide = refs[:n], refs[n], refs[n + 1], refs[n + 2]
    rows = cot.shape[0]
    plane = pl.program_id(0)

    @pl.when(plane == 0)
    def _():
        fill_padded(padded, cot[...], -1)
        for t in range(27):
            wide[:, t * rows : (t + 1) * rows] = w[t]

    lhs = jnp.concatenate([tap_cells(padded, plane, tap, -1) for tap in TAPS], axis=1)
    sums = lax.dot_general(lhs, wide[...], NT, preferred_element_type=F32).astype(BF16)
    for j in range(n):
        shares[j] = sums[:, j * rows : (j + 1) * rows]
    for m in range(n):
        outs[m][...] = shares[idx[0] ^ m]


def spread_shares(kernel, name, idx, n, field, w, extra):
    rows = field.shape[0]
    return pl.pallas_call(
        functools.partial(kernel, n),
        grid=(DEPTH,),
        in_specs=[smem(), whole(field.shape), whole(w.shape)],
        out_specs=[pl.BlockSpec((PLANE, rows), lambda d: (d, 0))] * n,
        out_shape=[jax.ShapeDtypeStruct((CELLS, rows), BF16)] * n,
        scratch_shapes=[
            pltpu.VMEM((3, DEPTH + 2, HEIGHT + 2, WIDTH, rows), BF16),
            pltpu.VMEM((n, PLANE, rows), BF16),
        ]
        + extra,
        compiler_params=params(),
        cost_estimate=pl.CostEstimate(
            flops=2 * 27 * rows * rows * n * CELLS, bytes_accessed=2 * w.size, transcendentals=0
        ),
        name=name,
    )(idx, field, w)


def norm_kernel(n, gain, *refs):
    shares, act, normed_out, inverse_out = refs[:n], refs[n], refs[n + 1], refs[n + 2]
    pre = shares[0][...].astype(F32)
    for m in range(1, n):
        pre = pre + shares[m][...].astype(F32)
    center = pre - jnp.mean(pre, axis=0, keepdims=True)
    inverse = lax.rsqrt(jnp.mean(center * center, axis=0, keepdims=True) + NORM_EPS)
    normed = center * inverse
    scaled = gain[...] * normed
    act[...] = (scaled * jax.nn.sigmoid(scaled)).astype(BF16)
    normed_out[...] = normed
    inverse_out[...] = inverse


def norm_back_kernel(n, gain, normed_in, inverse, *refs):
    shares, dpre, gain_part = refs[:n], refs[n], refs[n + 1]
    dact = shares[0][...].astype(F32)
    for m in range(1, n):
        dact = dact + shares[m][...].astype(F32)
    normed = normed_in[...]
    scaled = gain[...] * normed
    sigma = jax.nn.sigmoid(scaled)
    dscaled = dact * sigma * (1.0 + scaled * (1.0 - sigma))
    product = dscaled * normed
    gain_part[...] = jnp.sum(product, axis=0, keepdims=True)
    dnormed = gain[...] * dscaled
    mean_first = jnp.mean(dnormed, axis=0, keepdims=True)
    mean_second = jnp.mean(dnormed * normed, axis=0, keepdims=True)
    dpre[...] = ((dnormed - mean_first - normed * mean_second) * inverse[...]).astype(BF16)


def conv_back_add(sums, products, plane, taps, rows, sign):
    for at, tap in enumerate(taps):
        a, b, c = tap
        a, b = sign * a, sign * b
        part = products[:, at * rows : (at + 1) * rows].reshape(HEIGHT, WIDTH, rows)
        low, high = max(0, b), HEIGHT + min(0, b)
        sums[1 + c, plane + (1 - a), low - b : high - b] += part[low:high]


def conv_finish(sums, out, sign):
    rows = out.shape[0]
    total = None
    for c in (-1, 0, 1):
        off = sign * c
        part = sums[1 + c, 1 : 1 + DEPTH].reshape(CELLS, rows)
        if off != 0:
            width_at = lax.broadcasted_iota(jnp.int32, part.shape, 0) % WIDTH
            inside = (width_at + off >= 0) & (width_at + off < WIDTH)
            part = jnp.where(inside, pltpu.roll(part, (-off) % CELLS, 0), 0.0)
        total = part if total is None else total + part
    out[...] = total.T.astype(BF16)


def conv_kernel(n, sign, transposed, idx, w, *refs):
    blocks, out, ordered, sums = refs[:n], refs[n], refs[n + 1], refs[n + 2]
    rows = out.shape[0]
    plane = pl.program_id(0)

    @pl.when(plane == 0)
    def _():
        sums[...] = jnp.zeros_like(sums)
        for m in range(n):
            ordered[idx[0] ^ m] = blocks[m][...]

    begin = pl.multiple_of(plane * PLANE, PLANE)
    lhs = jnp.concatenate([ordered[j, pl.ds(begin, PLANE)] for j in range(n)], axis=1)
    for t in range(0, 27, 2):
        taps = TAPS[t : t + 2]
        if transposed:
            rhs = w[t * rows : (t + len(taps)) * rows]
            products = lax.dot_general(lhs, rhs, NT, preferred_element_type=F32)
        else:
            rhs = jnp.concatenate([w[t + k] for k in range(len(taps))], axis=1)
            products = jnp.dot(lhs, rhs, preferred_element_type=F32)
        conv_back_add(sums, products, plane, taps, rows, sign)

    @pl.when(plane == DEPTH - 1)
    def _():
        conv_finish(sums, out, sign)


def conv_full(name, sign, transposed, idx, w, blocks):
    n, rows = len(blocks), blocks[0].shape[1]
    return pl.pallas_call(
        functools.partial(conv_kernel, n, sign, transposed),
        grid=(DEPTH,),
        in_specs=[smem(), whole(w.shape)] + [whole(blocks[0].shape)] * n,
        out_specs=whole((rows, CELLS)),
        out_shape=jax.ShapeDtypeStruct((rows, CELLS), BF16),
        scratch_shapes=[
            pltpu.VMEM((n, CELLS, rows), BF16),
            pltpu.VMEM((3, DEPTH + 2, HEIGHT, WIDTH, rows), F32),
        ],
        compiler_params=params(),
        cost_estimate=pl.CostEstimate(
            flops=2 * 27 * rows * rows * n * CELLS, bytes_accessed=2 * w.size, transcendentals=0
        ),
        name=name,
    )(idx, w, *blocks)


def grad_first_kernel(n, idx, vol, *refs):
    blocks, out, ordered, moved = refs[:n], refs[n], refs[n + 1], refs[n + 2]
    rows = vol.shape[0]
    step = pl.program_id(0)

    @pl.when(step == 0)
    def _():
        for m in range(n):
            ordered[idx[0] ^ m] = blocks[m][...]
        moved[...] = jnp.zeros_like(moved)
        cells = vol[...].astype(F32)
        at = lax.broadcasted_iota(jnp.int32, cells.shape, 1)
        height_at, width_at = at // WIDTH % HEIGHT, at % WIDTH
        for k in range(9):
            b, c = k // 3 - 1, k % 3 - 1
            off = b * WIDTH + c
            part = cells if off == 0 else pltpu.roll(cells, (-off) % CELLS, 1)
            inside = (height_at + b >= 0) & (height_at + b < HEIGHT)
            inside = inside & (width_at + c >= 0) & (width_at + c < WIDTH)
            part = jnp.where(inside, part, 0.0).astype(BF16)
            moved[k * rows : (k + 1) * rows, PLANE : PLANE + CELLS] = part

    lhs = moved[:, pl.ds(pl.multiple_of(step * PLANE, PLANE), CELLS)]
    rhs = jnp.concatenate([ordered[j] for j in range(n)], axis=1)
    grads = jnp.dot(lhs, rhs, preferred_element_type=F32).astype(BF16)
    out[...] = grads.reshape(9, rows, n * rows)


def grad_first(idx, vol, blocks):
    n, rows = len(blocks), vol.shape[0]
    return pl.pallas_call(
        functools.partial(grad_first_kernel, n),
        grid=(3,),
        in_specs=[smem(), whole(vol.shape)] + [whole(blocks[0].shape)] * n,
        out_specs=pl.BlockSpec((9, rows, n * rows), lambda a: (a, 0, 0)),
        out_shape=jax.ShapeDtypeStruct((27, rows, n * rows), BF16),
        scratch_shapes=[
            pltpu.VMEM((n, CELLS, rows), BF16),
            pltpu.VMEM((9 * rows, CELLS + 2 * PLANE), BF16),
        ],
        compiler_params=params(),
        cost_estimate=pl.CostEstimate(
            flops=2 * 27 * rows * rows * n * CELLS,
            bytes_accessed=2 * 27 * rows * rows * n,
            transcendentals=0,
        ),
        name="grad_first",
    )(idx, vol, *blocks)


def grad_second_kernel(n, idx, cot, *refs):
    blocks, out, ordered, padded = refs[:n], refs[n], refs[n + 1], refs[n + 2]
    rows = cot.shape[0]
    step = pl.program_id(0)

    @pl.when(step == 0)
    def _():
        for m in range(n):
            begin = pl.multiple_of((idx[0] ^ m) * rows, rows)
            ordered[pl.ds(begin, rows)] = blocks[m][...].astype(F32).T.astype(BF16)
        fill_padded(padded, cot[...], -1)

    lhs = ordered[...]
    for k in range(0, 9, 2):
        pieces = []
        for at in range(k, min(k + 2, 9)):
            b, c = at // 3 - 1, at % 3 - 1
            planes = padded[1 + c, pl.ds(2 - step, DEPTH), 1 - b : 1 - b + HEIGHT]
            pieces.append(planes.reshape(CELLS, rows))
        rhs = jnp.concatenate(pieces, axis=1)
        grads = jnp.dot(lhs, rhs, preferred_element_type=F32).astype(BF16)
        for at in range(len(pieces)):
            out[k + at] = grads[:, at * rows : (at + 1) * rows]


def grad_second(idx, cot, blocks):
    n, rows = len(blocks), cot.shape[0]
    return pl.pallas_call(
        functools.partial(grad_second_kernel, n),
        grid=(3,),
        in_specs=[smem(), whole(cot.shape)] + [whole(blocks[0].shape)] * n,
        out_specs=pl.BlockSpec((9, n * rows, rows), lambda a: (a, 0, 0)),
        out_shape=jax.ShapeDtypeStruct((27, n * rows, rows), BF16),
        scratch_shapes=[
            pltpu.VMEM((n * rows, CELLS), BF16),
            pltpu.VMEM((3, DEPTH + 2, HEIGHT + 2, WIDTH, rows), BF16),
        ],
        compiler_params=params(),
        cost_estimate=pl.CostEstimate(
            flops=2 * 27 * rows * rows * n * CELLS,
            bytes_accessed=2 * 27 * rows * rows * n,
            transcendentals=0,
        ),
        name="grad_second",
    )(idx, cot, *blocks)


def shards(volume, w_first, gain, w_second, cotangent):
    n = lax.axis_size("chan")
    rows = volume.shape[1]
    vol, cot = volume[0], cotangent[0]
    chan = lax.axis_index("chan")
    idx = chan.astype(jnp.int32).reshape(1)
    own_gain = lax.dynamic_slice_in_dim(gain, chan * rows, rows, 0)[None]

    def to_partner(x, m):
        return lax.ppermute(x, "chan", [(i, i ^ m) for i in range(n)])

    order = sorted(range(1, n), reverse=True)

    def swap(parts):
        got = {m: to_partner(parts[m], m) for m in order}
        return [parts[0]] + [got[m] for m in range(1, n)]

    def spread(own):
        return swap([own] * n)

    pre_shares = swap(
        spread_shares(pre_kernel, "pre", idx, n, vol, w_first.reshape(27 * rows, n * rows), [])
    )
    dact_shares = swap(
        spread_shares(
            dact_kernel, "dact", idx, n, cot, w_second, [pltpu.VMEM((n * rows, 27 * rows), BF16)]
        )
    )
    act, normed, inverse = pl.pallas_call(
        functools.partial(norm_kernel, n),
        out_shape=[
            jax.ShapeDtypeStruct((CELLS, rows), BF16),
            jax.ShapeDtypeStruct((CELLS, rows), F32),
            jax.ShapeDtypeStruct((1, rows), F32),
        ],
        compiler_params=pltpu.CompilerParams(vmem_limit_bytes=LIMIT),
        name="norm",
    )(own_gain, *pre_shares)
    act_blocks = spread(act)
    dpre, gain_part = pl.pallas_call(
        functools.partial(norm_back_kernel, n),
        out_shape=[
            jax.ShapeDtypeStruct((CELLS, rows), BF16),
            jax.ShapeDtypeStruct((1, rows), F32),
        ],
        compiler_params=pltpu.CompilerParams(vmem_limit_bytes=LIMIT),
        name="norm_back",
    )(own_gain, normed, inverse, *dact_shares)
    dpre_blocks = spread(dpre)
    factor = 1.0 / math.sqrt(lax.axis_size("dp") * CELLS)

    second_part = grad_second(idx, cot, act_blocks)
    second_total = lax.psum(second_part, "dp").astype(F32) * factor
    first_part = grad_first(idx, vol, dpre_blocks)
    first_total = lax.psum(first_part, "dp").astype(F32) * factor
    output = conv_full("output", 1, False, idx, w_second, act_blocks)
    grad_volume = conv_full(
        "grad_volume", -1, True, idx, w_first.reshape(27 * rows, n * rows), dpre_blocks
    )
    gain_total = lax.psum(gain_part[0], "dp") * factor
    return (output[None], grad_volume[None], first_total, gain_total, second_total)


def solution(mesh):
    placed = (
        P("dp", "chan", None),
        P(None, "chan", None),
        P(),
        P(None, None, "chan"),
        P("dp", "chan", None),
    )
    return jax.shard_map(
        shards,
        mesh=mesh,
        in_specs=placed,
        out_specs=(
            P("dp", "chan", None),
            P("dp", "chan", None),
            P(None, "chan", None),
            P("chan"),
            P(None, None, "chan"),
        ),
        check_vma=False,
    )
```

time: 675 us -> 250 us (0.37)
  waiting for transfers between devices: 356 us -> 139 us
  matrix products: 129 us -> 0 us
  other arithmetic: 110 us -> 10.5 us
  Pallas kernels: 0 us -> 52.6 us
  local copies, waits for them, and re-layouts: 42.3 us -> 5.05 us
  starting transfers between devices: 0.39 us -> 12 us
    psum x1, waiting for transfers between devices: 269 us -> 121 us  [shards(): first_total = lax.psum(first_part, 'dp').astype(F32) * factor]
    dot_general x34 -> x0, matrix products: 129 us -> none  [the longest x8 50.6 us: first_one_block(): lax.dot_general(volume_cols, rows, contract_cells, preferred_element_type...]
    reduce_scatter x2 -> x0, waiting for transfers between devices: 64.6 us -> none  [the longest x1 36 us: shards(): lax.psum_scatter(lax.dot_general(weights, target_cols, contract_second, p...]
    while x416 -> x0, other arithmetic: 52.8 us -> none
    pallas_call x0 -> x8, Pallas kernels: none -> 52.6 us  [the longest x2 16.3 us: spread_shares(): pl.pallas_call(functools.partial(kernel, n), grid=(DEPTH,), in_specs=[sme...]
    unnamed x53 -> x0, other arithmetic: 30.7 us -> none
    all_gather x2 -> x0, waiting for transfers between devices: 22.9 us -> none  [the longest x1 22.9 us: shards(): grad_rows = lax.all_gather(dpre_own, 'chan', axis=0, tiled=True)]
    ppermute x0 -> x12, waiting for transfers between devices: none -> 18 us  [to_partner(): return lax.ppermute(x, 'chan', [(i, i ^ m) for i in range(n)])]
  transfers between devices with their start and end apart: 5 -> 13, of which waited for: 4 -> 6; matrix products, arithmetic and copies ran while one was open for 20% -> 0% of each run, Pallas kernels for 0% -> 14%
where the time goes in v1:
time: 250 us; the launch traced here: 249 us
  waiting for transfers between devices  139 us (56%)
  Pallas kernels  52.6 us (21%)
  blocking collectives  15.8 us (6%)
  between operations  14.1 us (6%)
  starting transfers between devices  12 us (5%)
  other arithmetic  10.5 us (4%)
  local copies, waits for them, and re-layouts  5.05 us (2%)
    psum x1, waiting for transfers between devices, shards(): first_total = lax.psum(first_part, 'dp').astype(F32) * factor  121 us
    ppermute x12, waiting for transfers between devices, to_partner(): return lax.ppermute(x, 'chan', [(i, i ^ m) for i in range(n)])  18 us
    pallas_call x2, Pallas kernels, spread_shares(): pl.pallas_call(functools.partial(kernel, n), grid=(DEPTH,), in_specs=[sme...  16.3 us
    pallas_call x2, Pallas kernels, conv_full(): pl.pallas_call(functools.partial(conv_kernel, n, sign, transposed), grid=...  16.2 us
    psum x1, blocking collectives, shards(): gain_total = lax.psum(gain_part[0], 'dp') * factor  15.8 us
    ppermute x12, starting transfers between devices, to_partner(): return lax.ppermute(x, 'chan', [(i, i ^ m) for i in range(n)])  11.9 us
    pallas_call x1, Pallas kernels, grad_second(): pl.pallas_call(functools.partial(grad_second_kernel, n), grid=(3,), in_sp...  7.61 us
    pallas_call x1, Pallas kernels, grad_first(): pl.pallas_call(functools.partial(grad_first_kernel, n), grid=(3,), in_spe...  7.36 us
  transfers between devices with their start and end apart: 13, of which 6 were waited for; matrix products, arithmetic and copies ran while one was open for 0% of the time, Pallas kernels for 14%

profile of v1, /device:TPU:1, one launch (start us, length us, event | category | flops | bytes accessed | tf_op | source)
XLA Modules:
  0.0 248.8 jit_solution(17186345208590200365)
XLA Ops:
  7.2 7.8 %pre.1 = (bf16[1024,128]{1,0:T(8,128)(2,1)}, bf16[1024,128]{1,0:T(8,128)(2,1)}, bf16[1024,128]{1,0:T(8,128)(2,1)}, bf16[1024,128]{1,0:T(8,128)(2,1)}) custom-call(s32[1]{0:T(128)} %bitcast.idx, bf16[128,1024]{1,0:T(8,128)(2,1)} %bitcast.11, bf16[3456,512]{1,0:T(8,128)(2,1)} %bitcast.9), custom_call_target="tpu_custom_call" | custom-call | flops 3623878656 | bytes 3538944 | tf_op jit(solution)/shard_map/pre/pallas_call | solution.py:94
  15.0 2.0 collective-permute-start
  17.1 1.2 collective-permute-start.1
  18.3 8.5 %dact.1 = (bf16[1024,128]{1,0:T(8,128)(2,1)}, bf16[1024,128]{1,0:T(8,128)(2,1)}, bf16[1024,128]{1,0:T(8,128)(2,1)}, bf16[1024,128]{1,0:T(8,128)(2,1)}) custom-call(s32[1]{0:T(128)} %bitcast.idx, bf16[128,1024]{1,0:T(8,128)(2,1)} %bitcast.13, bf16[27,512,128]{2,1,0:T(8,128)(2,1)} %w.3), custom_call_target="tpu_custom_call" | custom-call | flops 3623878656 | bytes 3538944 | tf_op jit(solution)/shard_map/dact/pallas_call | solution.py:94
  26.8 1.4 collective-permute-start.6
  28.2 1.2 collective-permute-start.7
  29.5 0.6 dynamic-slice_bitcast_fusion.gain
  30.1 0.7 copy-done.5
  30.9 2.5 norm.1
  33.7 0.9 collective-permute-done.7.refs_2_
  34.6 5.8 %collective-permute-done.8.refs_3_ = bf16[1024,128]{1,0:T(8,128)(2,1)S(1)} collective-permute-done((bf16[1024,128]{1,0:T(8,128)(2,1)}, bf16[1024,128]{1,0:T(8,128)(2,1)S(1)}, u32[]{:S(2)}, u32[]{:S(2)}) %collective-permute-start.8) | collective-permute-done | bytes 262176 | tf_op jit(solution)/shard_map/ppermute | solution.py:321
  40.4 0.7 copy-done.7
  41.1 2.7 %norm_back.1 = (bf16[1024,128]{1,0:T(8,128)(2,1)}, f32[1,128]{1,0:T(1,128)}) custom-call(f32[1,128]{1,0:T(1,128)} %dynamic-slice_bitcast_fusion.gain, f32[1024,128]{1,0:T(8,128)} %get-tuple-element.23.normed_in, f32[1,128]{1,0:T(1,128)} %get-tuple-element.24.inverse, bf16[1024,128]{1,0:T(8,128)(2,1)} %get-tuple-element.25.refs_0_, ...), custom_call_target="tpu_custom_call" | custom-call | tf_op jit(solution)/shard_map/norm_back/pallas_call | solution.py:351
  43.7 1.2 collective-permute-start.11
  44.9 1.1 collective-permute-start.10
  46.4 1.2 collective-permute-start.5
  47.5 1.1 collective-permute-start.4
  48.6 1.5 collective-permute-done.11.refs_3_
  50.2 1.1 collective-permute-start.3
  51.2 9.3 %collective-permute-done.10.refs_2_ = bf16[1024,128]{1,0:T(8,128)(2,1)S(1)} collective-permute-done((bf16[1024,128]{1,0:T(8,128)(2,1)}, bf16[1024,128]{1,0:T(8,128)(2,1)S(1)}, u32[]{:S(2)}, u32[]{:S(2)}) %collective-permute-start.10) | collective-permute-done | bytes 262176 | tf_op jit(solution)/shard_map/ppermute | solution.py:321
  60.6 0.7 copy-done.9
  61.3 0.7 copy-done.10
  62.0 7.4 %grad_first.1 = bf16[27,128,512]{2,1,0:T(8,128)(2,1)} custom-call(s32[1]{0:T(128)} %bitcast.idx, bf16[128,1024]{1,0:T(8,128)(2,1)} %bitcast.12, bf16[1024,128]{1,0:T(8,128)(2,1)} %get-tuple-element.29.refs_0_, bf16[1024,128]{1,0:T(8,128)(2,1)} %copy-done.10, bf16[1024,128]{1,0:T(8,128)(2,1)} %copy-done.9, bf16[1024,128]{1,0:T(8,128)(2,1)} %copy-done.8), custom_call_target="tpu_custom_call" | custom-call | flops 3623878656 | bytes 3538944 | tf_op jit(solution)/shard_map/grad_first/pallas_call | solution.py:245
  69.4 0.7 copy-done.11
  70.3 0.7 copy-done.13
  71.0 7.6 %grad_second.1 = bf16[27,512,128]{2,1,0:T(8,128)(2,1)} custom-call(s32[1]{0:T(128)} %bitcast.idx, bf16[128,1024]{1,0:T(8,128)(2,1)} %bitcast.14, bf16[1024,128]{1,0:T(8,128)(2,1)} %get-tuple-element.22.refs_0_, bf16[1024,128]{1,0:T(8,128)(2,1)} %copy-done.13, bf16[1024,128]{1,0:T(8,128)(2,1)} %copy-done.12, bf16[1024,128]{1,0:T(8,128)(2,1)} %copy-done.11), custom_call_target="tpu_custom_call" | custom-call | flops 3623878656 | bytes 3538944 | tf_op jit(solution)/shard_map/grad_second/pallas_call | solution.py:292
  78.6 15.8 %psum.22 = f32[128]{0:T(128)S(1)} all-reduce(f32[128]{0:T(128)S(1)} %bitcast.15), channel_id=1, replica_groups=mesh['dp'=8,'chan'=4] {'dp'}, use_global_device_ids=true, to_apply=%region_1.0 | all-reduce | flops 128 | bytes 1024 | tf_op jit(solution)/shard_map/psum | solution.py:371
  95.0 8.1 %output.1 = bf16[128,1024]{1,0:T(8,128)(2,1)} custom-call(s32[1]{0:T(128)} %bitcast.idx, bf16[27,512,128]{2,1,0:T(8,128)(2,1)} %w.3, bf16[1024,128]{1,0:T(8,128)(2,1)} %get-tuple-element.22.refs_0_, bf16[1024,128]{1,0:T(8,128)(2,1)} %copy-done.13, bf16[1024,128]{1,0:T(8,128)(2,1)} %copy-done.12, bf16[1024,128]{1,0:T(8,128)(2,1)} %copy-done.11), custom_call_target="tpu_custom_call" | custom-call | flops 3623878656 | bytes 3538944 | tf_op jit(solution)/shard_map/output/pallas_call | solution.py:197
  103.0 8.2 %grad_volume.1 = bf16[128,1024]{1,0:T(8,128)(2,1)} custom-call(s32[1]{0:T(128)} %bitcast.idx, bf16[3456,512]{1,0:T(8,128)(2,1)} %bitcast.10, bf16[1024,128]{1,0:T(8,128)(2,1)} %get-tuple-element.29.refs_0_, bf16[1024,128]{1,0:T(8,128)(2,1)} %copy-done.10, bf16[1024,128]{1,0:T(8,128)(2,1)} %copy-done.9, bf16[1024,128]{1,0:T(8,128)(2,1)} %copy-done.8), custom_call_target="tpu_custom_call" | custom-call | flops 3623878656 | bytes 3538944 | tf_op jit(solution)/shard_map/grad_volume/pallas_call | solution.py:197
  111.2 120.8 %all-reduce.3.cloned.1.call-done = (bf16[27,128,512]{2,1,0:T(8,128)(2,1)}, bf16[27,512,128]{2,1,0:T(8,128)(2,1)}) async-done(((bf16[27,128,512]{2,1,0:T(8,128)(2,1)}, bf16[27,512,128]{2,1,0:T(8,128)(2,1)}), (bf16[27,128,512]{2,1,0:T(8,128)(2,1)}, bf16[27,512,128]{2,1,0:T(8,128)(2,1)})) %all-reduce.3.cloned.1.call-update) | async-done | bytes 7077904 | tf_op jit(solution)/shard_map/psum | solution.py:366
  232.0 6.2 %convert_multiply_fusion.1 = f32[27,128,512]{2,1,0:T(8,128)} fusion(bf16[27,128,512]{2,1,0:T(8,128)(2,1)} %get-tuple-element.31), kind=kLoop, calls=%fused_computation.1 | loop fusion | flops 3538944 | bytes 10616832 | tf_op jit(solution)/shard_map/mul | solution.py:366
  238.2 3.8 %convert_multiply_fusion = f32[27,512,128]{2,1,0:T(8,128)} fusion(bf16[27,512,128]{2,1,0:T(8,128)(2,1)S(1)} %copy-done.1), kind=kLoop, calls=%fused_computation | loop fusion | flops 3538944 | bytes 10616832 | tf_op jit(solution)/shard_map/mul | solution.py:364
  (38 shorter events, 1.8 us)
Async XLA Ops:
  7.2 22.3 %copy-start = (f32[512]{0:T(512)S(1)}, f32[512]{0:T(512)}, u32[]{:S(2)}) copy-start(f32[512]{0:T(512)} %param.7) | copy-start | bytes 6148
  7.2 224.8 %all-reduce.3.cloned.1.call-start = ((), (), s32[]{:S(2)}) async-start(), calls=%async_computation | async-start | bytes 14155776 | tf_op jit(solution)/shard_map/psum | solution.py:366
  15.0 14.4 %collective-permute-start = (bf16[1024,128]{1,0:T(8,128)(2,1)}, bf16[1024,128]{1,0:T(8,128)(2,1)S(1)}, u32[]{:S(2)}, u32[]{:S(2)}) collective-permute-start(bf16[1024,128]{1,0:T(8,128)(2,1)} %get-tuple-element.19), channel_id=1, source_target_pairs={{0,1},{1,0},{2,3},{3,2},{4,5},{5,4},{6,7},{7,6},{8,9},{9,8},{10,11... | collective-permute-start | bytes 786440 | tf_op jit(solution)/shard_map/ppermute | solution.py:321
  17.1 13.0 %collective-permute-start.1 = (bf16[1024,128]{1,0:T(8,128)(2,1)}, bf16[1024,128]{1,0:T(8,128)(2,1)S(1)}, u32[]{:S(2)}, u32[]{:S(2)}) collective-permute-start(bf16[1024,128]{1,0:T(8,128)(2,1)} %get-tuple-element.20), channel_id=1, source_target_pairs={{0,2},{1,3},{2,0},{3,1},{4,6},{5,7},{6,4},{7,5},{8,10},{9,11},{10,... | collective-permute-start | bytes 786440 | tf_op jit(solution)/shard_map/ppermute | solution.py:321
  18.3 11.8 %collective-permute-start.2 = (bf16[1024,128]{1,0:T(8,128)(2,1)}, bf16[1024,128]{1,0:T(8,128)(2,1)S(1)}, u32[]{:S(2)}, u32[]{:S(2)}) collective-permute-start(bf16[1024,128]{1,0:T(8,128)(2,1)} %get-tuple-element.21), channel_id=1, source_target_pairs={{0,3},{1,2},{2,1},{3,0},{4,7},{5,6},{6,5},{7,4},{8,11},{9,10},{10,... | collective-permute-start | bytes 786440 | tf_op jit(solution)/shard_map/ppermute | solution.py:321
  26.8 6.9 %collective-permute-start.6 = (bf16[1024,128]{1,0:T(8,128)(2,1)}, bf16[1024,128]{1,0:T(8,128)(2,1)S(1)}, u32[]{:S(2)}, u32[]{:S(2)}) collective-permute-start(bf16[1024,128]{1,0:T(8,128)(2,1)} %get-tuple-element.26), channel_id=1, source_target_pairs={{0,1},{1,0},{2,3},{3,2},{4,5},{5,4},{6,7},{7,6},{8,9},{9,8},{10,11... | collective-permute-start | bytes 786440 | tf_op jit(solution)/shard_map/ppermute | solution.py:321
  28.2 6.4 %collective-permute-start.7 = (bf16[1024,128]{1,0:T(8,128)(2,1)}, bf16[1024,128]{1,0:T(8,128)(2,1)S(1)}, u32[]{:S(2)}, u32[]{:S(2)}) collective-permute-start(bf16[1024,128]{1,0:T(8,128)(2,1)} %get-tuple-element.27), channel_id=1, source_target_pairs={{0,2},{1,3},{2,0},{3,1},{4,6},{5,7},{6,4},{7,5},{8,10},{9,11},{10,... | collective-permute-start | bytes 786440 | tf_op jit(solution)/shard_map/ppermute | solution.py:321
  29.4 0.7 copy-start.3
  29.4 10.9 %collective-permute-start.8 = (bf16[1024,128]{1,0:T(8,128)(2,1)}, bf16[1024,128]{1,0:T(8,128)(2,1)S(1)}, u32[]{:S(2)}, u32[]{:S(2)}) collective-permute-start(bf16[1024,128]{1,0:T(8,128)(2,1)} %get-tuple-element.28), channel_id=1, source_target_pairs={{0,3},{1,2},{2,1},{3,0},{4,7},{5,6},{6,5},{7,4},{8,11},{9,10},{10,... | collective-permute-start | bytes 786440 | tf_op jit(solution)/shard_map/ppermute | solution.py:321
  30.1 0.7 copy-start.5
  30.1 0.8 copy-start.6
  33.7 6.7 %copy-start.2 = (bf16[1024,128]{1,0:T(8,128)(2,1)}, bf16[1024,128]{1,0:T(8,128)(2,1)S(1)}, u32[]{:S(2)}) copy-start(bf16[1024,128]{1,0:T(8,128)(2,1)S(1)} %collective-permute-done.6.refs_1_) | copy-start | bytes 786436
  34.6 5.8 %copy-start.4 = (bf16[1024,128]{1,0:T(8,128)(2,1)}, bf16[1024,128]{1,0:T(8,128)(2,1)S(1)}, u32[]{:S(2)}) copy-start(bf16[1024,128]{1,0:T(8,128)(2,1)S(1)} %collective-permute-done.7.refs_2_) | copy-start | bytes 786436
  40.4 0.7 copy-start.7
  43.7 6.4 %collective-permute-start.11 = (bf16[1024,128]{1,0:T(8,128)(2,1)}, bf16[1024,128]{1,0:T(8,128)(2,1)S(1)}, u32[]{:S(2)}, u32[]{:S(2)}) collective-permute-start(bf16[1024,128]{1,0:T(8,128)(2,1)} %get-tuple-element.29.refs_0_), channel_id=1, source_target_pairs={{0,3},{1,2},{2,1},{3,0},{4,7},{5,6},{6,5},{7,4},{8,11},{9,10},{10,... | collective-permute-start | bytes 786440 | tf_op jit(solution)/shard_map/ppermute | solution.py:321
  44.9 15.7 %collective-permute-start.10 = (bf16[1024,128]{1,0:T(8,128)(2,1)}, bf16[1024,128]{1,0:T(8,128)(2,1)S(1)}, u32[]{:S(2)}, u32[]{:S(2)}) collective-permute-start(bf16[1024,128]{1,0:T(8,128)(2,1)} %get-tuple-element.29.refs_0_), channel_id=1, source_target_pairs={{0,2},{1,3},{2,0},{3,1},{4,6},{5,7},{6,4},{7,5},{8,10},{9,11},{10,... | collective-permute-start | bytes 786440 | tf_op jit(solution)/shard_map/ppermute | solution.py:321
  46.0 14.6 %collective-permute-start.9 = (bf16[1024,128]{1,0:T(8,128)(2,1)}, bf16[1024,128]{1,0:T(8,128)(2,1)S(1)}, u32[]{:S(2)}, u32[]{:S(2)}) collective-permute-start(bf16[1024,128]{1,0:T(8,128)(2,1)} %get-tuple-element.29.refs_0_), channel_id=1, source_target_pairs={{0,1},{1,0},{2,3},{3,2},{4,5},{5,4},{6,7},{7,6},{8,9},{9,8},{10,11... | collective-permute-start | bytes 786440 | tf_op jit(solution)/shard_map/ppermute | solution.py:321
  46.4 23.0 %collective-permute-start.5 = (bf16[1024,128]{1,0:T(8,128)(2,1)}, bf16[1024,128]{1,0:T(8,128)(2,1)S(1)}, u32[]{:S(2)}, u32[]{:S(2)}) collective-permute-start(bf16[1024,128]{1,0:T(8,128)(2,1)} %get-tuple-element.22.refs_0_), channel_id=1, source_target_pairs={{0,3},{1,2},{2,1},{3,0},{4,7},{5,6},{6,5},{7,4},{8,11},{9,10},{10,... | collective-permute-start | bytes 786440 | tf_op jit(solution)/shard_map/ppermute | solution.py:321
  47.5 21.9 %collective-permute-start.4 = (bf16[1024,128]{1,0:T(8,128)(2,1)}, bf16[1024,128]{1,0:T(8,128)(2,1)S(1)}, u32[]{:S(2)}, u32[]{:S(2)}) collective-permute-start(bf16[1024,128]{1,0:T(8,128)(2,1)} %get-tuple-element.22.refs_0_), channel_id=1, source_target_pairs={{0,2},{1,3},{2,0},{3,1},{4,6},{5,7},{6,4},{7,5},{8,10},{9,11},{10,... | collective-permute-start | bytes 786440 | tf_op jit(solution)/shard_map/ppermute | solution.py:321
  50.2 10.4 %copy-start.8 = (bf16[1024,128]{1,0:T(8,128)(2,1)}, bf16[1024,128]{1,0:T(8,128)(2,1)S(1)}, u32[]{:S(2)}) copy-start(bf16[1024,128]{1,0:T(8,128)(2,1)S(1)} %collective-permute-done.11.refs_3_) | copy-start | bytes 786436
  50.2 19.3 %collective-permute-start.3 = (bf16[1024,128]{1,0:T(8,128)(2,1)}, bf16[1024,128]{1,0:T(8,128)(2,1)S(1)}, u32[]{:S(2)}, u32[]{:S(2)}) collective-permute-start(bf16[1024,128]{1,0:T(8,128)(2,1)} %get-tuple-element.22.refs_0_), channel_id=1, source_target_pairs={{0,1},{1,0},{2,3},{3,2},{4,5},{5,4},{6,7},{7,6},{8,9},{9,8},{10,11... | collective-permute-start | bytes 786440 | tf_op jit(solution)/shard_map/ppermute | solution.py:321
  60.6 0.7 copy-start.9
  61.3 0.7 copy-start.10
  69.4 9.2 %copy-start.14 = (f32[1,128]{1,0:T(1,128)S(1)}, f32[1,128]{1,0:T(1,128)}, u32[]{:S(2)}) copy-start(f32[1,128]{1,0:T(1,128)} %get-tuple-element.30) | copy-start | bytes 1540
  69.4 0.7 copy-start.11
  69.4 0.8 copy-start.12
  70.3 0.7 copy-start.13
  232.0 6.2 %copy-start.1 = (bf16[27,512,128]{2,1,0:T(8,128)(2,1)S(1)}, bf16[27,512,128]{2,1,0:T(8,128)(2,1)}, u32[]{:S(2)}) copy-start(bf16[27,512,128]{2,1,0:T(8,128)(2,1)} %get-tuple-element.32) | copy-start | bytes 10616836
Sparse Core Ops, SparseCore 0:
  78.7 153.2 all-reduce.2

commit v2 on v1

--- a/solution.py
+++ b/solution.py
@@ -13,7 +13,7 @@
 CELLS = DEPTH * PLANE
 TAPS = [(a, b, c) for a in (-1, 0, 1) for b in (-1, 0, 1) for c in (-1, 0, 1)]
 NORM_EPS = 1e-05
-LIMIT = 56 * 1024 * 1024
+LIMIT = 26 * 1024 * 1024
 F32, BF16 = jnp.float32, jnp.bfloat16
 NT = (((1,), (1,)), ((), ()))
 
@@ -212,122 +212,235 @@
     )(idx, w, *blocks)
 
 
-def grad_first_kernel(n, idx, vol, *refs):
-    blocks, out, ordered, moved = refs[:n], refs[n], refs[n + 1], refs[n + 2]
-    rows = vol.shape[0]
-    step = pl.program_id(0)
-
-    @pl.when(step == 0)
-    def _():
-        for m in range(n):
-            ordered[idx[0] ^ m] = blocks[m][...]
-        moved[...] = jnp.zeros_like(moved)
-        cells = vol[...].astype(F32)
+def halves_kernel(n, turned, idx, *refs):
+    blocks, keep, send = refs[:n], refs[n], refs[n + 1]
+    half = n // 2
+    rows = blocks[0].shape[1]
+
+    def put(out, at, block):
+        if turned:
+            out[pl.ds(pl.multiple_of(at * rows, rows), rows)] = block[...].astype(F32).T.astype(BF16)
+        else:
+            out[at] = block[...]
+
+    def split(kept, sent):
+        for m in range(half):
+            at = (idx[0] ^ m) & (half - 1)
+            put(keep, at, blocks[kept + m])
+            put(send, at, blocks[sent + m])
+
+    @pl.when(idx[1] == 0)
+    def _():
+        split(0, half)
+
+    @pl.when(idx[1] != 0)
+    def _():
+        split(half, 0)
+
+
+def halves(name, turned, idx, blocks):
+    n, rows = len(blocks), blocks[0].shape[1]
+    shape = (n // 2 * rows, CELLS) if turned else (n // 2, CELLS, rows)
+    return pl.pallas_call(
+        functools.partial(halves_kernel, n, turned),
+        in_specs=[smem()] + [pl.BlockSpec(memory_space=pltpu.VMEM)] * n,
+        out_shape=[jax.ShapeDtypeStruct(shape, BF16)] * 2,
+        compiler_params=pltpu.CompilerParams(vmem_limit_bytes=LIMIT),
+        name=name,
+    )(idx, *blocks)
+
+
+def moved_first_kernel(own, other, out):
+    for which, ref in enumerate((own, other)):
+        cells = ref[...].astype(F32)
         at = lax.broadcasted_iota(jnp.int32, cells.shape, 1)
         height_at, width_at = at // WIDTH % HEIGHT, at % WIDTH
+        rows = cells.shape[0]
         for k in range(9):
             b, c = k // 3 - 1, k % 3 - 1
             off = b * WIDTH + c
             part = cells if off == 0 else pltpu.roll(cells, (-off) % CELLS, 1)
             inside = (height_at + b >= 0) & (height_at + b < HEIGHT)
             inside = inside & (width_at + c >= 0) & (width_at + c < WIDTH)
+            out[which, k * rows : (k + 1) * rows] = jnp.where(inside, part, 0.0).astype(BF16)
+
+
+def moved_second_kernel(own, other, out):
+    out[...] = jnp.zeros_like(out)
+    for which, ref in enumerate((own, other)):
+        cells = ref[...].astype(F32).T
+        width_at = lax.broadcasted_iota(jnp.int32, cells.shape, 0) % WIDTH
+        for c in (-1, 0, 1):
+            part = cells if c == 0 else pltpu.roll(cells, c % CELLS, 0)
+            inside = (width_at - c >= 0) & (width_at - c < WIDTH)
             part = jnp.where(inside, part, 0.0).astype(BF16)
-            moved[k * rows : (k + 1) * rows, PLANE : PLANE + CELLS] = part
-
-    lhs = moved[:, pl.ds(pl.multiple_of(step * PLANE, PLANE), CELLS)]
-    rhs = jnp.concatenate([ordered[j] for j in range(n)], axis=1)
-    grads = jnp.dot(lhs, rhs, preferred_element_type=F32).astype(BF16)
-    out[...] = grads.reshape(9, rows, n * rows)
-
-
-def grad_first(idx, vol, blocks):
-    n, rows = len(blocks), vol.shape[0]
-    return pl.pallas_call(
-        functools.partial(grad_first_kernel, n),
+            out[which, 1 + c, :, 1 : 1 + HEIGHT] = part.reshape(
+                DEPTH, HEIGHT, WIDTH, cells.shape[1]
+            )
+
+
+def moved_fields(kernel, name, shape, own, other):
+    return pl.pallas_call(
+        kernel,
+        out_shape=jax.ShapeDtypeStruct(shape, BF16),
+        compiler_params=pltpu.CompilerParams(vmem_limit_bytes=LIMIT),
+        name=name,
+    )(own, other)
+
+
+def grad_first_kernel(a, moved, own, other, out):
+    rows, half = out.shape[1], own.shape[0]
+    begin, count = max(0, -a) * PLANE, (DEPTH - abs(a)) * PLANE
+    grads = None
+    for which, ref in enumerate((own, other)):
+        rhs = jnp.concatenate([ref[j, begin : begin + count] for j in range(half)], axis=1)
+        lhs = moved[which, :, begin + a * PLANE : begin + a * PLANE + count]
+        part = jnp.dot(lhs, rhs, preferred_element_type=F32)
+        grads = part if grads is None else grads + part
+    out[...] = grads.astype(BF16).reshape(out.shape)
+
+
+def grad_first(a, moved, own, other):
+    half, cells, rows = own.shape
+    return pl.pallas_call(
+        functools.partial(grad_first_kernel, a),
         grid=(3,),
-        in_specs=[smem(), whole(vol.shape)] + [whole(blocks[0].shape)] * n,
-        out_specs=pl.BlockSpec((9, rows, n * rows), lambda a: (a, 0, 0)),
-        out_shape=jax.ShapeDtypeStruct((27, rows, n * rows), BF16),
-        scratch_shapes=[
-            pltpu.VMEM((n, CELLS, rows), BF16),
-            pltpu.VMEM((9 * rows, CELLS + 2 * PLANE), BF16),
+        in_specs=[
+            pl.BlockSpec((2, 3 * rows, cells), lambda b: (0, b, 0)),
+            whole(own.shape),
+            whole(own.shape),
         ],
+        out_specs=pl.BlockSpec((3, rows, half * rows), lambda b: (b, 0, 0)),
+        out_shape=jax.ShapeDtypeStruct((9, rows, half * rows), BF16),
         compiler_params=params(),
         cost_estimate=pl.CostEstimate(
-            flops=2 * 27 * rows * rows * n * CELLS,
-            bytes_accessed=2 * 27 * rows * rows * n,
+            flops=2 * 9 * rows * rows * half * 2 * (DEPTH - abs(a)) * PLANE,
+            bytes_accessed=2 * moved.size,
             transcendentals=0,
         ),
         name="grad_first",
-    )(idx, vol, *blocks)
-
-
-def grad_second_kernel(n, idx, cot, *refs):
-    blocks, out, ordered, padded = refs[:n], refs[n], refs[n + 1], refs[n + 2]
-    rows = cot.shape[0]
-    step = pl.program_id(0)
-
-    @pl.when(step == 0)
-    def _():
-        for m in range(n):
-            begin = pl.multiple_of((idx[0] ^ m) * rows, rows)
-            ordered[pl.ds(begin, rows)] = blocks[m][...].astype(F32).T.astype(BF16)
-        fill_padded(padded, cot[...], -1)
-
-    lhs = ordered[...]
+    )(moved, own, other)
+
+
+def grad_second_kernel(a, moved, own, other, out):
+    rows = out.shape[2]
+    begin, planes = max(0, a), DEPTH - abs(a)
+    lhs = [
+        ref[:, begin * PLANE : (begin + planes) * PLANE] for ref in (own, other)
+    ]
     for k in range(0, 9, 2):
-        pieces = []
-        for at in range(k, min(k + 2, 9)):
-            b, c = at // 3 - 1, at % 3 - 1
-            planes = padded[1 + c, pl.ds(2 - step, DEPTH), 1 - b : 1 - b + HEIGHT]
-            pieces.append(planes.reshape(CELLS, rows))
-        rhs = jnp.concatenate(pieces, axis=1)
-        grads = jnp.dot(lhs, rhs, preferred_element_type=F32).astype(BF16)
-        for at in range(len(pieces)):
-            out[k + at] = grads[:, at * rows : (at + 1) * rows]
-
-
-def grad_second(idx, cot, blocks):
-    n, rows = len(blocks), cot.shape[0]
-    return pl.pallas_call(
-        functools.partial(grad_second_kernel, n),
-        grid=(3,),
-        in_specs=[smem(), whole(cot.shape)] + [whole(blocks[0].shape)] * n,
-        out_specs=pl.BlockSpec((9, n * rows, rows), lambda a: (a, 0, 0)),
-        out_shape=jax.ShapeDtypeStruct((27, n * rows, rows), BF16),
-        scratch_shapes=[
-            pltpu.VMEM((n * rows, CELLS), BF16),
-            pltpu.VMEM((3, DEPTH + 2, HEIGHT + 2, WIDTH, rows), BF16),
-        ],
-        compiler_params=params(),
+        taps = range(k, min(k + 2, 9))
+        grads = None
+        for which in range(2):
+            pieces = []
+            for at in taps:
+                b, c = at // 3 - 1, at % 3 - 1
+                piece = moved[which, 1 + c, begin - a : begin - a + planes, 1 - b : 1 - b + HEIGHT]
+                pieces.append(piece.reshape(planes * PLANE, rows))
+            rhs = jnp.concatenate(pieces, axis=1)
+            part = jnp.dot(lhs[which], rhs, preferred_element_type=F32)
+            grads = part if grads is None else grads + part
+        for place, at in enumerate(taps):
+            out[at] = grads[:, place * rows : (place + 1) * rows].astype(BF16)
+
+
+def grad_second(a, moved, own, other):
+    wide, rows = own.shape[0], moved.shape[-1]
+    return pl.pallas_call(
+        functools.partial(grad_second_kernel, a),
+        out_shape=jax.ShapeDtypeStruct((9, wide, rows), BF16),
+        compiler_params=pltpu.CompilerParams(vmem_limit_bytes=LIMIT),
         cost_estimate=pl.CostEstimate(
-            flops=2 * 27 * rows * rows * n * CELLS,
-            bytes_accessed=2 * 27 * rows * rows * n,
+            flops=2 * 9 * rows * wide * 2 * (DEPTH - abs(a)) * PLANE,
+            bytes_accessed=2 * moved.size,
             transcendentals=0,
         ),
         name="grad_second",
-    )(idx, cot, *blocks)
+    )(moved, own, other)
+
+
+def finish_kernel(n, axis, factor, idx, own, other, *refs):
+    out = refs[-1]
+    upper = (idx[0] >= n // 2).astype(jnp.int32) ^ idx[1]
+    wide = own.shape[axis]
+
+    def put(low, high):
+        parts = (low[...].astype(F32) * factor, high[...].astype(F32) * factor)
+        if axis == 1:
+            out[:, :wide] = parts[0]
+            out[:, wide:] = parts[1]
+        else:
+            out[:, :, :wide] = parts[0]
+            out[:, :, wide:] = parts[1]
+
+    @pl.when(upper == 0)
+    def _():
+        put(own, other)
+
+    @pl.when(upper != 0)
+    def _():
+        put(other, own)
+
+
+def finish(name, n, axis, factor, idx, chunk, own, other, before):
+    taps, height, width = own.shape
+    block = (3, height * 2, width) if axis == 1 else (3, height, width * 2)
+    steps = taps // 3
+    part = pl.BlockSpec((3, height, width), lambda k: (k, 0, 0))
+    given = [] if before is None else [before]
+    return pl.pallas_call(
+        functools.partial(finish_kernel, n, axis, factor),
+        grid=(steps,),
+        in_specs=[smem(), part, part] + [pl.BlockSpec(memory_space=pl.ANY)] * len(given),
+        out_specs=pl.BlockSpec(block, lambda k: (chunk * steps + k, 0, 0)),
+        out_shape=jax.ShapeDtypeStruct((27,) + block[1:], F32),
+        input_output_aliases={3: 0} if given else {},
+        compiler_params=params(),
+        name=name,
+    )(idx, own, other, *given)
+
+
+def add_rounded(x, y):
+    return (x.astype(F32) + y.astype(F32)).astype(BF16)
+
+
+def line_sum(part):
+    chips = lax.axis_size("dp") // 2
+    at = lax.axis_index("dp") // 2
+
+    def send(x, moves):
+        return lax.ppermute(x, "dp", [(2 * i + k, 2 * j + k) for i, j in moves for k in (0, 1)])
+
+    total = part
+    for hop in range(chips // 2 - 1):
+        got = send(total, [(hop, hop + 1), (chips - 1 - hop, chips - 2 - hop)])
+        total = add_rounded(part, got)
+    mid = chips // 2
+    total = add_rounded(total, send(total, [(mid - 1, mid), (mid, mid - 1)]))
+    for hop in reversed(range(chips // 2 - 1)):
+        got = send(total, [(hop + 1, hop), (chips - 2 - hop, chips - 1 - hop)])
+        total = jnp.where((at == hop) | (at == chips - 1 - hop), got, total)
+    return total
 
 
 def shards(volume, w_first, gain, w_second, cotangent):
     n = lax.axis_size("chan")
     rows = volume.shape[1]
     vol, cot = volume[0], cotangent[0]
-    chan = lax.axis_index("chan")
-    idx = chan.astype(jnp.int32).reshape(1)
+    chan, place = lax.axis_index("chan"), lax.axis_index("dp")
+    idx = jnp.stack([chan, place % 2]).astype(jnp.int32)
     own_gain = lax.dynamic_slice_in_dim(gain, chan * rows, rows, 0)[None]
+    factor = 1.0 / math.sqrt(lax.axis_size("dp") * CELLS)
 
     def to_partner(x, m):
         return lax.ppermute(x, "chan", [(i, i ^ m) for i in range(n)])
 
-    order = sorted(range(1, n), reverse=True)
+    def to_core(x):
+        return lax.ppermute(x, "dp", [(i, i ^ 1) for i in range(lax.axis_size("dp"))])
 
     def swap(parts):
-        got = {m: to_partner(parts[m], m) for m in order}
+        got = {m: to_partner(parts[m], m) for m in reversed(range(1, n))}
         return [parts[0]] + [got[m] for m in range(1, n)]
-
-    def spread(own):
-        return swap([own] * n)
 
     pre_shares = swap(
         spread_shares(pre_kernel, "pre", idx, n, vol, w_first.reshape(27 * rows, n * rows), [])
@@ -336,6 +449,16 @@
         spread_shares(
             dact_kernel, "dact", idx, n, cot, w_second, [pltpu.VMEM((n * rows, 27 * rows), BF16)]
         )
+    )
+    moved_cot = moved_fields(
+        moved_second_kernel,
+        "moved_second",
+        (2, 3, DEPTH, HEIGHT + 2, WIDTH, rows),
+        cot,
+        to_core(cot),
+    )
+    moved_vol = moved_fields(
+        moved_first_kernel, "moved_first", (2, 9 * rows, CELLS), vol, to_core(vol)
     )
     act, normed, inverse = pl.pallas_call(
         functools.partial(norm_kernel, n),
@@ -347,7 +470,17 @@
         compiler_params=pltpu.CompilerParams(vmem_limit_bytes=LIMIT),
         name="norm",
     )(own_gain, *pre_shares)
-    act_blocks = spread(act)
+    act_blocks = swap([act] * n)
+    act_keep, act_send = halves("act_halves", True, idx, act_blocks)
+    act_other = to_core(act_send)
+    second_total = None
+    for chunk, a in enumerate((-1, 0, 1)):
+        summed = line_sum(grad_second(a, moved_cot, act_keep, act_other))
+        second_total = finish(
+            "finish_second", n, 1, factor, idx, chunk, summed, to_core(summed), second_total
+        )
+    output = conv_full("output", 1, False, idx, w_second, act_blocks)
+
     dpre, gain_part = pl.pallas_call(
         functools.partial(norm_back_kernel, n),
         out_shape=[
@@ -357,18 +490,19 @@
         compiler_params=pltpu.CompilerParams(vmem_limit_bytes=LIMIT),
         name="norm_back",
     )(own_gain, normed, inverse, *dact_shares)
-    dpre_blocks = spread(dpre)
-    factor = 1.0 / math.sqrt(lax.axis_size("dp") * CELLS)
-
-    second_part = grad_second(idx, cot, act_blocks)
-    second_total = lax.psum(second_part, "dp").astype(F32) * factor
-    first_part = grad_first(idx, vol, dpre_blocks)
-    first_total = lax.psum(first_part, "dp").astype(F32) * factor
-    output = conv_full("output", 1, False, idx, w_second, act_blocks)
+    dpre_blocks = swap([dpre] * n)
+    dpre_keep, dpre_send = halves("dpre_halves", False, idx, dpre_blocks)
+    dpre_other = to_core(dpre_send)
+    first_total = None
+    for chunk, a in enumerate((-1, 0, 1)):
+        summed = line_sum(grad_first(a, moved_vol, dpre_keep, dpre_other))
+        first_total = finish(
+            "finish_first", n, 2, factor, idx, chunk, summed, to_core(summed), first_total
+        )
     grad_volume = conv_full(
         "grad_volume", -1, True, idx, w_first.reshape(27 * rows, n * rows), dpre_blocks
     )
-    gain_total = lax.psum(gain_part[0], "dp") * factor
+    gain_total = jnp.sum(lax.all_gather(gain_part[0], "dp"), axis=0) * factor
     return (output[None], grad_volume[None], first_total, gain_total, second_total)
 
 

time: 250 us -> 272 us (1.088)
  starting transfers between devices: 12 us -> 50.1 us
  between operations: 14.1 us -> 1.29 us
  other arithmetic: 10.5 us -> 2.92 us
  waiting for transfers between devices: 139 us -> 144 us
  blocking collectives: 15.8 us -> 12.1 us
  Pallas kernels: 52.6 us -> 55.9 us
    ppermute x0 -> x28, waiting for transfers between devices: none -> 122 us  [the longest x18 122 us: send(): lax.ppermute(x, 'dp', [(2 * i + k, 2 * j + k) for i, j in moves for k in...]
    psum x1 -> x0, waiting for transfers between devices: 121 us -> none  [shards(): first_total = lax.psum(first_part, 'dp').astype(F32) * factor]
    ppermute x0 -> x28, starting transfers between devices: none -> 37.6 us  [the longest x18 20 us: send(): lax.ppermute(x, 'dp', [(2 * i + k, 2 * j + k) for i, j in moves for k in...]
    psum x1 -> x0, blocking collectives: 15.8 us -> none  [shards(): gain_total = lax.psum(gain_part[0], 'dp') * factor]
    pallas_call x2 -> x16, Pallas kernels: 15 us -> 29.5 us  [the longest x6 14.7 us: finish(): pl.pallas_call(functools.partial(finish_kernel, n, axis, factor), grid=(s...]
    all_gather x0 -> x1, blocking collectives: none -> 12.1 us  [shards(): gain_total = jnp.sum(lax.all_gather(gain_part[0], 'dp'), axis=0) * factor]
    mul x3 -> x1, other arithmetic: 10.5 us -> 0.51 us  [shards(): gain_total = jnp.sum(lax.all_gather(gain_part[0], 'dp'), axis=0) * factor]
    ppermute x12, waiting for transfers between devices: 18 us -> 22.5 us  [to_partner(): return lax.ppermute(x, 'chan', [(i, i ^ m) for i in range(n)])]
  transfers between devices with their start and end apart: 13 -> 40, of which waited for: 6 -> 15; matrix products, arithmetic and copies ran while one was open for 0% -> 1% of each run, Pallas kernels for 14% -> 17%
where the time goes in v2:
time: 272 us
  waiting for transfers between devices  144 us (53%)
  Pallas kernels  55.9 us (21%)
  starting transfers between devices  50.1 us (18%)
  blocking collectives  12.1 us (4%)
  local copies, waits for them, and re-layouts  5.12 us (2%)
  other arithmetic  2.92 us (1%)
    ppermute x18, waiting for transfers between devices, send(): lax.ppermute(x, 'dp', [(2 * i + k, 2 * j + k) for i, j in moves for k in...  122 us
    ppermute x12, waiting for transfers between devices, to_partner(): return lax.ppermute(x, 'chan', [(i, i ^ m) for i in range(n)])  22.5 us
    ppermute x18, starting transfers between devices, send(): lax.ppermute(x, 'dp', [(2 * i + k, 2 * j + k) for i, j in moves for k in...  20 us
    ppermute x10, starting transfers between devices, to_core(): lax.ppermute(x, 'dp', [(i, i ^ 1) for i in range(lax.axis_size('dp'))])  17.6 us
    pallas_call x6, Pallas kernels, finish(): pl.pallas_call(functools.partial(finish_kernel, n, axis, factor), grid=(s...  14.7 us
    pallas_call x2, Pallas kernels, conv_full(): pl.pallas_call(functools.partial(conv_kernel, n, sign, transposed), grid=...  13.4 us
    ppermute x12, starting transfers between devices, to_partner(): return lax.ppermute(x, 'chan', [(i, i ^ m) for i in range(n)])  12.4 us
    all_gather x1, blocking collectives, shards(): gain_total = jnp.sum(lax.all_gather(gain_part[0], 'dp'), axis=0) * factor  12.1 us
  transfers between devices with their start and end apart: 40, of which 15 were waited for; matrix products, arithmetic and copies ran while one was open for 1% of the time, Pallas kernels for 17%

profile of v2, /device:TPU:1, one launch (start us, length us, event | category | flops | bytes accessed | tf_op | source)
XLA Modules:
  0.0 271.5 jit_solution(14962005001729351434)
XLA Ops:
  3.7 5.6 %pre.1 = (bf16[1024,128]{1,0:T(8,128)(2,1)S(1)}, bf16[1024,128]{1,0:T(8,128)(2,1)S(1)}, bf16[1024,128]{1,0:T(8,128)(2,1)S(1)}, bf16[1024,128]{1,0:T(8,128)(2,1)S(1)}) custom-call(s32[2]{0:T(128)S(1)} %pad_add_fusion.idx, bf16[128,1024]{1,0:T(8,128)(2,1)S(1)} %bitcast.13, bf16[3456,512]{1,0:T(8,128)(2,1)S(1)} %bitcast.17), custom_call_target="tpu_custom_call" | custom-call | flops 3623878656 | bytes 3538944 | tf_op jit(solution)/shard_map/pre/pallas_call | solution.py:94
  9.3 2.1 collective-permute-start
  12.7 4.7 %collective-permute-done.refs_1_ = bf16[1024,128]{1,0:T(8,128)(2,1)S(1)} collective-permute-done((bf16[1024,128]{1,0:T(8,128)(2,1)S(1)}, bf16[1024,128]{1,0:T(8,128)(2,1)S(1)}, u32[]{:S(2)}, u32[]{:S(2)}) %collective-permute-start) | collective-permute-done | bytes 262176 | tf_op jit(solution)/shard_map/ppermute | solution.py:436
  18.2 5.7 %collective-permute-done.2.refs_3_ = bf16[1024,128]{1,0:T(8,128)(2,1)S(1)} collective-permute-done((bf16[1024,128]{1,0:T(8,128)(2,1)S(1)}, bf16[1024,128]{1,0:T(8,128)(2,1)S(1)}, u32[]{:S(2)}, u32[]{:S(2)}) %collective-permute-start.2) | collective-permute-done | bytes 262176 | tf_op jit(solution)/shard_map/ppermute | solution.py:436
  27.2 2.0 copy-done.19
  29.2 6.2 %dact.1 = (bf16[1024,128]{1,0:T(8,128)(2,1)S(1)}, bf16[1024,128]{1,0:T(8,128)(2,1)S(1)}, bf16[1024,128]{1,0:T(8,128)(2,1)S(1)}, bf16[1024,128]{1,0:T(8,128)(2,1)S(1)}) custom-call(s32[2]{0:T(128)S(1)} %pad_add_fusion.idx, bf16[128,1024]{1,0:T(8,128)(2,1)S(1)} %bitcast.10, bf16[27,512,128]{2,1,0:T(8,128)(2,1)S(1)} %copy-done.19), custom_call_target="tpu_custom_call" | custom-call | flops 3623878656 | bytes 3538944 | tf_op jit(solution)/shard_map/dact/pallas_call | solution.py:94
  41.0 2.3 collective-permute-start.27
  43.3 4.2 %collective-permute-done.8.refs_3_ = bf16[1024,128]{1,0:T(8,128)(2,1)S(1)} collective-permute-done((bf16[1024,128]{1,0:T(8,128)(2,1)S(1)}, bf16[1024,128]{1,0:T(8,128)(2,1)S(1)}, u32[]{:S(2)}, u32[]{:S(2)}) %collective-permute-start.8) | collective-permute-done | bytes 262176 | tf_op jit(solution)/shard_map/ppermute | solution.py:436
  51.9 3.6 %collective-permute-start.26 = (bf16[128,1024]{1,0:T(8,128)(2,1)S(1)}, bf16[128,1024]{1,0:T(8,128)(2,1)S(1)}, u32[]{:S(2)}, u32[]{:S(2)}) collective-permute-start(bf16[128,1024]{1,0:T(8,128)(2,1)S(1)} %bitcast.11), channel_id=1, source_target_pairs={{0,4},{4,0},{8,12},{12,8},{16,20},{20,16},{24,28},{28,24},{1,5},{5... | collective-permute-start | bytes 786440 | tf_op jit(solution)/shard_map/ppermute | solution.py:439
  55.4 5.9 %collective-permute-done.10.refs_2_ = bf16[1024,128]{1,0:T(8,128)(2,1)S(1)} collective-permute-done((bf16[1024,128]{1,0:T(8,128)(2,1)S(1)}, bf16[1024,128]{1,0:T(8,128)(2,1)S(1)}, u32[]{:S(2)}, u32[]{:S(2)}) %collective-permute-start.10) | collective-permute-done | bytes 262176 | tf_op jit(solution)/shard_map/ppermute | solution.py:436
  62.8 2.3 collective-permute-start.13
  65.2 12.1 %all-gather = f32[8,1,128]{2,1,0:T(1,128)S(1)} all-gather(f32[1,1,128]{2,1,0:T(1,128)S(1)} %bitcast.16), channel_id=1, replica_groups=mesh['dp'=8,'chan'=4] {'dp'}, dimensions={0}, use_global_device_ids=true | all-gather | bytes 4608 | tf_op jit(solution)/shard_map/all_gather | solution.py:505
  91.2 2.1 grad_first.4
  97.9 8.0 %collective-permute-done.32 = bf16[9,256,128]{2,1,0:T(8,128)(2,1)S(1)} collective-permute-done((bf16[9,256,128]{2,1,0:T(8,128)(2,1)S(1)}, bf16[9,256,128]{2,1,0:T(8,128)(2,1)S(1)}, u32[]{:S(2)}, u32[]{:S(2)}) %collective-permute-start.32) | collective-permute-done | bytes 589856 | tf_op jit(solution)/shard_map/ppermute | solution.py:412
  106.8 11.8 %collective-permute-done.36 = bf16[9,256,128]{2,1,0:T(8,128)(2,1)S(1)} collective-permute-done((bf16[9,256,128]{2,1,0:T(8,128)(2,1)S(1)}, bf16[9,256,128]{2,1,0:T(8,128)(2,1)S(1)}, u32[]{:S(2)}, u32[]{:S(2)}) %collective-permute-start.36) | collective-permute-done | bytes 589856 | tf_op jit(solution)/shard_map/ppermute | solution.py:412
  119.4 11.8 %collective-permute-done.14 = bf16[9,128,256]{2,1,0:T(8,128)(2,1)S(1)} collective-permute-done((bf16[9,128,256]{2,1,0:T(8,128)(2,1)S(1)}, bf16[9,128,256]{2,1,0:T(8,128)(2,1)S(1)}, u32[]{:S(2)}, u32[]{:S(2)}) %collective-permute-start.14) | collective-permute-done | bytes 589856 | tf_op jit(solution)/shard_map/ppermute | solution.py:412
  132.1 11.8 %collective-permute-done.18 = bf16[9,128,256]{2,1,0:T(8,128)(2,1)S(1)} collective-permute-done((bf16[9,128,256]{2,1,0:T(8,128)(2,1)S(1)}, bf16[9,128,256]{2,1,0:T(8,128)(2,1)S(1)}, u32[]{:S(2)}, u32[]{:S(2)}) %collective-permute-start.18) | collective-permute-done | bytes 589856 | tf_op jit(solution)/shard_map/ppermute | solution.py:412
  144.7 11.8 %collective-permute-done.22 = bf16[9,128,256]{2,1,0:T(8,128)(2,1)S(1)} collective-permute-done((bf16[9,128,256]{2,1,0:T(8,128)(2,1)S(1)}, bf16[9,128,256]{2,1,0:T(8,128)(2,1)S(1)}, u32[]{:S(2)}, u32[]{:S(2)}) %collective-permute-start.22) | collective-permute-done | bytes 589856 | tf_op jit(solution)/shard_map/ppermute | solution.py:412
  165.6 12.4 %collective-permute-done.30 = bf16[9,256,128]{2,1,0:T(8,128)(2,1)S(1)} collective-permute-done((bf16[9,256,128]{2,1,0:T(8,128)(2,1)S(1)}, bf16[9,256,128]{2,1,0:T(8,128)(2,1)S(1)}, u32[]{:S(2)}, u32[]{:S(2)}) %collective-permute-start.30) | collective-permute-done | bytes 589856 | tf_op jit(solution)/shard_map/ppermute | solution.py:412
  179.4 11.3 %collective-permute-done.34 = bf16[9,256,128]{2,1,0:T(8,128)(2,1)S(1)} collective-permute-done((bf16[9,256,128]{2,1,0:T(8,128)(2,1)S(1)}, bf16[9,256,128]{2,1,0:T(8,128)(2,1)S(1)}, u32[]{:S(2)}, u32[]{:S(2)}) %collective-permute-start.34) | collective-permute-done | bytes 589856 | tf_op jit(solution)/shard_map/ppermute | solution.py:412
  190.6 3.4 %collective-permute-start.31 = (bf16[9,256,128]{2,1,0:T(8,128)(2,1)S(1)}, bf16[9,256,128]{2,1,0:T(8,128)(2,1)S(1)}, u32[]{:S(2)}, u32[]{:S(2)}) collective-permute-start(bf16[9,256,128]{2,1,0:T(8,128)(2,1)S(1)} %broadcast_select_fusion.2.own), channel_id=1, source_target_pairs={{0,4},{4,0},{8,12},{12,8},{16,20},{20,16},{24,28},{28,24},{1,5},{5... | collective-permute-start | bytes 1769480 | tf_op jit(solution)/shard_map/ppermute | solution.py:439
  194.1 34.5 %collective-permute-done.24 = bf16[9,128,256]{2,1,0:T(8,128)(2,1)S(1)} collective-permute-done((bf16[9,128,256]{2,1,0:T(8,128)(2,1)S(1)}, bf16[9,128,256]{2,1,0:T(8,128)(2,1)S(1)}, u32[]{:S(2)}, u32[]{:S(2)}) %collective-permute-start.24) | collective-permute-done | bytes 589856 | tf_op jit(solution)/shard_map/ppermute | solution.py:412
  228.6 3.4 %collective-permute-start.35 = (bf16[9,256,128]{2,1,0:T(8,128)(2,1)S(1)}, bf16[9,256,128]{2,1,0:T(8,128)(2,1)S(1)}, u32[]{:S(2)}, u32[]{:S(2)}) collective-permute-start(bf16[9,256,128]{2,1,0:T(8,128)(2,1)S(1)} %broadcast_select_fusion.1.own), channel_id=1, source_target_pairs={{0,4},{4,0},{8,12},{12,8},{16,20},{20,16},{24,28},{28,24},{1,5},{5... | collective-permute-start | bytes 1769480 | tf_op jit(solution)/shard_map/ppermute | solution.py:439
  232.9 8.3 %collective-permute-done.20 = bf16[9,128,256]{2,1,0:T(8,128)(2,1)S(1)} collective-permute-done((bf16[9,128,256]{2,1,0:T(8,128)(2,1)S(1)}, bf16[9,128,256]{2,1,0:T(8,128)(2,1)S(1)}, u32[]{:S(2)}, u32[]{:S(2)}) %collective-permute-start.20) | collective-permute-done | bytes 589856 | tf_op jit(solution)/shard_map/ppermute | solution.py:412
  243.3 6.6 %output.1 = bf16[128,1024]{1,0:T(8,128)(2,1)} custom-call(s32[2]{0:T(128)S(1)} %pad_add_fusion.idx, bf16[27,512,128]{2,1,0:T(8,128)(2,1)S(1)} %copy-done.20, bf16[1024,128]{1,0:T(8,128)(2,1)S(1)} %get-tuple-element.26.refs_0_, bf16[1024,128]{1,0:T(8,128)(2,1)S(1)} %copy-done.10, bf16[1024,128]{1,0:T(8,128)(2,1)S(1)} %copy-done.8, bf16[1024,128]{1,0:T(8,128)(2,1)S(1)} %copy-done.6), custom_call_target="tpu_custom_call" | custom-call | flops 3623878656 | bytes 3538944 | tf_op jit(solution)/shard_map/output/pallas_call | solution.py:197
  249.9 6.8 %grad_volume.1 = bf16[128,1024]{1,0:T(8,128)(2,1)} custom-call(s32[2]{0:T(128)S(1)} %pad_add_fusion.idx, bf16[3456,512]{1,0:T(8,128)(2,1)S(1)} %bitcast.18, bf16[1024,128]{1,0:T(8,128)(2,1)S(1)} %copy-done.12, bf16[1024,128]{1,0:T(8,128)(2,1)S(1)} %copy-done.18, bf16[1024,128]{1,0:T(8,128)(2,1)S(1)} %copy-done.16, bf16[1024,128]{1,0:T(8,128)(2,1)S(1)} %copy-done.14), custom_call_target="tpu_custom_call" | custom-call | flops 3623878656 | bytes 3538944 | tf_op jit(solution)/shard_map/grad_volume/pallas_call | solution.py:197
  256.8 2.5 finish_first.3.refs_0_
  259.2 2.5 finish_second.3.refs_0_
  261.7 2.5 finish_first.4.refs_0_
  264.1 2.5 finish_first.5
  266.6 2.5 finish_second.4.refs_0_
  269.0 2.5 finish_second.5
  (139 shorter events, 55.0 us)
Async XLA Ops:
  12.6 11.3 %collective-permute-start.2 = (bf16[1024,128]{1,0:T(8,128)(2,1)S(1)}, bf16[1024,128]{1,0:T(8,128)(2,1)S(1)}, u32[]{:S(2)}, u32[]{:S(2)}) collective-permute-start(bf16[1024,128]{1,0:T(8,128)(2,1)S(1)} %get-tuple-element.25), channel_id=1, source_target_pairs={{0,3},{1,2},{2,1},{3,0},{4,7},{5,6},{6,5},{7,4},{8,11},{9,10},{10,... | collective-permute-start | bytes 786440 | tf_op jit(solution)/shard_map/ppermute | solution.py:436
  24.5 12.5 %collective-permute-start.5 = (bf16[1024,128]{1,0:T(8,128)(2,1)S(1)}, bf16[1024,128]{1,0:T(8,128)(2,1)S(1)}, u32[]{:S(2)}, u32[]{:S(2)}) collective-permute-start(bf16[1024,128]{1,0:T(8,128)(2,1)S(1)} %get-tuple-element.26.refs_0_), channel_id=1, source_target_pairs={{0,3},{1,2},{2,1},{3,0},{4,7},{5,6},{6,5},{7,4},{8,11},{9,10},{10,... | collective-permute-start | bytes 786440 | tf_op jit(solution)/shard_map/ppermute | solution.py:436
  25.7 13.6 %collective-permute-start.4 = (bf16[1024,128]{1,0:T(8,128)(2,1)S(1)}, bf16[1024,128]{1,0:T(8,128)(2,1)S(1)}, u32[]{:S(2)}, u32[]{:S(2)}) collective-permute-start(bf16[1024,128]{1,0:T(8,128)(2,1)S(1)} %get-tuple-element.26.refs_0_), channel_id=1, source_target_pairs={{0,2},{1,3},{2,0},{3,1},{4,6},{5,7},{6,4},{7,5},{8,10},{9,11},{10,... | collective-permute-start | bytes 786440 | tf_op jit(solution)/shard_map/ppermute | solution.py:436
  26.9 12.4 %collective-permute-start.3 = (bf16[1024,128]{1,0:T(8,128)(2,1)S(1)}, bf16[1024,128]{1,0:T(8,128)(2,1)S(1)}, u32[]{:S(2)}, u32[]{:S(2)}) collective-permute-start(bf16[1024,128]{1,0:T(8,128)(2,1)S(1)} %get-tuple-element.26.refs_0_), channel_id=1, source_target_pairs={{0,1},{1,0},{2,3},{3,2},{4,5},{5,4},{6,7},{7,6},{8,9},{9,8},{10,11... | collective-permute-start | bytes 786440 | tf_op jit(solution)/shard_map/ppermute | solution.py:436
  37.0 10.6 %collective-permute-start.8 = (bf16[1024,128]{1,0:T(8,128)(2,1)S(1)}, bf16[1024,128]{1,0:T(8,128)(2,1)S(1)}, u32[]{:S(2)}, u32[]{:S(2)}) collective-permute-start(bf16[1024,128]{1,0:T(8,128)(2,1)S(1)} %get-tuple-element.32), channel_id=1, source_target_pairs={{0,3},{1,2},{2,1},{3,0},{4,7},{5,6},{6,5},{7,4},{8,11},{9,10},{10,... | collective-permute-start | bytes 786440 | tf_op jit(solution)/shard_map/ppermute | solution.py:436
  41.0 37.0 %collective-permute-start.27 = (bf16[256,1024]{1,0:T(8,128)(2,1)}, bf16[256,1024]{1,0:T(8,128)(2,1)S(1)}, u32[]{:S(2)}, u32[]{:S(2)}) collective-permute-start(bf16[256,1024]{1,0:T(8,128)(2,1)} %get-tuple-element.38), channel_id=1, source_target_pairs={{0,4},{4,0},{8,12},{12,8},{16,20},{20,16},{24,28},{28,24},{1,5},{5... | collective-permute-start | bytes 1572872 | tf_op jit(solution)/shard_map/ppermute | solution.py:439
  50.0 11.3 %collective-permute-start.10 = (bf16[1024,128]{1,0:T(8,128)(2,1)S(1)}, bf16[1024,128]{1,0:T(8,128)(2,1)S(1)}, u32[]{:S(2)}, u32[]{:S(2)}) collective-permute-start(bf16[1024,128]{1,0:T(8,128)(2,1)S(1)} %get-tuple-element.33.refs_0_), channel_id=1, source_target_pairs={{0,2},{1,3},{2,0},{3,1},{4,6},{5,7},{6,4},{7,5},{8,10},{9,11},{10,... | collective-permute-start | bytes 786440 | tf_op jit(solution)/shard_map/ppermute | solution.py:436
  51.9 25.4 %collective-permute-start.26 = (bf16[128,1024]{1,0:T(8,128)(2,1)S(1)}, bf16[128,1024]{1,0:T(8,128)(2,1)S(1)}, u32[]{:S(2)}, u32[]{:S(2)}) collective-permute-start(bf16[128,1024]{1,0:T(8,128)(2,1)S(1)} %bitcast.11), channel_id=1, source_target_pairs={{0,4},{4,0},{8,12},{12,8},{16,20},{20,16},{24,28},{28,24},{1,5},{5... | collective-permute-start | bytes 786440 | tf_op jit(solution)/shard_map/ppermute | solution.py:439
  62.8 25.3 %collective-permute-start.13 = (bf16[2,1024,128]{2,1,0:T(8,128)(2,1)}, bf16[2,1024,128]{2,1,0:T(8,128)(2,1)S(1)}, u32[]{:S(2)}, u32[]{:S(2)}) collective-permute-start(bf16[2,1024,128]{2,1,0:T(8,128)(2,1)} %get-tuple-element.35), channel_id=1, source_target_pairs={{0,4},{4,0},{8,12},{12,8},{16,20},{20,16},{24,28},{28,24},{1,5},{5... | collective-permute-start | bytes 1572872 | tf_op jit(solution)/shard_map/ppermute | solution.py:439
  65.1 16.0 %collective-permute-start.12 = (bf16[128,1024]{1,0:T(8,128)(2,1)S(1)}, bf16[128,1024]{1,0:T(8,128)(2,1)S(1)}, u32[]{:S(2)}, u32[]{:S(2)}) collective-permute-start(bf16[128,1024]{1,0:T(8,128)(2,1)S(1)} %bitcast.14), channel_id=1, source_target_pairs={{0,4},{4,0},{8,12},{12,8},{16,20},{20,16},{24,28},{28,24},{1,5},{5... | collective-permute-start | bytes 786440 | tf_op jit(solution)/shard_map/ppermute | solution.py:439
  79.2 17.2 %collective-permute-start.28 = (bf16[9,256,128]{2,1,0:T(8,128)(2,1)S(1)}, bf16[9,256,128]{2,1,0:T(8,128)(2,1)S(1)}, u32[]{:S(2)}, u32[]{:S(2)}) collective-permute-start(bf16[9,256,128]{2,1,0:T(8,128)(2,1)S(1)} %grad_second.3), channel_id=1, source_target_pairs={{0,8},{4,12},{24,16},{28,20},{1,9},{5,13},{25,17},{29,21},{2,10},{... | collective-permute-start | bytes 1769480 | tf_op jit(solution)/shard_map/ppermute | solution.py:412
  84.0 21.9 %collective-permute-start.32 = (bf16[9,256,128]{2,1,0:T(8,128)(2,1)S(1)}, bf16[9,256,128]{2,1,0:T(8,128)(2,1)S(1)}, u32[]{:S(2)}, u32[]{:S(2)}) collective-permute-start(bf16[9,256,128]{2,1,0:T(8,128)(2,1)S(1)} %grad_second.4), channel_id=1, source_target_pairs={{0,8},{4,12},{24,16},{28,20},{1,9},{5,13},{25,17},{29,21},{2,10},{... | collective-permute-start | bytes 1769480 | tf_op jit(solution)/shard_map/ppermute | solution.py:412
  86.7 31.9 %collective-permute-start.36 = (bf16[9,256,128]{2,1,0:T(8,128)(2,1)S(1)}, bf16[9,256,128]{2,1,0:T(8,128)(2,1)S(1)}, u32[]{:S(2)}, u32[]{:S(2)}) collective-permute-start(bf16[9,256,128]{2,1,0:T(8,128)(2,1)S(1)} %grad_second.5), channel_id=1, source_target_pairs={{0,8},{4,12},{24,16},{28,20},{1,9},{5,13},{25,17},{29,21},{2,10},{... | collective-permute-start | bytes 1769480 | tf_op jit(solution)/shard_map/ppermute | solution.py:412
  89.9 41.4 %collective-permute-start.14 = (bf16[9,128,256]{2,1,0:T(8,128)(2,1)S(1)}, bf16[9,128,256]{2,1,0:T(8,128)(2,1)S(1)}, u32[]{:S(2)}, u32[]{:S(2)}) collective-permute-start(bf16[9,128,256]{2,1,0:T(8,128)(2,1)S(1)} %grad_first.3), channel_id=1, source_target_pairs={{0,8},{4,12},{24,16},{28,20},{1,9},{5,13},{25,17},{29,21},{2,10},{... | collective-permute-start | bytes 1769480 | tf_op jit(solution)/shard_map/ppermute | solution.py:412
  93.3 50.6 %collective-permute-start.18 = (bf16[9,128,256]{2,1,0:T(8,128)(2,1)S(1)}, bf16[9,128,256]{2,1,0:T(8,128)(2,1)S(1)}, u32[]{:S(2)}, u32[]{:S(2)}) collective-permute-start(bf16[9,128,256]{2,1,0:T(8,128)(2,1)S(1)} %grad_first.4), channel_id=1, source_target_pairs={{0,8},{4,12},{24,16},{28,20},{1,9},{5,13},{25,17},{29,21},{2,10},{... | collective-permute-start | bytes 1769480 | tf_op jit(solution)/shard_map/ppermute | solution.py:412
  96.4 60.1 %collective-permute-start.22 = (bf16[9,128,256]{2,1,0:T(8,128)(2,1)S(1)}, bf16[9,128,256]{2,1,0:T(8,128)(2,1)S(1)}, u32[]{:S(2)}, u32[]{:S(2)}) collective-permute-start(bf16[9,128,256]{2,1,0:T(8,128)(2,1)S(1)} %grad_first.5), channel_id=1, source_target_pairs={{0,8},{4,12},{24,16},{28,20},{1,9},{5,13},{25,17},{29,21},{2,10},{... | collective-permute-start | bytes 1769480 | tf_op jit(solution)/shard_map/ppermute | solution.py:412
  105.9 51.4 %collective-permute-start.29 = (bf16[9,256,128]{2,1,0:T(8,128)(2,1)S(1)}, bf16[9,256,128]{2,1,0:T(8,128)(2,1)S(1)}, u32[]{:S(2)}, u32[]{:S(2)}) collective-permute-start(bf16[9,256,128]{2,1,0:T(8,128)(2,1)S(1)} %add_convert_fusion.5), channel_id=1, source_target_pairs={{8,16},{12,20},{16,8},{20,12},{9,17},{13,21},{17,9},{21,13},{10,18... | collective-permute-start | bytes 1769480 | tf_op jit(solution)/shard_map/ppermute | solution.py:412
  118.6 39.7 %collective-permute-start.33 = (bf16[9,256,128]{2,1,0:T(8,128)(2,1)S(1)}, bf16[9,256,128]{2,1,0:T(8,128)(2,1)S(1)}, u32[]{:S(2)}, u32[]{:S(2)}) collective-permute-start(bf16[9,256,128]{2,1,0:T(8,128)(2,1)S(1)} %add_convert_fusion.3), channel_id=1, source_target_pairs={{8,16},{12,20},{16,8},{20,12},{9,17},{13,21},{17,9},{21,13},{10,18... | collective-permute-start | bytes 1769480 | tf_op jit(solution)/shard_map/ppermute | solution.py:412
  131.2 28.5 %collective-permute-start.37 = (bf16[9,256,128]{2,1,0:T(8,128)(2,1)S(1)}, bf16[9,256,128]{2,1,0:T(8,128)(2,1)S(1)}, u32[]{:S(2)}, u32[]{:S(2)}) collective-permute-start(bf16[9,256,128]{2,1,0:T(8,128)(2,1)S(1)} %add_convert_fusion.1), channel_id=1, source_target_pairs={{8,16},{12,20},{16,8},{20,12},{9,17},{13,21},{17,9},{21,13},{10,18... | collective-permute-start | bytes 1769480 | tf_op jit(solution)/shard_map/ppermute | solution.py:412
  143.9 17.3 %collective-permute-start.15 = (bf16[9,128,256]{2,1,0:T(8,128)(2,1)S(1)}, bf16[9,128,256]{2,1,0:T(8,128)(2,1)S(1)}, u32[]{:S(2)}, u32[]{:S(2)}) collective-permute-start(bf16[9,128,256]{2,1,0:T(8,128)(2,1)S(1)} %add_convert_fusion.11), channel_id=1, source_target_pairs={{8,16},{12,20},{16,8},{20,12},{9,17},{13,21},{17,9},{21,13},{10,18... | collective-permute-start | bytes 1769480 | tf_op jit(solution)/shard_map/ppermute | solution.py:412
  158.2 19.8 %collective-permute-start.30 = (bf16[9,256,128]{2,1,0:T(8,128)(2,1)S(1)}, bf16[9,256,128]{2,1,0:T(8,128)(2,1)S(1)}, u32[]{:S(2)}, u32[]{:S(2)}) collective-permute-start(bf16[9,256,128]{2,1,0:T(8,128)(2,1)S(1)} %add_convert_fusion.4), channel_id=1, source_target_pairs={{8,0},{12,4},{16,24},{20,28},{9,1},{13,5},{17,25},{21,29},{10,2},{... | collective-permute-start | bytes 1769480 | tf_op jit(solution)/shard_map/ppermute | solution.py:412
  159.7 30.9 %collective-permute-start.34 = (bf16[9,256,128]{2,1,0:T(8,128)(2,1)S(1)}, bf16[9,256,128]{2,1,0:T(8,128)(2,1)S(1)}, u32[]{:S(2)}, u32[]{:S(2)}) collective-permute-start(bf16[9,256,128]{2,1,0:T(8,128)(2,1)S(1)} %add_convert_fusion.2), channel_id=1, source_target_pairs={{8,0},{12,4},{16,24},{20,28},{9,1},{13,5},{17,25},{21,29},{10,2},{... | collective-permute-start | bytes 1769480 | tf_op jit(solution)/shard_map/ppermute | solution.py:412
  161.2 70.8 %collective-permute-start.38 = (bf16[9,256,128]{2,1,0:T(8,128)(2,1)S(1)}, bf16[9,256,128]{2,1,0:T(8,128)(2,1)S(1)}, u32[]{:S(2)}, u32[]{:S(2)}) collective-permute-start(bf16[9,256,128]{2,1,0:T(8,128)(2,1)S(1)} %add_convert_fusion), channel_id=1, source_target_pairs={{8,0},{12,4},{16,24},{20,28},{9,1},{13,5},{17,25},{21,29},{10,2},{... | collective-permute-start | bytes 1769480 | tf_op jit(solution)/shard_map/ppermute | solution.py:412
  162.7 69.5 %collective-permute-start.16 = (bf16[9,128,256]{2,1,0:T(8,128)(2,1)S(1)}, bf16[9,128,256]{2,1,0:T(8,128)(2,1)S(1)}, u32[]{:S(2)}, u32[]{:S(2)}) collective-permute-start(bf16[9,128,256]{2,1,0:T(8,128)(2,1)S(1)} %add_convert_fusion.10), channel_id=1, source_target_pairs={{8,0},{12,4},{16,24},{20,28},{9,1},{13,5},{17,25},{21,29},{10,2},{... | collective-permute-start | bytes 1769480 | tf_op jit(solution)/shard_map/ppermute | solution.py:412
  164.2 64.4 %collective-permute-start.24 = (bf16[9,128,256]{2,1,0:T(8,128)(2,1)S(1)}, bf16[9,128,256]{2,1,0:T(8,128)(2,1)S(1)}, u32[]{:S(2)}, u32[]{:S(2)}) collective-permute-start(bf16[9,128,256]{2,1,0:T(8,128)(2,1)S(1)} %add_convert_fusion.6), channel_id=1, source_target_pairs={{8,0},{12,4},{16,24},{20,28},{9,1},{13,5},{17,25},{21,29},{10,2},{... | collective-permute-start | bytes 1769480 | tf_op jit(solution)/shard_map/ppermute | solution.py:412
  178.0 63.2 %collective-permute-start.20 = (bf16[9,128,256]{2,1,0:T(8,128)(2,1)S(1)}, bf16[9,128,256]{2,1,0:T(8,128)(2,1)S(1)}, u32[]{:S(2)}, u32[]{:S(2)}) collective-permute-start(bf16[9,128,256]{2,1,0:T(8,128)(2,1)S(1)} %add_convert_fusion.8), channel_id=1, source_target_pairs={{8,0},{12,4},{16,24},{20,28},{9,1},{13,5},{17,25},{21,29},{10,2},{... | collective-permute-start | bytes 1769480 | tf_op jit(solution)/shard_map/ppermute | solution.py:412
  190.6 78.4 %collective-permute-start.31 = (bf16[9,256,128]{2,1,0:T(8,128)(2,1)S(1)}, bf16[9,256,128]{2,1,0:T(8,128)(2,1)S(1)}, u32[]{:S(2)}, u32[]{:S(2)}) collective-permute-start(bf16[9,256,128]{2,1,0:T(8,128)(2,1)S(1)} %broadcast_select_fusion.2.own), channel_id=1, source_target_pairs={{0,4},{4,0},{8,12},{12,8},{16,20},{20,16},{24,28},{28,24},{1,5},{5... | collective-permute-start | bytes 1769480 | tf_op jit(solution)/shard_map/ppermute | solution.py:439
  228.6 38.0 %collective-permute-start.35 = (bf16[9,256,128]{2,1,0:T(8,128)(2,1)S(1)}, bf16[9,256,128]{2,1,0:T(8,128)(2,1)S(1)}, u32[]{:S(2)}, u32[]{:S(2)}) collective-permute-start(bf16[9,256,128]{2,1,0:T(8,128)(2,1)S(1)} %broadcast_select_fusion.1.own), channel_id=1, source_target_pairs={{0,4},{4,0},{8,12},{12,8},{16,20},{20,16},{24,28},{28,24},{1,5},{5... | collective-permute-start | bytes 1769480 | tf_op jit(solution)/shard_map/ppermute | solution.py:439
  232.0 11.2 %collective-permute-start.25 = (bf16[9,128,256]{2,1,0:T(8,128)(2,1)S(1)}, bf16[9,128,256]{2,1,0:T(8,128)(2,1)S(1)}, u32[]{:S(2)}, u32[]{:S(2)}) collective-permute-start(bf16[9,128,256]{2,1,0:T(8,128)(2,1)S(1)} %broadcast_select_fusion.3.own), channel_id=1, source_target_pairs={{0,4},{4,0},{8,12},{12,8},{16,20},{20,16},{24,28},{28,24},{1,5},{5... | collective-permute-start | bytes 1769480 | tf_op jit(solution)/shard_map/ppermute | solution.py:439
  232.2 27.0 %collective-permute-start.39 = (bf16[9,256,128]{2,1,0:T(8,128)(2,1)S(1)}, bf16[9,256,128]{2,1,0:T(8,128)(2,1)S(1)}, u32[]{:S(2)}, u32[]{:S(2)}) collective-permute-start(bf16[9,256,128]{2,1,0:T(8,128)(2,1)S(1)} %broadcast_select_fusion.own), channel_id=1, source_target_pairs={{0,4},{4,0},{8,12},{12,8},{16,20},{20,16},{24,28},{28,24},{1,5},{5... | collective-permute-start | bytes 1769480 | tf_op jit(solution)/shard_map/ppermute | solution.py:439
  241.2 22.9 %collective-permute-start.17 = (bf16[9,128,256]{2,1,0:T(8,128)(2,1)S(1)}, bf16[9,128,256]{2,1,0:T(8,128)(2,1)S(1)}, u32[]{:S(2)}, u32[]{:S(2)}) collective-permute-start(bf16[9,128,256]{2,1,0:T(8,128)(2,1)S(1)} %broadcast_select_fusion.5.own), channel_id=1, source_target_pairs={{0,4},{4,0},{8,12},{12,8},{16,20},{20,16},{24,28},{28,24},{1,5},{5... | collective-permute-start | bytes 1769480 | tf_op jit(solution)/shard_map/ppermute | solution.py:439
  243.2 18.4 %collective-permute-start.21 = (bf16[9,128,256]{2,1,0:T(8,128)(2,1)S(1)}, bf16[9,128,256]{2,1,0:T(8,128)(2,1)S(1)}, u32[]{:S(2)}, u32[]{:S(2)}) collective-permute-start(bf16[9,128,256]{2,1,0:T(8,128)(2,1)S(1)} %broadcast_select_fusion.4.own), channel_id=1, source_target_pairs={{0,4},{4,0},{8,12},{12,8},{16,20},{20,16},{24,28},{28,24},{1,5},{5... | collective-permute-start | bytes 1769480 | tf_op jit(solution)/shard_map/ppermute | solution.py:439
  (31 other events, 237.7 us)

commit v3 on v2

--- a/solution.py
+++ b/solution.py
@@ -16,6 +16,7 @@
 LIMIT = 26 * 1024 * 1024
 F32, BF16 = jnp.float32, jnp.bfloat16
 NT = (((1,), (1,)), ((), ()))
+UNREAD = pl.BlockSpec(memory_space=pl.ANY)
 
 
 def params():
@@ -111,7 +112,8 @@
 
 
 def norm_kernel(n, gain, *refs):
-    shares, act, normed_out, inverse_out = refs[:n], refs[n], refs[n + 1], refs[n + 2]
+    shares = refs[:n]
+    act, normed_out, inverse_out = refs[-3:]
     pre = shares[0][...].astype(F32)
     for m in range(1, n):
         pre = pre + shares[m][...].astype(F32)
@@ -125,7 +127,8 @@
 
 
 def norm_back_kernel(n, gain, normed_in, inverse, *refs):
-    shares, dpre, gain_part = refs[:n], refs[n], refs[n + 1]
+    shares = refs[:n]
+    dpre, gain_part = refs[-2:]
     dact = shares[0][...].astype(F32)
     for m in range(1, n):
         dact = dact + shares[m][...].astype(F32)
@@ -165,7 +168,8 @@
 
 
 def conv_kernel(n, sign, transposed, idx, w, *refs):
-    blocks, out, ordered, sums = refs[:n], refs[n], refs[n + 1], refs[n + 2]
+    blocks = refs[:n]
+    out, ordered, sums = refs[-3:]
     rows = out.shape[0]
     plane = pl.program_id(0)
 
@@ -192,12 +196,12 @@
         conv_finish(sums, out, sign)
 
 
-def conv_full(name, sign, transposed, idx, w, blocks):
+def conv_full(name, sign, transposed, idx, w, blocks, after):
     n, rows = len(blocks), blocks[0].shape[1]
     return pl.pallas_call(
         functools.partial(conv_kernel, n, sign, transposed),
         grid=(DEPTH,),
-        in_specs=[smem(), whole(w.shape)] + [whole(blocks[0].shape)] * n,
+        in_specs=[smem(), whole(w.shape)] + [whole(blocks[0].shape)] * n + [UNREAD] * len(after),
         out_specs=whole((rows, CELLS)),
         out_shape=jax.ShapeDtypeStruct((rows, CELLS), BF16),
         scratch_shapes=[
@@ -209,11 +213,12 @@
             flops=2 * 27 * rows * rows * n * CELLS, bytes_accessed=2 * w.size, transcendentals=0
         ),
         name=name,
-    )(idx, w, *blocks)
-
-
-def halves_kernel(n, turned, idx, *refs):
-    blocks, keep, send = refs[:n], refs[n], refs[n + 1]
+    )(idx, w, *blocks, *after)
+
+
+def halves_kernel(n, held, turned, idx, *refs):
+    blocks = refs[:n]
+    keep, send = refs[len(refs) - held - 2], refs[len(refs) - held - 1]
     half = n // 2
     rows = blocks[0].shape[1]
 
@@ -238,19 +243,25 @@
         split(half, 0)
 
 
-def halves(name, turned, idx, blocks):
+def halves(name, turned, idx, blocks, after=(), held=()):
     n, rows = len(blocks), blocks[0].shape[1]
     shape = (n // 2 * rows, CELLS) if turned else (n // 2, CELLS, rows)
-    return pl.pallas_call(
-        functools.partial(halves_kernel, n, turned),
-        in_specs=[smem()] + [pl.BlockSpec(memory_space=pltpu.VMEM)] * n,
-        out_shape=[jax.ShapeDtypeStruct(shape, BF16)] * 2,
+    first = 1 + n + len(after)
+    return pl.pallas_call(
+        functools.partial(halves_kernel, n, len(held), turned),
+        in_specs=[smem()]
+        + [pl.BlockSpec(memory_space=pltpu.VMEM)] * n
+        + [UNREAD] * (len(after) + len(held)),
+        out_specs=[pl.BlockSpec(memory_space=pltpu.VMEM)] * 2 + [UNREAD] * len(held),
+        out_shape=[jax.ShapeDtypeStruct(shape, BF16)] * 2
+        + [jax.ShapeDtypeStruct(x.shape, x.dtype) for x in held],
+        input_output_aliases={first + k: 2 + k for k in range(len(held))},
         compiler_params=pltpu.CompilerParams(vmem_limit_bytes=LIMIT),
         name=name,
-    )(idx, *blocks)
-
-
-def moved_first_kernel(own, other, out):
+    )(idx, *blocks, *after, *held)
+
+
+def moved_first_kernel(own, other, _, out):
     for which, ref in enumerate((own, other)):
         cells = ref[...].astype(F32)
         at = lax.broadcasted_iota(jnp.int32, cells.shape, 1)
@@ -265,7 +276,7 @@
             out[which, k * rows : (k + 1) * rows] = jnp.where(inside, part, 0.0).astype(BF16)
 
 
-def moved_second_kernel(own, other, out):
+def moved_second_kernel(own, other, _, out):
     out[...] = jnp.zeros_like(out)
     for which, ref in enumerate((own, other)):
         cells = ref[...].astype(F32).T
@@ -279,16 +290,18 @@
             )
 
 
-def moved_fields(kernel, name, shape, own, other):
+def moved_fields(kernel, name, shape, own, other, after):
     return pl.pallas_call(
         kernel,
+        in_specs=[pl.BlockSpec(memory_space=pltpu.VMEM)] * 2 + [UNREAD],
         out_shape=jax.ShapeDtypeStruct(shape, BF16),
         compiler_params=pltpu.CompilerParams(vmem_limit_bytes=LIMIT),
         name=name,
-    )(own, other)
-
-
-def grad_first_kernel(a, moved, own, other, out):
+    )(own, other, after)
+
+
+def grad_first_kernel(a, moved, own, other, *refs):
+    out = refs[-1]
     rows, half = out.shape[1], own.shape[0]
     begin, count = max(0, -a) * PLANE, (DEPTH - abs(a)) * PLANE
     grads = None
@@ -300,7 +313,7 @@
     out[...] = grads.astype(BF16).reshape(out.shape)
 
 
-def grad_first(a, moved, own, other):
+def grad_first(a, moved, own, other, after):
     half, cells, rows = own.shape
     return pl.pallas_call(
         functools.partial(grad_first_kernel, a),
@@ -309,7 +322,8 @@
             pl.BlockSpec((2, 3 * rows, cells), lambda b: (0, b, 0)),
             whole(own.shape),
             whole(own.shape),
-        ],
+        ]
+        + [UNREAD] * len(after),
         out_specs=pl.BlockSpec((3, rows, half * rows), lambda b: (b, 0, 0)),
         out_shape=jax.ShapeDtypeStruct((9, rows, half * rows), BF16),
         compiler_params=params(),
@@ -319,10 +333,11 @@
             transcendentals=0,
         ),
         name="grad_first",
-    )(moved, own, other)
-
-
-def grad_second_kernel(a, moved, own, other, out):
+    )(moved, own, other, *after)
+
+
+def grad_second_kernel(a, moved, own, other, *refs):
+    out = refs[-1]
     rows = out.shape[2]
     begin, planes = max(0, a), DEPTH - abs(a)
     lhs = [
@@ -344,10 +359,11 @@
             out[at] = grads[:, place * rows : (place + 1) * rows].astype(BF16)
 
 
-def grad_second(a, moved, own, other):
+def grad_second(a, moved, own, other, after):
     wide, rows = own.shape[0], moved.shape[-1]
     return pl.pallas_call(
         functools.partial(grad_second_kernel, a),
+        in_specs=[pl.BlockSpec(memory_space=pltpu.VMEM)] * 3 + [UNREAD] * len(after),
         out_shape=jax.ShapeDtypeStruct((9, wide, rows), BF16),
         compiler_params=pltpu.CompilerParams(vmem_limit_bytes=LIMIT),
         cost_estimate=pl.CostEstimate(
@@ -356,11 +372,12 @@
             transcendentals=0,
         ),
         name="grad_second",
-    )(moved, own, other)
+    )(moved, own, other, *after)
 
 
 def finish_kernel(n, axis, factor, idx, own, other, *refs):
-    out = refs[-1]
+    out, mark = refs[-2:]
+    mark[...] = jnp.zeros_like(mark)
     upper = (idx[0] >= n // 2).astype(jnp.int32) ^ idx[1]
     wide = own.shape[axis]
 
@@ -382,45 +399,82 @@
         put(other, own)
 
 
-def finish(name, n, axis, factor, idx, chunk, own, other, before):
+def finish(name, n, axis, factor, idx, chunk, own, other, before, after):
     taps, height, width = own.shape
-    block = (3, height * 2, width) if axis == 1 else (3, height, width * 2)
-    steps = taps // 3
-    part = pl.BlockSpec((3, height, width), lambda k: (k, 0, 0))
+    block = (1, height * 2, width) if axis == 1 else (1, height, width * 2)
+    part = pl.BlockSpec((1, height, width), lambda k: (k, 0, 0))
     given = [] if before is None else [before]
     return pl.pallas_call(
         functools.partial(finish_kernel, n, axis, factor),
-        grid=(steps,),
-        in_specs=[smem(), part, part] + [pl.BlockSpec(memory_space=pl.ANY)] * len(given),
-        out_specs=pl.BlockSpec(block, lambda k: (chunk * steps + k, 0, 0)),
-        out_shape=jax.ShapeDtypeStruct((27,) + block[1:], F32),
+        grid=(taps,),
+        in_specs=[smem(), part, part] + [UNREAD] * (len(given) + len(after)),
+        out_specs=[
+            pl.BlockSpec(block, lambda k: (chunk * taps + k, 0, 0)),
+            whole((8, 128)),
+        ],
+        out_shape=[
+            jax.ShapeDtypeStruct((27,) + block[1:], F32),
+            jax.ShapeDtypeStruct((8, 128), F32),
+        ],
         input_output_aliases={3: 0} if given else {},
         compiler_params=params(),
         name=name,
-    )(idx, own, other, *given)
-
-
-def add_rounded(x, y):
-    return (x.astype(F32) + y.astype(F32)).astype(BF16)
-
-
-def line_sum(part):
-    chips = lax.axis_size("dp") // 2
-    at = lax.axis_index("dp") // 2
-
-    def send(x, moves):
-        return lax.ppermute(x, "dp", [(2 * i + k, 2 * j + k) for i, j in moves for k in (0, 1)])
-
-    total = part
-    for hop in range(chips // 2 - 1):
-        got = send(total, [(hop, hop + 1), (chips - 1 - hop, chips - 2 - hop)])
-        total = add_rounded(part, got)
+    )(idx, own, other, *given, *after)
+
+
+def add_kernel(x, y, *refs):
+    out = refs[-1]
+    out[...] = (x[...].astype(F32) + y[...].astype(F32)).astype(out.dtype)
+
+
+def pick_kernel(idx, x, y, *refs):
+    out = refs[-1]
+
+    @pl.when(idx[2] == 0)
+    def _():
+        out[...] = x[...]
+
+    @pl.when(idx[2] != 0)
+    def _():
+        out[...] = y[...]
+
+
+def whole_call(kernel, name, x, y, after, idx=None):
+    given = [] if idx is None else [idx]
+    return pl.pallas_call(
+        kernel,
+        in_specs=[smem()] * len(given)
+        + [pl.BlockSpec(memory_space=pltpu.VMEM)] * 2
+        + [UNREAD] * len(after),
+        out_shape=jax.ShapeDtypeStruct(x.shape, x.dtype),
+        compiler_params=pltpu.CompilerParams(vmem_limit_bytes=LIMIT),
+        name=name,
+    )(*given, x, y, *after)
+
+
+def line_moves(chips):
+    inward = [[(h, h + 1), (chips - 1 - h, chips - 2 - h)] for h in range(chips // 2 - 1)]
     mid = chips // 2
-    total = add_rounded(total, send(total, [(mid - 1, mid), (mid, mid - 1)]))
-    for hop in reversed(range(chips // 2 - 1)):
-        got = send(total, [(hop + 1, hop), (chips - 2 - hop, chips - 1 - hop)])
-        total = jnp.where((at == hop) | (at == chips - 1 - hop), got, total)
-    return total
+    outward = [[(j, i) for i, j in moves] for moves in reversed(inward)]
+    return inward + [[(mid - 1, mid), (mid, mid - 1)]], outward
+
+
+def line_send(x, moves):
+    pairs = [(2 * i + k, 2 * j + k) for i, j in moves for k in (0, 1)]
+    return lax.ppermute(x, "dp", pairs)
+
+
+def line_step(step, part, total, idx, place, after):
+    sums, outward = line_moves(lax.axis_size("dp") // 2)
+    if step < len(sums):
+        got = line_send(total, sums[step])
+        base = total if step == len(sums) - 1 else part
+        return whole_call(add_kernel, "line_add", base, got, after)
+    moves = outward[step - len(sums)]
+    got = line_send(total, moves)
+    takes = functools.reduce(jnp.logical_or, [place // 2 == j for _, j in moves])
+    marked = jnp.stack([idx[0], idx[1], takes.astype(jnp.int32)])
+    return whole_call(pick_kernel, "line_pick", total, got, after, marked)
 
 
 def shards(volume, w_first, gain, w_second, cotangent):
@@ -442,26 +496,15 @@
         got = {m: to_partner(parts[m], m) for m in reversed(range(1, n))}
         return [parts[0]] + [got[m] for m in range(1, n)]
 
-    pre_shares = swap(
-        spread_shares(pre_kernel, "pre", idx, n, vol, w_first.reshape(27 * rows, n * rows), [])
-    )
-    dact_shares = swap(
-        spread_shares(
-            dact_kernel, "dact", idx, n, cot, w_second, [pltpu.VMEM((n * rows, 27 * rows), BF16)]
-        )
-    )
-    moved_cot = moved_fields(
-        moved_second_kernel,
-        "moved_second",
-        (2, 3, DEPTH, HEIGHT + 2, WIDTH, rows),
-        cot,
-        to_core(cot),
-    )
-    moved_vol = moved_fields(
-        moved_first_kernel, "moved_first", (2, 9 * rows, CELLS), vol, to_core(vol)
+    first_flat = w_first.reshape(27 * rows, n * rows)
+    pre_parts = spread_shares(pre_kernel, "pre", idx, n, vol, first_flat, [])
+    pre_shares = swap(pre_parts)
+    dact_parts = spread_shares(
+        dact_kernel, "dact", idx, n, cot, w_second, [pltpu.VMEM((n * rows, 27 * rows), BF16)]
     )
     act, normed, inverse = pl.pallas_call(
         functools.partial(norm_kernel, n),
+        in_specs=[pl.BlockSpec(memory_space=pltpu.VMEM)] * (1 + n) + [UNREAD],
         out_shape=[
             jax.ShapeDtypeStruct((CELLS, rows), BF16),
             jax.ShapeDtypeStruct((CELLS, rows), F32),
@@ -469,40 +512,89 @@
         ],
         compiler_params=pltpu.CompilerParams(vmem_limit_bytes=LIMIT),
         name="norm",
-    )(own_gain, *pre_shares)
+    )(own_gain, *pre_shares, dact_parts[0])
     act_blocks = swap([act] * n)
-    act_keep, act_send = halves("act_halves", True, idx, act_blocks)
+    moved_cot = moved_fields(
+        moved_second_kernel,
+        "moved_second",
+        (2, 3, DEPTH, HEIGHT + 2, WIDTH, rows),
+        cot,
+        to_core(cot),
+        act,
+    )
+    moved_vol = moved_fields(
+        moved_first_kernel, "moved_first", (2, 9 * rows, CELLS), vol, to_core(vol), act
+    )
+    act_keep, act_send, *dact_held = halves(
+        "act_halves", True, idx, act_blocks, (moved_cot, moved_vol), dact_parts[1:]
+    )
     act_other = to_core(act_send)
-    second_total = None
-    for chunk, a in enumerate((-1, 0, 1)):
-        summed = line_sum(grad_second(a, moved_cot, act_keep, act_other))
-        second_total = finish(
-            "finish_second", n, 1, factor, idx, chunk, summed, to_core(summed), second_total
+    dact_shares = swap([dact_parts[0]] + dact_held)
+
+    second_parts = []
+    for a in (-1, 0, 1):
+        second_parts.append(
+            grad_second(a, moved_cot, act_keep, act_other, tuple(second_parts[-1:]))
         )
-    output = conv_full("output", 1, False, idx, w_second, act_blocks)
+    output = conv_full("output", 1, False, idx, w_second, act_blocks, (second_parts[-1],))
 
     dpre, gain_part = pl.pallas_call(
         functools.partial(norm_back_kernel, n),
+        in_specs=[pl.BlockSpec(memory_space=pltpu.VMEM)] * (3 + n) + [UNREAD],
         out_shape=[
             jax.ShapeDtypeStruct((CELLS, rows), BF16),
             jax.ShapeDtypeStruct((1, rows), F32),
         ],
         compiler_params=pltpu.CompilerParams(vmem_limit_bytes=LIMIT),
         name="norm_back",
-    )(own_gain, normed, inverse, *dact_shares)
+    )(own_gain, normed, inverse, *dact_shares, output)
     dpre_blocks = swap([dpre] * n)
     dpre_keep, dpre_send = halves("dpre_halves", False, idx, dpre_blocks)
     dpre_other = to_core(dpre_send)
-    first_total = None
-    for chunk, a in enumerate((-1, 0, 1)):
-        summed = line_sum(grad_first(a, moved_vol, dpre_keep, dpre_other))
-        first_total = finish(
-            "finish_first", n, 2, factor, idx, chunk, summed, to_core(summed), first_total
+    first_parts = []
+    for a in (-1, 0, 1):
+        first_parts.append(
+            grad_first(a, moved_vol, dpre_keep, dpre_other, tuple(first_parts[-1:]))
         )
-    grad_volume = conv_full(
-        "grad_volume", -1, True, idx, w_first.reshape(27 * rows, n * rows), dpre_blocks
-    )
-    gain_total = jnp.sum(lax.all_gather(gain_part[0], "dp"), axis=0) * factor
+    parts = second_parts + first_parts
+    totals = list(parts)
+    sums, outward = line_moves(lax.axis_size("dp") // 2)
+    steps = len(sums) + len(outward)
+    crossed = [None] * len(parts)
+    second_total = first_total = None
+    last = ()
+    for turn in range(len(parts) + steps + 1):
+        for step in range(steps):
+            chunk = turn - step
+            if 0 <= chunk < len(parts):
+                totals[chunk] = line_step(step, parts[chunk], totals[chunk], idx, place, last)
+                last = (totals[chunk],)
+                if step == steps - 1:
+                    crossed[chunk] = to_core(totals[chunk])
+        if turn == 5:
+            grad_volume = conv_full(
+                "grad_volume", -1, True, idx, first_flat, dpre_blocks, (first_parts[-1],) + last
+            )
+            last = (grad_volume,)
+        if turn == 2:
+            gain_own = whole_call(add_kernel, "gain_add", gain_part, to_core(gain_part), last)
+            gain_sum = gain_own
+            last = (gain_sum,)
+        if 3 <= turn < 3 + steps:
+            gain_sum = line_step(turn - 3, gain_own, gain_sum, idx, place, last)
+            last = (gain_sum,)
+        chunk = turn - steps
+        if 0 <= chunk < 3:
+            second_total, mark = finish(
+                "finish_second", n, 1, factor, idx, chunk, totals[chunk], crossed[chunk], second_total, last
+            )
+            last = (mark,)
+        elif 3 <= chunk < 6:
+            first_total, mark = finish(
+                "finish_first", n, 2, factor, idx, chunk - 3, totals[chunk], crossed[chunk], first_total, last
+            )
+            last = (mark,)
+    gain_total = gain_sum[0] * factor
     return (output[None], grad_volume[None], first_total, gain_total, second_total)
 
 

time: 272 us -> 200 us (0.74)
  waiting for transfers between devices: 144 us -> 56.3 us
  Pallas kernels: 55.9 us -> 75 us
  blocking collectives: 12.1 us -> 0 us
  starting transfers between devices: 50.1 us -> 58.7 us
    ppermute x18 -> x21, waiting for transfers between devices: 122 us -> 30 us  [line_send(): return lax.ppermute(x, 'dp', pairs)]
    ppermute x18 -> x21, starting transfers between devices: 20 us -> 39.7 us  [line_send(): return lax.ppermute(x, 'dp', pairs)]
    pallas_call x15 -> x37, Pallas kernels: 25 us -> 43.9 us  [the longest x6 25.6 us: finish(): pl.pallas_call(functools.partial(finish_kernel, n, axis, factor), grid=(t...]
    all_gather x1 -> x0, blocking collectives: 12.1 us -> none  [shards(): gain_total = jnp.sum(lax.all_gather(gain_part[0], 'dp'), axis=0) * factor]
    ppermute x10 -> x11, starting transfers between devices: 17.6 us -> 7.34 us  [to_core(): lax.ppermute(x, 'dp', [(i, i ^ 1) for i in range(lax.axis_size('dp'))])]
    unnamed x46 -> x42, local copies, waits for them, and re-layouts: 5.05 us -> 6.93 us
  transfers between devices with their start and end apart: 40 -> 44, of which waited for: 15 -> 13; matrix products, arithmetic and copies ran while one was open for 1% -> 0% of each run, Pallas kernels for 17% -> 35%
where the time goes in v3:
time: 200 us; the launch traced here: 199 us
  Pallas kernels  75 us (38%)
  starting transfers between devices  58.7 us (29%)
  waiting for transfers between devices  56.3 us (28%)
  local copies, waits for them, and re-layouts  7 us (4%)
    ppermute x21, starting transfers between devices, line_send(): return lax.ppermute(x, 'dp', pairs)  39.7 us
    ppermute x21, waiting for transfers between devices, line_send(): return lax.ppermute(x, 'dp', pairs)  30 us
    pallas_call x6, Pallas kernels, finish(): pl.pallas_call(functools.partial(finish_kernel, n, axis, factor), grid=(t...  25.6 us
    ppermute x12, waiting for transfers between devices, to_partner(): return lax.ppermute(x, 'chan', [(i, i ^ m) for i in range(n)])  24.6 us
    pallas_call x2, Pallas kernels, conv_full(): pl.pallas_call(functools.partial(conv_kernel, n, sign, transposed), grid=...  13.1 us
    pallas_call x2, Pallas kernels, spread_shares(): pl.pallas_call(functools.partial(kernel, n), grid=(DEPTH,), in_specs=[sme...  12.4 us
    ppermute x12, starting transfers between devices, to_partner(): return lax.ppermute(x, 'chan', [(i, i ^ m) for i in range(n)])  11.7 us
    pallas_call x22, Pallas kernels, whole_call(): pl.pallas_call(kernel, in_specs=[smem()] * len(given) + [pl.BlockSpec(mem...  9.58 us
  transfers between devices with their start and end apart: 44, of which 13 were waited for; matrix products, arithmetic and copies ran while one was open for 0% of the time, Pallas kernels for 35%

profile of v3, /device:TPU:1, one launch (start us, length us, event | category | flops | bytes accessed | tf_op | source)
XLA Modules:
  0.0 199.0 jit_solution(710550740529393037)
XLA Ops:
  2.3 2.0 %copy-done.19 = bf16[27,128,512]{2,1,0:T(8,128)(2,1)S(1)} copy-done((bf16[27,128,512]{2,1,0:T(8,128)(2,1)S(1)}, bf16[27,128,512]{2,1,0:T(8,128)(2,1)}, u32[]{:S(2)}) %copy-start.19) | copy-done | bytes 3538968
  4.3 6.2 %pre.1 = (bf16[1024,128]{1,0:T(8,128)(2,1)S(1)}, bf16[1024,128]{1,0:T(8,128)(2,1)}, bf16[1024,128]{1,0:T(8,128)(2,1)S(1)}, bf16[1024,128]{1,0:T(8,128)(2,1)S(1)}) custom-call(s32[2]{0:T(128)S(1)} %pad_add_fusion.idx, bf16[128,1024]{1,0:T(8,128)(2,1)S(1)} %bitcast.18, bf16[3456,512]{1,0:T(8,128)(2,1)S(1)} %bitcast.20), custom_call_target="tpu_custom_call" | custom-call | flops 3623878656 | bytes 3538944 | tf_op jit(solution)/shard_map/pre/pallas_call | solution.py:95
  10.5 2.3 %collective-permute-start = (bf16[1024,128]{1,0:T(8,128)(2,1)}, bf16[1024,128]{1,0:T(8,128)(2,1)S(1)}, u32[]{:S(2)}, u32[]{:S(2)}) collective-permute-start(bf16[1024,128]{1,0:T(8,128)(2,1)} %get-tuple-element.37), channel_id=1, source_target_pairs={{0,1},{1,0},{2,3},{3,2},{4,5},{5,4},{6,7},{7,6},{8,9},{9,8},{10,11... | collective-permute-start | bytes 786440 | tf_op jit(solution)/shard_map/ppermute | solution.py:490
  14.1 2.0 %copy-done.17 = bf16[27,512,128]{2,1,0:T(8,128)(2,1)S(1)} copy-done((bf16[27,512,128]{2,1,0:T(8,128)(2,1)S(1)}, bf16[27,512,128]{2,1,0:T(8,128)(2,1)}, u32[]{:S(2)}) %copy-start.17) | copy-done | bytes 3538968
  16.1 6.2 %dact.1 = (bf16[1024,128]{1,0:T(8,128)(2,1)S(1)}, bf16[1024,128]{1,0:T(8,128)(2,1)S(1)}, bf16[1024,128]{1,0:T(8,128)(2,1)S(1)}, bf16[1024,128]{1,0:T(8,128)(2,1)S(1)}) custom-call(s32[2]{0:T(128)S(1)} %pad_add_fusion.idx, bf16[128,1024]{1,0:T(8,128)(2,1)S(1)} %bitcast.13, bf16[27,512,128]{2,1,0:T(8,128)(2,1)S(1)} %copy-done.17), custom_call_target="tpu_custom_call" | custom-call | flops 3623878656 | bytes 3538944 | tf_op jit(solution)/shard_map/dact/pallas_call | solution.py:95
  22.3 3.5 %collective-permute-done.2.refs_3_ = bf16[1024,128]{1,0:T(8,128)(2,1)S(1)} collective-permute-done((bf16[1024,128]{1,0:T(8,128)(2,1)S(1)}, bf16[1024,128]{1,0:T(8,128)(2,1)S(1)}, u32[]{:S(2)}, u32[]{:S(2)}) %collective-permute-start.2) | collective-permute-done | bytes 262176 | tf_op jit(solution)/shard_map/ppermute | solution.py:490
  31.2 2.6 %collective-permute-done.5.refs_3_ = bf16[1024,128]{1,0:T(8,128)(2,1)S(1)} collective-permute-done((bf16[1024,128]{1,0:T(8,128)(2,1)S(1)}, bf16[1024,128]{1,0:T(8,128)(2,1)S(1)}, u32[]{:S(2)}, u32[]{:S(2)}) %collective-permute-start.5) | collective-permute-done | bytes 262176 | tf_op jit(solution)/shard_map/ppermute | solution.py:490
  33.8 7.3 %collective-permute-done.4.refs_2_ = bf16[1024,128]{1,0:T(8,128)(2,1)S(1)} collective-permute-done((bf16[1024,128]{1,0:T(8,128)(2,1)S(1)}, bf16[1024,128]{1,0:T(8,128)(2,1)S(1)}, u32[]{:S(2)}, u32[]{:S(2)}) %collective-permute-start.4) | collective-permute-done | bytes 262176 | tf_op jit(solution)/shard_map/ppermute | solution.py:490
  45.4 3.2 %collective-permute-start.18 = (bf16[9,256,128]{2,1,0:T(8,128)(2,1)S(1)}, bf16[9,256,128]{2,1,0:T(8,128)(2,1)S(1)}, u32[]{:S(2)}, u32[]{:S(2)}) collective-permute-start(bf16[9,256,128]{2,1,0:T(8,128)(2,1)S(1)} %grad_second.3.refs_0_.x), channel_id=1, source_target_pairs={{0,8},{4,12},{24,16},{28,20},{1,9},{5,13},{25,17},{29,21},{2,10},{... | collective-permute-start | bytes 1769480 | tf_op jit(solution)/shard_map/ppermute | solution.py:464
  55.6 6.3 %output.1.refs_4_ = bf16[128,1024]{1,0:T(8,128)(2,1)} custom-call(s32[2]{0:T(128)S(1)} %pad_add_fusion.idx, bf16[27,512,128]{2,1,0:T(8,128)(2,1)S(1)} %copy-done.18, bf16[1024,128]{1,0:T(8,128)(2,1)S(1)} %get-tuple-element.41._.refs_0_, bf16[1024,128]{1,0:T(8,128)(2,1)S(1)} %collective-permute-done.3.refs_1_, ...), custom_call_target="tpu_custom_call" | custom-call | flops 3623878656 | bytes 3538944 | tf_op jit(solution)/shard_map/output/pallas_call | solution.py:201
  67.1 3.6 %collective-permute-done.14.refs_3_ = bf16[1024,128]{1,0:T(8,128)(2,1)S(1)} collective-permute-done((bf16[1024,128]{1,0:T(8,128)(2,1)S(1)}, bf16[1024,128]{1,0:T(8,128)(2,1)S(1)}, u32[]{:S(2)}, u32[]{:S(2)}) %collective-permute-start.14) | collective-permute-done | bytes 262176 | tf_op jit(solution)/shard_map/ppermute | solution.py:490
  70.7 7.6 %collective-permute-done.13.refs_2_ = bf16[1024,128]{1,0:T(8,128)(2,1)S(1)} collective-permute-done((bf16[1024,128]{1,0:T(8,128)(2,1)S(1)}, bf16[1024,128]{1,0:T(8,128)(2,1)S(1)}, u32[]{:S(2)}, u32[]{:S(2)}) %collective-permute-start.13) | collective-permute-done | bytes 262176 | tf_op jit(solution)/shard_map/ppermute | solution.py:490
  79.5 2.1 %collective-permute-start.23 = (bf16[9,256,128]{2,1,0:T(8,128)(2,1)S(1)}, bf16[9,256,128]{2,1,0:T(8,128)(2,1)}, u32[]{:S(2)}, u32[]{:S(2)}) collective-permute-start(bf16[9,256,128]{2,1,0:T(8,128)(2,1)S(1)} %grad_second.5.refs_4_.x), channel_id=1, source_target_pairs={{0,8},{4,12},{24,16},{28,20},{1,9},{5,13},{25,17},{29,21},{2,10},{... | collective-permute-start | bytes 1769480 | tf_op jit(solution)/shard_map/ppermute | solution.py:464
  84.8 1.8 grad_first.3.refs_0_.x
  86.6 5.7 %collective-permute-start.16 = (bf16[9,128,256]{2,1,0:T(8,128)(2,1)S(1)}, bf16[9,128,256]{2,1,0:T(8,128)(2,1)}, u32[]{:S(2)}, u32[]{:S(2)}) collective-permute-start(bf16[9,128,256]{2,1,0:T(8,128)(2,1)S(1)} %grad_first.3.refs_0_.x), channel_id=1, source_target_pairs={{0,8},{4,12},{24,16},{28,20},{1,9},{5,13},{25,17},{29,21},{2,10},{... | collective-permute-start | bytes 1769480 | tf_op jit(solution)/shard_map/ppermute | solution.py:464
  98.2 1.9 collective-permute-done.21.y
  102.5 2.1 %grad_first.4.refs_0_.x = bf16[9,128,256]{2,1,0:T(8,128)(2,1)S(1)} custom-call(bf16[2,1152,1024]{2,1,0:T(8,128)(2,1)S(1)} %copy-done.3, bf16[2,1024,128]{2,1,0:T(8,128)(2,1)S(1)} %get-tuple-element.53.own, bf16[2,1024,128]{2,1,0:T(8,128)(2,1)S(1)} %collective-permute-done.15.other, bf16[9,128,256]{2,1,0:T(8,128)(2,1)S(1)} %grad_first.3.refs_0_.x), custom_call_target="tpu_custom_call" | custom-call | flops 1207959552 | bytes 4718592 | tf_op jit(solution)/shard_map/grad_first/pallas_call | solution.py:318
  104.6 5.1 %collective-permute-start.25 = (bf16[9,128,256]{2,1,0:T(8,128)(2,1)S(1)}, bf16[9,128,256]{2,1,0:T(8,128)(2,1)S(1)}, u32[]{:S(2)}, u32[]{:S(2)}) collective-permute-start(bf16[9,128,256]{2,1,0:T(8,128)(2,1)S(1)} %grad_first.4.refs_0_.x), channel_id=1, source_target_pairs={{0,8},{4,12},{24,16},{28,20},{1,9},{5,13},{25,17},{29,21},{2,10},{... | collective-permute-start | bytes 1769480 | tf_op jit(solution)/shard_map/ppermute | solution.py:464
  111.6 3.3 %collective-permute-start.27 = (f32[1,128]{1,0:T(1,128)S(1)}, f32[1,128]{1,0:T(1,128)S(1)}, u32[]{:S(2)}, u32[]{:S(2)}) collective-permute-start(f32[1,128]{1,0:T(1,128)S(1)} %gain_add.1.refs_0_.x), channel_id=1, source_target_pairs={{0,8},{4,12},{24,16},{28,20},{1,9},{5,13},{25,17},{29,21},{2,10},{... | collective-permute-start | bytes 1544 | tf_op jit(solution)/shard_map/ppermute | solution.py:464
  117.0 5.0 %collective-permute-done.27.y = f32[1,128]{1,0:T(1,128)S(1)} collective-permute-done((f32[1,128]{1,0:T(1,128)S(1)}, f32[1,128]{1,0:T(1,128)S(1)}, u32[]{:S(2)}, u32[]{:S(2)}) %collective-permute-start.27) | collective-permute-done | bytes 544 | tf_op jit(solution)/shard_map/ppermute | solution.py:464
  123.2 1.8 grad_first.5.x.refs_4_
  125.0 4.2 %collective-permute-start.32 = (bf16[9,128,256]{2,1,0:T(8,128)(2,1)S(1)}, bf16[9,128,256]{2,1,0:T(8,128)(2,1)S(1)}, u32[]{:S(2)}, u32[]{:S(2)}) collective-permute-start(bf16[9,128,256]{2,1,0:T(8,128)(2,1)S(1)} %grad_first.5.x.refs_4_), channel_id=1, source_target_pairs={{0,8},{4,12},{24,16},{28,20},{1,9},{5,13},{25,17},{29,21},{2,10},{... | collective-permute-start | bytes 1769480 | tf_op jit(solution)/shard_map/ppermute | solution.py:464
  129.2 4.3 %finish_second.3 = (f32[27,512,128]{2,1,0:T(8,128)}, f32[8,128]{1,0:T(8,128)S(1)}) custom-call(s32[2]{0:T(128)S(1)} %pad_add_fusion.idx, bf16[9,256,128]{2,1,0:T(8,128)(2,1)S(1)} %line_pick.7.refs_0_.own, bf16[9,256,128]{2,1,0:T(8,128)(2,1)S(1)} %collective-permute-done.26.other, f32[1,128]{1,0:T(1,128)S(1)} %line_add.21.refs_0_.x), custom_call_target="tpu_custom_call" | custom-call | tf_op jit(solution)/shard_map/finish_second/pallas_call | solution.py:407
  137.4 4.3 %finish_second.4 = (f32[27,512,128]{2,1,0:T(8,128)}, f32[8,128]{1,0:T(8,128)S(1)}) custom-call(s32[2]{0:T(128)S(1)} %pad_add_fusion.idx, bf16[9,256,128]{2,1,0:T(8,128)(2,1)S(1)} %line_pick.8.refs_0_.own, bf16[9,256,128]{2,1,0:T(8,128)(2,1)S(1)} %collective-permute-done.33.other, ...), custom_call_target="tpu_custom_call", output_to_operand_aliasing={{0}: (3, {})} | custom-call | tf_op jit(solution)/shard_map/finish_second/pallas_call | solution.py:407
  145.5 5.5 %collective-permute-done.30.y = bf16[9,128,256]{2,1,0:T(8,128)(2,1)S(1)} collective-permute-done((bf16[9,128,256]{2,1,0:T(8,128)(2,1)S(1)}, bf16[9,128,256]{2,1,0:T(8,128)(2,1)S(1)}, u32[]{:S(2)}, u32[]{:S(2)}) %collective-permute-start.30) | collective-permute-done | bytes 589856 | tf_op jit(solution)/shard_map/ppermute | solution.py:464
  152.8 6.8 %grad_volume.1.refs_0_ = bf16[128,1024]{1,0:T(8,128)(2,1)} custom-call(s32[2]{0:T(128)S(1)} %pad_add_fusion.idx, bf16[3456,512]{1,0:T(8,128)(2,1)S(1)} %bitcast.21, bf16[1024,128]{1,0:T(8,128)(2,1)S(1)} %copy-done.8, bf16[1024,128]{1,0:T(8,128)(2,1)S(1)} %copy-done.14, bf16[1024,128]{1,0:T(8,128)(2,1)S(1)} %copy-done.12, bf16[1024,128]{1,0:T(8,128)(2,1)S(1)} %copy-done.10, ...), custom_call_target="tpu_custom_call" | custom-call | flops 3623878656 | bytes 3538944 | tf_op jit(solution)/shard_map/grad_volume/pallas_call | solution.py:201
  161.1 4.3 %finish_second.5 = (f32[27,512,128]{2,1,0:T(8,128)}, f32[8,128]{1,0:T(8,128)S(1)}) custom-call(s32[2]{0:T(128)S(1)} %pad_add_fusion.idx, bf16[9,256,128]{2,1,0:T(8,128)(2,1)S(1)} %line_pick.9.refs_0_.own, bf16[9,256,128]{2,1,0:T(8,128)(2,1)S(1)} %collective-permute-done.37.other, ...), custom_call_target="tpu_custom_call", output_to_operand_aliasing={{0}: (3, {})} | custom-call | tf_op jit(solution)/shard_map/finish_second/pallas_call | solution.py:407
  166.8 6.6 %collective-permute-done.41.y = bf16[9,128,256]{2,1,0:T(8,128)(2,1)S(1)} collective-permute-done((bf16[9,128,256]{2,1,0:T(8,128)(2,1)S(1)}, bf16[9,128,256]{2,1,0:T(8,128)(2,1)S(1)}, u32[]{:S(2)}, u32[]{:S(2)}) %collective-permute-start.41) | collective-permute-done | bytes 589856 | tf_op jit(solution)/shard_map/ppermute | solution.py:464
  174.9 4.2 %finish_first.3 = (f32[27,128,512]{2,1,0:T(8,128)}, f32[8,128]{1,0:T(8,128)S(1)}) custom-call(s32[2]{0:T(128)S(1)} %pad_add_fusion.idx, bf16[9,128,256]{2,1,0:T(8,128)(2,1)S(1)} %line_pick.10.refs_5_.own, bf16[9,128,256]{2,1,0:T(8,128)(2,1)S(1)} %collective-permute-done.40.other, bf16[9,128,256]{2,1,0:T(8,128)(2,1)S(1)} %line_pick.12.refs_0_.own), custom_call_target="tpu_custom_call" | custom-call | tf_op jit(solution)/shard_map/finish_first/pallas_call | solution.py:407
  179.1 9.5 %collective-permute-done.39.y = bf16[9,128,256]{2,1,0:T(8,128)(2,1)S(1)} collective-permute-done((bf16[9,128,256]{2,1,0:T(8,128)(2,1)S(1)}, bf16[9,128,256]{2,1,0:T(8,128)(2,1)S(1)}, u32[]{:S(2)}, u32[]{:S(2)}) %collective-permute-start.39) | collective-permute-done | bytes 589856 | tf_op jit(solution)/shard_map/ppermute | solution.py:464
  190.5 4.2 %finish_first.4 = (f32[27,128,512]{2,1,0:T(8,128)}, f32[8,128]{1,0:T(8,128)S(1)}) custom-call(s32[2]{0:T(128)S(1)} %pad_add_fusion.idx, bf16[9,128,256]{2,1,0:T(8,128)(2,1)S(1)} %line_pick.12.refs_0_.own, bf16[9,128,256]{2,1,0:T(8,128)(2,1)S(1)} %collective-permute-done.43.other, ...), custom_call_target="tpu_custom_call", output_to_operand_aliasing={{0}: (3, {})} | custom-call | tf_op jit(solution)/shard_map/finish_first/pallas_call | solution.py:407
  194.7 4.2 %finish_first.5 = (f32[27,128,512]{2,1,0:T(8,128)}, f32[8,128]{1,0:T(8,128)}) custom-call(s32[2]{0:T(128)S(1)} %pad_add_fusion.idx, bf16[9,128,256]{2,1,0:T(8,128)(2,1)S(1)} %line_pick.13.refs_1_.own, bf16[9,128,256]{2,1,0:T(8,128)(2,1)S(1)} %collective-permute-done.42.other, ...), custom_call_target="tpu_custom_call", output_to_operand_aliasing={{0}: (3, {})} | custom-call | tf_op jit(solution)/shard_map/finish_first/pallas_call | solution.py:407
  (146 shorter events, 58.0 us)
Async XLA Ops:
  0.7 29.1 %collective-permute-start.7 = (bf16[128,1024]{1,0:T(8,128)(2,1)}, bf16[128,1024]{1,0:T(8,128)(2,1)S(1)}, u32[]{:S(2)}, u32[]{:S(2)}) collective-permute-start(bf16[128,1024]{1,0:T(8,128)(2,1)} %bitcast.17), channel_id=1, source_target_pairs={{0,4},{4,0},{8,12},{12,8},{16,20},{20,16},{24,28},{28,24},{1,5},{5... | collective-permute-start | bytes 786440 | tf_op jit(solution)/shard_map/ppermute | solution.py:493
  0.8 28.3 %collective-permute-start.6 = (bf16[128,1024]{1,0:T(8,128)(2,1)}, bf16[128,1024]{1,0:T(8,128)(2,1)S(1)}, u32[]{:S(2)}, u32[]{:S(2)}) collective-permute-start(bf16[128,1024]{1,0:T(8,128)(2,1)} %bitcast.12), channel_id=1, source_target_pairs={{0,4},{4,0},{8,12},{12,8},{16,20},{20,16},{24,28},{28,24},{1,5},{5... | collective-permute-start | bytes 786440 | tf_op jit(solution)/shard_map/ppermute | solution.py:493
  10.5 11.8 %collective-permute-start = (bf16[1024,128]{1,0:T(8,128)(2,1)}, bf16[1024,128]{1,0:T(8,128)(2,1)S(1)}, u32[]{:S(2)}, u32[]{:S(2)}) collective-permute-start(bf16[1024,128]{1,0:T(8,128)(2,1)} %get-tuple-element.37), channel_id=1, source_target_pairs={{0,1},{1,0},{2,3},{3,2},{4,5},{5,4},{6,7},{7,6},{8,9},{9,8},{10,11... | collective-permute-start | bytes 786440 | tf_op jit(solution)/shard_map/ppermute | solution.py:490
  27.6 13.5 %collective-permute-start.4 = (bf16[1024,128]{1,0:T(8,128)(2,1)S(1)}, bf16[1024,128]{1,0:T(8,128)(2,1)S(1)}, u32[]{:S(2)}, u32[]{:S(2)}) collective-permute-start(bf16[1024,128]{1,0:T(8,128)(2,1)S(1)} %get-tuple-element.41._.refs_0_), channel_id=1, source_target_pairs={{0,2},{1,3},{2,0},{3,1},{4,6},{5,7},{6,4},{7,5},{8,10},{9,11},{10,... | collective-permute-start | bytes 786440 | tf_op jit(solution)/shard_map/ppermute | solution.py:490
  28.8 12.3 %collective-permute-start.3 = (bf16[1024,128]{1,0:T(8,128)(2,1)S(1)}, bf16[1024,128]{1,0:T(8,128)(2,1)S(1)}, u32[]{:S(2)}, u32[]{:S(2)}) collective-permute-start(bf16[1024,128]{1,0:T(8,128)(2,1)S(1)} %get-tuple-element.41._.refs_0_), channel_id=1, source_target_pairs={{0,1},{1,0},{2,3},{3,2},{4,5},{5,4},{6,7},{7,6},{8,9},{9,8},{10,11... | collective-permute-start | bytes 786440 | tf_op jit(solution)/shard_map/ppermute | solution.py:490
  45.4 20.9 %collective-permute-start.18 = (bf16[9,256,128]{2,1,0:T(8,128)(2,1)S(1)}, bf16[9,256,128]{2,1,0:T(8,128)(2,1)S(1)}, u32[]{:S(2)}, u32[]{:S(2)}) collective-permute-start(bf16[9,256,128]{2,1,0:T(8,128)(2,1)S(1)} %grad_second.3.refs_0_.x), channel_id=1, source_target_pairs={{0,8},{4,12},{24,16},{28,20},{1,9},{5,13},{25,17},{29,21},{2,10},{... | collective-permute-start | bytes 1769480 | tf_op jit(solution)/shard_map/ppermute | solution.py:464
  48.6 13.3 %collective-permute-start.9 = (bf16[1024,128]{1,0:T(8,128)(2,1)S(1)}, bf16[1024,128]{1,0:T(8,128)(2,1)S(1)}, u32[]{:S(2)}, u32[]{:S(2)}) collective-permute-start(bf16[1024,128]{1,0:T(8,128)(2,1)S(1)} %get-tuple-element.49), channel_id=1, source_target_pairs={{0,1},{1,0},{2,3},{3,2},{4,5},{5,4},{6,7},{7,6},{8,9},{9,8},{10,11... | collective-permute-start | bytes 786440 | tf_op jit(solution)/shard_map/ppermute | solution.py:490
  49.2 12.7 %collective-permute-start.10 = (bf16[1024,128]{1,0:T(8,128)(2,1)S(1)}, bf16[1024,128]{1,0:T(8,128)(2,1)S(1)}, u32[]{:S(2)}, u32[]{:S(2)}) collective-permute-start(bf16[1024,128]{1,0:T(8,128)(2,1)S(1)} %get-tuple-element.50), channel_id=1, source_target_pairs={{0,2},{1,3},{2,0},{3,1},{4,6},{5,7},{6,4},{7,5},{8,10},{9,11},{10,... | collective-permute-start | bytes 786440 | tf_op jit(solution)/shard_map/ppermute | solution.py:490
  52.8 28.8 %collective-permute-start.20 = (bf16[9,256,128]{2,1,0:T(8,128)(2,1)S(1)}, bf16[9,256,128]{2,1,0:T(8,128)(2,1)S(1)}, u32[]{:S(2)}, u32[]{:S(2)}) collective-permute-start(bf16[9,256,128]{2,1,0:T(8,128)(2,1)S(1)} %grad_second.4.refs_0_.x), channel_id=1, source_target_pairs={{0,8},{4,12},{24,16},{28,20},{1,9},{5,13},{25,17},{29,21},{2,10},{... | collective-permute-start | bytes 1769480 | tf_op jit(solution)/shard_map/ppermute | solution.py:464
  64.8 13.5 %collective-permute-start.13 = (bf16[1024,128]{1,0:T(8,128)(2,1)S(1)}, bf16[1024,128]{1,0:T(8,128)(2,1)S(1)}, u32[]{:S(2)}, u32[]{:S(2)}) collective-permute-start(bf16[1024,128]{1,0:T(8,128)(2,1)S(1)} %get-tuple-element.52.refs_0_), channel_id=1, source_target_pairs={{0,2},{1,3},{2,0},{3,1},{4,6},{5,7},{6,4},{7,5},{8,10},{9,11},{10,... | collective-permute-start | bytes 786440 | tf_op jit(solution)/shard_map/ppermute | solution.py:490
  65.6 12.7 %collective-permute-start.12 = (bf16[1024,128]{1,0:T(8,128)(2,1)S(1)}, bf16[1024,128]{1,0:T(8,128)(2,1)S(1)}, u32[]{:S(2)}, u32[]{:S(2)}) collective-permute-start(bf16[1024,128]{1,0:T(8,128)(2,1)S(1)} %get-tuple-element.52.refs_0_), channel_id=1, source_target_pairs={{0,1},{1,0},{2,3},{3,2},{4,5},{5,4},{6,7},{7,6},{8,9},{9,8},{10,11... | collective-permute-start | bytes 786440 | tf_op jit(solution)/shard_map/ppermute | solution.py:490
  66.4 16.9 %collective-permute-start.19 = (bf16[9,256,128]{2,1,0:T(8,128)(2,1)S(1)}, bf16[9,256,128]{2,1,0:T(8,128)(2,1)S(1)}, u32[]{:S(2)}, u32[]{:S(2)}) collective-permute-start(bf16[9,256,128]{2,1,0:T(8,128)(2,1)S(1)} %line_add.14.refs_0_.x), channel_id=1, source_target_pairs={{8,16},{12,20},{16,8},{20,12},{9,17},{13,21},{17,9},{21,13},{10,18... | collective-permute-start | bytes 1769480 | tf_op jit(solution)/shard_map/ppermute | solution.py:464
  79.5 14.1 %collective-permute-start.23 = (bf16[9,256,128]{2,1,0:T(8,128)(2,1)S(1)}, bf16[9,256,128]{2,1,0:T(8,128)(2,1)}, u32[]{:S(2)}, u32[]{:S(2)}) collective-permute-start(bf16[9,256,128]{2,1,0:T(8,128)(2,1)S(1)} %grad_second.5.refs_4_.x), channel_id=1, source_target_pairs={{0,8},{4,12},{24,16},{28,20},{1,9},{5,13},{25,17},{29,21},{2,10},{... | collective-permute-start | bytes 1769480 | tf_op jit(solution)/shard_map/ppermute | solution.py:464
  81.8 13.8 %collective-permute-start.22 = (bf16[9,256,128]{2,1,0:T(8,128)(2,1)S(1)}, bf16[9,256,128]{2,1,0:T(8,128)(2,1)}, u32[]{:S(2)}, u32[]{:S(2)}) collective-permute-start(bf16[9,256,128]{2,1,0:T(8,128)(2,1)S(1)} %line_add.15.refs_0_.x), channel_id=1, source_target_pairs={{8,16},{12,20},{16,8},{20,12},{9,17},{13,21},{17,9},{21,13},{10,18... | collective-permute-start | bytes 1769480 | tf_op jit(solution)/shard_map/ppermute | solution.py:464
  83.4 16.7 %collective-permute-start.21 = (bf16[9,256,128]{2,1,0:T(8,128)(2,1)S(1)}, bf16[9,256,128]{2,1,0:T(8,128)(2,1)}, u32[]{:S(2)}, u32[]{:S(2)}) collective-permute-start(bf16[9,256,128]{2,1,0:T(8,128)(2,1)S(1)} %line_add.16.refs_0_.x), channel_id=1, source_target_pairs={{8,0},{12,4},{16,24},{20,28},{9,1},{13,5},{17,25},{21,29},{10,2},{... | collective-permute-start | bytes 1769480 | tf_op jit(solution)/shard_map/ppermute | solution.py:464
  86.6 23.1 %collective-permute-start.16 = (bf16[9,128,256]{2,1,0:T(8,128)(2,1)S(1)}, bf16[9,128,256]{2,1,0:T(8,128)(2,1)}, u32[]{:S(2)}, u32[]{:S(2)}) collective-permute-start(bf16[9,128,256]{2,1,0:T(8,128)(2,1)S(1)} %grad_first.3.refs_0_.x), channel_id=1, source_target_pairs={{0,8},{4,12},{24,16},{28,20},{1,9},{5,13},{25,17},{29,21},{2,10},{... | collective-permute-start | bytes 1769480 | tf_op jit(solution)/shard_map/ppermute | solution.py:464
  94.9 16.7 %collective-permute-start.29 = (bf16[9,256,128]{2,1,0:T(8,128)(2,1)S(1)}, bf16[9,256,128]{2,1,0:T(8,128)(2,1)S(1)}, u32[]{:S(2)}, u32[]{:S(2)}) collective-permute-start(bf16[9,256,128]{2,1,0:T(8,128)(2,1)S(1)} %line_add.17.refs_0_.x), channel_id=1, source_target_pairs={{8,16},{12,20},{16,8},{20,12},{9,17},{13,21},{17,9},{21,13},{10,18... | collective-permute-start | bytes 1769480 | tf_op jit(solution)/shard_map/ppermute | solution.py:464
  96.8 18.3 %collective-permute-start.28 = (bf16[9,256,128]{2,1,0:T(8,128)(2,1)S(1)}, bf16[9,256,128]{2,1,0:T(8,128)(2,1)S(1)}, u32[]{:S(2)}, u32[]{:S(2)}) collective-permute-start(bf16[9,256,128]{2,1,0:T(8,128)(2,1)S(1)} %line_add.18.refs_0_.x), channel_id=1, source_target_pairs={{8,0},{12,4},{16,24},{20,28},{9,1},{13,5},{17,25},{21,29},{10,2},{... | collective-permute-start | bytes 1769480 | tf_op jit(solution)/shard_map/ppermute | solution.py:464
  101.2 23.7 %collective-permute-start.26 = (bf16[9,256,128]{2,1,0:T(8,128)(2,1)S(1)}, bf16[9,256,128]{2,1,0:T(8,128)(2,1)S(1)}, u32[]{:S(2)}, u32[]{:S(2)}) collective-permute-start(bf16[9,256,128]{2,1,0:T(8,128)(2,1)S(1)} %line_pick.7.refs_0_.own), channel_id=1, source_target_pairs={{0,4},{4,0},{8,12},{12,8},{16,20},{20,16},{24,28},{28,24},{1,5},{5... | collective-permute-start | bytes 1769480 | tf_op jit(solution)/shard_map/ppermute | solution.py:493
  104.6 28.9 %collective-permute-start.25 = (bf16[9,128,256]{2,1,0:T(8,128)(2,1)S(1)}, bf16[9,128,256]{2,1,0:T(8,128)(2,1)S(1)}, u32[]{:S(2)}, u32[]{:S(2)}) collective-permute-start(bf16[9,128,256]{2,1,0:T(8,128)(2,1)S(1)} %grad_first.4.refs_0_.x), channel_id=1, source_target_pairs={{0,8},{4,12},{24,16},{28,20},{1,9},{5,13},{25,17},{29,21},{2,10},{... | collective-permute-start | bytes 1769480 | tf_op jit(solution)/shard_map/ppermute | solution.py:464
  110.9 23.4 %collective-permute-start.24 = (bf16[9,128,256]{2,1,0:T(8,128)(2,1)S(1)}, bf16[9,128,256]{2,1,0:T(8,128)(2,1)S(1)}, u32[]{:S(2)}, u32[]{:S(2)}) collective-permute-start(bf16[9,128,256]{2,1,0:T(8,128)(2,1)S(1)} %line_add.19.refs_0_.x), channel_id=1, source_target_pairs={{8,16},{12,20},{16,8},{20,12},{9,17},{13,21},{17,9},{21,13},{10,18... | collective-permute-start | bytes 1769480 | tf_op jit(solution)/shard_map/ppermute | solution.py:464
  115.1 20.7 %collective-permute-start.35 = (bf16[9,256,128]{2,1,0:T(8,128)(2,1)S(1)}, bf16[9,256,128]{2,1,0:T(8,128)(2,1)S(1)}, u32[]{:S(2)}, u32[]{:S(2)}) collective-permute-start(bf16[9,256,128]{2,1,0:T(8,128)(2,1)S(1)} %line_add.20.refs_0_.x), channel_id=1, source_target_pairs={{8,0},{12,4},{16,24},{20,28},{9,1},{13,5},{17,25},{21,29},{10,2},{... | collective-permute-start | bytes 1769480 | tf_op jit(solution)/shard_map/ppermute | solution.py:464
  121.9 15.5 %collective-permute-start.33 = (bf16[9,256,128]{2,1,0:T(8,128)(2,1)S(1)}, bf16[9,256,128]{2,1,0:T(8,128)(2,1)S(1)}, u32[]{:S(2)}, u32[]{:S(2)}) collective-permute-start(bf16[9,256,128]{2,1,0:T(8,128)(2,1)S(1)} %line_pick.8.refs_0_.own), channel_id=1, source_target_pairs={{0,4},{4,0},{8,12},{12,8},{16,20},{20,16},{24,28},{28,24},{1,5},{5... | collective-permute-start | bytes 1769480 | tf_op jit(solution)/shard_map/ppermute | solution.py:493
  125.0 16.9 %collective-permute-start.32 = (bf16[9,128,256]{2,1,0:T(8,128)(2,1)S(1)}, bf16[9,128,256]{2,1,0:T(8,128)(2,1)S(1)}, u32[]{:S(2)}, u32[]{:S(2)}) collective-permute-start(bf16[9,128,256]{2,1,0:T(8,128)(2,1)S(1)} %grad_first.5.x.refs_4_), channel_id=1, source_target_pairs={{0,8},{4,12},{24,16},{28,20},{1,9},{5,13},{25,17},{29,21},{2,10},{... | collective-permute-start | bytes 1769480 | tf_op jit(solution)/shard_map/ppermute | solution.py:464
  134.4 16.5 %collective-permute-start.30 = (bf16[9,128,256]{2,1,0:T(8,128)(2,1)S(1)}, bf16[9,128,256]{2,1,0:T(8,128)(2,1)S(1)}, u32[]{:S(2)}, u32[]{:S(2)}) collective-permute-start(bf16[9,128,256]{2,1,0:T(8,128)(2,1)S(1)} %line_add.23.refs_0_.x), channel_id=1, source_target_pairs={{8,0},{12,4},{16,24},{20,28},{9,1},{13,5},{17,25},{21,29},{10,2},{... | collective-permute-start | bytes 1769480 | tf_op jit(solution)/shard_map/ppermute | solution.py:464
  137.0 24.1 %collective-permute-start.37 = (bf16[9,256,128]{2,1,0:T(8,128)(2,1)S(1)}, bf16[9,256,128]{2,1,0:T(8,128)(2,1)S(1)}, u32[]{:S(2)}, u32[]{:S(2)}) collective-permute-start(bf16[9,256,128]{2,1,0:T(8,128)(2,1)S(1)} %line_pick.9.refs_0_.own), channel_id=1, source_target_pairs={{0,4},{4,0},{8,12},{12,8},{16,20},{20,16},{24,28},{28,24},{1,5},{5... | collective-permute-start | bytes 1769480 | tf_op jit(solution)/shard_map/ppermute | solution.py:493
  142.0 23.4 %collective-permute-start.36 = (bf16[9,128,256]{2,1,0:T(8,128)(2,1)S(1)}, bf16[9,128,256]{2,1,0:T(8,128)(2,1)S(1)}, u32[]{:S(2)}, u32[]{:S(2)}) collective-permute-start(bf16[9,128,256]{2,1,0:T(8,128)(2,1)S(1)} %line_add.25.refs_0_.x), channel_id=1, source_target_pairs={{8,16},{12,20},{16,8},{20,12},{9,17},{13,21},{17,9},{21,13},{10,18... | collective-permute-start | bytes 1769480 | tf_op jit(solution)/shard_map/ppermute | solution.py:464
  142.7 16.9 %collective-permute-start.38 = (f32[1,128]{1,0:T(1,128)S(1)}, f32[1,128]{1,0:T(1,128)S(1)}, u32[]{:S(2)}, u32[]{:S(2)}) collective-permute-start(f32[1,128]{1,0:T(1,128)S(1)} %line_add.24.refs_1_.x), channel_id=1, source_target_pairs={{8,0},{12,4},{16,24},{20,28},{9,1},{13,5},{17,25},{21,29},{10,2},{... | collective-permute-start | bytes 1544 | tf_op jit(solution)/shard_map/ppermute | solution.py:464
  144.2 29.3 %collective-permute-start.41 = (bf16[9,128,256]{2,1,0:T(8,128)(2,1)S(1)}, bf16[9,128,256]{2,1,0:T(8,128)(2,1)S(1)}, u32[]{:S(2)}, u32[]{:S(2)}) collective-permute-start(bf16[9,128,256]{2,1,0:T(8,128)(2,1)S(1)} %line_add.26.refs_0_.x), channel_id=1, source_target_pairs={{8,0},{12,4},{16,24},{20,28},{9,1},{13,5},{17,25},{21,29},{10,2},{... | collective-permute-start | bytes 1769480 | tf_op jit(solution)/shard_map/ppermute | solution.py:464
  151.6 23.3 %collective-permute-start.40 = (bf16[9,128,256]{2,1,0:T(8,128)(2,1)S(1)}, bf16[9,128,256]{2,1,0:T(8,128)(2,1)S(1)}, u32[]{:S(2)}, u32[]{:S(2)}) collective-permute-start(bf16[9,128,256]{2,1,0:T(8,128)(2,1)S(1)} %line_pick.10.refs_5_.own), channel_id=1, source_target_pairs={{0,4},{4,0},{8,12},{12,8},{16,20},{20,16},{24,28},{28,24},{1,5},{5... | collective-permute-start | bytes 1769480 | tf_op jit(solution)/shard_map/ppermute | solution.py:493
  165.5 23.1 %collective-permute-start.39 = (bf16[9,128,256]{2,1,0:T(8,128)(2,1)S(1)}, bf16[9,128,256]{2,1,0:T(8,128)(2,1)S(1)}, u32[]{:S(2)}, u32[]{:S(2)}) collective-permute-start(bf16[9,128,256]{2,1,0:T(8,128)(2,1)S(1)} %line_add.27.refs_0_.x), channel_id=1, source_target_pairs={{8,0},{12,4},{16,24},{20,28},{9,1},{13,5},{17,25},{21,29},{10,2},{... | collective-permute-start | bytes 1769480 | tf_op jit(solution)/shard_map/ppermute | solution.py:464
  174.0 16.5 %collective-permute-start.43 = (bf16[9,128,256]{2,1,0:T(8,128)(2,1)S(1)}, bf16[9,128,256]{2,1,0:T(8,128)(2,1)S(1)}, u32[]{:S(2)}, u32[]{:S(2)}) collective-permute-start(bf16[9,128,256]{2,1,0:T(8,128)(2,1)S(1)} %line_pick.12.refs_0_.own), channel_id=1, source_target_pairs={{0,4},{4,0},{8,12},{12,8},{16,20},{20,16},{24,28},{28,24},{1,5},{5... | collective-permute-start | bytes 1769480 | tf_op jit(solution)/shard_map/ppermute | solution.py:493
  (33 other events, 342.9 us)

commit v4 on v3

--- a/solution.py
+++ b/solution.py
@@ -13,7 +13,9 @@
 CELLS = DEPTH * PLANE
 TAPS = [(a, b, c) for a in (-1, 0, 1) for b in (-1, 0, 1) for c in (-1, 0, 1)]
 NORM_EPS = 1e-05
-LIMIT = 26 * 1024 * 1024
+LIMIT = 24 * 1024 * 1024
+SMALL = 8 * 1024 * 1024
+EXTRA = 16
 F32, BF16 = jnp.float32, jnp.bfloat16
 NT = (((1,), (1,)), ((), ()))
 UNREAD = pl.BlockSpec(memory_space=pl.ANY)
@@ -300,40 +302,47 @@
     )(own, other, after)
 
 
-def grad_first_kernel(a, moved, own, other, *refs):
+def split_rows(values):
+    high = values.astype(BF16)
+    low = (values - high.astype(F32)).astype(BF16)
+    empty = jnp.zeros((EXTRA - 2, values.shape[1]), F32)
+    return jnp.concatenate([high.astype(F32), low.astype(F32), empty], axis=0).astype(BF16)
+
+
+def grad_first_kernel(a, moved, own, other, gain_part, *refs):
     out = refs[-1]
-    rows, half = out.shape[1], own.shape[0]
+    half, rows = own.shape[0], own.shape[2]
     begin, count = max(0, -a) * PLANE, (DEPTH - abs(a)) * PLANE
-    grads = None
-    for which, ref in enumerate((own, other)):
-        rhs = jnp.concatenate([ref[j, begin : begin + count] for j in range(half)], axis=1)
-        lhs = moved[which, :, begin + a * PLANE : begin + a * PLANE + count]
-        part = jnp.dot(lhs, rhs, preferred_element_type=F32)
-        grads = part if grads is None else grads + part
-    out[...] = grads.astype(BF16).reshape(out.shape)
-
-
-def grad_first(a, moved, own, other, after):
+    rhs = [
+        jnp.concatenate([ref[j, begin : begin + count] for j in range(half)], axis=1)
+        for ref in (own, other)
+    ]
+    for b in range(3):
+        span = slice(3 * rows * b, 3 * rows * (b + 1))
+        grads = None
+        for which in range(2):
+            lhs = moved[which, span, begin + a * PLANE : begin + a * PLANE + count]
+            part = jnp.dot(lhs, rhs[which], preferred_element_type=F32)
+            grads = part if grads is None else grads + part
+        out[span] = grads.astype(BF16)
+    filler = jnp.zeros((1, out.shape[1] - rows), F32)
+    out[9 * rows :] = split_rows(jnp.concatenate([gain_part[...], filler], axis=1))
+
+
+def grad_first(a, moved, own, other, gain_part, after):
     half, cells, rows = own.shape
     return pl.pallas_call(
         functools.partial(grad_first_kernel, a),
-        grid=(3,),
-        in_specs=[
-            pl.BlockSpec((2, 3 * rows, cells), lambda b: (0, b, 0)),
-            whole(own.shape),
-            whole(own.shape),
-        ]
-        + [UNREAD] * len(after),
-        out_specs=pl.BlockSpec((3, rows, half * rows), lambda b: (b, 0, 0)),
-        out_shape=jax.ShapeDtypeStruct((9, rows, half * rows), BF16),
-        compiler_params=params(),
+        in_specs=[pl.BlockSpec(memory_space=pltpu.VMEM)] * 4 + [UNREAD] * len(after),
+        out_shape=jax.ShapeDtypeStruct((9 * rows + EXTRA, half * rows), BF16),
+        compiler_params=pltpu.CompilerParams(vmem_limit_bytes=LIMIT),
         cost_estimate=pl.CostEstimate(
             flops=2 * 9 * rows * rows * half * 2 * (DEPTH - abs(a)) * PLANE,
             bytes_accessed=2 * moved.size,
             transcendentals=0,
         ),
         name="grad_first",
-    )(moved, own, other, *after)
+    )(moved, own, other, gain_part, *after)
 
 
 def grad_second_kernel(a, moved, own, other, *refs):
@@ -375,56 +384,52 @@
     )(moved, own, other, *after)
 
 
-def finish_kernel(n, axis, factor, idx, own, other, *refs):
-    out, mark = refs[-2:]
+def finish_kernel(n, axis, factor, chunk, idx, own, other, *refs):
+    out, mark, wide, sems = refs[-4:]
+    upper = (idx[0] >= n // 2).astype(jnp.int32) ^ idx[1]
+    taps, height, width = wide.shape[1:]
+    copies = []
+    for k, (part, place) in enumerate(((own, upper), (other, 1 - upper))):
+        rows = part[: taps * height] if len(part.shape) == 2 else part[...]
+        wide[k] = rows.reshape(taps, height, width).astype(F32) * factor
+        size = (height, width)[axis - 1]
+        span = pl.ds(pl.multiple_of(place * size, size), size)
+        target = out.at[pl.ds(chunk * taps, taps)]
+        target = target.at[:, span] if axis == 1 else target.at[:, :, span]
+        copies.append(pltpu.make_async_copy(wide.at[k], target, sems.at[k]))
+        copies[-1].start()
     mark[...] = jnp.zeros_like(mark)
-    upper = (idx[0] >= n // 2).astype(jnp.int32) ^ idx[1]
-    wide = own.shape[axis]
-
-    def put(low, high):
-        parts = (low[...].astype(F32) * factor, high[...].astype(F32) * factor)
-        if axis == 1:
-            out[:, :wide] = parts[0]
-            out[:, wide:] = parts[1]
-        else:
-            out[:, :, :wide] = parts[0]
-            out[:, :, wide:] = parts[1]
-
-    @pl.when(upper == 0)
-    def _():
-        put(own, other)
-
-    @pl.when(upper != 0)
-    def _():
-        put(other, own)
-
-
-def finish(name, n, axis, factor, idx, chunk, own, other, before, after):
-    taps, height, width = own.shape
-    block = (1, height * 2, width) if axis == 1 else (1, height, width * 2)
-    part = pl.BlockSpec((1, height, width), lambda k: (k, 0, 0))
+    for copy in copies:
+        copy.wait()
+
+
+def finish(name, n, axis, factor, idx, chunk, shape, own, other, before, after):
+    taps, height, width = shape
     given = [] if before is None else [before]
-    return pl.pallas_call(
-        functools.partial(finish_kernel, n, axis, factor),
-        grid=(taps,),
-        in_specs=[smem(), part, part] + [UNREAD] * (len(given) + len(after)),
-        out_specs=[
-            pl.BlockSpec(block, lambda k: (chunk * taps + k, 0, 0)),
-            whole((8, 128)),
-        ],
-        out_shape=[
-            jax.ShapeDtypeStruct((27,) + block[1:], F32),
-            jax.ShapeDtypeStruct((8, 128), F32),
-        ],
+    full = (27, height * 2, width) if axis == 1 else (27, height, width * 2)
+    return pl.pallas_call(
+        functools.partial(finish_kernel, n, axis, factor, chunk),
+        in_specs=[smem()]
+        + [pl.BlockSpec(memory_space=pltpu.VMEM)] * 2
+        + [UNREAD] * (len(given) + len(after)),
+        out_specs=[UNREAD, pl.BlockSpec(memory_space=pltpu.VMEM)],
+        out_shape=[jax.ShapeDtypeStruct(full, F32), jax.ShapeDtypeStruct((8, 128), F32)],
+        scratch_shapes=[pltpu.VMEM((2,) + shape, F32), pltpu.SemaphoreType.DMA((2,))],
         input_output_aliases={3: 0} if given else {},
-        compiler_params=params(),
+        compiler_params=pltpu.CompilerParams(vmem_limit_bytes=SMALL),
         name=name,
     )(idx, own, other, *given, *after)
 
 
 def add_kernel(x, y, *refs):
     out = refs[-1]
-    out[...] = (x[...].astype(F32) + y[...].astype(F32)).astype(out.dtype)
+    if len(x.shape) == 3:
+        out[...] = (x[...].astype(F32) + y[...].astype(F32)).astype(BF16)
+    else:
+        rows = x.shape[0] - EXTRA
+        out[:rows] = (x[:rows].astype(F32) + y[:rows].astype(F32)).astype(BF16)
+        tail = x[rows:].astype(F32) + y[rows:].astype(F32)
+        out[rows:] = split_rows(tail[:1] + tail[1:2])
 
 
 def pick_kernel(idx, x, y, *refs):
@@ -447,7 +452,7 @@
         + [pl.BlockSpec(memory_space=pltpu.VMEM)] * 2
         + [UNREAD] * len(after),
         out_shape=jax.ShapeDtypeStruct(x.shape, x.dtype),
-        compiler_params=pltpu.CompilerParams(vmem_limit_bytes=LIMIT),
+        compiler_params=pltpu.CompilerParams(vmem_limit_bytes=SMALL),
         name=name,
     )(*given, x, y, *after)
 
@@ -531,13 +536,48 @@
     act_other = to_core(act_send)
     dact_shares = swap([dact_parts[0]] + dact_held)
 
-    second_parts = []
-    for a in (-1, 0, 1):
-        second_parts.append(
-            grad_second(a, moved_cot, act_keep, act_other, tuple(second_parts[-1:]))
-        )
-    output = conv_full("output", 1, False, idx, w_second, act_blocks, (second_parts[-1],))
-
+    sums, outward = line_moves(lax.axis_size("dp") // 2)
+    steps = len(sums) + len(outward)
+    parts, totals, crossed = {}, {}, {}
+    last = ()
+
+    def line(chunk, step):
+        nonlocal last
+        before = totals.get(chunk, parts[chunk])
+        totals[chunk] = line_step(step, parts[chunk], before, idx, place, last)
+        last = (totals[chunk],)
+        if step == steps - 1:
+            crossed[chunk] = to_core(totals[chunk])
+
+    def turn(at, written):
+        nonlocal last
+        for step in range(steps):
+            if 0 <= at - step < 6:
+                line(at - step, step)
+        chunk = at - steps
+        if 0 <= chunk < 6:
+            name, axis = ("finish_second", 1) if chunk < 3 else ("finish_first", 2)
+            shape = (9, n // 2 * rows, rows) if chunk < 3 else (9, rows, n // 2 * rows)
+            written[axis], mark = finish(
+                name,
+                n,
+                axis,
+                factor,
+                idx,
+                chunk % 3,
+                shape,
+                totals[chunk],
+                crossed[chunk],
+                written.get(axis),
+                last,
+            )
+            last = (mark,)
+
+    written = {}
+    for chunk in range(3):
+        parts[chunk] = grad_second(chunk - 1, moved_cot, act_keep, act_other, last)
+        last = (parts[chunk],)
+    turn(0, written)
     dpre, gain_part = pl.pallas_call(
         functools.partial(norm_back_kernel, n),
         in_specs=[pl.BlockSpec(memory_space=pltpu.VMEM)] * (3 + n) + [UNREAD],
@@ -545,57 +585,30 @@
             jax.ShapeDtypeStruct((CELLS, rows), BF16),
             jax.ShapeDtypeStruct((1, rows), F32),
         ],
-        compiler_params=pltpu.CompilerParams(vmem_limit_bytes=LIMIT),
+        compiler_params=pltpu.CompilerParams(vmem_limit_bytes=SMALL),
         name="norm_back",
-    )(own_gain, normed, inverse, *dact_shares, output)
+    )(own_gain, normed, inverse, *dact_shares, *last)
     dpre_blocks = swap([dpre] * n)
-    dpre_keep, dpre_send = halves("dpre_halves", False, idx, dpre_blocks)
+    output = conv_full("output", 1, False, idx, w_second, act_blocks, (dpre,))
+    last = (output,)
+    turn(1, written)
+    dpre_keep, dpre_send = halves("dpre_halves", False, idx, dpre_blocks, last)
     dpre_other = to_core(dpre_send)
-    first_parts = []
-    for a in (-1, 0, 1):
-        first_parts.append(
-            grad_first(a, moved_vol, dpre_keep, dpre_other, tuple(first_parts[-1:]))
-        )
-    parts = second_parts + first_parts
-    totals = list(parts)
-    sums, outward = line_moves(lax.axis_size("dp") // 2)
-    steps = len(sums) + len(outward)
-    crossed = [None] * len(parts)
-    second_total = first_total = None
-    last = ()
-    for turn in range(len(parts) + steps + 1):
-        for step in range(steps):
-            chunk = turn - step
-            if 0 <= chunk < len(parts):
-                totals[chunk] = line_step(step, parts[chunk], totals[chunk], idx, place, last)
-                last = (totals[chunk],)
-                if step == steps - 1:
-                    crossed[chunk] = to_core(totals[chunk])
-        if turn == 5:
-            grad_volume = conv_full(
-                "grad_volume", -1, True, idx, first_flat, dpre_blocks, (first_parts[-1],) + last
-            )
-            last = (grad_volume,)
-        if turn == 2:
-            gain_own = whole_call(add_kernel, "gain_add", gain_part, to_core(gain_part), last)
-            gain_sum = gain_own
-            last = (gain_sum,)
-        if 3 <= turn < 3 + steps:
-            gain_sum = line_step(turn - 3, gain_own, gain_sum, idx, place, last)
-            last = (gain_sum,)
-        chunk = turn - steps
-        if 0 <= chunk < 3:
-            second_total, mark = finish(
-                "finish_second", n, 1, factor, idx, chunk, totals[chunk], crossed[chunk], second_total, last
-            )
-            last = (mark,)
-        elif 3 <= chunk < 6:
-            first_total, mark = finish(
-                "finish_first", n, 2, factor, idx, chunk - 3, totals[chunk], crossed[chunk], first_total, last
-            )
-            last = (mark,)
-    gain_total = gain_sum[0] * factor
-    return (output[None], grad_volume[None], first_total, gain_total, second_total)
+    parts[3] = grad_first(-1, moved_vol, dpre_keep, dpre_other, gain_part, last)
+    last = (parts[3],)
+    turn(2, written)
+    for chunk in (4, 5):
+        parts[chunk] = grad_first(chunk - 4, moved_vol, dpre_keep, dpre_other, gain_part, last)
+        last = (parts[chunk],)
+    turn(3, written)
+    grad_volume = conv_full("grad_volume", -1, True, idx, first_flat, dpre_blocks, last)
+    last = (grad_volume,)
+    for at in range(4, 6 + steps):
+        turn(at, written)
+    gain_rows = totals[3][9 * rows : 9 * rows + 2, :rows].astype(F32)
+    gain_rows_other = crossed[3][9 * rows : 9 * rows + 2, :rows].astype(F32)
+    gain_total = (jnp.sum(gain_rows, axis=0) + jnp.sum(gain_rows_other, axis=0)) * factor
+    return (output[None], grad_volume[None], written[2], gain_total, written[1])
 
 
 def solution(mesh):

time: 200 us -> 191 us (0.955)
  Pallas kernels: 75 us -> 58.1 us
  local copies, waits for them, and re-layouts: 7 us -> 11.5 us
  starting transfers between devices: 58.7 us -> 61.4 us
    pallas_call x9, Pallas kernels: 31.2 us -> 16.4 us  [the longest x6 12.9 us: finish(): pl.pallas_call(functools.partial(finish_kernel, n, axis, factor, chunk),...]
    ppermute x21 -> x18, waiting for transfers between devices: 30 us -> 40 us  [line_send(): return lax.ppermute(x, 'dp', pairs)]
    ppermute x12, waiting for transfers between devices: 24.6 us -> 15.9 us  [to_partner(): return lax.ppermute(x, 'chan', [(i, i ^ m) for i in range(n)])]
    unnamed x42, local copies, waits for them, and re-layouts: 6.93 us -> 11.4 us
    ppermute x11 -> x10, starting transfers between devices: 7.34 us -> 10.7 us  [to_core(): lax.ppermute(x, 'dp', [(i, i ^ 1) for i in range(lax.axis_size('dp'))])]
    pallas_call x22 -> x18, Pallas kernels: 9.58 us -> 7.37 us  [whole_call(): pl.pallas_call(kernel, in_specs=[smem()] * len(given) + [pl.BlockSpec(mem...]
    ppermute x21 -> x18, starting transfers between devices: 39.7 us -> 38.9 us  [line_send(): return lax.ppermute(x, 'dp', pairs)]
  transfers between devices with their start and end apart: 44 -> 40, of which waited for: 13 -> 12; matrix products, arithmetic and copies ran while one was open for 0% -> 0% of each run, Pallas kernels for 35% -> 27%
where the time goes in v4:
time: 191 us
  starting transfers between devices  61.4 us (32%)
  Pallas kernels  58.1 us (30%)
  waiting for transfers between devices  57.4 us (30%)
  local copies, waits for them, and re-layouts  11.5 us (6%)
    ppermute x18, waiting for transfers between devices, line_send(): return lax.ppermute(x, 'dp', pairs)  40 us
    ppermute x18, starting transfers between devices, line_send(): return lax.ppermute(x, 'dp', pairs)  38.9 us
    ppermute x12, waiting for transfers between devices, to_partner(): return lax.ppermute(x, 'chan', [(i, i ^ m) for i in range(n)])  15.9 us
    pallas_call x2, Pallas kernels, conv_full(): pl.pallas_call(functools.partial(conv_kernel, n, sign, transposed), grid=...  13 us
    pallas_call x6, Pallas kernels, finish(): pl.pallas_call(functools.partial(finish_kernel, n, axis, factor, chunk),...  12.9 us
    pallas_call x2, Pallas kernels, spread_shares(): pl.pallas_call(functools.partial(kernel, n), grid=(DEPTH,), in_specs=[sme...  11.8 us
    ppermute x12, starting transfers between devices, to_partner(): return lax.ppermute(x, 'chan', [(i, i ^ m) for i in range(n)])  11.8 us
    unnamed x42, local copies, waits for them, and re-layouts  11.4 us
  transfers between devices with their start and end apart: 40, of which 12 were waited for; matrix products, arithmetic and copies ran while one was open for 0% of the time, Pallas kernels for 27%

profile of v4, /device:TPU:1, one launch (start us, length us, event | category | flops | bytes accessed | tf_op | source)
XLA Modules:
  0.0 190.6 jit_solution(4752849989122248482)
XLA Ops:
  2.3 2.0 %copy-done.19 = bf16[27,128,512]{2,1,0:T(8,128)(2,1)S(1)} copy-done((bf16[27,128,512]{2,1,0:T(8,128)(2,1)S(1)}, bf16[27,128,512]{2,1,0:T(8,128)(2,1)}, u32[]{:S(2)}) %copy-start.19) | copy-done | bytes 3538968
  4.3 5.6 %pre.1 = (bf16[1024,128]{1,0:T(8,128)(2,1)S(1)}, bf16[1024,128]{1,0:T(8,128)(2,1)S(1)}, bf16[1024,128]{1,0:T(8,128)(2,1)S(1)}, bf16[1024,128]{1,0:T(8,128)(2,1)S(1)}) custom-call(s32[2]{0:T(128)S(1)} %pad_add_fusion.idx, bf16[128,1024]{1,0:T(8,128)(2,1)S(1)} %bitcast.16, bf16[3456,512]{1,0:T(8,128)(2,1)S(1)} %bitcast.18), custom_call_target="tpu_custom_call" | custom-call | flops 3623878656 | bytes 3538944 | tf_op jit(solution)/shard_map/pre/pallas_call | solution.py:97
  9.8 2.4 %collective-permute-start = (bf16[1024,128]{1,0:T(8,128)(2,1)S(1)}, bf16[1024,128]{1,0:T(8,128)(2,1)S(1)}, u32[]{:S(2)}, u32[]{:S(2)}) collective-permute-start(bf16[1024,128]{1,0:T(8,128)(2,1)S(1)} %get-tuple-element.37), channel_id=1, source_target_pairs={{0,1},{1,0},{2,3},{3,2},{4,5},{5,4},{6,7},{7,6},{8,9},{9,8},{10,11... | collective-permute-start | bytes 786440 | tf_op jit(solution)/shard_map/ppermute | solution.py:495
  13.5 2.0 %copy-done.17 = bf16[27,512,128]{2,1,0:T(8,128)(2,1)S(1)} copy-done((bf16[27,512,128]{2,1,0:T(8,128)(2,1)S(1)}, bf16[27,512,128]{2,1,0:T(8,128)(2,1)}, u32[]{:S(2)}) %copy-start.17) | copy-done | bytes 3538968
  15.5 6.2 %dact.1 = (bf16[1024,128]{1,0:T(8,128)(2,1)S(1)}, bf16[1024,128]{1,0:T(8,128)(2,1)S(1)}, bf16[1024,128]{1,0:T(8,128)(2,1)S(1)}, bf16[1024,128]{1,0:T(8,128)(2,1)S(1)}) custom-call(s32[2]{0:T(128)S(1)} %pad_add_fusion.idx, bf16[128,1024]{1,0:T(8,128)(2,1)S(1)} %bitcast.11, bf16[27,512,128]{2,1,0:T(8,128)(2,1)S(1)} %copy-done.17), custom_call_target="tpu_custom_call" | custom-call | flops 3623878656 | bytes 3538944 | tf_op jit(solution)/shard_map/dact/pallas_call | solution.py:97
  21.8 3.3 %collective-permute-done.2.refs_3_ = bf16[1024,128]{1,0:T(8,128)(2,1)S(1)} collective-permute-done((bf16[1024,128]{1,0:T(8,128)(2,1)S(1)}, bf16[1024,128]{1,0:T(8,128)(2,1)S(1)}, u32[]{:S(2)}, u32[]{:S(2)}) %collective-permute-start.2) | collective-permute-done | bytes 262176 | tf_op jit(solution)/shard_map/ppermute | solution.py:495
  30.5 2.5 %collective-permute-done.5.refs_3_ = bf16[1024,128]{1,0:T(8,128)(2,1)S(1)} collective-permute-done((bf16[1024,128]{1,0:T(8,128)(2,1)S(1)}, bf16[1024,128]{1,0:T(8,128)(2,1)S(1)}, u32[]{:S(2)}, u32[]{:S(2)}) %collective-permute-start.5) | collective-permute-done | bytes 262176 | tf_op jit(solution)/shard_map/ppermute | solution.py:495
  32.9 7.5 %collective-permute-done.4.refs_2_ = bf16[1024,128]{1,0:T(8,128)(2,1)S(1)} collective-permute-done((bf16[1024,128]{1,0:T(8,128)(2,1)S(1)}, bf16[1024,128]{1,0:T(8,128)(2,1)S(1)}, u32[]{:S(2)}, u32[]{:S(2)}) %collective-permute-start.4) | collective-permute-done | bytes 262176 | tf_op jit(solution)/shard_map/ppermute | solution.py:495
  41.3 2.2 %copy-done.2 = bf16[2,1152,1024]{2,1,0:T(8,128)(2,1)} copy-done((bf16[2,1152,1024]{2,1,0:T(8,128)(2,1)}, bf16[2,1152,1024]{2,1,0:T(8,128)(2,1)S(1)}, u32[]{:S(2)}) %copy-start.2) | copy-done | bytes 4718616
  46.7 3.5 %collective-permute-start.12 = (bf16[9,256,128]{2,1,0:T(8,128)(2,1)S(1)}, bf16[9,256,128]{2,1,0:T(8,128)(2,1)S(1)}, u32[]{:S(2)}, u32[]{:S(2)}) collective-permute-start(bf16[9,256,128]{2,1,0:T(8,128)(2,1)S(1)} %grad_second.3.refs_0_.x), channel_id=1, source_target_pairs={{0,8},{4,12},{24,16},{28,20},{1,9},{5,13},{25,17},{29,21},{2,10},{... | collective-permute-start | bytes 1769480 | tf_op jit(solution)/shard_map/ppermute | solution.py:469
  57.0 5.5 %collective-permute-done.12.y = bf16[9,256,128]{2,1,0:T(8,128)(2,1)S(1)} collective-permute-done((bf16[9,256,128]{2,1,0:T(8,128)(2,1)S(1)}, bf16[9,256,128]{2,1,0:T(8,128)(2,1)S(1)}, u32[]{:S(2)}, u32[]{:S(2)}) %collective-permute-start.12) | collective-permute-done | bytes 589856 | tf_op jit(solution)/shard_map/ppermute | solution.py:469
  67.0 6.6 %output.1.refs_0_ = bf16[128,1024]{1,0:T(8,128)(2,1)} custom-call(s32[2]{0:T(128)S(1)} %pad_add_fusion.idx, bf16[27,512,128]{2,1,0:T(8,128)(2,1)S(1)} %copy-done.18, bf16[1024,128]{1,0:T(8,128)(2,1)S(1)} %get-tuple-element.41._.refs_0_, bf16[1024,128]{1,0:T(8,128)(2,1)S(1)} %collective-permute-done.3.refs_1_, ...), custom_call_target="tpu_custom_call" | custom-call | flops 3623878656 | bytes 3538944 | tf_op jit(solution)/shard_map/output/pallas_call | solution.py:203
  73.5 1.6 collective-permute-done.17.y
  76.4 2.6 %collective-permute-done.14.refs_2_ = bf16[1024,128]{1,0:T(8,128)(2,1)S(1)} collective-permute-done((bf16[1024,128]{1,0:T(8,128)(2,1)S(1)}, bf16[1024,128]{1,0:T(8,128)(2,1)S(1)}, u32[]{:S(2)}, u32[]{:S(2)}) %collective-permute-start.14) | collective-permute-done | bytes 262176 | tf_op jit(solution)/shard_map/ppermute | solution.py:495
  81.0 7.4 %collective-permute-start.20 = (bf16[9,256,128]{2,1,0:T(8,128)(2,1)S(1)}, bf16[9,256,128]{2,1,0:T(8,128)(2,1)}, u32[]{:S(2)}, u32[]{:S(2)}) collective-permute-start(bf16[9,256,128]{2,1,0:T(8,128)(2,1)S(1)} %grad_second.5.refs_0_.x), channel_id=1, source_target_pairs={{0,8},{4,12},{24,16},{28,20},{1,9},{5,13},{25,17},{29,21},{2,10},{... | collective-permute-start | bytes 1769480 | tf_op jit(solution)/shard_map/ppermute | solution.py:469
  91.3 2.3 %copy-done.3 = bf16[2,1152,1024]{2,1,0:T(8,128)(2,1)S(1)} copy-done((bf16[2,1152,1024]{2,1,0:T(8,128)(2,1)S(1)}, bf16[2,1152,1024]{2,1,0:T(8,128)(2,1)}, u32[]{:S(2)}) %copy-start.3) | copy-done | bytes 4718616
  94.7 4.1 %collective-permute-start.25 = (bf16[1168,256]{1,0:T(8,128)(2,1)S(1)}, bf16[1168,256]{1,0:T(8,128)(2,1)S(1)}, u32[]{:S(2)}, u32[]{:S(2)}) collective-permute-start(bf16[1168,256]{1,0:T(8,128)(2,1)S(1)} %grad_first.3.refs_0_.x), channel_id=1, source_target_pairs={{0,8},{4,12},{24,16},{28,20},{1,9},{5,13},{25,17},{29,21},{2,10},{... | collective-permute-start | bytes 1794056 | tf_op jit(solution)/shard_map/ppermute | solution.py:469
  98.7 1.6 collective-permute-done.20.y
  109.7 4.7 %collective-permute-start.30 = (bf16[1168,256]{1,0:T(8,128)(2,1)S(1)}, bf16[1168,256]{1,0:T(8,128)(2,1)S(1)}, u32[]{:S(2)}, u32[]{:S(2)}) collective-permute-start(bf16[1168,256]{1,0:T(8,128)(2,1)S(1)} %grad_first.4.refs_0_.x), channel_id=1, source_target_pairs={{0,8},{4,12},{24,16},{28,20},{1,9},{5,13},{25,17},{29,21},{2,10},{... | collective-permute-start | bytes 1794056 | tf_op jit(solution)/shard_map/ppermute | solution.py:469
  116.3 5.0 %collective-permute-start.26 = (bf16[1168,256]{1,0:T(8,128)(2,1)S(1)}, bf16[1168,256]{1,0:T(8,128)(2,1)S(1)}, u32[]{:S(2)}, u32[]{:S(2)}) collective-permute-start(bf16[1168,256]{1,0:T(8,128)(2,1)S(1)} %grad_first.5.refs_0_.x), channel_id=1, source_target_pairs={{0,8},{4,12},{24,16},{28,20},{1,9},{5,13},{25,17},{29,21},{2,10},{... | collective-permute-start | bytes 1794056 | tf_op jit(solution)/shard_map/ppermute | solution.py:469
  123.4 3.4 %collective-permute-start.27 = (bf16[9,256,128]{2,1,0:T(8,128)(2,1)S(1)}, bf16[9,256,128]{2,1,0:T(8,128)(2,1)S(1)}, u32[]{:S(2)}, u32[]{:S(2)}) collective-permute-start(bf16[9,256,128]{2,1,0:T(8,128)(2,1)S(1)} %line_pick.7.refs_0_.own), channel_id=1, source_target_pairs={{0,4},{4,0},{8,12},{12,8},{16,20},{20,16},{24,28},{28,24},{1,5},{5... | collective-permute-start | bytes 1769480 | tf_op jit(solution)/shard_map/ppermute | solution.py:498
  126.8 2.0 %finish_second.3 = (f32[27,512,128]{2,1,0:T(8,128)}, f32[8,128]{1,0:T(8,128)S(1)}) custom-call(s32[2]{0:T(128)S(1)} %pad_add_fusion.idx, bf16[9,256,128]{2,1,0:T(8,128)(2,1)S(1)} %line_pick.6.refs_0_.own, bf16[9,256,128]{2,1,0:T(8,128)(2,1)S(1)} %collective-permute-done.22.other, bf16[9,256,128]{2,1,0:T(8,128)(2,1)S(1)} %line_pick.7.refs_0_.own), custom_call_target="tpu_custom_call" | custom-call | tf_op jit(solution)/shard_map/finish_second/pallas_call | solution.py:410
  128.9 6.4 %grad_volume.1.refs_0_ = bf16[128,1024]{1,0:T(8,128)(2,1)} custom-call(s32[2]{0:T(128)S(1)} %pad_add_fusion.idx, bf16[3456,512]{1,0:T(8,128)(2,1)S(1)} %bitcast.19, bf16[1024,128]{1,0:T(8,128)(2,1)S(1)} %copy-done.6, bf16[1024,128]{1,0:T(8,128)(2,1)S(1)} %copy-done.12, bf16[1024,128]{1,0:T(8,128)(2,1)S(1)} %copy-done.10, bf16[1024,128]{1,0:T(8,128)(2,1)S(1)} %copy-done.8, ...), custom_call_target="tpu_custom_call" | custom-call | flops 3623878656 | bytes 3538944 | tf_op jit(solution)/shard_map/grad_volume/pallas_call | solution.py:203
  139.2 2.1 %finish_second.4 = (f32[27,512,128]{2,1,0:T(8,128)}, f32[8,128]{1,0:T(8,128)S(1)}) custom-call(s32[2]{0:T(128)S(1)} %pad_add_fusion.idx, bf16[9,256,128]{2,1,0:T(8,128)(2,1)S(1)} %line_pick.7.refs_0_.own, bf16[9,256,128]{2,1,0:T(8,128)(2,1)S(1)} %collective-permute-done.27.other, ...), custom_call_target="tpu_custom_call", output_to_operand_aliasing={{0}: (3, {})} | custom-call | tf_op jit(solution)/shard_map/finish_second/pallas_call | solution.py:410
  144.2 11.8 %collective-permute-done.33.y = bf16[1168,256]{1,0:T(8,128)(2,1)S(1)} collective-permute-done((bf16[1168,256]{1,0:T(8,128)(2,1)S(1)}, bf16[1168,256]{1,0:T(8,128)(2,1)S(1)}, u32[]{:S(2)}, u32[]{:S(2)}) %collective-permute-start.33) | collective-permute-done | bytes 598048 | tf_op jit(solution)/shard_map/ppermute | solution.py:469
  157.3 2.0 %finish_second.5 = (f32[27,512,128]{2,1,0:T(8,128)}, f32[8,128]{1,0:T(8,128)S(1)}) custom-call(s32[2]{0:T(128)S(1)} %pad_add_fusion.idx, bf16[9,256,128]{2,1,0:T(8,128)(2,1)S(1)} %line_pick.8.refs_1_.own, bf16[9,256,128]{2,1,0:T(8,128)(2,1)S(1)} %collective-permute-done.32.other, ...), custom_call_target="tpu_custom_call", output_to_operand_aliasing={{0}: (3, {})} | custom-call | tf_op jit(solution)/shard_map/finish_second/pallas_call | solution.py:410
  160.8 9.1 %collective-permute-done.37.y = bf16[1168,256]{1,0:T(8,128)(2,1)S(1)} collective-permute-done((bf16[1168,256]{1,0:T(8,128)(2,1)S(1)}, bf16[1168,256]{1,0:T(8,128)(2,1)S(1)}, u32[]{:S(2)}, u32[]{:S(2)}) %collective-permute-start.37) | collective-permute-done | bytes 598048 | tf_op jit(solution)/shard_map/ppermute | solution.py:469
  170.5 1.9 collective-permute-start.39
  172.3 2.0 %finish_first.3 = (f32[27,128,512]{2,1,0:T(8,128)}, f32[8,128]{1,0:T(8,128)S(1)}) custom-call(s32[2]{0:T(128)S(1)} %pad_add_fusion.idx, bf16[1168,256]{1,0:T(8,128)(2,1)S(1)} %line_pick.9.refs_1_.own, bf16[1168,256]{1,0:T(8,128)(2,1)S(1)} %collective-permute-done.36.other, bf16[1168,256]{1,0:T(8,128)(2,1)S(1)} %line_pick.10.refs_0_.own), custom_call_target="tpu_custom_call" | custom-call | tf_op jit(solution)/shard_map/finish_first/pallas_call | solution.py:410
  174.4 8.7 %collective-permute-done.35.y = bf16[1168,256]{1,0:T(8,128)(2,1)S(1)} collective-permute-done((bf16[1168,256]{1,0:T(8,128)(2,1)S(1)}, bf16[1168,256]{1,0:T(8,128)(2,1)S(1)}, u32[]{:S(2)}, u32[]{:S(2)}) %collective-permute-start.35) | collective-permute-done | bytes 598048 | tf_op jit(solution)/shard_map/ppermute | solution.py:469
  185.7 2.0 %finish_first.4 = (f32[27,128,512]{2,1,0:T(8,128)}, f32[8,128]{1,0:T(8,128)S(1)}) custom-call(s32[2]{0:T(128)S(1)} %pad_add_fusion.idx, bf16[1168,256]{1,0:T(8,128)(2,1)S(1)} %line_pick.10.refs_0_.own, bf16[1168,256]{1,0:T(8,128)(2,1)S(1)} %collective-permute-done.39.other, ...), custom_call_target="tpu_custom_call", output_to_operand_aliasing={{0}: (3, {})} | custom-call | tf_op jit(solution)/shard_map/finish_first/pallas_call | solution.py:410
  187.8 2.6 %finish_first.5 = (f32[27,128,512]{2,1,0:T(8,128)}, f32[8,128]{1,0:T(8,128)}) custom-call(s32[2]{0:T(128)S(1)} %pad_add_fusion.idx, bf16[1168,256]{1,0:T(8,128)(2,1)S(1)} %line_pick.11.refs_1_.own, bf16[1168,256]{1,0:T(8,128)(2,1)S(1)} %collective-permute-done.38.other, f32[27,128,512]{2,1,0:T(8,128)} %get-tuple-element.63.refs_0_, ...), custom_call_target="tpu_custom_call", output_to_operand_aliasing={{0}: (3, {})} | custom-call | tf_op jit(solution)/shard_map/finish_first/pallas_call | solution.py:410
  (136 shorter events, 56.4 us)
Async XLA Ops:
  0.7 28.3 %collective-permute-start.7 = (bf16[128,1024]{1,0:T(8,128)(2,1)}, bf16[128,1024]{1,0:T(8,128)(2,1)S(1)}, u32[]{:S(2)}, u32[]{:S(2)}) collective-permute-start(bf16[128,1024]{1,0:T(8,128)(2,1)} %bitcast.15), channel_id=1, source_target_pairs={{0,4},{4,0},{8,12},{12,8},{16,20},{20,16},{24,28},{28,24},{1,5},{5... | collective-permute-start | bytes 786440 | tf_op jit(solution)/shard_map/ppermute | solution.py:498
  0.8 27.5 %collective-permute-start.6 = (bf16[128,1024]{1,0:T(8,128)(2,1)}, bf16[128,1024]{1,0:T(8,128)(2,1)S(1)}, u32[]{:S(2)}, u32[]{:S(2)}) collective-permute-start(bf16[128,1024]{1,0:T(8,128)(2,1)} %bitcast.10), channel_id=1, source_target_pairs={{0,4},{4,0},{8,12},{12,8},{16,20},{20,16},{24,28},{28,24},{1,5},{5... | collective-permute-start | bytes 786440 | tf_op jit(solution)/shard_map/ppermute | solution.py:498
  9.8 11.9 %collective-permute-start = (bf16[1024,128]{1,0:T(8,128)(2,1)S(1)}, bf16[1024,128]{1,0:T(8,128)(2,1)S(1)}, u32[]{:S(2)}, u32[]{:S(2)}) collective-permute-start(bf16[1024,128]{1,0:T(8,128)(2,1)S(1)} %get-tuple-element.37), channel_id=1, source_target_pairs={{0,1},{1,0},{2,3},{3,2},{4,5},{5,4},{6,7},{7,6},{8,9},{9,8},{10,11... | collective-permute-start | bytes 786440 | tf_op jit(solution)/shard_map/ppermute | solution.py:495
  26.8 13.6 %collective-permute-start.4 = (bf16[1024,128]{1,0:T(8,128)(2,1)S(1)}, bf16[1024,128]{1,0:T(8,128)(2,1)S(1)}, u32[]{:S(2)}, u32[]{:S(2)}) collective-permute-start(bf16[1024,128]{1,0:T(8,128)(2,1)S(1)} %get-tuple-element.41._.refs_0_), channel_id=1, source_target_pairs={{0,2},{1,3},{2,0},{3,1},{4,6},{5,7},{6,4},{7,5},{8,10},{9,11},{10,... | collective-permute-start | bytes 786440 | tf_op jit(solution)/shard_map/ppermute | solution.py:495
  28.0 12.4 %collective-permute-start.3 = (bf16[1024,128]{1,0:T(8,128)(2,1)S(1)}, bf16[1024,128]{1,0:T(8,128)(2,1)S(1)}, u32[]{:S(2)}, u32[]{:S(2)}) collective-permute-start(bf16[1024,128]{1,0:T(8,128)(2,1)S(1)} %get-tuple-element.41._.refs_0_), channel_id=1, source_target_pairs={{0,1},{1,0},{2,3},{3,2},{4,5},{5,4},{6,7},{7,6},{8,9},{9,8},{10,11... | collective-permute-start | bytes 786440 | tf_op jit(solution)/shard_map/ppermute | solution.py:495
  46.7 15.8 %collective-permute-start.12 = (bf16[9,256,128]{2,1,0:T(8,128)(2,1)S(1)}, bf16[9,256,128]{2,1,0:T(8,128)(2,1)S(1)}, u32[]{:S(2)}, u32[]{:S(2)}) collective-permute-start(bf16[9,256,128]{2,1,0:T(8,128)(2,1)S(1)} %grad_second.3.refs_0_.x), channel_id=1, source_target_pairs={{0,8},{4,12},{24,16},{28,20},{1,9},{5,13},{25,17},{29,21},{2,10},{... | collective-permute-start | bytes 1769480 | tf_op jit(solution)/shard_map/ppermute | solution.py:469
  50.2 13.3 %collective-permute-start.8 = (bf16[1024,128]{1,0:T(8,128)(2,1)S(1)}, bf16[1024,128]{1,0:T(8,128)(2,1)S(1)}, u32[]{:S(2)}, u32[]{:S(2)}) collective-permute-start(bf16[1024,128]{1,0:T(8,128)(2,1)S(1)} %get-tuple-element.47), channel_id=1, source_target_pairs={{0,1},{1,0},{2,3},{3,2},{4,5},{5,4},{6,7},{7,6},{8,9},{9,8},{10,11... | collective-permute-start | bytes 786440 | tf_op jit(solution)/shard_map/ppermute | solution.py:495
  50.8 12.7 %collective-permute-start.9 = (bf16[1024,128]{1,0:T(8,128)(2,1)S(1)}, bf16[1024,128]{1,0:T(8,128)(2,1)S(1)}, u32[]{:S(2)}, u32[]{:S(2)}) collective-permute-start(bf16[1024,128]{1,0:T(8,128)(2,1)S(1)} %get-tuple-element.48), channel_id=1, source_target_pairs={{0,2},{1,3},{2,0},{3,1},{4,6},{5,7},{6,4},{7,5},{8,10},{9,11},{10,... | collective-permute-start | bytes 786440 | tf_op jit(solution)/shard_map/ppermute | solution.py:495
  54.5 20.7 %collective-permute-start.17 = (bf16[9,256,128]{2,1,0:T(8,128)(2,1)S(1)}, bf16[9,256,128]{2,1,0:T(8,128)(2,1)S(1)}, u32[]{:S(2)}, u32[]{:S(2)}) collective-permute-start(bf16[9,256,128]{2,1,0:T(8,128)(2,1)S(1)} %grad_second.4.refs_0_.x), channel_id=1, source_target_pairs={{0,8},{4,12},{24,16},{28,20},{1,9},{5,13},{25,17},{29,21},{2,10},{... | collective-permute-start | bytes 1769480 | tf_op jit(solution)/shard_map/ppermute | solution.py:469
  62.7 13.6 %collective-permute-start.16 = (bf16[9,256,128]{2,1,0:T(8,128)(2,1)S(1)}, bf16[9,256,128]{2,1,0:T(8,128)(2,1)S(1)}, u32[]{:S(2)}, u32[]{:S(2)}) collective-permute-start(bf16[9,256,128]{2,1,0:T(8,128)(2,1)S(1)} %line_add.12.refs_4_.x), channel_id=1, source_target_pairs={{8,16},{12,20},{16,8},{20,12},{9,17},{13,21},{17,9},{21,13},{10,18... | collective-permute-start | bytes 1769480 | tf_op jit(solution)/shard_map/ppermute | solution.py:469
  64.2 12.2 %collective-permute-start.15 = (bf16[1024,128]{1,0:T(8,128)(2,1)S(1)}, bf16[1024,128]{1,0:T(8,128)(2,1)S(1)}, u32[]{:S(2)}, u32[]{:S(2)}) collective-permute-start(bf16[1024,128]{1,0:T(8,128)(2,1)S(1)} %get-tuple-element.52.refs_4_.refs_0_), channel_id=1, source_target_pairs={{0,3},{1,2},{2,1},{3,0},{4,7},{5,6},{6,5},{7,4},{8,11},{9,10},{10,... | collective-permute-start | bytes 786440 | tf_op jit(solution)/shard_map/ppermute | solution.py:495
  65.5 13.5 %collective-permute-start.14 = (bf16[1024,128]{1,0:T(8,128)(2,1)S(1)}, bf16[1024,128]{1,0:T(8,128)(2,1)S(1)}, u32[]{:S(2)}, u32[]{:S(2)}) collective-permute-start(bf16[1024,128]{1,0:T(8,128)(2,1)S(1)} %get-tuple-element.52.refs_4_.refs_0_), channel_id=1, source_target_pairs={{0,2},{1,3},{2,0},{3,1},{4,6},{5,7},{6,4},{7,5},{8,10},{9,11},{10,... | collective-permute-start | bytes 786440 | tf_op jit(solution)/shard_map/ppermute | solution.py:495
  66.3 12.8 %collective-permute-start.13 = (bf16[1024,128]{1,0:T(8,128)(2,1)S(1)}, bf16[1024,128]{1,0:T(8,128)(2,1)S(1)}, u32[]{:S(2)}, u32[]{:S(2)}) collective-permute-start(bf16[1024,128]{1,0:T(8,128)(2,1)S(1)} %get-tuple-element.52.refs_4_.refs_0_), channel_id=1, source_target_pairs={{0,1},{1,0},{2,3},{3,2},{4,5},{5,4},{6,7},{7,6},{8,9},{9,8},{10,11... | collective-permute-start | bytes 786440 | tf_op jit(solution)/shard_map/ppermute | solution.py:495
  81.0 19.4 %collective-permute-start.20 = (bf16[9,256,128]{2,1,0:T(8,128)(2,1)S(1)}, bf16[9,256,128]{2,1,0:T(8,128)(2,1)}, u32[]{:S(2)}, u32[]{:S(2)}) collective-permute-start(bf16[9,256,128]{2,1,0:T(8,128)(2,1)S(1)} %grad_second.5.refs_0_.x), channel_id=1, source_target_pairs={{0,8},{4,12},{24,16},{28,20},{1,9},{5,13},{25,17},{29,21},{2,10},{... | collective-permute-start | bytes 1769480 | tf_op jit(solution)/shard_map/ppermute | solution.py:469
  88.4 13.9 %collective-permute-start.19 = (bf16[9,256,128]{2,1,0:T(8,128)(2,1)S(1)}, bf16[9,256,128]{2,1,0:T(8,128)(2,1)}, u32[]{:S(2)}, u32[]{:S(2)}) collective-permute-start(bf16[9,256,128]{2,1,0:T(8,128)(2,1)S(1)} %line_add.13.refs_0_.x), channel_id=1, source_target_pairs={{8,16},{12,20},{16,8},{20,12},{9,17},{13,21},{17,9},{21,13},{10,18... | collective-permute-start | bytes 1769480 | tf_op jit(solution)/shard_map/ppermute | solution.py:469
  89.9 16.5 %collective-permute-start.18 = (bf16[9,256,128]{2,1,0:T(8,128)(2,1)S(1)}, bf16[9,256,128]{2,1,0:T(8,128)(2,1)S(1)}, u32[]{:S(2)}, u32[]{:S(2)}) collective-permute-start(bf16[9,256,128]{2,1,0:T(8,128)(2,1)S(1)} %line_add.14.refs_4_.refs_0_.x), channel_id=1, source_target_pairs={{8,0},{12,4},{16,24},{20,28},{9,1},{13,5},{17,25},{21,29},{10,2},{... | collective-permute-start | bytes 1769480 | tf_op jit(solution)/shard_map/ppermute | solution.py:469
  94.7 20.8 %collective-permute-start.25 = (bf16[1168,256]{1,0:T(8,128)(2,1)S(1)}, bf16[1168,256]{1,0:T(8,128)(2,1)S(1)}, u32[]{:S(2)}, u32[]{:S(2)}) collective-permute-start(bf16[1168,256]{1,0:T(8,128)(2,1)S(1)} %grad_first.3.refs_0_.x), channel_id=1, source_target_pairs={{0,8},{4,12},{24,16},{28,20},{1,9},{5,13},{25,17},{29,21},{2,10},{... | collective-permute-start | bytes 1794056 | tf_op jit(solution)/shard_map/ppermute | solution.py:469
  101.5 14.7 %collective-permute-start.24 = (bf16[9,256,128]{2,1,0:T(8,128)(2,1)S(1)}, bf16[9,256,128]{2,1,0:T(8,128)(2,1)S(1)}, u32[]{:S(2)}, u32[]{:S(2)}) collective-permute-start(bf16[9,256,128]{2,1,0:T(8,128)(2,1)S(1)} %line_add.15.refs_0_.x), channel_id=1, source_target_pairs={{8,16},{12,20},{16,8},{20,12},{9,17},{13,21},{17,9},{21,13},{10,18... | collective-permute-start | bytes 1769480 | tf_op jit(solution)/shard_map/ppermute | solution.py:469
  103.5 17.9 %collective-permute-start.23 = (bf16[9,256,128]{2,1,0:T(8,128)(2,1)S(1)}, bf16[9,256,128]{2,1,0:T(8,128)(2,1)S(1)}, u32[]{:S(2)}, u32[]{:S(2)}) collective-permute-start(bf16[9,256,128]{2,1,0:T(8,128)(2,1)S(1)} %line_add.16.refs_0_.x), channel_id=1, source_target_pairs={{8,0},{12,4},{16,24},{20,28},{9,1},{13,5},{17,25},{21,29},{10,2},{... | collective-permute-start | bytes 1769480 | tf_op jit(solution)/shard_map/ppermute | solution.py:469
  107.0 16.4 %collective-permute-start.22 = (bf16[9,256,128]{2,1,0:T(8,128)(2,1)S(1)}, bf16[9,256,128]{2,1,0:T(8,128)(2,1)S(1)}, u32[]{:S(2)}, u32[]{:S(2)}) collective-permute-start(bf16[9,256,128]{2,1,0:T(8,128)(2,1)S(1)} %line_pick.6.refs_0_.own), channel_id=1, source_target_pairs={{0,4},{4,0},{8,12},{12,8},{16,20},{20,16},{24,28},{28,24},{1,5},{5... | collective-permute-start | bytes 1769480 | tf_op jit(solution)/shard_map/ppermute | solution.py:498
  109.7 25.6 %collective-permute-start.30 = (bf16[1168,256]{1,0:T(8,128)(2,1)S(1)}, bf16[1168,256]{1,0:T(8,128)(2,1)S(1)}, u32[]{:S(2)}, u32[]{:S(2)}) collective-permute-start(bf16[1168,256]{1,0:T(8,128)(2,1)S(1)} %grad_first.4.refs_0_.x), channel_id=1, source_target_pairs={{0,8},{4,12},{24,16},{28,20},{1,9},{5,13},{25,17},{29,21},{2,10},{... | collective-permute-start | bytes 1794056 | tf_op jit(solution)/shard_map/ppermute | solution.py:469
  115.6 21.5 %collective-permute-start.29 = (bf16[1168,256]{1,0:T(8,128)(2,1)S(1)}, bf16[1168,256]{1,0:T(8,128)(2,1)S(1)}, u32[]{:S(2)}, u32[]{:S(2)}) collective-permute-start(bf16[1168,256]{1,0:T(8,128)(2,1)S(1)} %line_add.17.refs_0_.x), channel_id=1, source_target_pairs={{8,16},{12,20},{16,8},{20,12},{9,17},{13,21},{17,9},{21,13},{10,18... | collective-permute-start | bytes 1794056 | tf_op jit(solution)/shard_map/ppermute | solution.py:469
  116.3 24.9 %collective-permute-start.26 = (bf16[1168,256]{1,0:T(8,128)(2,1)S(1)}, bf16[1168,256]{1,0:T(8,128)(2,1)S(1)}, u32[]{:S(2)}, u32[]{:S(2)}) collective-permute-start(bf16[1168,256]{1,0:T(8,128)(2,1)S(1)} %grad_first.5.refs_0_.x), channel_id=1, source_target_pairs={{0,8},{4,12},{24,16},{28,20},{1,9},{5,13},{25,17},{29,21},{2,10},{... | collective-permute-start | bytes 1794056 | tf_op jit(solution)/shard_map/ppermute | solution.py:469
  121.5 17.1 %collective-permute-start.28 = (bf16[9,256,128]{2,1,0:T(8,128)(2,1)S(1)}, bf16[9,256,128]{2,1,0:T(8,128)(2,1)S(1)}, u32[]{:S(2)}, u32[]{:S(2)}) collective-permute-start(bf16[9,256,128]{2,1,0:T(8,128)(2,1)S(1)} %line_add.18.refs_0_.x), channel_id=1, source_target_pairs={{8,0},{12,4},{16,24},{20,28},{9,1},{13,5},{17,25},{21,29},{10,2},{... | collective-permute-start | bytes 1769480 | tf_op jit(solution)/shard_map/ppermute | solution.py:469
  123.4 15.8 %collective-permute-start.27 = (bf16[9,256,128]{2,1,0:T(8,128)(2,1)S(1)}, bf16[9,256,128]{2,1,0:T(8,128)(2,1)S(1)}, u32[]{:S(2)}, u32[]{:S(2)}) collective-permute-start(bf16[9,256,128]{2,1,0:T(8,128)(2,1)S(1)} %line_pick.7.refs_0_.own), channel_id=1, source_target_pairs={{0,4},{4,0},{8,12},{12,8},{16,20},{20,16},{24,28},{28,24},{1,5},{5... | collective-permute-start | bytes 1769480 | tf_op jit(solution)/shard_map/ppermute | solution.py:498
  137.3 18.8 %collective-permute-start.33 = (bf16[1168,256]{1,0:T(8,128)(2,1)S(1)}, bf16[1168,256]{1,0:T(8,128)(2,1)S(1)}, u32[]{:S(2)}, u32[]{:S(2)}) collective-permute-start(bf16[1168,256]{1,0:T(8,128)(2,1)S(1)} %line_add.20.refs_0_.x), channel_id=1, source_target_pairs={{8,0},{12,4},{16,24},{20,28},{9,1},{13,5},{17,25},{21,29},{10,2},{... | collective-permute-start | bytes 1794056 | tf_op jit(solution)/shard_map/ppermute | solution.py:469
  141.4 17.9 %collective-permute-start.31 = (bf16[1168,256]{1,0:T(8,128)(2,1)S(1)}, bf16[1168,256]{1,0:T(8,128)(2,1)S(1)}, u32[]{:S(2)}, u32[]{:S(2)}) collective-permute-start(bf16[1168,256]{1,0:T(8,128)(2,1)S(1)} %line_add.21.refs_0_.x), channel_id=1, source_target_pairs={{8,16},{12,20},{16,8},{20,12},{9,17},{13,21},{17,9},{21,13},{10,18... | collective-permute-start | bytes 1794056 | tf_op jit(solution)/shard_map/ppermute | solution.py:469
  142.1 15.2 %collective-permute-start.32 = (bf16[9,256,128]{2,1,0:T(8,128)(2,1)S(1)}, bf16[9,256,128]{2,1,0:T(8,128)(2,1)S(1)}, u32[]{:S(2)}, u32[]{:S(2)}) collective-permute-start(bf16[9,256,128]{2,1,0:T(8,128)(2,1)S(1)} %line_pick.8.refs_1_.own), channel_id=1, source_target_pairs={{0,4},{4,0},{8,12},{12,8},{16,20},{20,16},{24,28},{28,24},{1,5},{5... | collective-permute-start | bytes 1769480 | tf_op jit(solution)/shard_map/ppermute | solution.py:498
  142.9 27.0 %collective-permute-start.37 = (bf16[1168,256]{1,0:T(8,128)(2,1)S(1)}, bf16[1168,256]{1,0:T(8,128)(2,1)S(1)}, u32[]{:S(2)}, u32[]{:S(2)}) collective-permute-start(bf16[1168,256]{1,0:T(8,128)(2,1)S(1)} %line_add.22.refs_0_.x), channel_id=1, source_target_pairs={{8,0},{12,4},{16,24},{20,28},{9,1},{13,5},{17,25},{21,29},{10,2},{... | collective-permute-start | bytes 1794056 | tf_op jit(solution)/shard_map/ppermute | solution.py:469
  156.6 15.7 %collective-permute-start.36 = (bf16[1168,256]{1,0:T(8,128)(2,1)S(1)}, bf16[1168,256]{1,0:T(8,128)(2,1)S(1)}, u32[]{:S(2)}, u32[]{:S(2)}) collective-permute-start(bf16[1168,256]{1,0:T(8,128)(2,1)S(1)} %line_pick.9.refs_1_.own), channel_id=1, source_target_pairs={{0,4},{4,0},{8,12},{12,8},{16,20},{20,16},{24,28},{28,24},{1,5},{5... | collective-permute-start | bytes 1794056 | tf_op jit(solution)/shard_map/ppermute | solution.py:498
  159.5 23.6 %collective-permute-start.35 = (bf16[1168,256]{1,0:T(8,128)(2,1)S(1)}, bf16[1168,256]{1,0:T(8,128)(2,1)S(1)}, u32[]{:S(2)}, u32[]{:S(2)}) collective-permute-start(bf16[1168,256]{1,0:T(8,128)(2,1)S(1)} %line_add.23.refs_0_.x), channel_id=1, source_target_pairs={{8,0},{12,4},{16,24},{20,28},{9,1},{13,5},{17,25},{21,29},{10,2},{... | collective-permute-start | bytes 1794056 | tf_op jit(solution)/shard_map/ppermute | solution.py:469
  170.5 15.3 %collective-permute-start.39 = (bf16[1168,256]{1,0:T(8,128)(2,1)S(1)}, bf16[1168,256]{1,0:T(8,128)(2,1)S(1)}, u32[]{:S(2)}, u32[]{:S(2)}) collective-permute-start(bf16[1168,256]{1,0:T(8,128)(2,1)S(1)} %line_pick.10.refs_0_.own), channel_id=1, source_target_pairs={{0,4},{4,0},{8,12},{12,8},{16,20},{20,16},{24,28},{28,24},{1,5},{5... | collective-permute-start | bytes 1794056 | tf_op jit(solution)/shard_map/ppermute | solution.py:498
  (29 other events, 283.6 us)

commit v5 on v4

--- a/solution.py
+++ b/solution.py
@@ -15,10 +15,14 @@
 NORM_EPS = 1e-05
 LIMIT = 24 * 1024 * 1024
 SMALL = 8 * 1024 * 1024
+LARGE = 61 * 1024 * 1024
 EXTRA = 16
 F32, BF16 = jnp.float32, jnp.bfloat16
 NT = (((1,), (1,)), ((), ()))
 UNREAD = pl.BlockSpec(memory_space=pl.ANY)
+IN_HBM = pl.BlockSpec(memory_space=pltpu.HBM)
+PLANE_ORDER = (0, -1, 1)
+LIGHT = pl.CostEstimate(flops=1024, bytes_accessed=1024, transcendentals=0)
 
 
 def params():
@@ -49,66 +53,69 @@
         )
 
 
-def tap_cells(padded, plane, tap, sign):
-    a, b, c = tap
-    low = 1 + sign * b
-    rows = padded[1 + c, plane + (1 + sign * a), low : low + HEIGHT]
-    return rows.reshape(PLANE, rows.shape[-1])
-
-
-def pre_kernel(n, idx, vol, w, *refs):
-    outs, padded, shares = refs[:n], refs[n], refs[n + 1]
-    rows = vol.shape[0]
-    plane = pl.program_id(0)
-
-    @pl.when(plane == 0)
-    def _():
-        fill_padded(padded, vol[...], 1)
-
-    lhs = jnp.concatenate([tap_cells(padded, plane, tap, 1) for tap in TAPS], axis=1)
-    sums = jnp.dot(lhs, w[...], preferred_element_type=F32).astype(BF16)
+def span_of(a, sign):
+    return max(0, -sign * a), DEPTH - abs(a)
+
+
+def start_parts(source, buffer, sems):
+    size = source.shape[0] // 3
+    copies = {}
+    for a in PLANE_ORDER:
+        span = pl.ds((a + 1) * size, size)
+        copies[a] = pltpu.make_async_copy(source.at[span], buffer.at[span], sems.at[a + 1])
+        copies[a].start()
+    return copies
+
+
+def share_kernel(n, sign, idx, field, w, *refs):
+    outs = refs[:n]
+    padded, sums, shares, buffer, sems = refs[n:]
+    rows = field.shape[0]
+    copies = start_parts(w, buffer, sems)
+    fill_padded(padded, field[...], sign)
+    for a in PLANE_ORDER:
+        begin, planes = span_of(a, sign)
+        pieces = []
+        for b in (-1, 0, 1):
+            for c in (-1, 0, 1):
+                low, first = 1 + sign * b, 1 + begin + sign * a
+                piece = padded[1 + c, first : first + planes, low : low + HEIGHT]
+                pieces.append(piece.reshape(planes * PLANE, rows))
+        lhs = jnp.concatenate(pieces, axis=1)
+        copies[a].wait()
+        if sign == 1:
+            rhs = buffer[(a + 1) * 9 * rows : (a + 2) * 9 * rows]
+            part = jnp.dot(lhs, rhs, preferred_element_type=F32)
+        else:
+            rhs = jnp.concatenate([buffer[(a + 1) * 9 + k] for k in range(9)], axis=1)
+            part = lax.dot_general(lhs, rhs, NT, preferred_element_type=F32)
+        span = slice(begin * PLANE, (begin + planes) * PLANE)
+        if a == 0:
+            sums[...] = part
+        else:
+            sums[span] += part
     for j in range(n):
-        shares[j] = sums[:, j * rows : (j + 1) * rows]
+        shares[j] = sums[:, j * rows : (j + 1) * rows].astype(BF16)
     for m in range(n):
         outs[m][...] = shares[idx[0] ^ m]
 
 
-def dact_kernel(n, idx, cot, w, *refs):
-    outs, padded, shares, wide = refs[:n], refs[n], refs[n + 1], refs[n + 2]
-    rows = cot.shape[0]
-    plane = pl.program_id(0)
-
-    @pl.when(plane == 0)
-    def _():
-        fill_padded(padded, cot[...], -1)
-        for t in range(27):
-            wide[:, t * rows : (t + 1) * rows] = w[t]
-
-    lhs = jnp.concatenate([tap_cells(padded, plane, tap, -1) for tap in TAPS], axis=1)
-    sums = lax.dot_general(lhs, wide[...], NT, preferred_element_type=F32).astype(BF16)
-    for j in range(n):
-        shares[j] = sums[:, j * rows : (j + 1) * rows]
-    for m in range(n):
-        outs[m][...] = shares[idx[0] ^ m]
-
-
-def spread_shares(kernel, name, idx, n, field, w, extra):
+def spread_shares(sign, name, idx, n, field, w, limit):
     rows = field.shape[0]
     return pl.pallas_call(
-        functools.partial(kernel, n),
-        grid=(DEPTH,),
-        in_specs=[smem(), whole(field.shape), whole(w.shape)],
-        out_specs=[pl.BlockSpec((PLANE, rows), lambda d: (d, 0))] * n,
+        functools.partial(share_kernel, n, sign),
+        in_specs=[smem(), pl.BlockSpec(memory_space=pltpu.VMEM), IN_HBM],
+        out_specs=[pl.BlockSpec(memory_space=pltpu.VMEM)] * n,
         out_shape=[jax.ShapeDtypeStruct((CELLS, rows), BF16)] * n,
         scratch_shapes=[
             pltpu.VMEM((3, DEPTH + 2, HEIGHT + 2, WIDTH, rows), BF16),
-            pltpu.VMEM((n, PLANE, rows), BF16),
-        ]
-        + extra,
-        compiler_params=params(),
-        cost_estimate=pl.CostEstimate(
-            flops=2 * 27 * rows * rows * n * CELLS, bytes_accessed=2 * w.size, transcendentals=0
-        ),
+            pltpu.VMEM((CELLS, n * rows), F32),
+            pltpu.VMEM((n, CELLS, rows), BF16),
+            pltpu.VMEM(w.shape, BF16),
+            pltpu.SemaphoreType.DMA((3,)),
+        ],
+        compiler_params=pltpu.CompilerParams(vmem_limit_bytes=limit),
+        cost_estimate=LIGHT,
         name=name,
     )(idx, field, w)
 
@@ -146,13 +153,13 @@
     dpre[...] = ((dnormed - mean_first - normed * mean_second) * inverse[...]).astype(BF16)
 
 
-def conv_back_add(sums, products, plane, taps, rows, sign):
+def conv_back_add(sums, products, begin, planes, taps, rows, sign):
     for at, tap in enumerate(taps):
         a, b, c = tap
         a, b = sign * a, sign * b
-        part = products[:, at * rows : (at + 1) * rows].reshape(HEIGHT, WIDTH, rows)
+        part = products[:, at * rows : (at + 1) * rows].reshape(planes, HEIGHT, WIDTH, rows)
         low, high = max(0, b), HEIGHT + min(0, b)
-        sums[1 + c, plane + (1 - a), low - b : high - b] += part[low:high]
+        sums[1 + c, begin - a : begin - a + planes, low - b : high - b] += part[:, low:high]
 
 
 def conv_finish(sums, out, sign):
@@ -160,7 +167,7 @@
     total = None
     for c in (-1, 0, 1):
         off = sign * c
-        part = sums[1 + c, 1 : 1 + DEPTH].reshape(CELLS, rows)
+        part = sums[1 + c].reshape(CELLS, rows)
         if off != 0:
             width_at = lax.broadcasted_iota(jnp.int32, part.shape, 0) % WIDTH
             inside = (width_at + off >= 0) & (width_at + off < WIDTH)
@@ -171,56 +178,54 @@
 
 def conv_kernel(n, sign, transposed, idx, w, *refs):
     blocks = refs[:n]
-    out, ordered, sums = refs[-3:]
+    out, ordered, sums, buffer, sems = refs[-5:]
     rows = out.shape[0]
-    plane = pl.program_id(0)
-
-    @pl.when(plane == 0)
-    def _():
-        sums[...] = jnp.zeros_like(sums)
-        for m in range(n):
-            ordered[idx[0] ^ m] = blocks[m][...]
-
-    begin = pl.multiple_of(plane * PLANE, PLANE)
-    lhs = jnp.concatenate([ordered[j, pl.ds(begin, PLANE)] for j in range(n)], axis=1)
-    for t in range(0, 27, 2):
-        taps = TAPS[t : t + 2]
-        if transposed:
-            rhs = w[t * rows : (t + len(taps)) * rows]
-            products = lax.dot_general(lhs, rhs, NT, preferred_element_type=F32)
-        else:
-            rhs = jnp.concatenate([w[t + k] for k in range(len(taps))], axis=1)
-            products = jnp.dot(lhs, rhs, preferred_element_type=F32)
-        conv_back_add(sums, products, plane, taps, rows, sign)
-
-    @pl.when(plane == DEPTH - 1)
-    def _():
-        conv_finish(sums, out, sign)
+    copies = start_parts(w, buffer, sems)
+    sums[...] = jnp.zeros_like(sums)
+    for m in range(n):
+        ordered[idx[0] ^ m] = blocks[m][...]
+    for a in PLANE_ORDER:
+        begin, planes = span_of(-a, sign)
+        span = slice(begin * PLANE, (begin + planes) * PLANE)
+        lhs = jnp.concatenate([ordered[j, span] for j in range(n)], axis=1)
+        copies[a].wait()
+        for k in range(0, 9, 2):
+            t = (a + 1) * 9 + k
+            taps = TAPS[t : t + min(2, 9 - k)]
+            if transposed:
+                rhs = buffer[t * rows : (t + len(taps)) * rows]
+                products = lax.dot_general(lhs, rhs, NT, preferred_element_type=F32)
+            else:
+                rhs = jnp.concatenate([buffer[t + at] for at in range(len(taps))], axis=1)
+                products = jnp.dot(lhs, rhs, preferred_element_type=F32)
+            conv_back_add(sums, products, begin, planes, taps, rows, sign)
+    conv_finish(sums, out, sign)
 
 
 def conv_full(name, sign, transposed, idx, w, blocks, after):
     n, rows = len(blocks), blocks[0].shape[1]
     return pl.pallas_call(
         functools.partial(conv_kernel, n, sign, transposed),
-        grid=(DEPTH,),
-        in_specs=[smem(), whole(w.shape)] + [whole(blocks[0].shape)] * n + [UNREAD] * len(after),
-        out_specs=whole((rows, CELLS)),
+        in_specs=[smem(), IN_HBM]
+        + [pl.BlockSpec(memory_space=pltpu.VMEM)] * n
+        + [UNREAD] * len(after),
+        out_specs=pl.BlockSpec(memory_space=pltpu.VMEM),
         out_shape=jax.ShapeDtypeStruct((rows, CELLS), BF16),
         scratch_shapes=[
             pltpu.VMEM((n, CELLS, rows), BF16),
-            pltpu.VMEM((3, DEPTH + 2, HEIGHT, WIDTH, rows), F32),
+            pltpu.VMEM((3, DEPTH, HEIGHT, WIDTH, rows), F32),
+            pltpu.VMEM(w.shape, BF16),
+            pltpu.SemaphoreType.DMA((3,)),
         ],
-        compiler_params=params(),
-        cost_estimate=pl.CostEstimate(
-            flops=2 * 27 * rows * rows * n * CELLS, bytes_accessed=2 * w.size, transcendentals=0
-        ),
+        compiler_params=pltpu.CompilerParams(vmem_limit_bytes=LIMIT),
+        cost_estimate=LIGHT,
         name=name,
     )(idx, w, *blocks, *after)
 
 
-def halves_kernel(n, held, turned, idx, *refs):
+def halves_kernel(n, turned, idx, *refs):
     blocks = refs[:n]
-    keep, send = refs[len(refs) - held - 2], refs[len(refs) - held - 1]
+    keep, send = refs[-2:]
     half = n // 2
     rows = blocks[0].shape[1]
 
@@ -245,22 +250,19 @@
         split(half, 0)
 
 
-def halves(name, turned, idx, blocks, after=(), held=()):
+def halves(name, turned, idx, blocks, after):
     n, rows = len(blocks), blocks[0].shape[1]
     shape = (n // 2 * rows, CELLS) if turned else (n // 2, CELLS, rows)
-    first = 1 + n + len(after)
-    return pl.pallas_call(
-        functools.partial(halves_kernel, n, len(held), turned),
+    return pl.pallas_call(
+        functools.partial(halves_kernel, n, turned),
         in_specs=[smem()]
         + [pl.BlockSpec(memory_space=pltpu.VMEM)] * n
-        + [UNREAD] * (len(after) + len(held)),
-        out_specs=[pl.BlockSpec(memory_space=pltpu.VMEM)] * 2 + [UNREAD] * len(held),
-        out_shape=[jax.ShapeDtypeStruct(shape, BF16)] * 2
-        + [jax.ShapeDtypeStruct(x.shape, x.dtype) for x in held],
-        input_output_aliases={first + k: 2 + k for k in range(len(held))},
+        + [UNREAD] * len(after),
+        out_shape=[jax.ShapeDtypeStruct(shape, BF16)] * 2,
         compiler_params=pltpu.CompilerParams(vmem_limit_bytes=LIMIT),
+        cost_estimate=LIGHT,
         name=name,
-    )(idx, *blocks, *after, *held)
+    )(idx, *blocks, *after)
 
 
 def moved_first_kernel(own, other, _, out):
@@ -298,6 +300,7 @@
         in_specs=[pl.BlockSpec(memory_space=pltpu.VMEM)] * 2 + [UNREAD],
         out_shape=jax.ShapeDtypeStruct(shape, BF16),
         compiler_params=pltpu.CompilerParams(vmem_limit_bytes=LIMIT),
+        cost_estimate=LIGHT,
         name=name,
     )(own, other, after)
 
@@ -336,17 +339,13 @@
         in_specs=[pl.BlockSpec(memory_space=pltpu.VMEM)] * 4 + [UNREAD] * len(after),
         out_shape=jax.ShapeDtypeStruct((9 * rows + EXTRA, half * rows), BF16),
         compiler_params=pltpu.CompilerParams(vmem_limit_bytes=LIMIT),
-        cost_estimate=pl.CostEstimate(
-            flops=2 * 9 * rows * rows * half * 2 * (DEPTH - abs(a)) * PLANE,
-            bytes_accessed=2 * moved.size,
-            transcendentals=0,
-        ),
+        cost_estimate=LIGHT,
         name="grad_first",
     )(moved, own, other, gain_part, *after)
 
 
-def grad_second_kernel(a, moved, own, other, *refs):
-    out = refs[-1]
+def grad_second_kernel(a, held, moved, own, other, *refs):
+    out = refs[len(refs) - held - 1]
     rows = out.shape[2]
     begin, planes = max(0, a), DEPTH - abs(a)
     lhs = [
@@ -368,20 +367,20 @@
             out[at] = grads[:, place * rows : (place + 1) * rows].astype(BF16)
 
 
-def grad_second(a, moved, own, other, after):
+def grad_second(a, moved, own, other, after, held=()):
     wide, rows = own.shape[0], moved.shape[-1]
-    return pl.pallas_call(
-        functools.partial(grad_second_kernel, a),
-        in_specs=[pl.BlockSpec(memory_space=pltpu.VMEM)] * 3 + [UNREAD] * len(after),
-        out_shape=jax.ShapeDtypeStruct((9, wide, rows), BF16),
+    first = 3 + len(after)
+    return pl.pallas_call(
+        functools.partial(grad_second_kernel, a, len(held)),
+        in_specs=[pl.BlockSpec(memory_space=pltpu.VMEM)] * 3 + [UNREAD] * (len(after) + len(held)),
+        out_specs=[pl.BlockSpec(memory_space=pltpu.VMEM)] + [UNREAD] * len(held),
+        out_shape=[jax.ShapeDtypeStruct((9, wide, rows), BF16)]
+        + [jax.ShapeDtypeStruct(x.shape, x.dtype) for x in held],
+        input_output_aliases={first + k: 1 + k for k in range(len(held))},
         compiler_params=pltpu.CompilerParams(vmem_limit_bytes=LIMIT),
-        cost_estimate=pl.CostEstimate(
-            flops=2 * 9 * rows * wide * 2 * (DEPTH - abs(a)) * PLANE,
-            bytes_accessed=2 * moved.size,
-            transcendentals=0,
-        ),
+        cost_estimate=LIGHT,
         name="grad_second",
-    )(moved, own, other, *after)
+    )(moved, own, other, *after, *held)
 
 
 def finish_kernel(n, axis, factor, chunk, idx, own, other, *refs):
@@ -417,6 +416,7 @@
         scratch_shapes=[pltpu.VMEM((2,) + shape, F32), pltpu.SemaphoreType.DMA((2,))],
         input_output_aliases={3: 0} if given else {},
         compiler_params=pltpu.CompilerParams(vmem_limit_bytes=SMALL),
+        cost_estimate=LIGHT,
         name=name,
     )(idx, own, other, *given, *after)
 
@@ -453,6 +453,7 @@
         + [UNREAD] * len(after),
         out_shape=jax.ShapeDtypeStruct(x.shape, x.dtype),
         compiler_params=pltpu.CompilerParams(vmem_limit_bytes=SMALL),
+        cost_estimate=LIGHT,
         name=name,
     )(*given, x, y, *after)
 
@@ -502,11 +503,8 @@
         return [parts[0]] + [got[m] for m in range(1, n)]
 
     first_flat = w_first.reshape(27 * rows, n * rows)
-    pre_parts = spread_shares(pre_kernel, "pre", idx, n, vol, first_flat, [])
-    pre_shares = swap(pre_parts)
-    dact_parts = spread_shares(
-        dact_kernel, "dact", idx, n, cot, w_second, [pltpu.VMEM((n * rows, 27 * rows), BF16)]
-    )
+    pre_shares = swap(spread_shares(1, "pre", idx, n, vol, first_flat, LARGE))
+    dact_parts = spread_shares(-1, "dact", idx, n, cot, w_second, LIMIT)
     act, normed, inverse = pl.pallas_call(
         functools.partial(norm_kernel, n),
         in_specs=[pl.BlockSpec(memory_space=pltpu.VMEM)] * (1 + n) + [UNREAD],
@@ -516,6 +514,7 @@
             jax.ShapeDtypeStruct((1, rows), F32),
         ],
         compiler_params=pltpu.CompilerParams(vmem_limit_bytes=LIMIT),
+        cost_estimate=LIGHT,
         name="norm",
     )(own_gain, *pre_shares, dact_parts[0])
     act_blocks = swap([act] * n)
@@ -530,11 +529,8 @@
     moved_vol = moved_fields(
         moved_first_kernel, "moved_first", (2, 9 * rows, CELLS), vol, to_core(vol), act
     )
-    act_keep, act_send, *dact_held = halves(
-        "act_halves", True, idx, act_blocks, (moved_cot, moved_vol), dact_parts[1:]
-    )
+    act_keep, act_send = halves("act_halves", True, idx, act_blocks, (moved_cot, moved_vol))
     act_other = to_core(act_send)
-    dact_shares = swap([dact_parts[0]] + dact_held)
 
     sums, outward = line_moves(lax.axis_size("dp") // 2)
     steps = len(sums) + len(outward)
@@ -549,66 +545,107 @@
         if step == steps - 1:
             crossed[chunk] = to_core(totals[chunk])
 
-    def turn(at, written):
-        nonlocal last
+    def write(chunk):
+        nonlocal last
+        name, axis = ("finish_second", 1) if chunk < 3 else ("finish_first", 2)
+        shape = (9, n // 2 * rows, rows) if chunk < 3 else (9, rows, n // 2 * rows)
+        written[axis], mark = finish(
+            name,
+            n,
+            axis,
+            factor,
+            idx,
+            chunk % 3,
+            shape,
+            totals[chunk],
+            crossed[chunk],
+            written.get(axis),
+            last,
+        )
+        last = (mark,)
+
+    def second_part(chunk):
+        nonlocal last
+        held = tuple(dact_parts[1:]) if chunk == 0 else ()
+        parts[chunk], *passed = grad_second(
+            chunk - 1, moved_cot, act_keep, act_other, last, held
+        )
+        last = (parts[chunk],)
+        if chunk == 0:
+            done["dact"] = swap([dact_parts[0]] + passed)
+
+    def first_part(chunk):
+        nonlocal last
+        own, other = done["dpre_halves"]
+        parts[chunk] = grad_first(chunk - 4, moved_vol, own, other, done["gain"], last)
+        last = (parts[chunk],)
+
+    def norm_back():
+        nonlocal last
+        dpre, done["gain"] = pl.pallas_call(
+            functools.partial(norm_back_kernel, n),
+            in_specs=[pl.BlockSpec(memory_space=pltpu.VMEM)] * (3 + n) + [UNREAD],
+            out_shape=[
+                jax.ShapeDtypeStruct((CELLS, rows), BF16),
+                jax.ShapeDtypeStruct((1, rows), F32),
+            ],
+            compiler_params=pltpu.CompilerParams(vmem_limit_bytes=SMALL),
+            cost_estimate=LIGHT,
+            name="norm_back",
+        )(own_gain, normed, inverse, *done["dact"], *last)
+        done["dpre"] = swap([dpre] * n)
+        last = (dpre,)
+
+    def dpre_halves():
+        nonlocal last
+        keep, send = halves("dpre_halves", False, idx, done["dpre"], last)
+        done["dpre_halves"] = keep, to_core(send)
+        last = (keep,)
+
+    def output():
+        nonlocal last
+        done["output"] = conv_full("output", 1, False, idx, w_second, act_blocks, last)
+        last = (done["output"],)
+
+    def grad_volume():
+        nonlocal last
+        done["grad_volume"] = conv_full(
+            "grad_volume", -1, True, idx, first_flat, done["dpre"], last
+        )
+        last = (done["grad_volume"],)
+
+    def wave(at):
         for step in range(steps):
             if 0 <= at - step < 6:
                 line(at - step, step)
-        chunk = at - steps
-        if 0 <= chunk < 6:
-            name, axis = ("finish_second", 1) if chunk < 3 else ("finish_first", 2)
-            shape = (9, n // 2 * rows, rows) if chunk < 3 else (9, rows, n // 2 * rows)
-            written[axis], mark = finish(
-                name,
-                n,
-                axis,
-                factor,
-                idx,
-                chunk % 3,
-                shape,
-                totals[chunk],
-                crossed[chunk],
-                written.get(axis),
-                last,
-            )
-            last = (mark,)
-
-    written = {}
-    for chunk in range(3):
-        parts[chunk] = grad_second(chunk - 1, moved_cot, act_keep, act_other, last)
-        last = (parts[chunk],)
-    turn(0, written)
-    dpre, gain_part = pl.pallas_call(
-        functools.partial(norm_back_kernel, n),
-        in_specs=[pl.BlockSpec(memory_space=pltpu.VMEM)] * (3 + n) + [UNREAD],
-        out_shape=[
-            jax.ShapeDtypeStruct((CELLS, rows), BF16),
-            jax.ShapeDtypeStruct((1, rows), F32),
-        ],
-        compiler_params=pltpu.CompilerParams(vmem_limit_bytes=SMALL),
-        name="norm_back",
-    )(own_gain, normed, inverse, *dact_shares, *last)
-    dpre_blocks = swap([dpre] * n)
-    output = conv_full("output", 1, False, idx, w_second, act_blocks, (dpre,))
-    last = (output,)
-    turn(1, written)
-    dpre_keep, dpre_send = halves("dpre_halves", False, idx, dpre_blocks, last)
-    dpre_other = to_core(dpre_send)
-    parts[3] = grad_first(-1, moved_vol, dpre_keep, dpre_other, gain_part, last)
-    last = (parts[3],)
-    turn(2, written)
-    for chunk in (4, 5):
-        parts[chunk] = grad_first(chunk - 4, moved_vol, dpre_keep, dpre_other, gain_part, last)
-        last = (parts[chunk],)
-    turn(3, written)
-    grad_volume = conv_full("grad_volume", -1, True, idx, first_flat, dpre_blocks, last)
-    last = (grad_volume,)
+        if 0 <= at - steps < 6:
+            write(at - steps)
+
+    written, done = {}, {}
+    second_part(0)
+    output()
+    second_part(1)
+    norm_back()
+    line(0, 0)
+    second_part(2)
+    line(1, 0)
+    line(0, 1)
+    dpre_halves()
+    line(2, 0)
+    line(1, 1)
+    first_part(3)
+    for step in range(2, steps):
+        line(0, step)
+    first_part(4)
+    first_part(5)
+    wave(3)
+    grad_volume()
     for at in range(4, 6 + steps):
-        turn(at, written)
+        wave(at)
     gain_rows = totals[3][9 * rows : 9 * rows + 2, :rows].astype(F32)
     gain_rows_other = crossed[3][9 * rows : 9 * rows + 2, :rows].astype(F32)
     gain_total = (jnp.sum(gain_rows, axis=0) + jnp.sum(gain_rows_other, axis=0)) * factor
-    return (output[None], grad_volume[None], written[2], gain_total, written[1])
+    return (done["output"][None], done["grad_volume"][None], written[2], gain_total, written[1])
 
 
 def solution(mesh):

time: 191 us -> 191 us (level)
  waiting for transfers between devices: 57.4 us -> 49.2 us
  Pallas kernels: 58.1 us -> 62 us
  starting transfers between devices: 61.4 us -> 65.1 us
    ppermute x10, starting transfers between devices: 10.7 us -> 17 us  [to_core(): lax.ppermute(x, 'dp', [(i, i ^ 1) for i in range(lax.axis_size('dp'))])]
    ppermute x12, waiting for transfers between devices: 15.9 us -> 9.81 us  [to_partner(): return lax.ppermute(x, 'chan', [(i, i ^ m) for i in range(n)])]
    ppermute x18, starting transfers between devices: 38.9 us -> 36.6 us  [line_send(): return lax.ppermute(x, 'dp', pairs)]
    pallas_call x10, Pallas kernels: 31.6 us -> 33.9 us  [the longest x2 14.2 us: conv_full(): pl.pallas_call(functools.partial(conv_kernel, n, sign, transposed), in_sp...]
    ppermute x18, waiting for transfers between devices: 40 us -> 37.8 us  [line_send(): return lax.ppermute(x, 'dp', pairs)]
    unnamed x42 -> x38, local copies, waits for them, and re-layouts: 11.4 us -> 11 us
  transfers between devices with their start and end apart: 40 -> 40, of which waited for: 12 -> 9; matrix products, arithmetic and copies ran while one was open for 0% -> 0% of each run, Pallas kernels for 27% -> 26%
where the time goes in v5:
time: 191 us; the launch traced here: 190 us
  starting transfers between devices  65.1 us (34%)
  Pallas kernels  62 us (32%)
  waiting for transfers between devices  49.2 us (26%)
  local copies, waits for them, and re-layouts  11.1 us (6%)
    ppermute x18, waiting for transfers between devices, line_send(): return lax.ppermute(x, 'dp', pairs)  37.8 us
    ppermute x18, starting transfers between devices, line_send(): return lax.ppermute(x, 'dp', pairs)  36.6 us
    ppermute x10, starting transfers between devices, to_core(): lax.ppermute(x, 'dp', [(i, i ^ 1) for i in range(lax.axis_size('dp'))])  17 us
    pallas_call x2, Pallas kernels, conv_full(): pl.pallas_call(functools.partial(conv_kernel, n, sign, transposed), in_sp...  14.2 us
    pallas_call x6, Pallas kernels, finish(): pl.pallas_call(functools.partial(finish_kernel, n, axis, factor, chunk),...  12.9 us
    pallas_call x2, Pallas kernels, spread_shares(): pl.pallas_call(functools.partial(share_kernel, n, sign), in_specs=[smem()...  12.8 us
    ppermute x12, starting transfers between devices, to_partner(): return lax.ppermute(x, 'chan', [(i, i ^ m) for i in range(n)])  11.5 us
    unnamed x38, local copies, waits for them, and re-layouts  11 us
  transfers between devices with their start and end apart: 40, of which 9 were waited for; matrix products, arithmetic and copies ran while one was open for 0% of the time, Pallas kernels for 26%

profile of v5, /device:TPU:1, one launch (start us, length us, event | category | flops | bytes accessed | tf_op | source)
XLA Modules:
  0.0 190.1 jit_solution(1779670093249151372)
XLA Ops:
  1.3 7.1 %pre.1 = (bf16[1024,128]{1,0:T(8,128)(2,1)}, bf16[1024,128]{1,0:T(8,128)(2,1)}, bf16[1024,128]{1,0:T(8,128)(2,1)}, bf16[1024,128]{1,0:T(8,128)(2,1)}) custom-call(s32[2]{0:T(128)} %pad_add_fusion.idx, bf16[128,1024]{1,0:T(8,128)(2,1)} %bitcast.17, bf16[3456,512]{1,0:T(8,128)(2,1)} %bitcast.10), custom_call_target="tpu_custom_call" | custom-call | flops 1024 | bytes 1024 | tf_op jit(solution)/shard_map/pre/pallas_call | solution.py:105
  8.4 2.1 %collective-permute-start = (bf16[1024,128]{1,0:T(8,128)(2,1)}, bf16[1024,128]{1,0:T(8,128)(2,1)S(1)}, u32[]{:S(2)}, u32[]{:S(2)}) collective-permute-start(bf16[1024,128]{1,0:T(8,128)(2,1)} %get-tuple-element.38), channel_id=1, source_target_pairs={{0,1},{1,0},{2,3},{3,2},{4,5},{5,4},{6,7},{7,6},{8,9},{9,8},{10,11... | collective-permute-start | bytes 786440 | tf_op jit(solution)/shard_map/ppermute | solution.py:496
  13.0 2.0 %copy-done.4 = bf16[27,512,128]{2,1,0:T(8,128)(2,1)S(1)} copy-done((bf16[27,512,128]{2,1,0:T(8,128)(2,1)S(1)}, bf16[27,512,128]{2,1,0:T(8,128)(2,1)}, u32[]{:S(2)}) %copy-start.4) | copy-done | bytes 3538968
  16.6 5.7 %dact.1 = (bf16[1024,128]{1,0:T(8,128)(2,1)S(1)}, bf16[1024,128]{1,0:T(8,128)(2,1)S(1)}, bf16[1024,128]{1,0:T(8,128)(2,1)S(1)}, bf16[1024,128]{1,0:T(8,128)(2,1)S(1)}) custom-call(s32[2]{0:T(128)S(1)} %copy-done.17, bf16[128,1024]{1,0:T(8,128)(2,1)S(1)} %bitcast.14, bf16[27,512,128]{2,1,0:T(8,128)(2,1)S(1)} %copy-done.4), custom_call_target="tpu_custom_call" | custom-call | flops 1024 | bytes 1024 | tf_op jit(solution)/shard_map/dact/pallas_call | solution.py:105
  24.8 1.7 collective-permute-start.5
  28.2 2.5 %moved_first.1.refs_5_.moved = bf16[2,1152,1024]{2,1,0:T(8,128)(2,1)S(1)} custom-call(bf16[128,1024]{1,0:T(8,128)(2,1)S(1)} %bitcast.19, bf16[128,1024]{1,0:T(8,128)(2,1)} %collective-permute-done.7.other, bf16[1024,128]{1,0:T(8,128)(2,1)S(1)} %get-tuple-element.42._.refs_0_), custom_call_target="tpu_custom_call" | custom-call | flops 1024 | bytes 1024 | tf_op jit(solution)/shard_map/moved_first/pallas_call | solution.py:298
  31.9 7.7 %collective-permute-done.4.refs_2_ = bf16[1024,128]{1,0:T(8,128)(2,1)S(1)} collective-permute-done((bf16[1024,128]{1,0:T(8,128)(2,1)S(1)}, bf16[1024,128]{1,0:T(8,128)(2,1)S(1)}, u32[]{:S(2)}, u32[]{:S(2)}) %collective-permute-start.4) | collective-permute-done | bytes 262176 | tf_op jit(solution)/shard_map/ppermute | solution.py:496
  40.6 2.2 %copy-done.2 = bf16[2,1152,1024]{2,1,0:T(8,128)(2,1)} copy-done((bf16[2,1152,1024]{2,1,0:T(8,128)(2,1)}, bf16[2,1152,1024]{2,1,0:T(8,128)(2,1)S(1)}, u32[]{:S(2)}) %copy-start.2) | copy-done | bytes 4718616
  43.2 1.5 collective-permute-done.8.other
  46.0 3.4 %collective-permute-start.15 = (bf16[9,256,128]{2,1,0:T(8,128)(2,1)S(1)}, bf16[9,256,128]{2,1,0:T(8,128)(2,1)S(1)}, u32[]{:S(2)}, u32[]{:S(2)}) collective-permute-start(bf16[9,256,128]{2,1,0:T(8,128)(2,1)S(1)} %get-tuple-element.48.refs_4_.x), channel_id=1, source_target_pairs={{0,8},{4,12},{24,16},{28,20},{1,9},{5,13},{25,17},{29,21},{2,10},{... | collective-permute-start | bytes 1769480 | tf_op jit(solution)/shard_map/ppermute | solution.py:470
  52.1 7.0 %output.1.refs_0_ = bf16[128,1024]{1,0:T(8,128)(2,1)} custom-call(s32[2]{0:T(128)S(1)} %copy-done.18, bf16[27,512,128]{2,1,0:T(8,128)(2,1)S(1)} %copy-done.5, bf16[1024,128]{1,0:T(8,128)(2,1)S(1)} %get-tuple-element.42._.refs_0_, bf16[1024,128]{1,0:T(8,128)(2,1)S(1)} %collective-permute-done.3.refs_1_, bf16[1024,128]{1,0:T(8,128)(2,1)S(1)} %collective-permute-done.4.refs_2_, ...), custom_call_target="tpu_custom_call" | custom-call | flops 1024 | bytes 1024 | tf_op jit(solution)/shard_map/output/pallas_call | solution.py:207
  68.4 5.9 %collective-permute-done.17.y = bf16[9,256,128]{2,1,0:T(8,128)(2,1)S(1)} collective-permute-done((bf16[9,256,128]{2,1,0:T(8,128)(2,1)S(1)}, bf16[9,256,128]{2,1,0:T(8,128)(2,1)S(1)}, u32[]{:S(2)}, u32[]{:S(2)}) %collective-permute-start.17) | collective-permute-done | bytes 589856 | tf_op jit(solution)/shard_map/ppermute | solution.py:470
  74.3 4.9 %collective-permute-start.21 = (bf16[9,256,128]{2,1,0:T(8,128)(2,1)S(1)}, bf16[9,256,128]{2,1,0:T(8,128)(2,1)}, u32[]{:S(2)}, u32[]{:S(2)}) collective-permute-start(bf16[9,256,128]{2,1,0:T(8,128)(2,1)S(1)} %grad_second.5.refs_0_.x), channel_id=1, source_target_pairs={{0,8},{4,12},{24,16},{28,20},{1,9},{5,13},{25,17},{29,21},{2,10},{... | collective-permute-start | bytes 1769480 | tf_op jit(solution)/shard_map/ppermute | solution.py:470
  82.5 2.4 %collective-permute-start.19 = (bf16[2,1024,128]{2,1,0:T(8,128)(2,1)}, bf16[2,1024,128]{2,1,0:T(8,128)(2,1)S(1)}, u32[]{:S(2)}, u32[]{:S(2)}) collective-permute-start(bf16[2,1024,128]{2,1,0:T(8,128)(2,1)} %get-tuple-element.56), channel_id=1, source_target_pairs={{0,4},{4,0},{8,12},{12,8},{16,20},{20,16},{24,28},{28,24},{1,5},{5... | collective-permute-start | bytes 1572872 | tf_op jit(solution)/shard_map/ppermute | solution.py:499
  86.2 2.7 %collective-permute-done.21.y = bf16[9,256,128]{2,1,0:T(8,128)(2,1)} collective-permute-done((bf16[9,256,128]{2,1,0:T(8,128)(2,1)S(1)}, bf16[9,256,128]{2,1,0:T(8,128)(2,1)}, u32[]{:S(2)}, u32[]{:S(2)}) %collective-permute-start.21) | collective-permute-done | bytes 589856 | tf_op jit(solution)/shard_map/ppermute | solution.py:470
  92.0 2.3 %copy-done.3 = bf16[2,1152,1024]{2,1,0:T(8,128)(2,1)S(1)} copy-done((bf16[2,1152,1024]{2,1,0:T(8,128)(2,1)S(1)}, bf16[2,1152,1024]{2,1,0:T(8,128)(2,1)}, u32[]{:S(2)}) %copy-start.3) | copy-done | bytes 4718616
  95.4 6.8 %collective-permute-start.25 = (bf16[1168,256]{1,0:T(8,128)(2,1)S(1)}, bf16[1168,256]{1,0:T(8,128)(2,1)S(1)}, u32[]{:S(2)}, u32[]{:S(2)}) collective-permute-start(bf16[1168,256]{1,0:T(8,128)(2,1)S(1)} %grad_first.3.refs_0_.x), channel_id=1, source_target_pairs={{0,8},{4,12},{24,16},{28,20},{1,9},{5,13},{25,17},{29,21},{2,10},{... | collective-permute-start | bytes 1794056 | tf_op jit(solution)/shard_map/ppermute | solution.py:470
  104.7 3.7 %collective-permute-start.22 = (bf16[9,256,128]{2,1,0:T(8,128)(2,1)S(1)}, bf16[9,256,128]{2,1,0:T(8,128)(2,1)S(1)}, u32[]{:S(2)}, u32[]{:S(2)}) collective-permute-start(bf16[9,256,128]{2,1,0:T(8,128)(2,1)S(1)} %line_pick.6.refs_0_.own), channel_id=1, source_target_pairs={{0,4},{4,0},{8,12},{12,8},{16,20},{20,16},{24,28},{28,24},{1,5},{5... | collective-permute-start | bytes 1769480 | tf_op jit(solution)/shard_map/ppermute | solution.py:499
  109.8 4.8 %collective-permute-start.30 = (bf16[1168,256]{1,0:T(8,128)(2,1)S(1)}, bf16[1168,256]{1,0:T(8,128)(2,1)S(1)}, u32[]{:S(2)}, u32[]{:S(2)}) collective-permute-start(bf16[1168,256]{1,0:T(8,128)(2,1)S(1)} %grad_first.4.refs_0_.x), channel_id=1, source_target_pairs={{0,8},{4,12},{24,16},{28,20},{1,9},{5,13},{25,17},{29,21},{2,10},{... | collective-permute-start | bytes 1794056 | tf_op jit(solution)/shard_map/ppermute | solution.py:470
  116.6 2.7 %collective-permute-start.26 = (bf16[1168,256]{1,0:T(8,128)(2,1)S(1)}, bf16[1168,256]{1,0:T(8,128)(2,1)S(1)}, u32[]{:S(2)}, u32[]{:S(2)}) collective-permute-start(bf16[1168,256]{1,0:T(8,128)(2,1)S(1)} %grad_first.5.refs_0_.x), channel_id=1, source_target_pairs={{0,8},{4,12},{24,16},{28,20},{1,9},{5,13},{25,17},{29,21},{2,10},{... | collective-permute-start | bytes 1794056 | tf_op jit(solution)/shard_map/ppermute | solution.py:470
  121.4 4.1 %collective-permute-start.27 = (bf16[9,256,128]{2,1,0:T(8,128)(2,1)S(1)}, bf16[9,256,128]{2,1,0:T(8,128)(2,1)S(1)}, u32[]{:S(2)}, u32[]{:S(2)}) collective-permute-start(bf16[9,256,128]{2,1,0:T(8,128)(2,1)S(1)} %line_pick.7.refs_0_.own), channel_id=1, source_target_pairs={{0,4},{4,0},{8,12},{12,8},{16,20},{20,16},{24,28},{28,24},{1,5},{5... | collective-permute-start | bytes 1769480 | tf_op jit(solution)/shard_map/ppermute | solution.py:499
  125.5 2.0 %finish_second.3 = (f32[27,512,128]{2,1,0:T(8,128)}, f32[8,128]{1,0:T(8,128)S(1)}) custom-call(s32[2]{0:T(128)S(1)} %copy-done.18, bf16[9,256,128]{2,1,0:T(8,128)(2,1)S(1)} %line_pick.6.refs_0_.own, bf16[9,256,128]{2,1,0:T(8,128)(2,1)S(1)} %collective-permute-done.22.other, bf16[9,256,128]{2,1,0:T(8,128)(2,1)S(1)} %line_pick.7.refs_0_.own), custom_call_target="tpu_custom_call" | custom-call | flops 1024 | bytes 1024 | tf_op jit(solution)/shard_map/finish_second/pallas_call | solution.py:409
  127.6 7.2 %grad_volume.1.refs_0_ = bf16[128,1024]{1,0:T(8,128)(2,1)} custom-call(s32[2]{0:T(128)S(1)} %copy-done.18, bf16[3456,512]{1,0:T(8,128)(2,1)S(1)} %bitcast.11, bf16[1024,128]{1,0:T(8,128)(2,1)S(1)} %get-tuple-element.54.refs_0_, bf16[1024,128]{1,0:T(8,128)(2,1)S(1)} %copy-done.13, bf16[1024,128]{1,0:T(8,128)(2,1)S(1)} %copy-done.11, ...), custom_call_target="tpu_custom_call" | custom-call | flops 1024 | bytes 1024 | tf_op jit(solution)/shard_map/grad_volume/pallas_call | solution.py:207
  138.7 2.1 %finish_second.4 = (f32[27,512,128]{2,1,0:T(8,128)}, f32[8,128]{1,0:T(8,128)S(1)}) custom-call(s32[2]{0:T(128)S(1)} %copy-done.18, bf16[9,256,128]{2,1,0:T(8,128)(2,1)S(1)} %line_pick.7.refs_0_.own, bf16[9,256,128]{2,1,0:T(8,128)(2,1)S(1)} %collective-permute-done.27.other, ...), custom_call_target="tpu_custom_call", output_to_operand_aliasing={{0}: (3, {})} | custom-call | flops 1024 | bytes 1024 | tf_op jit(solution)/shard_map/finish_second/pallas_call | solution.py:409
  143.9 12.7 %collective-permute-done.33.y = bf16[1168,256]{1,0:T(8,128)(2,1)S(1)} collective-permute-done((bf16[1168,256]{1,0:T(8,128)(2,1)S(1)}, bf16[1168,256]{1,0:T(8,128)(2,1)S(1)}, u32[]{:S(2)}, u32[]{:S(2)}) %collective-permute-start.33) | collective-permute-done | bytes 598048 | tf_op jit(solution)/shard_map/ppermute | solution.py:470
  158.1 2.0 %finish_second.5 = (f32[27,512,128]{2,1,0:T(8,128)}, f32[8,128]{1,0:T(8,128)S(1)}) custom-call(s32[2]{0:T(128)S(1)} %copy-done.18, bf16[9,256,128]{2,1,0:T(8,128)(2,1)S(1)} %line_pick.8.refs_1_.own, bf16[9,256,128]{2,1,0:T(8,128)(2,1)S(1)} %collective-permute-done.32.other, ...), custom_call_target="tpu_custom_call", output_to_operand_aliasing={{0}: (3, {})} | custom-call | flops 1024 | bytes 1024 | tf_op jit(solution)/shard_map/finish_second/pallas_call | solution.py:409
  161.6 7.8 %collective-permute-done.37.y = bf16[1168,256]{1,0:T(8,128)(2,1)S(1)} collective-permute-done((bf16[1168,256]{1,0:T(8,128)(2,1)S(1)}, bf16[1168,256]{1,0:T(8,128)(2,1)S(1)}, u32[]{:S(2)}, u32[]{:S(2)}) %collective-permute-start.37) | collective-permute-done | bytes 598048 | tf_op jit(solution)/shard_map/ppermute | solution.py:470
  169.9 1.9 collective-permute-start.39
  171.8 2.0 %finish_first.3 = (f32[27,128,512]{2,1,0:T(8,128)}, f32[8,128]{1,0:T(8,128)S(1)}) custom-call(s32[2]{0:T(128)S(1)} %copy-done.18, bf16[1168,256]{1,0:T(8,128)(2,1)S(1)} %line_pick.9.refs_1_.own, bf16[1168,256]{1,0:T(8,128)(2,1)S(1)} %collective-permute-done.36.other, bf16[1168,256]{1,0:T(8,128)(2,1)S(1)} %line_pick.10.refs_0_.own), custom_call_target="tpu_custom_call" | custom-call | flops 1024 | bytes 1024 | tf_op jit(solution)/shard_map/finish_first/pallas_call | solution.py:409
  173.9 8.7 %collective-permute-done.35.y = bf16[1168,256]{1,0:T(8,128)(2,1)S(1)} collective-permute-done((bf16[1168,256]{1,0:T(8,128)(2,1)S(1)}, bf16[1168,256]{1,0:T(8,128)(2,1)S(1)}, u32[]{:S(2)}, u32[]{:S(2)}) %collective-permute-start.35) | collective-permute-done | bytes 598048 | tf_op jit(solution)/shard_map/ppermute | solution.py:470
  185.2 2.0 %finish_first.4 = (f32[27,128,512]{2,1,0:T(8,128)}, f32[8,128]{1,0:T(8,128)S(1)}) custom-call(s32[2]{0:T(128)S(1)} %copy-done.18, bf16[1168,256]{1,0:T(8,128)(2,1)S(1)} %line_pick.10.refs_0_.own, bf16[1168,256]{1,0:T(8,128)(2,1)S(1)} %collective-permute-done.39.other, f32[27,128,512]{2,1,0:T(8,128)} %get-tuple-element.64.refs_0_, ...), custom_call_target="tpu_custom_call", output_to_operand_aliasing={{0}: (3, {})} | custom-call | flops 1024 | bytes 1024 | tf_op jit(solution)/shard_map/finish_first/pallas_call | solution.py:409
  187.3 2.6 %finish_first.5 = (f32[27,128,512]{2,1,0:T(8,128)}, f32[8,128]{1,0:T(8,128)}) custom-call(s32[2]{0:T(128)S(1)} %copy-done.18, bf16[1168,256]{1,0:T(8,128)(2,1)S(1)} %line_pick.11.refs_1_.own, bf16[1168,256]{1,0:T(8,128)(2,1)S(1)} %collective-permute-done.38.other, f32[27,128,512]{2,1,0:T(8,128)} %get-tuple-element.65.refs_0_, ...), custom_call_target="tpu_custom_call", output_to_operand_aliasing={{0}: (3, {})} | custom-call | flops 1024 | bytes 1024 | tf_op jit(solution)/shard_map/finish_first/pallas_call | solution.py:409
  (132 shorter events, 53.9 us)
Async XLA Ops:
  8.4 14.0 %collective-permute-start = (bf16[1024,128]{1,0:T(8,128)(2,1)}, bf16[1024,128]{1,0:T(8,128)(2,1)S(1)}, u32[]{:S(2)}, u32[]{:S(2)}) collective-permute-start(bf16[1024,128]{1,0:T(8,128)(2,1)} %get-tuple-element.38), channel_id=1, source_target_pairs={{0,1},{1,0},{2,3},{3,2},{4,5},{5,4},{6,7},{7,6},{8,9},{9,8},{10,11... | collective-permute-start | bytes 786440 | tf_op jit(solution)/shard_map/ppermute | solution.py:496
  10.5 11.9 %collective-permute-start.1 = (bf16[1024,128]{1,0:T(8,128)(2,1)}, bf16[1024,128]{1,0:T(8,128)(2,1)S(1)}, u32[]{:S(2)}, u32[]{:S(2)}) collective-permute-start(bf16[1024,128]{1,0:T(8,128)(2,1)} %get-tuple-element.39), channel_id=1, source_target_pairs={{0,2},{1,3},{2,0},{3,1},{4,6},{5,7},{6,4},{7,5},{8,10},{9,11},{10,... | collective-permute-start | bytes 786440 | tf_op jit(solution)/shard_map/ppermute | solution.py:496
  11.8 16.4 %collective-permute-start.7 = (bf16[128,1024]{1,0:T(8,128)(2,1)}, bf16[128,1024]{1,0:T(8,128)(2,1)}, u32[]{:S(2)}, u32[]{:S(2)}) collective-permute-start(bf16[128,1024]{1,0:T(8,128)(2,1)} %bitcast.18), channel_id=1, source_target_pairs={{0,4},{4,0},{8,12},{12,8},{16,20},{20,16},{24,28},{28,24},{1,5},{5... | collective-permute-start | bytes 786440 | tf_op jit(solution)/shard_map/ppermute | solution.py:499
  13.0 14.5 %collective-permute-start.6 = (bf16[128,1024]{1,0:T(8,128)(2,1)}, bf16[128,1024]{1,0:T(8,128)(2,1)S(1)}, u32[]{:S(2)}, u32[]{:S(2)}) collective-permute-start(bf16[128,1024]{1,0:T(8,128)(2,1)} %bitcast.13), channel_id=1, source_target_pairs={{0,4},{4,0},{8,12},{12,8},{16,20},{20,16},{24,28},{28,24},{1,5},{5... | collective-permute-start | bytes 786440 | tf_op jit(solution)/shard_map/ppermute | solution.py:499
  26.6 13.1 %collective-permute-start.4 = (bf16[1024,128]{1,0:T(8,128)(2,1)S(1)}, bf16[1024,128]{1,0:T(8,128)(2,1)S(1)}, u32[]{:S(2)}, u32[]{:S(2)}) collective-permute-start(bf16[1024,128]{1,0:T(8,128)(2,1)S(1)} %get-tuple-element.42._.refs_0_), channel_id=1, source_target_pairs={{0,2},{1,3},{2,0},{3,1},{4,6},{5,7},{6,4},{7,5},{8,10},{9,11},{10,... | collective-permute-start | bytes 786440 | tf_op jit(solution)/shard_map/ppermute | solution.py:496
  27.2 12.4 %collective-permute-start.3 = (bf16[1024,128]{1,0:T(8,128)(2,1)S(1)}, bf16[1024,128]{1,0:T(8,128)(2,1)S(1)}, u32[]{:S(2)}, u32[]{:S(2)}) collective-permute-start(bf16[1024,128]{1,0:T(8,128)(2,1)S(1)} %get-tuple-element.42._.refs_0_), channel_id=1, source_target_pairs={{0,1},{1,0},{2,3},{3,2},{4,5},{5,4},{6,7},{7,6},{8,9},{9,8},{10,11... | collective-permute-start | bytes 786440 | tf_op jit(solution)/shard_map/ppermute | solution.py:496
  46.0 17.7 %collective-permute-start.15 = (bf16[9,256,128]{2,1,0:T(8,128)(2,1)S(1)}, bf16[9,256,128]{2,1,0:T(8,128)(2,1)S(1)}, u32[]{:S(2)}, u32[]{:S(2)}) collective-permute-start(bf16[9,256,128]{2,1,0:T(8,128)(2,1)S(1)} %get-tuple-element.48.refs_4_.x), channel_id=1, source_target_pairs={{0,8},{4,12},{24,16},{28,20},{1,9},{5,13},{25,17},{29,21},{2,10},{... | collective-permute-start | bytes 1769480 | tf_op jit(solution)/shard_map/ppermute | solution.py:470
  49.4 13.6 %collective-permute-start.9 = (bf16[1024,128]{1,0:T(8,128)(2,1)S(1)}, bf16[1024,128]{1,0:T(8,128)(2,1)S(1)}, u32[]{:S(2)}, u32[]{:S(2)}) collective-permute-start(bf16[1024,128]{1,0:T(8,128)(2,1)S(1)} %get-tuple-element.51), channel_id=1, source_target_pairs={{0,1},{1,0},{2,3},{3,2},{4,5},{5,4},{6,7},{7,6},{8,9},{9,8},{10,11... | collective-permute-start | bytes 786440 | tf_op jit(solution)/shard_map/ppermute | solution.py:496
  50.5 12.5 %collective-permute-start.10 = (bf16[1024,128]{1,0:T(8,128)(2,1)S(1)}, bf16[1024,128]{1,0:T(8,128)(2,1)S(1)}, u32[]{:S(2)}, u32[]{:S(2)}) collective-permute-start(bf16[1024,128]{1,0:T(8,128)(2,1)S(1)} %get-tuple-element.52), channel_id=1, source_target_pairs={{0,2},{1,3},{2,0},{3,1},{4,6},{5,7},{6,4},{7,5},{8,10},{9,11},{10,... | collective-permute-start | bytes 786440 | tf_op jit(solution)/shard_map/ppermute | solution.py:496
  61.6 12.7 %collective-permute-start.17 = (bf16[9,256,128]{2,1,0:T(8,128)(2,1)S(1)}, bf16[9,256,128]{2,1,0:T(8,128)(2,1)S(1)}, u32[]{:S(2)}, u32[]{:S(2)}) collective-permute-start(bf16[9,256,128]{2,1,0:T(8,128)(2,1)S(1)} %grad_second.4.refs_4_.x), channel_id=1, source_target_pairs={{0,8},{4,12},{24,16},{28,20},{1,9},{5,13},{25,17},{29,21},{2,10},{... | collective-permute-start | bytes 1769480 | tf_op jit(solution)/shard_map/ppermute | solution.py:470
  63.8 15.6 %collective-permute-start.16 = (bf16[9,256,128]{2,1,0:T(8,128)(2,1)S(1)}, bf16[9,256,128]{2,1,0:T(8,128)(2,1)S(1)}, u32[]{:S(2)}, u32[]{:S(2)}) collective-permute-start(bf16[9,256,128]{2,1,0:T(8,128)(2,1)S(1)} %line_add.12.refs_0_.x), channel_id=1, source_target_pairs={{8,16},{12,20},{16,8},{20,12},{9,17},{13,21},{17,9},{21,13},{10,18... | collective-permute-start | bytes 1769480 | tf_op jit(solution)/shard_map/ppermute | solution.py:470
  64.5 16.5 %collective-permute-start.14 = (bf16[1024,128]{1,0:T(8,128)(2,1)S(1)}, bf16[1024,128]{1,0:T(8,128)(2,1)S(1)}, u32[]{:S(2)}, u32[]{:S(2)}) collective-permute-start(bf16[1024,128]{1,0:T(8,128)(2,1)S(1)} %get-tuple-element.54.refs_0_), channel_id=1, source_target_pairs={{0,3},{1,2},{2,1},{3,0},{4,7},{5,6},{6,5},{7,4},{8,11},{9,10},{10,... | collective-permute-start | bytes 786440 | tf_op jit(solution)/shard_map/ppermute | solution.py:496
  66.0 15.0 %collective-permute-start.13 = (bf16[1024,128]{1,0:T(8,128)(2,1)S(1)}, bf16[1024,128]{1,0:T(8,128)(2,1)S(1)}, u32[]{:S(2)}, u32[]{:S(2)}) collective-permute-start(bf16[1024,128]{1,0:T(8,128)(2,1)S(1)} %get-tuple-element.54.refs_0_), channel_id=1, source_target_pairs={{0,2},{1,3},{2,0},{3,1},{4,6},{5,7},{6,4},{7,5},{8,10},{9,11},{10,... | collective-permute-start | bytes 786440 | tf_op jit(solution)/shard_map/ppermute | solution.py:496
  66.8 14.3 %collective-permute-start.12 = (bf16[1024,128]{1,0:T(8,128)(2,1)S(1)}, bf16[1024,128]{1,0:T(8,128)(2,1)S(1)}, u32[]{:S(2)}, u32[]{:S(2)}) collective-permute-start(bf16[1024,128]{1,0:T(8,128)(2,1)S(1)} %get-tuple-element.54.refs_0_), channel_id=1, source_target_pairs={{0,1},{1,0},{2,3},{3,2},{4,5},{5,4},{6,7},{7,6},{8,9},{9,8},{10,11... | collective-permute-start | bytes 786440 | tf_op jit(solution)/shard_map/ppermute | solution.py:496
  74.3 14.6 %collective-permute-start.21 = (bf16[9,256,128]{2,1,0:T(8,128)(2,1)S(1)}, bf16[9,256,128]{2,1,0:T(8,128)(2,1)}, u32[]{:S(2)}, u32[]{:S(2)}) collective-permute-start(bf16[9,256,128]{2,1,0:T(8,128)(2,1)S(1)} %grad_second.5.refs_0_.x), channel_id=1, source_target_pairs={{0,8},{4,12},{24,16},{28,20},{1,9},{5,13},{25,17},{29,21},{2,10},{... | collective-permute-start | bytes 1769480 | tf_op jit(solution)/shard_map/ppermute | solution.py:470
  84.9 18.7 %collective-permute-start.18 = (bf16[9,256,128]{2,1,0:T(8,128)(2,1)S(1)}, bf16[9,256,128]{2,1,0:T(8,128)(2,1)}, u32[]{:S(2)}, u32[]{:S(2)}) collective-permute-start(bf16[9,256,128]{2,1,0:T(8,128)(2,1)S(1)} %line_add.14.refs_4_.x), channel_id=1, source_target_pairs={{8,0},{12,4},{16,24},{20,28},{9,1},{13,5},{17,25},{21,29},{10,2},{... | collective-permute-start | bytes 1769480 | tf_op jit(solution)/shard_map/ppermute | solution.py:470
  90.1 26.5 %collective-permute-start.24 = (bf16[9,256,128]{2,1,0:T(8,128)(2,1)S(1)}, bf16[9,256,128]{2,1,0:T(8,128)(2,1)S(1)}, u32[]{:S(2)}, u32[]{:S(2)}) collective-permute-start(bf16[9,256,128]{2,1,0:T(8,128)(2,1)S(1)} %line_add.15.refs_0_.x), channel_id=1, source_target_pairs={{8,16},{12,20},{16,8},{20,12},{9,17},{13,21},{17,9},{21,13},{10,18... | collective-permute-start | bytes 1769480 | tf_op jit(solution)/shard_map/ppermute | solution.py:470
  95.4 20.3 %collective-permute-start.25 = (bf16[1168,256]{1,0:T(8,128)(2,1)S(1)}, bf16[1168,256]{1,0:T(8,128)(2,1)S(1)}, u32[]{:S(2)}, u32[]{:S(2)}) collective-permute-start(bf16[1168,256]{1,0:T(8,128)(2,1)S(1)} %grad_first.3.refs_0_.x), channel_id=1, source_target_pairs={{0,8},{4,12},{24,16},{28,20},{1,9},{5,13},{25,17},{29,21},{2,10},{... | collective-permute-start | bytes 1794056 | tf_op jit(solution)/shard_map/ppermute | solution.py:470
  102.3 17.2 %collective-permute-start.23 = (bf16[9,256,128]{2,1,0:T(8,128)(2,1)S(1)}, bf16[9,256,128]{2,1,0:T(8,128)(2,1)S(1)}, u32[]{:S(2)}, u32[]{:S(2)}) collective-permute-start(bf16[9,256,128]{2,1,0:T(8,128)(2,1)S(1)} %line_add.16.refs_0_.x), channel_id=1, source_target_pairs={{8,0},{12,4},{16,24},{20,28},{9,1},{13,5},{17,25},{21,29},{10,2},{... | collective-permute-start | bytes 1769480 | tf_op jit(solution)/shard_map/ppermute | solution.py:470
  104.7 16.7 %collective-permute-start.22 = (bf16[9,256,128]{2,1,0:T(8,128)(2,1)S(1)}, bf16[9,256,128]{2,1,0:T(8,128)(2,1)S(1)}, u32[]{:S(2)}, u32[]{:S(2)}) collective-permute-start(bf16[9,256,128]{2,1,0:T(8,128)(2,1)S(1)} %line_pick.6.refs_0_.own), channel_id=1, source_target_pairs={{0,4},{4,0},{8,12},{12,8},{16,20},{20,16},{24,28},{28,24},{1,5},{5... | collective-permute-start | bytes 1769480 | tf_op jit(solution)/shard_map/ppermute | solution.py:499
  109.8 24.9 %collective-permute-start.30 = (bf16[1168,256]{1,0:T(8,128)(2,1)S(1)}, bf16[1168,256]{1,0:T(8,128)(2,1)S(1)}, u32[]{:S(2)}, u32[]{:S(2)}) collective-permute-start(bf16[1168,256]{1,0:T(8,128)(2,1)S(1)} %grad_first.4.refs_0_.x), channel_id=1, source_target_pairs={{0,8},{4,12},{24,16},{28,20},{1,9},{5,13},{25,17},{29,21},{2,10},{... | collective-permute-start | bytes 1794056 | tf_op jit(solution)/shard_map/ppermute | solution.py:470
  115.9 20.7 %collective-permute-start.29 = (bf16[1168,256]{1,0:T(8,128)(2,1)S(1)}, bf16[1168,256]{1,0:T(8,128)(2,1)S(1)}, u32[]{:S(2)}, u32[]{:S(2)}) collective-permute-start(bf16[1168,256]{1,0:T(8,128)(2,1)S(1)} %line_add.17.refs_0_.x), channel_id=1, source_target_pairs={{8,16},{12,20},{16,8},{20,12},{9,17},{13,21},{17,9},{21,13},{10,18... | collective-permute-start | bytes 1794056 | tf_op jit(solution)/shard_map/ppermute | solution.py:470
  116.6 24.1 %collective-permute-start.26 = (bf16[1168,256]{1,0:T(8,128)(2,1)S(1)}, bf16[1168,256]{1,0:T(8,128)(2,1)S(1)}, u32[]{:S(2)}, u32[]{:S(2)}) collective-permute-start(bf16[1168,256]{1,0:T(8,128)(2,1)S(1)} %grad_first.5.refs_0_.x), channel_id=1, source_target_pairs={{0,8},{4,12},{24,16},{28,20},{1,9},{5,13},{25,17},{29,21},{2,10},{... | collective-permute-start | bytes 1794056 | tf_op jit(solution)/shard_map/ppermute | solution.py:470
  119.5 18.6 %collective-permute-start.28 = (bf16[9,256,128]{2,1,0:T(8,128)(2,1)S(1)}, bf16[9,256,128]{2,1,0:T(8,128)(2,1)S(1)}, u32[]{:S(2)}, u32[]{:S(2)}) collective-permute-start(bf16[9,256,128]{2,1,0:T(8,128)(2,1)S(1)} %line_add.18.refs_0_.x), channel_id=1, source_target_pairs={{8,0},{12,4},{16,24},{20,28},{9,1},{13,5},{17,25},{21,29},{10,2},{... | collective-permute-start | bytes 1769480 | tf_op jit(solution)/shard_map/ppermute | solution.py:470
  121.4 17.3 %collective-permute-start.27 = (bf16[9,256,128]{2,1,0:T(8,128)(2,1)S(1)}, bf16[9,256,128]{2,1,0:T(8,128)(2,1)S(1)}, u32[]{:S(2)}, u32[]{:S(2)}) collective-permute-start(bf16[9,256,128]{2,1,0:T(8,128)(2,1)S(1)} %line_pick.7.refs_0_.own), channel_id=1, source_target_pairs={{0,4},{4,0},{8,12},{12,8},{16,20},{20,16},{24,28},{28,24},{1,5},{5... | collective-permute-start | bytes 1769480 | tf_op jit(solution)/shard_map/ppermute | solution.py:499
  136.8 19.8 %collective-permute-start.33 = (bf16[1168,256]{1,0:T(8,128)(2,1)S(1)}, bf16[1168,256]{1,0:T(8,128)(2,1)S(1)}, u32[]{:S(2)}, u32[]{:S(2)}) collective-permute-start(bf16[1168,256]{1,0:T(8,128)(2,1)S(1)} %line_add.20.refs_0_.x), channel_id=1, source_target_pairs={{8,0},{12,4},{16,24},{20,28},{9,1},{13,5},{17,25},{21,29},{10,2},{... | collective-permute-start | bytes 1794056 | tf_op jit(solution)/shard_map/ppermute | solution.py:470
  140.9 19.2 %collective-permute-start.31 = (bf16[1168,256]{1,0:T(8,128)(2,1)S(1)}, bf16[1168,256]{1,0:T(8,128)(2,1)S(1)}, u32[]{:S(2)}, u32[]{:S(2)}) collective-permute-start(bf16[1168,256]{1,0:T(8,128)(2,1)S(1)} %line_add.21.refs_0_.x), channel_id=1, source_target_pairs={{8,16},{12,20},{16,8},{20,12},{9,17},{13,21},{17,9},{21,13},{10,18... | collective-permute-start | bytes 1794056 | tf_op jit(solution)/shard_map/ppermute | solution.py:470
  141.6 16.4 %collective-permute-start.32 = (bf16[9,256,128]{2,1,0:T(8,128)(2,1)S(1)}, bf16[9,256,128]{2,1,0:T(8,128)(2,1)S(1)}, u32[]{:S(2)}, u32[]{:S(2)}) collective-permute-start(bf16[9,256,128]{2,1,0:T(8,128)(2,1)S(1)} %line_pick.8.refs_1_.own), channel_id=1, source_target_pairs={{0,4},{4,0},{8,12},{12,8},{16,20},{20,16},{24,28},{28,24},{1,5},{5... | collective-permute-start | bytes 1769480 | tf_op jit(solution)/shard_map/ppermute | solution.py:499
  142.6 26.8 %collective-permute-start.37 = (bf16[1168,256]{1,0:T(8,128)(2,1)S(1)}, bf16[1168,256]{1,0:T(8,128)(2,1)S(1)}, u32[]{:S(2)}, u32[]{:S(2)}) collective-permute-start(bf16[1168,256]{1,0:T(8,128)(2,1)S(1)} %line_add.22.refs_0_.x), channel_id=1, source_target_pairs={{8,0},{12,4},{16,24},{20,28},{9,1},{13,5},{17,25},{21,29},{10,2},{... | collective-permute-start | bytes 1794056 | tf_op jit(solution)/shard_map/ppermute | solution.py:470
  157.2 14.6 %collective-permute-start.36 = (bf16[1168,256]{1,0:T(8,128)(2,1)S(1)}, bf16[1168,256]{1,0:T(8,128)(2,1)S(1)}, u32[]{:S(2)}, u32[]{:S(2)}) collective-permute-start(bf16[1168,256]{1,0:T(8,128)(2,1)S(1)} %line_pick.9.refs_1_.own), channel_id=1, source_target_pairs={{0,4},{4,0},{8,12},{12,8},{16,20},{20,16},{24,28},{28,24},{1,5},{5... | collective-permute-start | bytes 1794056 | tf_op jit(solution)/shard_map/ppermute | solution.py:499
  160.3 22.3 %collective-permute-start.35 = (bf16[1168,256]{1,0:T(8,128)(2,1)S(1)}, bf16[1168,256]{1,0:T(8,128)(2,1)S(1)}, u32[]{:S(2)}, u32[]{:S(2)}) collective-permute-start(bf16[1168,256]{1,0:T(8,128)(2,1)S(1)} %line_add.23.refs_0_.x), channel_id=1, source_target_pairs={{8,0},{12,4},{16,24},{20,28},{9,1},{13,5},{17,25},{21,29},{10,2},{... | collective-permute-start | bytes 1794056 | tf_op jit(solution)/shard_map/ppermute | solution.py:470
  169.9 15.3 %collective-permute-start.39 = (bf16[1168,256]{1,0:T(8,128)(2,1)S(1)}, bf16[1168,256]{1,0:T(8,128)(2,1)S(1)}, u32[]{:S(2)}, u32[]{:S(2)}) collective-permute-start(bf16[1168,256]{1,0:T(8,128)(2,1)S(1)} %line_pick.10.refs_0_.own), channel_id=1, source_target_pairs={{0,4},{4,0},{8,12},{12,8},{16,20},{20,16},{24,28},{28,24},{1,5},{5... | collective-permute-start | bytes 1794056 | tf_op jit(solution)/shard_map/ppermute | solution.py:499
  (27 other events, 267.1 us)

commit v6 on v5

--- a/solution.py
+++ b/solution.py
@@ -13,7 +13,7 @@
 CELLS = DEPTH * PLANE
 TAPS = [(a, b, c) for a in (-1, 0, 1) for b in (-1, 0, 1) for c in (-1, 0, 1)]
 NORM_EPS = 1e-05
-LIMIT = 24 * 1024 * 1024
+LIMIT = 16 * 1024 * 1024
 SMALL = 8 * 1024 * 1024
 LARGE = 61 * 1024 * 1024
 EXTRA = 16
@@ -122,7 +122,7 @@
 
 def norm_kernel(n, gain, *refs):
     shares = refs[:n]
-    act, normed_out, inverse_out = refs[-3:]
+    act, normed_out, inverse_out = refs[2 * n - 1 : 2 * n + 2]
     pre = shares[0][...].astype(F32)
     for m in range(1, n):
         pre = pre + shares[m][...].astype(F32)
@@ -178,7 +178,8 @@
 
 def conv_kernel(n, sign, transposed, idx, w, *refs):
     blocks = refs[:n]
-    out, ordered, sums, buffer, sems = refs[-5:]
+    out, mark, ordered, sums, buffer, sems = refs[-6:]
+    mark[...] = jnp.zeros_like(mark)
     rows = out.shape[0]
     copies = start_parts(w, buffer, sems)
     sums[...] = jnp.zeros_like(sums)
@@ -209,8 +210,11 @@
         in_specs=[smem(), IN_HBM]
         + [pl.BlockSpec(memory_space=pltpu.VMEM)] * n
         + [UNREAD] * len(after),
-        out_specs=pl.BlockSpec(memory_space=pltpu.VMEM),
-        out_shape=jax.ShapeDtypeStruct((rows, CELLS), BF16),
+        out_specs=[pl.BlockSpec(memory_space=pltpu.VMEM)] * 2,
+        out_shape=[
+            jax.ShapeDtypeStruct((rows, CELLS), BF16),
+            jax.ShapeDtypeStruct((8, 128), F32),
+        ],
         scratch_shapes=[
             pltpu.VMEM((n, CELLS, rows), BF16),
             pltpu.VMEM((3, DEPTH, HEIGHT, WIDTH, rows), F32),
@@ -344,8 +348,8 @@
     )(moved, own, other, gain_part, *after)
 
 
-def grad_second_kernel(a, held, moved, own, other, *refs):
-    out = refs[len(refs) - held - 1]
+def grad_second_kernel(a, moved, own, other, *refs):
+    out = refs[-1]
     rows = out.shape[2]
     begin, planes = max(0, a), DEPTH - abs(a)
     lhs = [
@@ -367,20 +371,16 @@
             out[at] = grads[:, place * rows : (place + 1) * rows].astype(BF16)
 
 
-def grad_second(a, moved, own, other, after, held=()):
+def grad_second(a, moved, own, other, after):
     wide, rows = own.shape[0], moved.shape[-1]
-    first = 3 + len(after)
     return pl.pallas_call(
-        functools.partial(grad_second_kernel, a, len(held)),
-        in_specs=[pl.BlockSpec(memory_space=pltpu.VMEM)] * 3 + [UNREAD] * (len(after) + len(held)),
-        out_specs=[pl.BlockSpec(memory_space=pltpu.VMEM)] + [UNREAD] * len(held),
-        out_shape=[jax.ShapeDtypeStruct((9, wide, rows), BF16)]
-        + [jax.ShapeDtypeStruct(x.shape, x.dtype) for x in held],
-        input_output_aliases={first + k: 1 + k for k in range(len(held))},
+        functools.partial(grad_second_kernel, a),
+        in_specs=[pl.BlockSpec(memory_space=pltpu.VMEM)] * 3 + [UNREAD] * len(after),
+        out_shape=jax.ShapeDtypeStruct((9, wide, rows), BF16),
         compiler_params=pltpu.CompilerParams(vmem_limit_bytes=LIMIT),
         cost_estimate=LIGHT,
         name="grad_second",
-    )(moved, own, other, *after, *held)
+    )(moved, own, other, *after)
 
 
 def finish_kernel(n, axis, factor, chunk, idx, own, other, *refs):
@@ -389,14 +389,22 @@
     taps, height, width = wide.shape[1:]
     copies = []
     for k, (part, place) in enumerate(((own, upper), (other, 1 - upper))):
-        rows = part[: taps * height] if len(part.shape) == 2 else part[...]
-        wide[k] = rows.reshape(taps, height, width).astype(F32) * factor
         size = (height, width)[axis - 1]
         span = pl.ds(pl.multiple_of(place * size, size), size)
-        target = out.at[pl.ds(chunk * taps, taps)]
-        target = target.at[:, span] if axis == 1 else target.at[:, :, span]
-        copies.append(pltpu.make_async_copy(wide.at[k], target, sems.at[k]))
-        copies[-1].start()
+        for third in range(3):
+            at = slice(3 * third, 3 * third + 3)
+            if len(part.shape) == 2:
+                rows = part[3 * third * height : (3 * third + 3) * height]
+                rows = rows.reshape(3, height, width)
+            else:
+                rows = part[at]
+            wide[k, at] = rows.astype(F32) * factor
+            target = out.at[pl.ds(chunk * taps + 3 * third, 3)]
+            target = target.at[:, span] if axis == 1 else target.at[:, :, span]
+            copies.append(
+                pltpu.make_async_copy(wide.at[k, at], target, sems.at[3 * k + third])
+            )
+            copies[-1].start()
     mark[...] = jnp.zeros_like(mark)
     for copy in copies:
         copy.wait()
@@ -413,7 +421,7 @@
         + [UNREAD] * (len(given) + len(after)),
         out_specs=[UNREAD, pl.BlockSpec(memory_space=pltpu.VMEM)],
         out_shape=[jax.ShapeDtypeStruct(full, F32), jax.ShapeDtypeStruct((8, 128), F32)],
-        scratch_shapes=[pltpu.VMEM((2,) + shape, F32), pltpu.SemaphoreType.DMA((2,))],
+        scratch_shapes=[pltpu.VMEM((2,) + shape, F32), pltpu.SemaphoreType.DMA((6,))],
         input_output_aliases={3: 0} if given else {},
         compiler_params=pltpu.CompilerParams(vmem_limit_bytes=SMALL),
         cost_estimate=LIGHT,
@@ -505,19 +513,24 @@
     first_flat = w_first.reshape(27 * rows, n * rows)
     pre_shares = swap(spread_shares(1, "pre", idx, n, vol, first_flat, LARGE))
     dact_parts = spread_shares(-1, "dact", idx, n, cot, w_second, LIMIT)
-    act, normed, inverse = pl.pallas_call(
+    held = dact_parts[1:]
+    act, normed, inverse, *held = pl.pallas_call(
         functools.partial(norm_kernel, n),
-        in_specs=[pl.BlockSpec(memory_space=pltpu.VMEM)] * (1 + n) + [UNREAD],
+        in_specs=[pl.BlockSpec(memory_space=pltpu.VMEM)] * (1 + n) + [UNREAD] * len(held),
+        out_specs=[pl.BlockSpec(memory_space=pltpu.VMEM)] * 3 + [UNREAD] * len(held),
         out_shape=[
             jax.ShapeDtypeStruct((CELLS, rows), BF16),
             jax.ShapeDtypeStruct((CELLS, rows), F32),
             jax.ShapeDtypeStruct((1, rows), F32),
-        ],
-        compiler_params=pltpu.CompilerParams(vmem_limit_bytes=LIMIT),
+        ]
+        + [jax.ShapeDtypeStruct(x.shape, x.dtype) for x in held],
+        input_output_aliases={1 + n + k: 3 + k for k in range(len(held))},
+        compiler_params=pltpu.CompilerParams(vmem_limit_bytes=SMALL),
         cost_estimate=LIGHT,
         name="norm",
-    )(own_gain, *pre_shares, dact_parts[0])
+    )(own_gain, *pre_shares, *held)
     act_blocks = swap([act] * n)
+    dact_shares = swap([dact_parts[0]] + held)
     moved_cot = moved_fields(
         moved_second_kernel,
         "moved_second",
@@ -526,10 +539,8 @@
         to_core(cot),
         act,
     )
-    moved_vol = moved_fields(
-        moved_first_kernel, "moved_first", (2, 9 * rows, CELLS), vol, to_core(vol), act
-    )
-    act_keep, act_send = halves("act_halves", True, idx, act_blocks, (moved_cot, moved_vol))
+    vol_other = to_core(vol)
+    act_keep, act_send = halves("act_halves", True, idx, act_blocks, (moved_cot,))
     act_other = to_core(act_send)
 
     sums, outward = line_moves(lax.axis_size("dp") // 2)
@@ -566,18 +577,13 @@
 
     def second_part(chunk):
         nonlocal last
-        held = tuple(dact_parts[1:]) if chunk == 0 else ()
-        parts[chunk], *passed = grad_second(
-            chunk - 1, moved_cot, act_keep, act_other, last, held
-        )
+        parts[chunk] = grad_second(chunk - 1, moved_cot, act_keep, act_other, last)
         last = (parts[chunk],)
-        if chunk == 0:
-            done["dact"] = swap([dact_parts[0]] + passed)
 
     def first_part(chunk):
         nonlocal last
         own, other = done["dpre_halves"]
-        parts[chunk] = grad_first(chunk - 4, moved_vol, own, other, done["gain"], last)
+        parts[chunk] = grad_first(chunk - 4, done["moved"], own, other, done["gain"], last)
         last = (parts[chunk],)
 
     def norm_back():
@@ -592,9 +598,12 @@
             compiler_params=pltpu.CompilerParams(vmem_limit_bytes=SMALL),
             cost_estimate=LIGHT,
             name="norm_back",
-        )(own_gain, normed, inverse, *done["dact"], *last)
+        )(own_gain, normed, inverse, *dact_shares, *last)
         done["dpre"] = swap([dpre] * n)
-        last = (dpre,)
+        done["moved"] = moved_fields(
+            moved_first_kernel, "moved_first", (2, 9 * rows, CELLS), vol, vol_other, dpre
+        )
+        last = (done["moved"],)
 
     def dpre_halves():
         nonlocal last
@@ -604,15 +613,15 @@
 
     def output():
         nonlocal last
-        done["output"] = conv_full("output", 1, False, idx, w_second, act_blocks, last)
-        last = (done["output"],)
+        done["output"], mark = conv_full("output", 1, False, idx, w_second, act_blocks, last)
+        last = (mark,)
 
     def grad_volume():
         nonlocal last
-        done["grad_volume"] = conv_full(
+        done["grad_volume"], mark = conv_full(
             "grad_volume", -1, True, idx, first_flat, done["dpre"], last
         )
-        last = (done["grad_volume"],)
+        last = (mark,)
 
     def wave(at):
         for step in range(steps):
@@ -623,25 +632,45 @@
 
     written, done = {}, {}
     second_part(0)
+    second_part(1)
     output()
-    second_part(1)
     norm_back()
     line(0, 0)
+    dpre_halves()
     second_part(2)
     line(1, 0)
+    first_part(3)
     line(0, 1)
-    dpre_halves()
     line(2, 0)
+    first_part(4)
     line(1, 1)
-    first_part(3)
     for step in range(2, steps):
         line(0, step)
-    first_part(4)
+    line(3, 0)
     first_part(5)
-    wave(3)
+    line(2, 1)
+    for step in range(2, steps):
+        line(1, step)
+    write(0)
+    line(4, 0)
+    line(3, 1)
+    for step in range(2, steps):
+        line(2, step)
+    write(1)
+    line(5, 0)
+    line(4, 1)
+    for step in range(2, steps):
+        line(3, step)
+    write(2)
     grad_volume()
-    for at in range(4, 6 + steps):
-        wave(at)
+    line(5, 1)
+    for step in range(2, steps):
+        line(4, step)
+    write(3)
+    write(4)
+    for step in range(2, steps):
+        line(5, step)
+    write(5)
     gain_rows = totals[3][9 * rows : 9 * rows + 2, :rows].astype(F32)
     gain_rows_other = crossed[3][9 * rows : 9 * rows + 2, :rows].astype(F32)
     gain_total = (jnp.sum(gain_rows, axis=0) + jnp.sum(gain_rows_other, axis=0)) * factor

time: 191 us -> 196 us (1.026)
  starting transfers between devices: 65.1 us -> 73.8 us
  local copies, waits for them, and re-layouts: 11.1 us -> 7.06 us
  waiting for transfers between devices: 49.2 us -> 51.6 us
    ppermute x10, starting transfers between devices: 17 us -> 28.1 us  [to_core(): lax.ppermute(x, 'dp', [(i, i ^ 1) for i in range(lax.axis_size('dp'))])]
    ppermute x12, waiting for transfers between devices: 9.81 us -> 18.6 us  [to_partner(): return lax.ppermute(x, 'chan', [(i, i ^ m) for i in range(n)])]
    ppermute x18, waiting for transfers between devices: 37.8 us -> 30.3 us  [line_send(): return lax.ppermute(x, 'dp', pairs)]
    unnamed x38 -> x42, local copies, waits for them, and re-layouts: 11 us -> 6.98 us
    ppermute x18, starting transfers between devices: 36.6 us -> 34.2 us  [line_send(): return lax.ppermute(x, 'dp', pairs)]
  transfers between devices with their start and end apart: 40 -> 40, of which waited for: 9 -> 17; matrix products, arithmetic and copies ran while one was open for 0% -> 0% of each run, Pallas kernels for 26% -> 24%
where the time goes in v6:
time: 196 us; the launch traced here: 195 us
  starting transfers between devices  73.8 us (38%)
  Pallas kernels  60.1 us (31%)
  waiting for transfers between devices  51.6 us (26%)
  local copies, waits for them, and re-layouts  7.06 us (4%)
    ppermute x18, starting transfers between devices, line_send(): return lax.ppermute(x, 'dp', pairs)  34.2 us
    ppermute x18, waiting for transfers between devices, line_send(): return lax.ppermute(x, 'dp', pairs)  30.3 us
    ppermute x10, starting transfers between devices, to_core(): lax.ppermute(x, 'dp', [(i, i ^ 1) for i in range(lax.axis_size('dp'))])  28.1 us
    ppermute x12, waiting for transfers between devices, to_partner(): return lax.ppermute(x, 'chan', [(i, i ^ m) for i in range(n)])  18.6 us
    pallas_call x2, Pallas kernels, conv_full(): pl.pallas_call(functools.partial(conv_kernel, n, sign, transposed), in_sp...  14.2 us
    pallas_call x2, Pallas kernels, spread_shares(): pl.pallas_call(functools.partial(share_kernel, n, sign), in_specs=[smem()...  12.8 us
    pallas_call x6, Pallas kernels, finish(): pl.pallas_call(functools.partial(finish_kernel, n, axis, factor, chunk),...  12.7 us
    ppermute x12, starting transfers between devices, to_partner(): return lax.ppermute(x, 'chan', [(i, i ^ m) for i in range(n)])  11.5 us
  transfers between devices with their start and end apart: 40, of which 17 were waited for; matrix products, arithmetic and copies ran while one was open for 0% of the time, Pallas kernels for 24%

profile of v6, /device:TPU:1, one launch (start us, length us, event | category | flops | bytes accessed | tf_op | source)
XLA Modules:
  0.0 195.4 jit_solution(14387550393395573277)
XLA Ops:
  1.3 7.1 %pre.1 = (bf16[1024,128]{1,0:T(8,128)(2,1)}, bf16[1024,128]{1,0:T(8,128)(2,1)}, bf16[1024,128]{1,0:T(8,128)(2,1)}, bf16[1024,128]{1,0:T(8,128)(2,1)}) custom-call(s32[2]{0:T(128)} %pad_add_fusion.idx, bf16[128,1024]{1,0:T(8,128)(2,1)} %bitcast.15, bf16[3456,512]{1,0:T(8,128)(2,1)} %bitcast.10), custom_call_target="tpu_custom_call" | custom-call | flops 1024 | bytes 1024 | tf_op jit(solution)/shard_map/pre/pallas_call | solution.py:105
  8.5 2.1 %collective-permute-start = (bf16[1024,128]{1,0:T(8,128)(2,1)}, bf16[1024,128]{1,0:T(8,128)(2,1)S(1)}, u32[]{:S(2)}, u32[]{:S(2)}) collective-permute-start(bf16[1024,128]{1,0:T(8,128)(2,1)} %get-tuple-element.41), channel_id=1, source_target_pairs={{0,1},{1,0},{2,3},{3,2},{4,5},{5,4},{6,7},{7,6},{8,9},{9,8},{10,11... | collective-permute-start | bytes 786440 | tf_op jit(solution)/shard_map/ppermute | solution.py:504
  13.1 2.0 %copy-done.4 = bf16[27,512,128]{2,1,0:T(8,128)(2,1)S(1)} copy-done((bf16[27,512,128]{2,1,0:T(8,128)(2,1)S(1)}, bf16[27,512,128]{2,1,0:T(8,128)(2,1)}, u32[]{:S(2)}) %copy-start.4) | copy-done | bytes 3538968
  16.7 5.7 %dact.1 = (bf16[1024,128]{1,0:T(8,128)(2,1)S(1)}, bf16[1024,128]{1,0:T(8,128)(2,1)S(1)}, bf16[1024,128]{1,0:T(8,128)(2,1)S(1)}, bf16[1024,128]{1,0:T(8,128)(2,1)S(1)}) custom-call(s32[2]{0:T(128)S(1)} %copy-done.19, bf16[128,1024]{1,0:T(8,128)(2,1)S(1)} %bitcast.13, bf16[27,512,128]{2,1,0:T(8,128)(2,1)S(1)} %copy-done.4), custom_call_target="tpu_custom_call" | custom-call | flops 1024 | bytes 1024 | tf_op jit(solution)/shard_map/dact/pallas_call | solution.py:105
  28.2 2.7 %collective-permute-done.3.refs_1_ = bf16[1024,128]{1,0:T(8,128)(2,1)S(1)} collective-permute-done((bf16[1024,128]{1,0:T(8,128)(2,1)S(1)}, bf16[1024,128]{1,0:T(8,128)(2,1)S(1)}, u32[]{:S(2)}, u32[]{:S(2)}) %collective-permute-start.3) | collective-permute-done | bytes 262176 | tf_op jit(solution)/shard_map/ppermute | solution.py:504
  30.9 2.1 %collective-permute-done.4.refs_2_ = bf16[1024,128]{1,0:T(8,128)(2,1)S(1)} collective-permute-done((bf16[1024,128]{1,0:T(8,128)(2,1)S(1)}, bf16[1024,128]{1,0:T(8,128)(2,1)S(1)}, u32[]{:S(2)}, u32[]{:S(2)}) %collective-permute-start.4) | collective-permute-done | bytes 262176 | tf_op jit(solution)/shard_map/ppermute | solution.py:504
  33.0 3.7 %collective-permute-done.5.refs_3_ = bf16[1024,128]{1,0:T(8,128)(2,1)S(1)} collective-permute-done((bf16[1024,128]{1,0:T(8,128)(2,1)S(1)}, bf16[1024,128]{1,0:T(8,128)(2,1)S(1)}, u32[]{:S(2)}, u32[]{:S(2)}) %collective-permute-start.5) | collective-permute-done | bytes 262176 | tf_op jit(solution)/shard_map/ppermute | solution.py:504
  37.6 3.8 %collective-permute-start.7 = (bf16[256,1024]{1,0:T(8,128)(2,1)S(1)}, bf16[256,1024]{1,0:T(8,128)(2,1)S(1)}, u32[]{:S(2)}, u32[]{:S(2)}) collective-permute-start(bf16[256,1024]{1,0:T(8,128)(2,1)S(1)} %get-tuple-element.49), channel_id=1, source_target_pairs={{0,4},{4,0},{8,12},{12,8},{16,20},{20,16},{24,28},{28,24},{1,5},{5... | collective-permute-start | bytes 1572872 | tf_op jit(solution)/shard_map/ppermute | solution.py:507
  41.4 1.5 collective-permute-done.7.other
  44.2 3.4 %collective-permute-start.14 = (bf16[9,256,128]{2,1,0:T(8,128)(2,1)S(1)}, bf16[9,256,128]{2,1,0:T(8,128)(2,1)S(1)}, u32[]{:S(2)}, u32[]{:S(2)}) collective-permute-start(bf16[9,256,128]{2,1,0:T(8,128)(2,1)S(1)} %grad_second.3.refs_0_.x), channel_id=1, source_target_pairs={{0,8},{4,12},{24,16},{28,20},{1,9},{5,13},{25,17},{29,21},{2,10},{... | collective-permute-start | bytes 1769480 | tf_op jit(solution)/shard_map/ppermute | solution.py:478
  50.3 1.5 collective-permute-start.15
  51.8 1.5 grad_second.4.refs_4_.x
  53.3 7.1 %output.1 = (bf16[128,1024]{1,0:T(8,128)(2,1)}, f32[8,128]{1,0:T(8,128)S(1)}) custom-call(s32[2]{0:T(128)S(1)} %copy-done.20, bf16[27,512,128]{2,1,0:T(8,128)(2,1)S(1)} %copy-done.5, bf16[1024,128]{1,0:T(8,128)(2,1)S(1)} %get-tuple-element.47._.refs_0_, bf16[1024,128]{1,0:T(8,128)(2,1)S(1)} %collective-permute-done.3.refs_1_, ...), custom_call_target="tpu_custom_call" | custom-call | flops 1024 | bytes 1024 | tf_op jit(solution)/shard_map/output/pallas_call | solution.py:208
  70.8 5.9 %collective-permute-done.13.refs_3_ = bf16[1024,128]{1,0:T(8,128)(2,1)S(1)} collective-permute-done((bf16[1024,128]{1,0:T(8,128)(2,1)S(1)}, bf16[1024,128]{1,0:T(8,128)(2,1)S(1)}, u32[]{:S(2)}, u32[]{:S(2)}) %collective-permute-start.13) | collective-permute-done | bytes 262176 | tf_op jit(solution)/shard_map/ppermute | solution.py:504
  80.0 2.1 %collective-permute-start.16 = (bf16[9,256,128]{2,1,0:T(8,128)(2,1)S(1)}, bf16[9,256,128]{2,1,0:T(8,128)(2,1)}, u32[]{:S(2)}, u32[]{:S(2)}) collective-permute-start(bf16[9,256,128]{2,1,0:T(8,128)(2,1)S(1)} %grad_second.5.refs_0_.x), channel_id=1, source_target_pairs={{0,8},{4,12},{24,16},{28,20},{1,9},{5,13},{25,17},{29,21},{2,10},{... | collective-permute-start | bytes 1769480 | tf_op jit(solution)/shard_map/ppermute | solution.py:478
  82.2 1.5 collective-permute-start.23
  86.3 7.7 %collective-permute-done.16.y = bf16[9,256,128]{2,1,0:T(8,128)(2,1)} collective-permute-done((bf16[9,256,128]{2,1,0:T(8,128)(2,1)S(1)}, bf16[9,256,128]{2,1,0:T(8,128)(2,1)}, u32[]{:S(2)}, u32[]{:S(2)}) %collective-permute-start.16) | collective-permute-done | bytes 589856 | tf_op jit(solution)/shard_map/ppermute | solution.py:478
  95.2 4.5 %collective-permute-start.21 = (bf16[1168,256]{1,0:T(8,128)(2,1)S(1)}, bf16[1168,256]{1,0:T(8,128)(2,1)S(1)}, u32[]{:S(2)}, u32[]{:S(2)}) collective-permute-start(bf16[1168,256]{1,0:T(8,128)(2,1)S(1)} %grad_first.3.refs_0_.x), channel_id=1, source_target_pairs={{0,8},{4,12},{24,16},{28,20},{1,9},{5,13},{25,17},{29,21},{2,10},{... | collective-permute-start | bytes 1794056 | tf_op jit(solution)/shard_map/ppermute | solution.py:478
  99.7 2.3 %copy-done.3 = bf16[2,1152,1024]{2,1,0:T(8,128)(2,1)S(1)} copy-done((bf16[2,1152,1024]{2,1,0:T(8,128)(2,1)S(1)}, bf16[2,1152,1024]{2,1,0:T(8,128)(2,1)}, u32[]{:S(2)}) %copy-start.3) | copy-done | bytes 4718616
  113.5 8.6 %collective-permute-start.33 = (bf16[1168,256]{1,0:T(8,128)(2,1)S(1)}, bf16[1168,256]{1,0:T(8,128)(2,1)S(1)}, u32[]{:S(2)}, u32[]{:S(2)}) collective-permute-start(bf16[1168,256]{1,0:T(8,128)(2,1)S(1)} %grad_first.5.refs_0_.x), channel_id=1, source_target_pairs={{0,8},{4,12},{24,16},{28,20},{1,9},{5,13},{25,17},{29,21},{2,10},{... | collective-permute-start | bytes 1794056 | tf_op jit(solution)/shard_map/ppermute | solution.py:478
  123.1 2.0 %finish_second.3 = (f32[27,512,128]{2,1,0:T(8,128)}, f32[8,128]{1,0:T(8,128)S(1)}) custom-call(s32[2]{0:T(128)S(1)} %copy-done.20, bf16[9,256,128]{2,1,0:T(8,128)(2,1)S(1)} %line_pick.6.refs_0_.own, bf16[9,256,128]{2,1,0:T(8,128)(2,1)S(1)} %collective-permute-done.27.other, bf16[9,256,128]{2,1,0:T(8,128)(2,1)S(1)} %line_pick.7.refs_0_.own), custom_call_target="tpu_custom_call" | custom-call | flops 1024 | bytes 1024 | tf_op jit(solution)/shard_map/finish_second/pallas_call | solution.py:417
  127.3 3.0 %collective-permute-start.30 = (bf16[9,256,128]{2,1,0:T(8,128)(2,1)S(1)}, bf16[9,256,128]{2,1,0:T(8,128)(2,1)S(1)}, u32[]{:S(2)}, u32[]{:S(2)}) collective-permute-start(bf16[9,256,128]{2,1,0:T(8,128)(2,1)S(1)} %line_pick.7.refs_0_.own), channel_id=1, source_target_pairs={{0,4},{4,0},{8,12},{12,8},{16,20},{20,16},{24,28},{28,24},{1,5},{5... | collective-permute-start | bytes 1769480 | tf_op jit(solution)/shard_map/ppermute | solution.py:507
  131.8 9.9 %collective-permute-done.24.y = bf16[9,256,128]{2,1,0:T(8,128)(2,1)S(1)} collective-permute-done((bf16[9,256,128]{2,1,0:T(8,128)(2,1)S(1)}, bf16[9,256,128]{2,1,0:T(8,128)(2,1)S(1)}, u32[]{:S(2)}, u32[]{:S(2)}) %collective-permute-start.24) | collective-permute-done | bytes 589856 | tf_op jit(solution)/shard_map/ppermute | solution.py:478
  142.2 2.0 %finish_second.4 = (f32[27,512,128]{2,1,0:T(8,128)}, f32[8,128]{1,0:T(8,128)S(1)}) custom-call(s32[2]{0:T(128)S(1)} %copy-done.20, bf16[9,256,128]{2,1,0:T(8,128)(2,1)S(1)} %line_pick.7.refs_0_.own, bf16[9,256,128]{2,1,0:T(8,128)(2,1)S(1)} %collective-permute-done.30.other, ...), custom_call_target="tpu_custom_call", output_to_operand_aliasing={{0}: (3, {})} | custom-call | flops 1024 | bytes 1024 | tf_op jit(solution)/shard_map/finish_second/pallas_call | solution.py:417
  146.9 7.3 %collective-permute-start.29 = (bf16[9,256,128]{2,1,0:T(8,128)(2,1)S(1)}, bf16[9,256,128]{2,1,0:T(8,128)(2,1)S(1)}, u32[]{:S(2)}, u32[]{:S(2)}) collective-permute-start(bf16[9,256,128]{2,1,0:T(8,128)(2,1)S(1)} %line_pick.8.refs_1_.own), channel_id=1, source_target_pairs={{0,4},{4,0},{8,12},{12,8},{16,20},{20,16},{24,28},{28,24},{1,5},{5... | collective-permute-start | bytes 1769480 | tf_op jit(solution)/shard_map/ppermute | solution.py:507
  155.1 7.3 %collective-permute-start.38 = (bf16[1168,256]{1,0:T(8,128)(2,1)S(1)}, bf16[1168,256]{1,0:T(8,128)(2,1)S(1)}, u32[]{:S(2)}, u32[]{:S(2)}) collective-permute-start(bf16[1168,256]{1,0:T(8,128)(2,1)S(1)} %line_pick.9.refs_1_.own), channel_id=1, source_target_pairs={{0,4},{4,0},{8,12},{12,8},{16,20},{20,16},{24,28},{28,24},{1,5},{5... | collective-permute-start | bytes 1794056 | tf_op jit(solution)/shard_map/ppermute | solution.py:507
  162.3 2.0 %finish_second.5 = (f32[27,512,128]{2,1,0:T(8,128)}, f32[8,128]{1,0:T(8,128)S(1)}) custom-call(s32[2]{0:T(128)S(1)} %copy-done.20, bf16[9,256,128]{2,1,0:T(8,128)(2,1)S(1)} %line_pick.8.refs_1_.own, bf16[9,256,128]{2,1,0:T(8,128)(2,1)S(1)} %collective-permute-done.29.other, ...), custom_call_target="tpu_custom_call", output_to_operand_aliasing={{0}: (3, {})} | custom-call | flops 1024 | bytes 1024 | tf_op jit(solution)/shard_map/finish_second/pallas_call | solution.py:417
  164.4 7.2 %grad_volume.1 = (bf16[128,1024]{1,0:T(8,128)(2,1)}, f32[8,128]{1,0:T(8,128)S(1)}) custom-call(s32[2]{0:T(128)S(1)} %copy-done.20, bf16[3456,512]{1,0:T(8,128)(2,1)S(1)} %bitcast.11, bf16[1024,128]{1,0:T(8,128)(2,1)S(1)} %copy-done.8, bf16[1024,128]{1,0:T(8,128)(2,1)S(1)} %copy-done.12, bf16[1024,128]{1,0:T(8,128)(2,1)S(1)} %copy-done.14, ...), custom_call_target="tpu_custom_call" | custom-call | flops 1024 | bytes 1024 | tf_op jit(solution)/shard_map/grad_volume/pallas_call | solution.py:208
  173.8 2.0 %finish_first.3 = (f32[27,128,512]{2,1,0:T(8,128)}, f32[8,128]{1,0:T(8,128)S(1)}) custom-call(s32[2]{0:T(128)S(1)} %copy-done.20, bf16[1168,256]{1,0:T(8,128)(2,1)S(1)} %line_pick.9.refs_1_.own, bf16[1168,256]{1,0:T(8,128)(2,1)S(1)} %collective-permute-done.38.other, bf16[1168,256]{1,0:T(8,128)(2,1)S(1)} %line_pick.10.refs_0_.own), custom_call_target="tpu_custom_call" | custom-call | flops 1024 | bytes 1024 | tf_op jit(solution)/shard_map/finish_first/pallas_call | solution.py:417
  175.8 2.0 %finish_first.4 = (f32[27,128,512]{2,1,0:T(8,128)}, f32[8,128]{1,0:T(8,128)S(1)}) custom-call(s32[2]{0:T(128)S(1)} %copy-done.20, bf16[1168,256]{1,0:T(8,128)(2,1)S(1)} %line_pick.10.refs_0_.own, bf16[1168,256]{1,0:T(8,128)(2,1)S(1)} %collective-permute-done.37.other, f32[27,128,512]{2,1,0:T(8,128)} %get-tuple-element.69.refs_0_, ...), custom_call_target="tpu_custom_call", output_to_operand_aliasing={{0}: (3, {})} | custom-call | flops 1024 | bytes 1024 | tf_op jit(solution)/shard_map/finish_first/pallas_call | solution.py:417
  177.8 11.1 %collective-permute-done.35.y = bf16[1168,256]{1,0:T(8,128)(2,1)S(1)} collective-permute-done((bf16[1168,256]{1,0:T(8,128)(2,1)S(1)}, bf16[1168,256]{1,0:T(8,128)(2,1)S(1)}, u32[]{:S(2)}, u32[]{:S(2)}) %collective-permute-start.35) | collective-permute-done | bytes 598048 | tf_op jit(solution)/shard_map/ppermute | solution.py:478
  192.6 2.6 %finish_first.5 = (f32[27,128,512]{2,1,0:T(8,128)}, f32[8,128]{1,0:T(8,128)}) custom-call(s32[2]{0:T(128)S(1)} %copy-done.20, bf16[1168,256]{1,0:T(8,128)(2,1)S(1)} %line_pick.11.own.refs_1_, bf16[1168,256]{1,0:T(8,128)(2,1)S(1)} %collective-permute-done.39.other, f32[27,128,512]{2,1,0:T(8,128)} %get-tuple-element.72.refs_0_, ...), custom_call_target="tpu_custom_call", output_to_operand_aliasing={{0}: (3, {})} | custom-call | flops 1024 | bytes 1024 | tf_op jit(solution)/shard_map/finish_first/pallas_call | solution.py:417
  (136 shorter events, 58.5 us)
Async XLA Ops:
  8.5 14.0 %collective-permute-start = (bf16[1024,128]{1,0:T(8,128)(2,1)}, bf16[1024,128]{1,0:T(8,128)(2,1)S(1)}, u32[]{:S(2)}, u32[]{:S(2)}) collective-permute-start(bf16[1024,128]{1,0:T(8,128)(2,1)} %get-tuple-element.41), channel_id=1, source_target_pairs={{0,1},{1,0},{2,3},{3,2},{4,5},{5,4},{6,7},{7,6},{8,9},{9,8},{10,11... | collective-permute-start | bytes 786440 | tf_op jit(solution)/shard_map/ppermute | solution.py:504
  10.6 11.9 %collective-permute-start.1 = (bf16[1024,128]{1,0:T(8,128)(2,1)}, bf16[1024,128]{1,0:T(8,128)(2,1)S(1)}, u32[]{:S(2)}, u32[]{:S(2)}) collective-permute-start(bf16[1024,128]{1,0:T(8,128)(2,1)} %get-tuple-element.42), channel_id=1, source_target_pairs={{0,2},{1,3},{2,0},{3,1},{4,6},{5,7},{6,4},{7,5},{8,10},{9,11},{10,... | collective-permute-start | bytes 786440 | tf_op jit(solution)/shard_map/ppermute | solution.py:504
  11.8 11.5 %collective-permute-start.2 = (bf16[1024,128]{1,0:T(8,128)(2,1)}, bf16[1024,128]{1,0:T(8,128)(2,1)S(1)}, u32[]{:S(2)}, u32[]{:S(2)}) collective-permute-start(bf16[1024,128]{1,0:T(8,128)(2,1)} %get-tuple-element.43), channel_id=1, source_target_pairs={{0,3},{1,2},{2,1},{3,0},{4,7},{5,6},{6,5},{7,4},{8,11},{9,10},{10,... | collective-permute-start | bytes 786440 | tf_op jit(solution)/shard_map/ppermute | solution.py:504
  11.8 15.7 %collective-permute-start.6 = (bf16[128,1024]{1,0:T(8,128)(2,1)}, bf16[128,1024]{1,0:T(8,128)(2,1)S(1)}, u32[]{:S(2)}, u32[]{:S(2)}) collective-permute-start(bf16[128,1024]{1,0:T(8,128)(2,1)} %bitcast.12), channel_id=1, source_target_pairs={{0,4},{4,0},{8,12},{12,8},{16,20},{20,16},{24,28},{28,24},{1,5},{5... | collective-permute-start | bytes 786440 | tf_op jit(solution)/shard_map/ppermute | solution.py:507
  27.0 9.7 %collective-permute-start.5 = (bf16[1024,128]{1,0:T(8,128)(2,1)S(1)}, bf16[1024,128]{1,0:T(8,128)(2,1)S(1)}, u32[]{:S(2)}, u32[]{:S(2)}) collective-permute-start(bf16[1024,128]{1,0:T(8,128)(2,1)S(1)} %get-tuple-element.47._.refs_0_), channel_id=1, source_target_pairs={{0,3},{1,2},{2,1},{3,0},{4,7},{5,6},{6,5},{7,4},{8,11},{9,10},{10,... | collective-permute-start | bytes 786440 | tf_op jit(solution)/shard_map/ppermute | solution.py:504
  44.2 24.4 %collective-permute-start.14 = (bf16[9,256,128]{2,1,0:T(8,128)(2,1)S(1)}, bf16[9,256,128]{2,1,0:T(8,128)(2,1)S(1)}, u32[]{:S(2)}, u32[]{:S(2)}) collective-permute-start(bf16[9,256,128]{2,1,0:T(8,128)(2,1)S(1)} %grad_second.3.refs_0_.x), channel_id=1, source_target_pairs={{0,8},{4,12},{24,16},{28,20},{1,9},{5,13},{25,17},{29,21},{2,10},{... | collective-permute-start | bytes 1769480 | tf_op jit(solution)/shard_map/ppermute | solution.py:478
  47.6 12.8 %collective-permute-start.10 = (bf16[1024,128]{1,0:T(8,128)(2,1)S(1)}, bf16[1024,128]{1,0:T(8,128)(2,1)S(1)}, u32[]{:S(2)}, u32[]{:S(2)}) collective-permute-start(bf16[1024,128]{1,0:T(8,128)(2,1)S(1)} %get-tuple-element.56), channel_id=1, source_target_pairs={{0,3},{1,2},{2,1},{3,0},{4,7},{5,6},{6,5},{7,4},{8,11},{9,10},{10,... | collective-permute-start | bytes 786440 | tf_op jit(solution)/shard_map/ppermute | solution.py:504
  48.6 12.5 %collective-permute-start.8 = (bf16[1024,128]{1,0:T(8,128)(2,1)S(1)}, bf16[1024,128]{1,0:T(8,128)(2,1)S(1)}, u32[]{:S(2)}, u32[]{:S(2)}) collective-permute-start(bf16[1024,128]{1,0:T(8,128)(2,1)S(1)} %get-tuple-element.54), channel_id=1, source_target_pairs={{0,1},{1,0},{2,3},{3,2},{4,5},{5,4},{6,7},{7,6},{8,9},{9,8},{10,11... | collective-permute-start | bytes 786440 | tf_op jit(solution)/shard_map/ppermute | solution.py:504
  49.7 12.7 %collective-permute-start.9 = (bf16[1024,128]{1,0:T(8,128)(2,1)S(1)}, bf16[1024,128]{1,0:T(8,128)(2,1)S(1)}, u32[]{:S(2)}, u32[]{:S(2)}) collective-permute-start(bf16[1024,128]{1,0:T(8,128)(2,1)S(1)} %get-tuple-element.55), channel_id=1, source_target_pairs={{0,2},{1,3},{2,0},{3,1},{4,6},{5,7},{6,4},{7,5},{8,10},{9,11},{10,... | collective-permute-start | bytes 786440 | tf_op jit(solution)/shard_map/ppermute | solution.py:504
  50.3 15.5 %collective-permute-start.15 = (bf16[128,1024]{1,0:T(8,128)(2,1)S(1)}, bf16[128,1024]{1,0:T(8,128)(2,1)S(1)}, u32[]{:S(2)}, u32[]{:S(2)}) collective-permute-start(bf16[128,1024]{1,0:T(8,128)(2,1)S(1)} %bitcast.16), channel_id=1, source_target_pairs={{0,4},{4,0},{8,12},{12,8},{16,20},{20,16},{24,28},{28,24},{1,5},{5... | collective-permute-start | bytes 786440 | tf_op jit(solution)/shard_map/ppermute | solution.py:507
  64.3 12.4 %collective-permute-start.13 = (bf16[1024,128]{1,0:T(8,128)(2,1)S(1)}, bf16[1024,128]{1,0:T(8,128)(2,1)S(1)}, u32[]{:S(2)}, u32[]{:S(2)}) collective-permute-start(bf16[1024,128]{1,0:T(8,128)(2,1)S(1)} %get-tuple-element.58._.refs_0_), channel_id=1, source_target_pairs={{0,3},{1,2},{2,1},{3,0},{4,7},{5,6},{6,5},{7,4},{8,11},{9,10},{10,... | collective-permute-start | bytes 786440 | tf_op jit(solution)/shard_map/ppermute | solution.py:504
  65.8 16.3 %collective-permute-start.19 = (bf16[9,256,128]{2,1,0:T(8,128)(2,1)S(1)}, bf16[9,256,128]{2,1,0:T(8,128)(2,1)S(1)}, u32[]{:S(2)}, u32[]{:S(2)}) collective-permute-start(bf16[9,256,128]{2,1,0:T(8,128)(2,1)S(1)} %grad_second.4.refs_4_.x), channel_id=1, source_target_pairs={{0,8},{4,12},{24,16},{28,20},{1,9},{5,13},{25,17},{29,21},{2,10},{... | collective-permute-start | bytes 1769480 | tf_op jit(solution)/shard_map/ppermute | solution.py:478
  68.7 16.2 %collective-permute-start.17 = (bf16[9,256,128]{2,1,0:T(8,128)(2,1)S(1)}, bf16[9,256,128]{2,1,0:T(8,128)(2,1)S(1)}, u32[]{:S(2)}, u32[]{:S(2)}) collective-permute-start(bf16[9,256,128]{2,1,0:T(8,128)(2,1)S(1)} %line_add.12.refs_4_.x), channel_id=1, source_target_pairs={{8,16},{12,20},{16,8},{20,12},{9,17},{13,21},{17,9},{21,13},{10,18... | collective-permute-start | bytes 1769480 | tf_op jit(solution)/shard_map/ppermute | solution.py:478
  80.0 14.1 %collective-permute-start.16 = (bf16[9,256,128]{2,1,0:T(8,128)(2,1)S(1)}, bf16[9,256,128]{2,1,0:T(8,128)(2,1)}, u32[]{:S(2)}, u32[]{:S(2)}) collective-permute-start(bf16[9,256,128]{2,1,0:T(8,128)(2,1)S(1)} %grad_second.5.refs_0_.x), channel_id=1, source_target_pairs={{0,8},{4,12},{24,16},{28,20},{1,9},{5,13},{25,17},{29,21},{2,10},{... | collective-permute-start | bytes 1769480 | tf_op jit(solution)/shard_map/ppermute | solution.py:478
  82.2 23.3 %collective-permute-start.23 = (bf16[9,256,128]{2,1,0:T(8,128)(2,1)S(1)}, bf16[9,256,128]{2,1,0:T(8,128)(2,1)}, u32[]{:S(2)}, u32[]{:S(2)}) collective-permute-start(bf16[9,256,128]{2,1,0:T(8,128)(2,1)S(1)} %line_add.13.refs_0_.x), channel_id=1, source_target_pairs={{8,16},{12,20},{16,8},{20,12},{9,17},{13,21},{17,9},{21,13},{10,18... | collective-permute-start | bytes 1769480 | tf_op jit(solution)/shard_map/ppermute | solution.py:478
  85.0 23.1 %collective-permute-start.22 = (bf16[9,256,128]{2,1,0:T(8,128)(2,1)S(1)}, bf16[9,256,128]{2,1,0:T(8,128)(2,1)}, u32[]{:S(2)}, u32[]{:S(2)}) collective-permute-start(bf16[9,256,128]{2,1,0:T(8,128)(2,1)S(1)} %line_add.14.refs_0_.x), channel_id=1, source_target_pairs={{8,0},{12,4},{16,24},{20,28},{9,1},{13,5},{17,25},{21,29},{10,2},{... | collective-permute-start | bytes 1769480 | tf_op jit(solution)/shard_map/ppermute | solution.py:478
  95.2 16.3 %collective-permute-start.21 = (bf16[1168,256]{1,0:T(8,128)(2,1)S(1)}, bf16[1168,256]{1,0:T(8,128)(2,1)S(1)}, u32[]{:S(2)}, u32[]{:S(2)}) collective-permute-start(bf16[1168,256]{1,0:T(8,128)(2,1)S(1)} %grad_first.3.refs_0_.x), channel_id=1, source_target_pairs={{0,8},{4,12},{24,16},{28,20},{1,9},{5,13},{25,17},{29,21},{2,10},{... | collective-permute-start | bytes 1794056 | tf_op jit(solution)/shard_map/ppermute | solution.py:478
  103.5 21.6 %collective-permute-start.26 = (bf16[1168,256]{1,0:T(8,128)(2,1)S(1)}, bf16[1168,256]{1,0:T(8,128)(2,1)S(1)}, u32[]{:S(2)}, u32[]{:S(2)}) collective-permute-start(bf16[1168,256]{1,0:T(8,128)(2,1)S(1)} %grad_first.4.refs_0_.x), channel_id=1, source_target_pairs={{0,8},{4,12},{24,16},{28,20},{1,9},{5,13},{25,17},{29,21},{2,10},{... | collective-permute-start | bytes 1794056 | tf_op jit(solution)/shard_map/ppermute | solution.py:478
  104.9 8.6 %collective-permute-start.20 = (bf16[9,256,128]{2,1,0:T(8,128)(2,1)S(1)}, bf16[9,256,128]{2,1,0:T(8,128)(2,1)S(1)}, u32[]{:S(2)}, u32[]{:S(2)}) collective-permute-start(bf16[9,256,128]{2,1,0:T(8,128)(2,1)S(1)} %line_add.15.refs_0_.x), channel_id=1, source_target_pairs={{8,16},{12,20},{16,8},{20,12},{9,17},{13,21},{17,9},{21,13},{10,18... | collective-permute-start | bytes 1769480 | tf_op jit(solution)/shard_map/ppermute | solution.py:478
  106.8 15.7 %collective-permute-start.28 = (bf16[9,256,128]{2,1,0:T(8,128)(2,1)S(1)}, bf16[9,256,128]{2,1,0:T(8,128)(2,1)S(1)}, u32[]{:S(2)}, u32[]{:S(2)}) collective-permute-start(bf16[9,256,128]{2,1,0:T(8,128)(2,1)S(1)} %line_add.16.refs_0_.x), channel_id=1, source_target_pairs={{8,0},{12,4},{16,24},{20,28},{9,1},{13,5},{17,25},{21,29},{10,2},{... | collective-permute-start | bytes 1769480 | tf_op jit(solution)/shard_map/ppermute | solution.py:478
  109.2 13.8 %collective-permute-start.27 = (bf16[9,256,128]{2,1,0:T(8,128)(2,1)S(1)}, bf16[9,256,128]{2,1,0:T(8,128)(2,1)S(1)}, u32[]{:S(2)}, u32[]{:S(2)}) collective-permute-start(bf16[9,256,128]{2,1,0:T(8,128)(2,1)S(1)} %line_pick.6.refs_0_.own), channel_id=1, source_target_pairs={{0,4},{4,0},{8,12},{12,8},{16,20},{20,16},{24,28},{28,24},{1,5},{5... | collective-permute-start | bytes 1769480 | tf_op jit(solution)/shard_map/ppermute | solution.py:507
  111.7 18.6 %collective-permute-start.25 = (bf16[1168,256]{1,0:T(8,128)(2,1)S(1)}, bf16[1168,256]{1,0:T(8,128)(2,1)S(1)}, u32[]{:S(2)}, u32[]{:S(2)}) collective-permute-start(bf16[1168,256]{1,0:T(8,128)(2,1)S(1)} %line_add.17.refs_0_.x), channel_id=1, source_target_pairs={{8,16},{12,20},{16,8},{20,12},{9,17},{13,21},{17,9},{21,13},{10,18... | collective-permute-start | bytes 1794056 | tf_op jit(solution)/shard_map/ppermute | solution.py:478
  113.5 30.8 %collective-permute-start.33 = (bf16[1168,256]{1,0:T(8,128)(2,1)S(1)}, bf16[1168,256]{1,0:T(8,128)(2,1)S(1)}, u32[]{:S(2)}, u32[]{:S(2)}) collective-permute-start(bf16[1168,256]{1,0:T(8,128)(2,1)S(1)} %grad_first.5.refs_0_.x), channel_id=1, source_target_pairs={{0,8},{4,12},{24,16},{28,20},{1,9},{5,13},{25,17},{29,21},{2,10},{... | collective-permute-start | bytes 1794056 | tf_op jit(solution)/shard_map/ppermute | solution.py:478
  125.3 20.1 %collective-permute-start.32 = (bf16[1168,256]{1,0:T(8,128)(2,1)S(1)}, bf16[1168,256]{1,0:T(8,128)(2,1)S(1)}, u32[]{:S(2)}, u32[]{:S(2)}) collective-permute-start(bf16[1168,256]{1,0:T(8,128)(2,1)S(1)} %line_add.19.refs_0_.x), channel_id=1, source_target_pairs={{8,16},{12,20},{16,8},{20,12},{9,17},{13,21},{17,9},{21,13},{10,18... | collective-permute-start | bytes 1794056 | tf_op jit(solution)/shard_map/ppermute | solution.py:478
  126.0 15.7 %collective-permute-start.24 = (bf16[9,256,128]{2,1,0:T(8,128)(2,1)S(1)}, bf16[9,256,128]{2,1,0:T(8,128)(2,1)S(1)}, u32[]{:S(2)}, u32[]{:S(2)}) collective-permute-start(bf16[9,256,128]{2,1,0:T(8,128)(2,1)S(1)} %line_add.18.refs_0_.x), channel_id=1, source_target_pairs={{8,0},{12,4},{16,24},{20,28},{9,1},{13,5},{17,25},{21,29},{10,2},{... | collective-permute-start | bytes 1769480 | tf_op jit(solution)/shard_map/ppermute | solution.py:478
  127.3 15.0 %collective-permute-start.30 = (bf16[9,256,128]{2,1,0:T(8,128)(2,1)S(1)}, bf16[9,256,128]{2,1,0:T(8,128)(2,1)S(1)}, u32[]{:S(2)}, u32[]{:S(2)}) collective-permute-start(bf16[9,256,128]{2,1,0:T(8,128)(2,1)S(1)} %line_pick.7.refs_0_.own), channel_id=1, source_target_pairs={{0,4},{4,0},{8,12},{12,8},{16,20},{20,16},{24,28},{28,24},{1,5},{5... | collective-permute-start | bytes 1769480 | tf_op jit(solution)/shard_map/ppermute | solution.py:507
  130.5 24.0 %collective-permute-start.31 = (bf16[1168,256]{1,0:T(8,128)(2,1)S(1)}, bf16[1168,256]{1,0:T(8,128)(2,1)S(1)}, u32[]{:S(2)}, u32[]{:S(2)}) collective-permute-start(bf16[1168,256]{1,0:T(8,128)(2,1)S(1)} %line_add.20.refs_0_.x), channel_id=1, source_target_pairs={{8,0},{12,4},{16,24},{20,28},{9,1},{13,5},{17,25},{21,29},{10,2},{... | collective-permute-start | bytes 1794056 | tf_op jit(solution)/shard_map/ppermute | solution.py:478
  144.5 27.1 %collective-permute-start.34 = (bf16[1168,256]{1,0:T(8,128)(2,1)S(1)}, bf16[1168,256]{1,0:T(8,128)(2,1)S(1)}, u32[]{:S(2)}, u32[]{:S(2)}) collective-permute-start(bf16[1168,256]{1,0:T(8,128)(2,1)S(1)} %line_add.21.refs_0_.x), channel_id=1, source_target_pairs={{8,16},{12,20},{16,8},{20,12},{9,17},{13,21},{17,9},{21,13},{10,18... | collective-permute-start | bytes 1794056 | tf_op jit(solution)/shard_map/ppermute | solution.py:478
  145.5 26.3 %collective-permute-start.36 = (bf16[1168,256]{1,0:T(8,128)(2,1)S(1)}, bf16[1168,256]{1,0:T(8,128)(2,1)S(1)}, u32[]{:S(2)}, u32[]{:S(2)}) collective-permute-start(bf16[1168,256]{1,0:T(8,128)(2,1)S(1)} %line_add.22.refs_0_.x), channel_id=1, source_target_pairs={{8,0},{12,4},{16,24},{20,28},{9,1},{13,5},{17,25},{21,29},{10,2},{... | collective-permute-start | bytes 1794056 | tf_op jit(solution)/shard_map/ppermute | solution.py:478
  146.9 15.4 %collective-permute-start.29 = (bf16[9,256,128]{2,1,0:T(8,128)(2,1)S(1)}, bf16[9,256,128]{2,1,0:T(8,128)(2,1)S(1)}, u32[]{:S(2)}, u32[]{:S(2)}) collective-permute-start(bf16[9,256,128]{2,1,0:T(8,128)(2,1)S(1)} %line_pick.8.refs_1_.own), channel_id=1, source_target_pairs={{0,4},{4,0},{8,12},{12,8},{16,20},{20,16},{24,28},{28,24},{1,5},{5... | collective-permute-start | bytes 1769480 | tf_op jit(solution)/shard_map/ppermute | solution.py:507
  155.1 18.7 %collective-permute-start.38 = (bf16[1168,256]{1,0:T(8,128)(2,1)S(1)}, bf16[1168,256]{1,0:T(8,128)(2,1)S(1)}, u32[]{:S(2)}, u32[]{:S(2)}) collective-permute-start(bf16[1168,256]{1,0:T(8,128)(2,1)S(1)} %line_pick.9.refs_1_.own), channel_id=1, source_target_pairs={{0,4},{4,0},{8,12},{12,8},{16,20},{20,16},{24,28},{28,24},{1,5},{5... | collective-permute-start | bytes 1794056 | tf_op jit(solution)/shard_map/ppermute | solution.py:507
  172.5 16.5 %collective-permute-start.35 = (bf16[1168,256]{1,0:T(8,128)(2,1)S(1)}, bf16[1168,256]{1,0:T(8,128)(2,1)S(1)}, u32[]{:S(2)}, u32[]{:S(2)}) collective-permute-start(bf16[1168,256]{1,0:T(8,128)(2,1)S(1)} %line_add.23.refs_0_.x), channel_id=1, source_target_pairs={{8,0},{12,4},{16,24},{20,28},{9,1},{13,5},{17,25},{21,29},{10,2},{... | collective-permute-start | bytes 1794056 | tf_op jit(solution)/shard_map/ppermute | solution.py:478
  (29 other events, 387.0 us)

commit v7 on v6

--- a/solution.py
+++ b/solution.py
@@ -15,7 +15,7 @@
 NORM_EPS = 1e-05
 LIMIT = 16 * 1024 * 1024
 SMALL = 8 * 1024 * 1024
-LARGE = 61 * 1024 * 1024
+LARGE = 59 * 1024 * 1024
 EXTRA = 16
 F32, BF16 = jnp.float32, jnp.bfloat16
 NT = (((1,), (1,)), ((), ()))
@@ -269,21 +269,6 @@
     )(idx, *blocks, *after)
 
 
-def moved_first_kernel(own, other, _, out):
-    for which, ref in enumerate((own, other)):
-        cells = ref[...].astype(F32)
-        at = lax.broadcasted_iota(jnp.int32, cells.shape, 1)
-        height_at, width_at = at // WIDTH % HEIGHT, at % WIDTH
-        rows = cells.shape[0]
-        for k in range(9):
-            b, c = k // 3 - 1, k % 3 - 1
-            off = b * WIDTH + c
-            part = cells if off == 0 else pltpu.roll(cells, (-off) % CELLS, 1)
-            inside = (height_at + b >= 0) & (height_at + b < HEIGHT)
-            inside = inside & (width_at + c >= 0) & (width_at + c < WIDTH)
-            out[which, k * rows : (k + 1) * rows] = jnp.where(inside, part, 0.0).astype(BF16)
-
-
 def moved_second_kernel(own, other, _, out):
     out[...] = jnp.zeros_like(out)
     for which, ref in enumerate((own, other)):
@@ -316,36 +301,53 @@
     return jnp.concatenate([high.astype(F32), low.astype(F32), empty], axis=0).astype(BF16)
 
 
-def grad_first_kernel(a, moved, own, other, gain_part, *refs):
-    out = refs[-1]
+def moved_lanes(cells, b, c):
+    off = b * WIDTH + c
+    if off == 0:
+        return cells.astype(BF16)
+    at = lax.broadcasted_iota(jnp.int32, cells.shape, 1)
+    height_at, width_at = at // WIDTH % HEIGHT, at % WIDTH
+    inside = (height_at + b >= 0) & (height_at + b < HEIGHT)
+    inside = inside & (width_at + c >= 0) & (width_at + c < WIDTH)
+    return jnp.where(inside, pltpu.roll(cells, (-off) % CELLS, 1), 0.0).astype(BF16)
+
+
+def grad_first_kernel(vol_own, vol_other, own, other, gain_part, *refs):
+    outs, moved = refs[-4:-1], refs[-1]
     half, rows = own.shape[0], own.shape[2]
-    begin, count = max(0, -a) * PLANE, (DEPTH - abs(a)) * PLANE
-    rhs = [
-        jnp.concatenate([ref[j, begin : begin + count] for j in range(half)], axis=1)
-        for ref in (own, other)
-    ]
+    fields = [ref[...].astype(F32) for ref in (vol_own, vol_other)]
+    rhs = [jnp.concatenate([ref[j] for j in range(half)], axis=1) for ref in (own, other)]
     for b in range(3):
-        span = slice(3 * rows * b, 3 * rows * (b + 1))
-        grads = None
         for which in range(2):
-            lhs = moved[which, span, begin + a * PLANE : begin + a * PLANE + count]
-            part = jnp.dot(lhs, rhs[which], preferred_element_type=F32)
-            grads = part if grads is None else grads + part
-        out[span] = grads.astype(BF16)
-    filler = jnp.zeros((1, out.shape[1] - rows), F32)
-    out[9 * rows :] = split_rows(jnp.concatenate([gain_part[...], filler], axis=1))
-
-
-def grad_first(a, moved, own, other, gain_part, after):
+            for c in range(3):
+                moved[which, c * rows : (c + 1) * rows] = moved_lanes(fields[which], b - 1, c - 1)
+        for a in (-1, 0, 1):
+            begin, count = max(0, -a) * PLANE, (DEPTH - abs(a)) * PLANE
+            shift = begin + a * PLANE
+            grads = None
+            for which in range(2):
+                lhs = moved[which, :, shift : shift + count]
+                part = jnp.dot(lhs, rhs[which][begin : begin + count], preferred_element_type=F32)
+                grads = part if grads is None else grads + part
+            outs[a + 1][3 * rows * b : 3 * rows * (b + 1)] = grads.astype(BF16)
+    filler = jnp.zeros((1, half * rows - rows), F32)
+    outs[0][9 * rows :] = split_rows(jnp.concatenate([gain_part[...], filler], axis=1))
+    for out in outs[1:]:
+        out[9 * rows :] = jnp.zeros((EXTRA, half * rows), BF16)
+
+
+def grad_first(vol_own, vol_other, own, other, gain_part, after):
     half, cells, rows = own.shape
     return pl.pallas_call(
-        functools.partial(grad_first_kernel, a),
-        in_specs=[pl.BlockSpec(memory_space=pltpu.VMEM)] * 4 + [UNREAD] * len(after),
-        out_shape=jax.ShapeDtypeStruct((9 * rows + EXTRA, half * rows), BF16),
+        grad_first_kernel,
+        in_specs=[pl.BlockSpec(memory_space=pltpu.VMEM)] * 5 + [UNREAD] * len(after),
+        out_specs=[pl.BlockSpec(memory_space=pltpu.VMEM)] * 3,
+        out_shape=[jax.ShapeDtypeStruct((9 * rows + EXTRA, half * rows), BF16)] * 3,
+        scratch_shapes=[pltpu.VMEM((2, 3 * rows, CELLS), BF16)],
         compiler_params=pltpu.CompilerParams(vmem_limit_bytes=LIMIT),
         cost_estimate=LIGHT,
         name="grad_first",
-    )(moved, own, other, gain_part, *after)
+    )(vol_own, vol_other, own, other, gain_part, *after)
 
 
 def grad_second_kernel(a, moved, own, other, *refs):
@@ -540,7 +542,7 @@
         act,
     )
     vol_other = to_core(vol)
-    act_keep, act_send = halves("act_halves", True, idx, act_blocks, (moved_cot,))
+    act_keep, act_send = halves("act_halves", True, idx, act_blocks, (moved_cot, vol_other))
     act_other = to_core(act_send)
 
     sums, outward = line_moves(lax.axis_size("dp") // 2)
@@ -580,11 +582,13 @@
         parts[chunk] = grad_second(chunk - 1, moved_cot, act_keep, act_other, last)
         last = (parts[chunk],)
 
-    def first_part(chunk):
+    def first_parts():
         nonlocal last
         own, other = done["dpre_halves"]
-        parts[chunk] = grad_first(chunk - 4, done["moved"], own, other, done["gain"], last)
-        last = (parts[chunk],)
+        parts[3], parts[4], parts[5] = grad_first(
+            vol, vol_other, own, other, done["gain"], last
+        )
+        last = (parts[3],)
 
     def norm_back():
         nonlocal last
@@ -600,10 +604,7 @@
             name="norm_back",
         )(own_gain, normed, inverse, *dact_shares, *last)
         done["dpre"] = swap([dpre] * n)
-        done["moved"] = moved_fields(
-            moved_first_kernel, "moved_first", (2, 9 * rows, CELLS), vol, vol_other, dpre
-        )
-        last = (done["moved"],)
+        last = (dpre,)
 
     def dpre_halves():
         nonlocal last
@@ -636,41 +637,18 @@
     output()
     norm_back()
     line(0, 0)
-    dpre_halves()
     second_part(2)
     line(1, 0)
-    first_part(3)
     line(0, 1)
-    line(2, 0)
-    first_part(4)
-    line(1, 1)
-    for step in range(2, steps):
-        line(0, step)
-    line(3, 0)
-    first_part(5)
-    line(2, 1)
-    for step in range(2, steps):
-        line(1, step)
-    write(0)
-    line(4, 0)
-    line(3, 1)
-    for step in range(2, steps):
-        line(2, step)
-    write(1)
-    line(5, 0)
-    line(4, 1)
-    for step in range(2, steps):
-        line(3, step)
-    write(2)
+    dpre_halves()
+    first_parts()
+    wave(2)
+    wave(3)
+    wave(4)
+    wave(5)
     grad_volume()
-    line(5, 1)
-    for step in range(2, steps):
-        line(4, step)
-    write(3)
-    write(4)
-    for step in range(2, steps):
-        line(5, step)
-    write(5)
+    for at in range(6, 6 + steps):
+        wave(at)
     gain_rows = totals[3][9 * rows : 9 * rows + 2, :rows].astype(F32)
     gain_rows_other = crossed[3][9 * rows : 9 * rows + 2, :rows].astype(F32)
     gain_total = (jnp.sum(gain_rows, axis=0) + jnp.sum(gain_rows_other, axis=0)) * factor

time: 196 us -> 180 us (0.918)
  starting transfers between devices: 73.8 us -> 66.7 us
  waiting for transfers between devices: 51.6 us -> 44.9 us
  local copies, waits for them, and re-layouts: 7.06 us -> 4.71 us
    ppermute x10, starting transfers between devices: 28.1 us -> 16.4 us  [to_core(): lax.ppermute(x, 'dp', [(i, i ^ 1) for i in range(lax.axis_size('dp'))])]
    ppermute x12, waiting for transfers between devices: 18.6 us -> 12.9 us  [to_partner(): return lax.ppermute(x, 'chan', [(i, i ^ m) for i in range(n)])]
    ppermute x18, starting transfers between devices: 34.2 us -> 38.9 us  [line_send(): return lax.ppermute(x, 'dp', pairs)]
    unnamed x42 -> x28, local copies, waits for them, and re-layouts: 6.98 us -> 4.63 us
    pallas_call x3 -> x1, Pallas kernels: 3.6 us -> 4.44 us  [grad_first(): pl.pallas_call(grad_first_kernel, in_specs=[pl.BlockSpec(memory_space=plt...]
  transfers between devices with their start and end apart: 40 -> 40, of which waited for: 17 -> 11; matrix products, arithmetic and copies ran while one was open for 0% -> 0% of each run, Pallas kernels for 24% -> 27%
where the time goes in v7:
time: 180 us
  starting transfers between devices  66.7 us (37%)
  Pallas kernels  60.5 us (34%)
  waiting for transfers between devices  44.9 us (25%)
  local copies, waits for them, and re-layouts  4.71 us (3%)
    ppermute x18, starting transfers between devices, line_send(): return lax.ppermute(x, 'dp', pairs)  38.9 us
    ppermute x18, waiting for transfers between devices, line_send(): return lax.ppermute(x, 'dp', pairs)  30.4 us
    ppermute x10, starting transfers between devices, to_core(): lax.ppermute(x, 'dp', [(i, i ^ 1) for i in range(lax.axis_size('dp'))])  16.4 us
    pallas_call x2, Pallas kernels, conv_full(): pl.pallas_call(functools.partial(conv_kernel, n, sign, transposed), in_sp...  14.2 us
    ppermute x12, waiting for transfers between devices, to_partner(): return lax.ppermute(x, 'chan', [(i, i ^ m) for i in range(n)])  12.9 us
    pallas_call x2, Pallas kernels, spread_shares(): pl.pallas_call(functools.partial(share_kernel, n, sign), in_specs=[smem()...  12.8 us
    pallas_call x6, Pallas kernels, finish(): pl.pallas_call(functools.partial(finish_kernel, n, axis, factor, chunk),...  12.7 us
    ppermute x12, starting transfers between devices, to_partner(): return lax.ppermute(x, 'chan', [(i, i ^ m) for i in range(n)])  11.5 us
  transfers between devices with their start and end apart: 40, of which 11 were waited for; matrix products, arithmetic and copies ran while one was open for 0% of the time, Pallas kernels for 27%

profile of v7, /device:TPU:1, one launch (start us, length us, event | category | flops | bytes accessed | tf_op | source)
XLA Modules:
  0.0 179.6 jit_solution(3896921356186290378)
XLA Ops:
  1.3 7.1 %pre.1 = (bf16[1024,128]{1,0:T(8,128)(2,1)}, bf16[1024,128]{1,0:T(8,128)(2,1)}, bf16[1024,128]{1,0:T(8,128)(2,1)}, bf16[1024,128]{1,0:T(8,128)(2,1)}) custom-call(s32[2]{0:T(128)} %pad_add_fusion.idx, bf16[128,1024]{1,0:T(8,128)(2,1)} %bitcast.15, bf16[3456,512]{1,0:T(8,128)(2,1)} %bitcast.10), custom_call_target="tpu_custom_call" | custom-call | flops 1024 | bytes 1024 | tf_op jit(solution)/shard_map/pre/pallas_call | solution.py:105
  8.5 2.1 %collective-permute-start = (bf16[1024,128]{1,0:T(8,128)(2,1)}, bf16[1024,128]{1,0:T(8,128)(2,1)S(1)}, u32[]{:S(2)}, u32[]{:S(2)}) collective-permute-start(bf16[1024,128]{1,0:T(8,128)(2,1)} %get-tuple-element.44), channel_id=1, source_target_pairs={{0,1},{1,0},{2,3},{3,2},{4,5},{5,4},{6,7},{7,6},{8,9},{9,8},{10,11... | collective-permute-start | bytes 786440 | tf_op jit(solution)/shard_map/ppermute | solution.py:506
  13.1 2.0 %copy-done.1 = bf16[27,512,128]{2,1,0:T(8,128)(2,1)S(1)} copy-done((bf16[27,512,128]{2,1,0:T(8,128)(2,1)S(1)}, bf16[27,512,128]{2,1,0:T(8,128)(2,1)}, u32[]{:S(2)}) %copy-start.1) | copy-done | bytes 3538968
  16.7 5.7 %dact.1 = (bf16[1024,128]{1,0:T(8,128)(2,1)S(1)}, bf16[1024,128]{1,0:T(8,128)(2,1)S(1)}, bf16[1024,128]{1,0:T(8,128)(2,1)S(1)}, bf16[1024,128]{1,0:T(8,128)(2,1)S(1)}) custom-call(s32[2]{0:T(128)S(1)} %copy-done.12, bf16[128,1024]{1,0:T(8,128)(2,1)S(1)} %bitcast.13, bf16[27,512,128]{2,1,0:T(8,128)(2,1)S(1)} %copy-done.1), custom_call_target="tpu_custom_call" | custom-call | flops 1024 | bytes 1024 | tf_op jit(solution)/shard_map/dact/pallas_call | solution.py:105
  24.9 1.8 %collective-permute-start.5 = (bf16[1024,128]{1,0:T(8,128)(2,1)S(1)}, bf16[1024,128]{1,0:T(8,128)(2,1)S(1)}, u32[]{:S(2)}, u32[]{:S(2)}) collective-permute-start(bf16[1024,128]{1,0:T(8,128)(2,1)S(1)} %get-tuple-element.50._.refs_0_), channel_id=1, source_target_pairs={{0,3},{1,2},{2,1},{3,0},{4,7},{5,6},{6,5},{7,4},{8,11},{9,10},{10,... | collective-permute-start | bytes 786440 | tf_op jit(solution)/shard_map/ppermute | solution.py:506
  28.3 3.7 %collective-permute-done.5.refs_3_ = bf16[1024,128]{1,0:T(8,128)(2,1)S(1)} collective-permute-done((bf16[1024,128]{1,0:T(8,128)(2,1)S(1)}, bf16[1024,128]{1,0:T(8,128)(2,1)S(1)}, u32[]{:S(2)}, u32[]{:S(2)}) %collective-permute-start.5) | collective-permute-done | bytes 262176 | tf_op jit(solution)/shard_map/ppermute | solution.py:506
  31.9 7.8 %collective-permute-done.4.refs_2_ = bf16[1024,128]{1,0:T(8,128)(2,1)S(1)} collective-permute-done((bf16[1024,128]{1,0:T(8,128)(2,1)S(1)}, bf16[1024,128]{1,0:T(8,128)(2,1)S(1)}, u32[]{:S(2)}, u32[]{:S(2)}) %collective-permute-start.4) | collective-permute-done | bytes 262176 | tf_op jit(solution)/shard_map/ppermute | solution.py:506
  41.2 1.5 collective-permute-done.8.other
  43.9 3.2 %collective-permute-start.15 = (bf16[9,256,128]{2,1,0:T(8,128)(2,1)S(1)}, bf16[9,256,128]{2,1,0:T(8,128)(2,1)S(1)}, u32[]{:S(2)}, u32[]{:S(2)}) collective-permute-start(bf16[9,256,128]{2,1,0:T(8,128)(2,1)S(1)} %grad_second.3.refs_0_.x), channel_id=1, source_target_pairs={{0,8},{4,12},{24,16},{28,20},{1,9},{5,13},{25,17},{29,21},{2,10},{... | collective-permute-start | bytes 1769480 | tf_op jit(solution)/shard_map/ppermute | solution.py:480
  49.9 1.5 grad_second.4.refs_4_.x
  51.4 1.5 collective-permute-start.18
  52.9 7.0 %output.1 = (bf16[128,1024]{1,0:T(8,128)(2,1)}, f32[8,128]{1,0:T(8,128)S(1)}) custom-call(s32[2]{0:T(128)S(1)} %copy-done.13, bf16[27,512,128]{2,1,0:T(8,128)(2,1)S(1)} %copy-done.2, bf16[1024,128]{1,0:T(8,128)(2,1)S(1)} %get-tuple-element.50._.refs_0_, bf16[1024,128]{1,0:T(8,128)(2,1)S(1)} %collective-permute-done.3.refs_1_, ...), custom_call_target="tpu_custom_call" | custom-call | flops 1024 | bytes 1024 | tf_op jit(solution)/shard_map/output/pallas_call | solution.py:208
  66.0 6.1 %collective-permute-done.18.y = bf16[9,256,128]{2,1,0:T(8,128)(2,1)S(1)} collective-permute-done((bf16[9,256,128]{2,1,0:T(8,128)(2,1)S(1)}, bf16[9,256,128]{2,1,0:T(8,128)(2,1)S(1)}, u32[]{:S(2)}, u32[]{:S(2)}) %collective-permute-start.18) | collective-permute-done | bytes 589856 | tf_op jit(solution)/shard_map/ppermute | solution.py:480
  72.1 4.9 %collective-permute-start.16 = (bf16[9,256,128]{2,1,0:T(8,128)(2,1)S(1)}, bf16[9,256,128]{2,1,0:T(8,128)(2,1)}, u32[]{:S(2)}, u32[]{:S(2)}) collective-permute-start(bf16[9,256,128]{2,1,0:T(8,128)(2,1)S(1)} %grad_second.5.refs_0_.x), channel_id=1, source_target_pairs={{0,8},{4,12},{24,16},{28,20},{1,9},{5,13},{25,17},{29,21},{2,10},{... | collective-permute-start | bytes 1769480 | tf_op jit(solution)/shard_map/ppermute | solution.py:480
  83.1 4.4 %grad_first.1 = (bf16[1168,256]{1,0:T(8,128)(2,1)S(1)}, bf16[1168,256]{1,0:T(8,128)(2,1)S(1)}, bf16[1168,256]{1,0:T(8,128)(2,1)S(1)}) custom-call(bf16[128,1024]{1,0:T(8,128)(2,1)S(1)} %bitcast.17, bf16[128,1024]{1,0:T(8,128)(2,1)S(1)} %collective-permute-done.7.refs_5_.vol_other, bf16[2,1024,128]{2,1,0:T(8,128)(2,1)S(1)} %get-tuple-element.62.own.refs_0_, ...), custom_call_target="tpu_custom_call" | custom-call | flops 1024 | bytes 1024 | tf_op jit(solution)/shard_map/grad_first/pallas_call | solution.py:341
  87.5 5.2 %collective-permute-start.21 = (bf16[1168,256]{1,0:T(8,128)(2,1)S(1)}, bf16[1168,256]{1,0:T(8,128)(2,1)S(1)}, u32[]{:S(2)}, u32[]{:S(2)}) collective-permute-start(bf16[1168,256]{1,0:T(8,128)(2,1)S(1)} %get-tuple-element.65.refs_0_.x), channel_id=1, source_target_pairs={{0,8},{4,12},{24,16},{28,20},{1,9},{5,13},{25,17},{29,21},{2,10},{... | collective-permute-start | bytes 1794056 | tf_op jit(solution)/shard_map/ppermute | solution.py:480
  97.4 1.7 collective-permute-done.22.y
  101.1 4.5 %collective-permute-start.26 = (bf16[1168,256]{1,0:T(8,128)(2,1)S(1)}, bf16[1168,256]{1,0:T(8,128)(2,1)S(1)}, u32[]{:S(2)}, u32[]{:S(2)}) collective-permute-start(bf16[1168,256]{1,0:T(8,128)(2,1)S(1)} %get-tuple-element.66.x), channel_id=1, source_target_pairs={{0,8},{4,12},{24,16},{28,20},{1,9},{5,13},{25,17},{29,21},{2,10},{... | collective-permute-start | bytes 1794056 | tf_op jit(solution)/shard_map/ppermute | solution.py:480
  106.5 6.7 %collective-permute-start.33 = (bf16[1168,256]{1,0:T(8,128)(2,1)S(1)}, bf16[1168,256]{1,0:T(8,128)(2,1)S(1)}, u32[]{:S(2)}, u32[]{:S(2)}) collective-permute-start(bf16[1168,256]{1,0:T(8,128)(2,1)S(1)} %get-tuple-element.70.x), channel_id=1, source_target_pairs={{0,8},{4,12},{24,16},{28,20},{1,9},{5,13},{25,17},{29,21},{2,10},{... | collective-permute-start | bytes 1794056 | tf_op jit(solution)/shard_map/ppermute | solution.py:480
  115.8 1.9 %collective-permute-start.30 = (bf16[9,256,128]{2,1,0:T(8,128)(2,1)S(1)}, bf16[9,256,128]{2,1,0:T(8,128)(2,1)S(1)}, u32[]{:S(2)}, u32[]{:S(2)}) collective-permute-start(bf16[9,256,128]{2,1,0:T(8,128)(2,1)S(1)} %line_pick.7.refs_0_.own), channel_id=1, source_target_pairs={{0,4},{4,0},{8,12},{12,8},{16,20},{20,16},{24,28},{28,24},{1,5},{5... | collective-permute-start | bytes 1769480 | tf_op jit(solution)/shard_map/ppermute | solution.py:509
  117.6 2.0 %finish_second.3 = (f32[27,512,128]{2,1,0:T(8,128)}, f32[8,128]{1,0:T(8,128)S(1)}) custom-call(s32[2]{0:T(128)S(1)} %copy-done.13, bf16[9,256,128]{2,1,0:T(8,128)(2,1)S(1)} %line_pick.6.refs_0_.own, bf16[9,256,128]{2,1,0:T(8,128)(2,1)S(1)} %collective-permute-done.27.other, bf16[9,256,128]{2,1,0:T(8,128)(2,1)S(1)} %line_pick.7.refs_0_.own), custom_call_target="tpu_custom_call" | custom-call | flops 1024 | bytes 1024 | tf_op jit(solution)/shard_map/finish_second/pallas_call | solution.py:419
  122.0 6.6 %collective-permute-done.24.y = bf16[9,256,128]{2,1,0:T(8,128)(2,1)S(1)} collective-permute-done((bf16[9,256,128]{2,1,0:T(8,128)(2,1)S(1)}, bf16[9,256,128]{2,1,0:T(8,128)(2,1)S(1)}, u32[]{:S(2)}, u32[]{:S(2)}) %collective-permute-start.24) | collective-permute-done | bytes 589856 | tf_op jit(solution)/shard_map/ppermute | solution.py:480
  129.2 2.0 %finish_second.4 = (f32[27,512,128]{2,1,0:T(8,128)}, f32[8,128]{1,0:T(8,128)S(1)}) custom-call(s32[2]{0:T(128)S(1)} %copy-done.13, bf16[9,256,128]{2,1,0:T(8,128)(2,1)S(1)} %line_pick.7.refs_0_.own, bf16[9,256,128]{2,1,0:T(8,128)(2,1)S(1)} %collective-permute-done.30.other, ...), custom_call_target="tpu_custom_call", output_to_operand_aliasing={{0}: (3, {})} | custom-call | flops 1024 | bytes 1024 | tf_op jit(solution)/shard_map/finish_second/pallas_call | solution.py:419
  132.3 5.1 %collective-permute-start.29 = (bf16[9,256,128]{2,1,0:T(8,128)(2,1)S(1)}, bf16[9,256,128]{2,1,0:T(8,128)(2,1)S(1)}, u32[]{:S(2)}, u32[]{:S(2)}) collective-permute-start(bf16[9,256,128]{2,1,0:T(8,128)(2,1)S(1)} %line_pick.8.refs_1_.own), channel_id=1, source_target_pairs={{0,4},{4,0},{8,12},{12,8},{16,20},{20,16},{24,28},{28,24},{1,5},{5... | collective-permute-start | bytes 1769480 | tf_op jit(solution)/shard_map/ppermute | solution.py:509
  138.8 2.6 %collective-permute-done.31.y = bf16[1168,256]{1,0:T(8,128)(2,1)S(1)} collective-permute-done((bf16[1168,256]{1,0:T(8,128)(2,1)S(1)}, bf16[1168,256]{1,0:T(8,128)(2,1)S(1)}, u32[]{:S(2)}, u32[]{:S(2)}) %collective-permute-start.31) | collective-permute-done | bytes 598048 | tf_op jit(solution)/shard_map/ppermute | solution.py:480
  142.0 4.3 %collective-permute-start.36 = (bf16[1168,256]{1,0:T(8,128)(2,1)S(1)}, bf16[1168,256]{1,0:T(8,128)(2,1)S(1)}, u32[]{:S(2)}, u32[]{:S(2)}) collective-permute-start(bf16[1168,256]{1,0:T(8,128)(2,1)S(1)} %line_pick.9.refs_1_.own), channel_id=1, source_target_pairs={{0,4},{4,0},{8,12},{12,8},{16,20},{20,16},{24,28},{28,24},{1,5},{5... | collective-permute-start | bytes 1794056 | tf_op jit(solution)/shard_map/ppermute | solution.py:509
  146.3 2.0 %finish_second.5 = (f32[27,512,128]{2,1,0:T(8,128)}, f32[8,128]{1,0:T(8,128)S(1)}) custom-call(s32[2]{0:T(128)S(1)} %copy-done.13, bf16[9,256,128]{2,1,0:T(8,128)(2,1)S(1)} %line_pick.8.refs_1_.own, bf16[9,256,128]{2,1,0:T(8,128)(2,1)S(1)} %collective-permute-done.29.other, ...), custom_call_target="tpu_custom_call", output_to_operand_aliasing={{0}: (3, {})} | custom-call | flops 1024 | bytes 1024 | tf_op jit(solution)/shard_map/finish_second/pallas_call | solution.py:419
  148.4 7.2 %grad_volume.1 = (bf16[128,1024]{1,0:T(8,128)(2,1)}, f32[8,128]{1,0:T(8,128)S(1)}) custom-call(s32[2]{0:T(128)S(1)} %copy-done.13, bf16[3456,512]{1,0:T(8,128)(2,1)S(1)} %bitcast.11, bf16[1024,128]{1,0:T(8,128)(2,1)S(1)} %get-tuple-element.61.refs_0_, bf16[1024,128]{1,0:T(8,128)(2,1)S(1)} %copy-done.10, bf16[1024,128]{1,0:T(8,128)(2,1)S(1)} %copy-done.8, ...), custom_call_target="tpu_custom_call" | custom-call | flops 1024 | bytes 1024 | tf_op jit(solution)/shard_map/grad_volume/pallas_call | solution.py:208
  157.8 2.0 %finish_first.3 = (f32[27,128,512]{2,1,0:T(8,128)}, f32[8,128]{1,0:T(8,128)S(1)}) custom-call(s32[2]{0:T(128)S(1)} %copy-done.13, bf16[1168,256]{1,0:T(8,128)(2,1)S(1)} %line_pick.9.refs_1_.own, bf16[1168,256]{1,0:T(8,128)(2,1)S(1)} %collective-permute-done.36.other, bf16[1168,256]{1,0:T(8,128)(2,1)S(1)} %line_pick.10.refs_0_.own), custom_call_target="tpu_custom_call" | custom-call | flops 1024 | bytes 1024 | tf_op jit(solution)/shard_map/finish_first/pallas_call | solution.py:419
  159.8 13.0 %collective-permute-done.35.y = bf16[1168,256]{1,0:T(8,128)(2,1)S(1)} collective-permute-done((bf16[1168,256]{1,0:T(8,128)(2,1)S(1)}, bf16[1168,256]{1,0:T(8,128)(2,1)S(1)}, u32[]{:S(2)}, u32[]{:S(2)}) %collective-permute-start.35) | collective-permute-done | bytes 598048 | tf_op jit(solution)/shard_map/ppermute | solution.py:480
  174.8 2.0 %finish_first.4 = (f32[27,128,512]{2,1,0:T(8,128)}, f32[8,128]{1,0:T(8,128)S(1)}) custom-call(s32[2]{0:T(128)S(1)} %copy-done.13, bf16[1168,256]{1,0:T(8,128)(2,1)S(1)} %line_pick.10.refs_0_.own, bf16[1168,256]{1,0:T(8,128)(2,1)S(1)} %collective-permute-done.39.other, f32[27,128,512]{2,1,0:T(8,128)} %get-tuple-element.76.refs_0_, ...), custom_call_target="tpu_custom_call", output_to_operand_aliasing={{0}: (3, {})} | custom-call | flops 1024 | bytes 1024 | tf_op jit(solution)/shard_map/finish_first/pallas_call | solution.py:419
  176.8 2.6 %finish_first.5 = (f32[27,128,512]{2,1,0:T(8,128)}, f32[8,128]{1,0:T(8,128)}) custom-call(s32[2]{0:T(128)S(1)} %copy-done.13, bf16[1168,256]{1,0:T(8,128)(2,1)S(1)} %line_pick.11.refs_1_.own, bf16[1168,256]{1,0:T(8,128)(2,1)S(1)} %collective-permute-done.38.other, f32[27,128,512]{2,1,0:T(8,128)} %get-tuple-element.77.refs_0_, ...), custom_call_target="tpu_custom_call", output_to_operand_aliasing={{0}: (3, {})} | custom-call | flops 1024 | bytes 1024 | tf_op jit(solution)/shard_map/finish_first/pallas_call | solution.py:419
  (119 shorter events, 46.2 us)
Async XLA Ops:
  8.5 14.0 %collective-permute-start = (bf16[1024,128]{1,0:T(8,128)(2,1)}, bf16[1024,128]{1,0:T(8,128)(2,1)S(1)}, u32[]{:S(2)}, u32[]{:S(2)}) collective-permute-start(bf16[1024,128]{1,0:T(8,128)(2,1)} %get-tuple-element.44), channel_id=1, source_target_pairs={{0,1},{1,0},{2,3},{3,2},{4,5},{5,4},{6,7},{7,6},{8,9},{9,8},{10,11... | collective-permute-start | bytes 786440 | tf_op jit(solution)/shard_map/ppermute | solution.py:506
  11.8 16.4 %collective-permute-start.7 = (bf16[128,1024]{1,0:T(8,128)(2,1)}, bf16[128,1024]{1,0:T(8,128)(2,1)S(1)}, u32[]{:S(2)}, u32[]{:S(2)}) collective-permute-start(bf16[128,1024]{1,0:T(8,128)(2,1)} %bitcast.16), channel_id=1, source_target_pairs={{0,4},{4,0},{8,12},{12,8},{16,20},{20,16},{24,28},{28,24},{1,5},{5... | collective-permute-start | bytes 786440 | tf_op jit(solution)/shard_map/ppermute | solution.py:509
  13.1 14.5 %collective-permute-start.6 = (bf16[128,1024]{1,0:T(8,128)(2,1)}, bf16[128,1024]{1,0:T(8,128)(2,1)S(1)}, u32[]{:S(2)}, u32[]{:S(2)}) collective-permute-start(bf16[128,1024]{1,0:T(8,128)(2,1)} %bitcast.12), channel_id=1, source_target_pairs={{0,4},{4,0},{8,12},{12,8},{16,20},{20,16},{24,28},{28,24},{1,5},{5... | collective-permute-start | bytes 786440 | tf_op jit(solution)/shard_map/ppermute | solution.py:509
  26.7 13.0 %collective-permute-start.4 = (bf16[1024,128]{1,0:T(8,128)(2,1)S(1)}, bf16[1024,128]{1,0:T(8,128)(2,1)S(1)}, u32[]{:S(2)}, u32[]{:S(2)}) collective-permute-start(bf16[1024,128]{1,0:T(8,128)(2,1)S(1)} %get-tuple-element.50._.refs_0_), channel_id=1, source_target_pairs={{0,2},{1,3},{2,0},{3,1},{4,6},{5,7},{6,4},{7,5},{8,10},{9,11},{10,... | collective-permute-start | bytes 786440 | tf_op jit(solution)/shard_map/ppermute | solution.py:506
  27.3 12.4 %collective-permute-start.3 = (bf16[1024,128]{1,0:T(8,128)(2,1)S(1)}, bf16[1024,128]{1,0:T(8,128)(2,1)S(1)}, u32[]{:S(2)}, u32[]{:S(2)}) collective-permute-start(bf16[1024,128]{1,0:T(8,128)(2,1)S(1)} %get-tuple-element.50._.refs_0_), channel_id=1, source_target_pairs={{0,1},{1,0},{2,3},{3,2},{4,5},{5,4},{6,7},{7,6},{8,9},{9,8},{10,11... | collective-permute-start | bytes 786440 | tf_op jit(solution)/shard_map/ppermute | solution.py:506
  43.9 17.4 %collective-permute-start.15 = (bf16[9,256,128]{2,1,0:T(8,128)(2,1)S(1)}, bf16[9,256,128]{2,1,0:T(8,128)(2,1)S(1)}, u32[]{:S(2)}, u32[]{:S(2)}) collective-permute-start(bf16[9,256,128]{2,1,0:T(8,128)(2,1)S(1)} %grad_second.3.refs_0_.x), channel_id=1, source_target_pairs={{0,8},{4,12},{24,16},{28,20},{1,9},{5,13},{25,17},{29,21},{2,10},{... | collective-permute-start | bytes 1769480 | tf_op jit(solution)/shard_map/ppermute | solution.py:480
  47.1 12.8 %collective-permute-start.9 = (bf16[1024,128]{1,0:T(8,128)(2,1)S(1)}, bf16[1024,128]{1,0:T(8,128)(2,1)S(1)}, u32[]{:S(2)}, u32[]{:S(2)}) collective-permute-start(bf16[1024,128]{1,0:T(8,128)(2,1)S(1)} %get-tuple-element.57), channel_id=1, source_target_pairs={{0,1},{1,0},{2,3},{3,2},{4,5},{5,4},{6,7},{7,6},{8,9},{9,8},{10,11... | collective-permute-start | bytes 786440 | tf_op jit(solution)/shard_map/ppermute | solution.py:506
  51.4 20.7 %collective-permute-start.18 = (bf16[9,256,128]{2,1,0:T(8,128)(2,1)S(1)}, bf16[9,256,128]{2,1,0:T(8,128)(2,1)S(1)}, u32[]{:S(2)}, u32[]{:S(2)}) collective-permute-start(bf16[9,256,128]{2,1,0:T(8,128)(2,1)S(1)} %grad_second.4.refs_4_.x), channel_id=1, source_target_pairs={{0,8},{4,12},{24,16},{28,20},{1,9},{5,13},{25,17},{29,21},{2,10},{... | collective-permute-start | bytes 1769480 | tf_op jit(solution)/shard_map/ppermute | solution.py:480
  61.4 15.7 %collective-permute-start.17 = (bf16[9,256,128]{2,1,0:T(8,128)(2,1)S(1)}, bf16[9,256,128]{2,1,0:T(8,128)(2,1)S(1)}, u32[]{:S(2)}, u32[]{:S(2)}) collective-permute-start(bf16[9,256,128]{2,1,0:T(8,128)(2,1)S(1)} %line_add.12.refs_0_.x), channel_id=1, source_target_pairs={{8,16},{12,20},{16,8},{20,12},{9,17},{13,21},{17,9},{21,13},{10,18... | collective-permute-start | bytes 1769480 | tf_op jit(solution)/shard_map/ppermute | solution.py:480
  62.1 15.2 %collective-permute-start.14 = (bf16[1024,128]{1,0:T(8,128)(2,1)S(1)}, bf16[1024,128]{1,0:T(8,128)(2,1)S(1)}, u32[]{:S(2)}, u32[]{:S(2)}) collective-permute-start(bf16[1024,128]{1,0:T(8,128)(2,1)S(1)} %get-tuple-element.61.refs_0_), channel_id=1, source_target_pairs={{0,3},{1,2},{2,1},{3,0},{4,7},{5,6},{6,5},{7,4},{8,11},{9,10},{10,... | collective-permute-start | bytes 786440 | tf_op jit(solution)/shard_map/ppermute | solution.py:506
  63.6 13.7 %collective-permute-start.13 = (bf16[1024,128]{1,0:T(8,128)(2,1)S(1)}, bf16[1024,128]{1,0:T(8,128)(2,1)S(1)}, u32[]{:S(2)}, u32[]{:S(2)}) collective-permute-start(bf16[1024,128]{1,0:T(8,128)(2,1)S(1)} %get-tuple-element.61.refs_0_), channel_id=1, source_target_pairs={{0,2},{1,3},{2,0},{3,1},{4,6},{5,7},{6,4},{7,5},{8,10},{9,11},{10,... | collective-permute-start | bytes 786440 | tf_op jit(solution)/shard_map/ppermute | solution.py:506
  64.2 13.1 %collective-permute-start.12 = (bf16[1024,128]{1,0:T(8,128)(2,1)S(1)}, bf16[1024,128]{1,0:T(8,128)(2,1)S(1)}, u32[]{:S(2)}, u32[]{:S(2)}) collective-permute-start(bf16[1024,128]{1,0:T(8,128)(2,1)S(1)} %get-tuple-element.61.refs_0_), channel_id=1, source_target_pairs={{0,1},{1,0},{2,3},{3,2},{4,5},{5,4},{6,7},{7,6},{8,9},{9,8},{10,11... | collective-permute-start | bytes 786440 | tf_op jit(solution)/shard_map/ppermute | solution.py:506
  72.1 20.7 %collective-permute-start.16 = (bf16[9,256,128]{2,1,0:T(8,128)(2,1)S(1)}, bf16[9,256,128]{2,1,0:T(8,128)(2,1)}, u32[]{:S(2)}, u32[]{:S(2)}) collective-permute-start(bf16[9,256,128]{2,1,0:T(8,128)(2,1)S(1)} %grad_second.5.refs_0_.x), channel_id=1, source_target_pairs={{0,8},{4,12},{24,16},{28,20},{1,9},{5,13},{25,17},{29,21},{2,10},{... | collective-permute-start | bytes 1769480 | tf_op jit(solution)/shard_map/ppermute | solution.py:480
  80.2 14.5 %collective-permute-start.23 = (bf16[9,256,128]{2,1,0:T(8,128)(2,1)S(1)}, bf16[9,256,128]{2,1,0:T(8,128)(2,1)}, u32[]{:S(2)}, u32[]{:S(2)}) collective-permute-start(bf16[9,256,128]{2,1,0:T(8,128)(2,1)S(1)} %line_add.13.refs_0_.x), channel_id=1, source_target_pairs={{8,16},{12,20},{16,8},{20,12},{9,17},{13,21},{17,9},{21,13},{10,18... | collective-permute-start | bytes 1769480 | tf_op jit(solution)/shard_map/ppermute | solution.py:480
  81.7 17.4 %collective-permute-start.22 = (bf16[9,256,128]{2,1,0:T(8,128)(2,1)S(1)}, bf16[9,256,128]{2,1,0:T(8,128)(2,1)}, u32[]{:S(2)}, u32[]{:S(2)}) collective-permute-start(bf16[9,256,128]{2,1,0:T(8,128)(2,1)S(1)} %line_add.14.refs_4_.x), channel_id=1, source_target_pairs={{8,0},{12,4},{16,24},{20,28},{9,1},{13,5},{17,25},{21,29},{10,2},{... | collective-permute-start | bytes 1769480 | tf_op jit(solution)/shard_map/ppermute | solution.py:480
  87.5 18.1 %collective-permute-start.21 = (bf16[1168,256]{1,0:T(8,128)(2,1)S(1)}, bf16[1168,256]{1,0:T(8,128)(2,1)S(1)}, u32[]{:S(2)}, u32[]{:S(2)}) collective-permute-start(bf16[1168,256]{1,0:T(8,128)(2,1)S(1)} %get-tuple-element.65.refs_0_.x), channel_id=1, source_target_pairs={{0,8},{4,12},{24,16},{28,20},{1,9},{5,13},{25,17},{29,21},{2,10},{... | collective-permute-start | bytes 1794056 | tf_op jit(solution)/shard_map/ppermute | solution.py:480
  94.0 12.4 %collective-permute-start.20 = (bf16[9,256,128]{2,1,0:T(8,128)(2,1)S(1)}, bf16[9,256,128]{2,1,0:T(8,128)(2,1)S(1)}, u32[]{:S(2)}, u32[]{:S(2)}) collective-permute-start(bf16[9,256,128]{2,1,0:T(8,128)(2,1)S(1)} %line_add.15.refs_0_.x), channel_id=1, source_target_pairs={{8,16},{12,20},{16,8},{20,12},{9,17},{13,21},{17,9},{21,13},{10,18... | collective-permute-start | bytes 1769480 | tf_op jit(solution)/shard_map/ppermute | solution.py:480
  96.1 17.6 %collective-permute-start.28 = (bf16[9,256,128]{2,1,0:T(8,128)(2,1)S(1)}, bf16[9,256,128]{2,1,0:T(8,128)(2,1)S(1)}, u32[]{:S(2)}, u32[]{:S(2)}) collective-permute-start(bf16[9,256,128]{2,1,0:T(8,128)(2,1)S(1)} %line_add.16.refs_0_.x), channel_id=1, source_target_pairs={{8,0},{12,4},{16,24},{20,28},{9,1},{13,5},{17,25},{21,29},{10,2},{... | collective-permute-start | bytes 1769480 | tf_op jit(solution)/shard_map/ppermute | solution.py:480
  100.2 15.6 %collective-permute-start.27 = (bf16[9,256,128]{2,1,0:T(8,128)(2,1)S(1)}, bf16[9,256,128]{2,1,0:T(8,128)(2,1)S(1)}, u32[]{:S(2)}, u32[]{:S(2)}) collective-permute-start(bf16[9,256,128]{2,1,0:T(8,128)(2,1)S(1)} %line_pick.6.refs_0_.own), channel_id=1, source_target_pairs={{0,4},{4,0},{8,12},{12,8},{16,20},{20,16},{24,28},{28,24},{1,5},{5... | collective-permute-start | bytes 1769480 | tf_op jit(solution)/shard_map/ppermute | solution.py:509
  101.1 18.6 %collective-permute-start.26 = (bf16[1168,256]{1,0:T(8,128)(2,1)S(1)}, bf16[1168,256]{1,0:T(8,128)(2,1)S(1)}, u32[]{:S(2)}, u32[]{:S(2)}) collective-permute-start(bf16[1168,256]{1,0:T(8,128)(2,1)S(1)} %get-tuple-element.66.x), channel_id=1, source_target_pairs={{0,8},{4,12},{24,16},{28,20},{1,9},{5,13},{25,17},{29,21},{2,10},{... | collective-permute-start | bytes 1794056 | tf_op jit(solution)/shard_map/ppermute | solution.py:480
  105.7 14.8 %collective-permute-start.25 = (bf16[1168,256]{1,0:T(8,128)(2,1)S(1)}, bf16[1168,256]{1,0:T(8,128)(2,1)S(1)}, u32[]{:S(2)}, u32[]{:S(2)}) collective-permute-start(bf16[1168,256]{1,0:T(8,128)(2,1)S(1)} %line_add.17.refs_0_.x), channel_id=1, source_target_pairs={{8,16},{12,20},{16,8},{20,12},{9,17},{13,21},{17,9},{21,13},{10,18... | collective-permute-start | bytes 1794056 | tf_op jit(solution)/shard_map/ppermute | solution.py:480
  106.5 24.8 %collective-permute-start.33 = (bf16[1168,256]{1,0:T(8,128)(2,1)S(1)}, bf16[1168,256]{1,0:T(8,128)(2,1)S(1)}, u32[]{:S(2)}, u32[]{:S(2)}) collective-permute-start(bf16[1168,256]{1,0:T(8,128)(2,1)S(1)} %get-tuple-element.70.x), channel_id=1, source_target_pairs={{0,8},{4,12},{24,16},{28,20},{1,9},{5,13},{25,17},{29,21},{2,10},{... | collective-permute-start | bytes 1794056 | tf_op jit(solution)/shard_map/ppermute | solution.py:480
  113.7 14.9 %collective-permute-start.24 = (bf16[9,256,128]{2,1,0:T(8,128)(2,1)S(1)}, bf16[9,256,128]{2,1,0:T(8,128)(2,1)S(1)}, u32[]{:S(2)}, u32[]{:S(2)}) collective-permute-start(bf16[9,256,128]{2,1,0:T(8,128)(2,1)S(1)} %line_add.18.refs_0_.x), channel_id=1, source_target_pairs={{8,0},{12,4},{16,24},{20,28},{9,1},{13,5},{17,25},{21,29},{10,2},{... | collective-permute-start | bytes 1769480 | tf_op jit(solution)/shard_map/ppermute | solution.py:480
  115.8 13.4 %collective-permute-start.30 = (bf16[9,256,128]{2,1,0:T(8,128)(2,1)S(1)}, bf16[9,256,128]{2,1,0:T(8,128)(2,1)S(1)}, u32[]{:S(2)}, u32[]{:S(2)}) collective-permute-start(bf16[9,256,128]{2,1,0:T(8,128)(2,1)S(1)} %line_pick.7.refs_0_.own), channel_id=1, source_target_pairs={{0,4},{4,0},{8,12},{12,8},{16,20},{20,16},{24,28},{28,24},{1,5},{5... | collective-permute-start | bytes 1769480 | tf_op jit(solution)/shard_map/ppermute | solution.py:509
  119.8 17.5 %collective-permute-start.32 = (bf16[1168,256]{1,0:T(8,128)(2,1)S(1)}, bf16[1168,256]{1,0:T(8,128)(2,1)S(1)}, u32[]{:S(2)}, u32[]{:S(2)}) collective-permute-start(bf16[1168,256]{1,0:T(8,128)(2,1)S(1)} %line_add.19.refs_0_.x), channel_id=1, source_target_pairs={{8,16},{12,20},{16,8},{20,12},{9,17},{13,21},{17,9},{21,13},{10,18... | collective-permute-start | bytes 1794056 | tf_op jit(solution)/shard_map/ppermute | solution.py:480
  120.7 20.7 %collective-permute-start.31 = (bf16[1168,256]{1,0:T(8,128)(2,1)S(1)}, bf16[1168,256]{1,0:T(8,128)(2,1)S(1)}, u32[]{:S(2)}, u32[]{:S(2)}) collective-permute-start(bf16[1168,256]{1,0:T(8,128)(2,1)S(1)} %line_add.20.refs_0_.x), channel_id=1, source_target_pairs={{8,0},{12,4},{16,24},{20,28},{9,1},{13,5},{17,25},{21,29},{10,2},{... | collective-permute-start | bytes 1794056 | tf_op jit(solution)/shard_map/ppermute | solution.py:480
  131.4 24.2 %collective-permute-start.34 = (bf16[1168,256]{1,0:T(8,128)(2,1)S(1)}, bf16[1168,256]{1,0:T(8,128)(2,1)S(1)}, u32[]{:S(2)}, u32[]{:S(2)}) collective-permute-start(bf16[1168,256]{1,0:T(8,128)(2,1)S(1)} %line_add.21.refs_0_.x), channel_id=1, source_target_pairs={{8,16},{12,20},{16,8},{20,12},{9,17},{13,21},{17,9},{21,13},{10,18... | collective-permute-start | bytes 1794056 | tf_op jit(solution)/shard_map/ppermute | solution.py:480
  132.3 14.1 %collective-permute-start.29 = (bf16[9,256,128]{2,1,0:T(8,128)(2,1)S(1)}, bf16[9,256,128]{2,1,0:T(8,128)(2,1)S(1)}, u32[]{:S(2)}, u32[]{:S(2)}) collective-permute-start(bf16[9,256,128]{2,1,0:T(8,128)(2,1)S(1)} %line_pick.8.refs_1_.own), channel_id=1, source_target_pairs={{0,4},{4,0},{8,12},{12,8},{16,20},{20,16},{24,28},{28,24},{1,5},{5... | collective-permute-start | bytes 1769480 | tf_op jit(solution)/shard_map/ppermute | solution.py:509
  137.5 19.5 %collective-permute-start.37 = (bf16[1168,256]{1,0:T(8,128)(2,1)S(1)}, bf16[1168,256]{1,0:T(8,128)(2,1)S(1)}, u32[]{:S(2)}, u32[]{:S(2)}) collective-permute-start(bf16[1168,256]{1,0:T(8,128)(2,1)S(1)} %line_add.22.refs_0_.x), channel_id=1, source_target_pairs={{8,0},{12,4},{16,24},{20,28},{9,1},{13,5},{17,25},{21,29},{10,2},{... | collective-permute-start | bytes 1794056 | tf_op jit(solution)/shard_map/ppermute | solution.py:480
  142.0 15.7 %collective-permute-start.36 = (bf16[1168,256]{1,0:T(8,128)(2,1)S(1)}, bf16[1168,256]{1,0:T(8,128)(2,1)S(1)}, u32[]{:S(2)}, u32[]{:S(2)}) collective-permute-start(bf16[1168,256]{1,0:T(8,128)(2,1)S(1)} %line_pick.9.refs_1_.own), channel_id=1, source_target_pairs={{0,4},{4,0},{8,12},{12,8},{16,20},{20,16},{24,28},{28,24},{1,5},{5... | collective-permute-start | bytes 1794056 | tf_op jit(solution)/shard_map/ppermute | solution.py:509
  155.7 17.0 %collective-permute-start.35 = (bf16[1168,256]{1,0:T(8,128)(2,1)S(1)}, bf16[1168,256]{1,0:T(8,128)(2,1)S(1)}, u32[]{:S(2)}, u32[]{:S(2)}) collective-permute-start(bf16[1168,256]{1,0:T(8,128)(2,1)S(1)} %line_add.23.refs_0_.x), channel_id=1, source_target_pairs={{8,0},{12,4},{16,24},{20,28},{9,1},{13,5},{17,25},{21,29},{10,2},{... | collective-permute-start | bytes 1794056 | tf_op jit(solution)/shard_map/ppermute | solution.py:480
  157.7 17.1 %collective-permute-start.39 = (bf16[1168,256]{1,0:T(8,128)(2,1)S(1)}, bf16[1168,256]{1,0:T(8,128)(2,1)S(1)}, u32[]{:S(2)}, u32[]{:S(2)}) collective-permute-start(bf16[1168,256]{1,0:T(8,128)(2,1)S(1)} %line_pick.10.refs_0_.own), channel_id=1, source_target_pairs={{0,4},{4,0},{8,12},{12,8},{16,20},{20,16},{24,28},{28,24},{1,5},{5... | collective-permute-start | bytes 1794056 | tf_op jit(solution)/shard_map/ppermute | solution.py:509
  (22 other events, 265.3 us)

commit v8 on v7

--- a/solution.py
+++ b/solution.py
@@ -67,11 +67,17 @@
     return copies
 
 
-def share_kernel(n, sign, idx, field, w, *refs):
-    outs = refs[:n]
-    padded, sums, shares, buffer, sems = refs[n:]
-    rows = field.shape[0]
-    copies = start_parts(w, buffer, sems)
+def share_kernel(n, sign, wanted, idx, field, w, *refs):
+    outs = refs[len(refs) - 4 - len(wanted) : -4]
+    padded, sums, buffer, sems = refs[-4:]
+    rows, wide = field.shape[0], sums.shape[1]
+    split = len(wanted) < n
+    half = (idx[0] >= n // 2).astype(jnp.int32) ^ (wanted[0] // (n // 2))
+    if split:
+        source = w.at[:, pl.ds(pl.multiple_of(half * wide, wide), wide)]
+    else:
+        source = w
+    copies = start_parts(source, buffer, sems)
     fill_padded(padded, field[...], sign)
     for a in PLANE_ORDER:
         begin, planes = span_of(a, sign)
@@ -94,37 +100,60 @@
             sums[...] = part
         else:
             sums[span] += part
-    for j in range(n):
-        shares[j] = sums[:, j * rows : (j + 1) * rows].astype(BF16)
-    for m in range(n):
-        outs[m][...] = shares[idx[0] ^ m]
-
-
-def spread_shares(sign, name, idx, n, field, w, limit):
-    rows = field.shape[0]
-    return pl.pallas_call(
-        functools.partial(share_kernel, n, sign),
-        in_specs=[smem(), pl.BlockSpec(memory_space=pltpu.VMEM), IN_HBM],
-        out_specs=[pl.BlockSpec(memory_space=pltpu.VMEM)] * n,
-        out_shape=[jax.ShapeDtypeStruct((CELLS, rows), BF16)] * n,
+    count = len(wanted)
+
+    def put(out, j):
+        out[...] = sums[:, j * rows : (j + 1) * rows].astype(BF16)
+
+    for out, m in zip(outs, wanted):
+        at = (idx[0] ^ m) & (count - 1)
+        for j in range(count):
+            pl.when(at == j)(functools.partial(put, out, j))
+
+
+def spread_shares(sign, name, idx, n, field, w, wanted, limit, after=()):
+    rows, count = field.shape[0], len(wanted)
+    wide = count * rows
+    kept = (w.shape[0], wide) if count < n else w.shape
+    return pl.pallas_call(
+        functools.partial(share_kernel, n, sign, wanted),
+        in_specs=[smem(), pl.BlockSpec(memory_space=pltpu.VMEM), IN_HBM]
+        + [UNREAD] * len(after),
+        out_specs=[pl.BlockSpec(memory_space=pltpu.VMEM)] * count,
+        out_shape=[jax.ShapeDtypeStruct((CELLS, rows), BF16)] * count,
         scratch_shapes=[
             pltpu.VMEM((3, DEPTH + 2, HEIGHT + 2, WIDTH, rows), BF16),
-            pltpu.VMEM((CELLS, n * rows), F32),
-            pltpu.VMEM((n, CELLS, rows), BF16),
-            pltpu.VMEM(w.shape, BF16),
+            pltpu.VMEM((CELLS, wide), F32),
+            pltpu.VMEM(kept, BF16),
             pltpu.SemaphoreType.DMA((3,)),
         ],
         compiler_params=pltpu.CompilerParams(vmem_limit_bytes=limit),
         cost_estimate=LIGHT,
         name=name,
-    )(idx, field, w)
+    )(idx, field, w, *after)
+
+
+def sum_kernel(x, y, *refs):
+    out = refs[-1]
+    out[...] = x[...].astype(F32) + y[...].astype(F32)
+
+
+def sum_shares(name, x, y, after):
+    return pl.pallas_call(
+        sum_kernel,
+        in_specs=[pl.BlockSpec(memory_space=pltpu.VMEM)] * 2 + [UNREAD] * len(after),
+        out_shape=jax.ShapeDtypeStruct(x.shape, F32),
+        compiler_params=pltpu.CompilerParams(vmem_limit_bytes=SMALL),
+        cost_estimate=LIGHT,
+        name=name,
+    )(x, y, *after)
 
 
 def norm_kernel(n, gain, *refs):
-    shares = refs[:n]
-    act, normed_out, inverse_out = refs[2 * n - 1 : 2 * n + 2]
+    shares = refs[: n - 1]
+    act, normed_out, inverse_out = refs[-3:]
     pre = shares[0][...].astype(F32)
-    for m in range(1, n):
+    for m in range(1, n - 1):
         pre = pre + shares[m][...].astype(F32)
     center = pre - jnp.mean(pre, axis=0, keepdims=True)
     inverse = lax.rsqrt(jnp.mean(center * center, axis=0, keepdims=True) + NORM_EPS)
@@ -136,10 +165,10 @@
 
 
 def norm_back_kernel(n, gain, normed_in, inverse, *refs):
-    shares = refs[:n]
+    shares = refs[: n - 1]
     dpre, gain_part = refs[-2:]
     dact = shares[0][...].astype(F32)
-    for m in range(1, n):
+    for m in range(1, n - 1):
         dact = dact + shares[m][...].astype(F32)
     normed = normed_in[...]
     scaled = gain[...] * normed
@@ -350,35 +379,36 @@
     )(vol_own, vol_other, own, other, gain_part, *after)
 
 
-def grad_second_kernel(a, moved, own, other, *refs):
+def grad_second_kernel(offsets, moved, own, other, *refs):
     out = refs[-1]
     rows = out.shape[2]
-    begin, planes = max(0, a), DEPTH - abs(a)
-    lhs = [
-        ref[:, begin * PLANE : (begin + planes) * PLANE] for ref in (own, other)
-    ]
-    for k in range(0, 9, 2):
-        taps = range(k, min(k + 2, 9))
-        grads = None
-        for which in range(2):
-            pieces = []
-            for at in taps:
-                b, c = at // 3 - 1, at % 3 - 1
-                piece = moved[which, 1 + c, begin - a : begin - a + planes, 1 - b : 1 - b + HEIGHT]
-                pieces.append(piece.reshape(planes * PLANE, rows))
-            rhs = jnp.concatenate(pieces, axis=1)
-            part = jnp.dot(lhs[which], rhs, preferred_element_type=F32)
-            grads = part if grads is None else grads + part
-        for place, at in enumerate(taps):
-            out[at] = grads[:, place * rows : (place + 1) * rows].astype(BF16)
-
-
-def grad_second(a, moved, own, other, after):
+    for which_a, a in enumerate(offsets):
+        begin, planes = max(0, a), DEPTH - abs(a)
+        lhs = [ref[:, begin * PLANE : (begin + planes) * PLANE] for ref in (own, other)]
+        for k in range(0, 9, 2):
+            taps = range(k, min(k + 2, 9))
+            grads = None
+            for which in range(2):
+                pieces = []
+                for at in taps:
+                    b, c = at // 3 - 1, at % 3 - 1
+                    first = begin - a
+                    piece = moved[which, 1 + c, first : first + planes, 1 - b : 1 - b + HEIGHT]
+                    pieces.append(piece.reshape(planes * PLANE, rows))
+                rhs = jnp.concatenate(pieces, axis=1)
+                part = jnp.dot(lhs[which], rhs, preferred_element_type=F32)
+                grads = part if grads is None else grads + part
+            for place, at in enumerate(taps):
+                piece = grads[:, place * rows : (place + 1) * rows]
+                out[9 * which_a + at] = piece.astype(BF16)
+
+
+def grad_second(offsets, moved, own, other, after):
     wide, rows = own.shape[0], moved.shape[-1]
     return pl.pallas_call(
-        functools.partial(grad_second_kernel, a),
+        functools.partial(grad_second_kernel, offsets),
         in_specs=[pl.BlockSpec(memory_space=pltpu.VMEM)] * 3 + [UNREAD] * len(after),
-        out_shape=jax.ShapeDtypeStruct((9, wide, rows), BF16),
+        out_shape=jax.ShapeDtypeStruct((9 * len(offsets), wide, rows), BF16),
         compiler_params=pltpu.CompilerParams(vmem_limit_bytes=LIMIT),
         cost_estimate=LIGHT,
         name="grad_second",
@@ -431,10 +461,11 @@
     )(idx, own, other, *given, *after)
 
 
-def add_kernel(x, y, *refs):
+def add_kernel(first, x, y, *refs):
     out = refs[-1]
     if len(x.shape) == 3:
-        out[...] = (x[...].astype(F32) + y[...].astype(F32)).astype(BF16)
+        span = slice(first, first + out.shape[0])
+        out[...] = (x[span].astype(F32) + y[span].astype(F32)).astype(BF16)
     else:
         rows = x.shape[0] - EXTRA
         out[:rows] = (x[:rows].astype(F32) + y[:rows].astype(F32)).astype(BF16)
@@ -454,14 +485,14 @@
         out[...] = y[...]
 
 
-def whole_call(kernel, name, x, y, after, idx=None):
+def whole_call(kernel, name, shape, x, y, after, idx=None):
     given = [] if idx is None else [idx]
     return pl.pallas_call(
         kernel,
         in_specs=[smem()] * len(given)
         + [pl.BlockSpec(memory_space=pltpu.VMEM)] * 2
         + [UNREAD] * len(after),
-        out_shape=jax.ShapeDtypeStruct(x.shape, x.dtype),
+        out_shape=jax.ShapeDtypeStruct(shape, BF16),
         compiler_params=pltpu.CompilerParams(vmem_limit_bytes=SMALL),
         cost_estimate=LIGHT,
         name=name,
@@ -480,17 +511,18 @@
     return lax.ppermute(x, "dp", pairs)
 
 
-def line_step(step, part, total, idx, place, after):
+def line_step(step, part, first, got, total, idx, place, after):
     sums, outward = line_moves(lax.axis_size("dp") // 2)
-    if step < len(sums):
-        got = line_send(total, sums[step])
-        base = total if step == len(sums) - 1 else part
-        return whole_call(add_kernel, "line_add", base, got, after)
+    shape = total.shape
+    if step < len(sums) - 1:
+        add = functools.partial(add_kernel, first)
+        return whole_call(add, "line_add", shape, part, got, after)
+    if step == len(sums) - 1:
+        return whole_call(functools.partial(add_kernel, 0), "line_add", shape, total, got, after)
     moves = outward[step - len(sums)]
-    got = line_send(total, moves)
     takes = functools.reduce(jnp.logical_or, [place // 2 == j for _, j in moves])
     marked = jnp.stack([idx[0], idx[1], takes.astype(jnp.int32)])
-    return whole_call(pick_kernel, "line_pick", total, got, after, marked)
+    return whole_call(pick_kernel, "line_pick", shape, total, got, after, marked)
 
 
 def shards(volume, w_first, gain, w_second, cotangent):
@@ -513,26 +545,29 @@
         return [parts[0]] + [got[m] for m in range(1, n)]
 
     first_flat = w_first.reshape(27 * rows, n * rows)
-    pre_shares = swap(spread_shares(1, "pre", idx, n, vol, first_flat, LARGE))
-    dact_parts = spread_shares(-1, "dact", idx, n, cot, w_second, LIMIT)
-    held = dact_parts[1:]
-    act, normed, inverse, *held = pl.pallas_call(
+    far, near = tuple(range(n // 2, n)), tuple(range(n // 2))
+    pre_far = spread_shares(1, "pre_far", idx, n, vol, first_flat, far, LARGE)
+    pre_near = spread_shares(
+        1, "pre_near", idx, n, vol, first_flat, near, LARGE, (pre_far[0],)
+    )
+    pre_shares = swap(pre_near + pre_far)
+    pre_first = sum_shares("pre_sum", pre_shares[0], pre_shares[-1], ())
+    act, normed, inverse = pl.pallas_call(
         functools.partial(norm_kernel, n),
-        in_specs=[pl.BlockSpec(memory_space=pltpu.VMEM)] * (1 + n) + [UNREAD] * len(held),
-        out_specs=[pl.BlockSpec(memory_space=pltpu.VMEM)] * 3 + [UNREAD] * len(held),
         out_shape=[
             jax.ShapeDtypeStruct((CELLS, rows), BF16),
             jax.ShapeDtypeStruct((CELLS, rows), F32),
             jax.ShapeDtypeStruct((1, rows), F32),
-        ]
-        + [jax.ShapeDtypeStruct(x.shape, x.dtype) for x in held],
-        input_output_aliases={1 + n + k: 3 + k for k in range(len(held))},
+        ],
         compiler_params=pltpu.CompilerParams(vmem_limit_bytes=SMALL),
         cost_estimate=LIGHT,
         name="norm",
-    )(own_gain, *pre_shares, *held)
+    )(own_gain, pre_first, *pre_shares[1:-1])
     act_blocks = swap([act] * n)
-    dact_shares = swap([dact_parts[0]] + held)
+    dact_parts = spread_shares(
+        -1, "dact", idx, n, cot, w_second, near + far, LIMIT, (act,)
+    )
+    dact_shares = swap(dact_parts)
     moved_cot = moved_fields(
         moved_second_kernel,
         "moved_second",
@@ -542,7 +577,7 @@
         act,
     )
     vol_other = to_core(vol)
-    act_keep, act_send = halves("act_halves", True, idx, act_blocks, (moved_cot, vol_other))
+    act_keep, act_send = halves("act_halves", True, idx, act_blocks, (moved_cot, vol_other, dact_parts[0]))
     act_other = to_core(act_send)
 
     sums, outward = line_moves(lax.axis_size("dp") // 2)
@@ -550,16 +585,37 @@
     parts, totals, crossed = {}, {}, {}
     last = ()
 
+    chunk_shape = [(9, n // 2 * rows, rows)] * 3 + [(9 * rows + EXTRA, n // 2 * rows)] * 3
+    first_moves = {}
+
+    reached = [0] * 6
+
     def line(chunk, step):
         nonlocal last
-        before = totals.get(chunk, parts[chunk])
-        totals[chunk] = line_step(step, parts[chunk], before, idx, place, last)
+        if reached[chunk] > step:
+            return
+        if reached[chunk] < step:
+            line(chunk, step - 1)
+        reached[chunk] = step + 1
+        part, first = parts[chunk]
+        moves = (sums + outward)[step]
+        if step == 0:
+            if id(part) not in first_moves:
+                first_moves[id(part)] = line_send(part, moves)
+            got, total = first_moves[id(part)], jax.ShapeDtypeStruct(chunk_shape[chunk], BF16)
+        else:
+            total = totals[chunk]
+            got = line_send(total, moves)
+            if 0 < step < len(sums) - 1:
+                part, first = part[first : first + 9] if chunk < 3 else part, 0
+        totals[chunk] = line_step(step, part, first, got, total, idx, place, last)
         last = (totals[chunk],)
         if step == steps - 1:
             crossed[chunk] = to_core(totals[chunk])
 
     def write(chunk):
         nonlocal last
+        line(chunk, steps - 1)
         name, axis = ("finish_second", 1) if chunk < 3 else ("finish_first", 2)
         shape = (9, n // 2 * rows, rows) if chunk < 3 else (9, rows, n // 2 * rows)
         written[axis], mark = finish(
@@ -577,24 +633,26 @@
         )
         last = (mark,)
 
-    def second_part(chunk):
+    def second_parts(offsets):
         nonlocal last
-        parts[chunk] = grad_second(chunk - 1, moved_cot, act_keep, act_other, last)
-        last = (parts[chunk],)
+        made = grad_second(offsets, moved_cot, act_keep, act_other, last)
+        for at, a in enumerate(offsets):
+            parts[a + 1] = made, 9 * at
+        last = (made,)
 
     def first_parts():
         nonlocal last
         own, other = done["dpre_halves"]
-        parts[3], parts[4], parts[5] = grad_first(
-            vol, vol_other, own, other, done["gain"], last
-        )
-        last = (parts[3],)
+        made = grad_first(vol, vol_other, own, other, done["gain"], last)
+        for at in range(3):
+            parts[3 + at] = made[at], 0
+        last = (made[0],)
 
     def norm_back():
         nonlocal last
         dpre, done["gain"] = pl.pallas_call(
             functools.partial(norm_back_kernel, n),
-            in_specs=[pl.BlockSpec(memory_space=pltpu.VMEM)] * (3 + n) + [UNREAD],
+            in_specs=[pl.BlockSpec(memory_space=pltpu.VMEM)] * (2 + n) + [UNREAD],
             out_shape=[
                 jax.ShapeDtypeStruct((CELLS, rows), BF16),
                 jax.ShapeDtypeStruct((1, rows), F32),
@@ -602,7 +660,7 @@
             compiler_params=pltpu.CompilerParams(vmem_limit_bytes=SMALL),
             cost_estimate=LIGHT,
             name="norm_back",
-        )(own_gain, normed, inverse, *dact_shares, *last)
+        )(own_gain, normed, inverse, done["dact"], *dact_shares[1:-1], *last)
         done["dpre"] = swap([dpre] * n)
         last = (dpre,)
 
@@ -624,31 +682,40 @@
         )
         last = (mark,)
 
-    def wave(at):
-        for step in range(steps):
-            if 0 <= at - step < 6:
-                line(at - step, step)
-        if 0 <= at - steps < 6:
-            write(at - steps)
-
     written, done = {}, {}
-    second_part(0)
-    second_part(1)
+    second_parts((-1,))
+    done["dact"] = sum_shares("dact_sum", dact_shares[0], dact_shares[-1], last)
+    last = (done["dact"],)
+    second_parts((0, 1))
     output()
     norm_back()
     line(0, 0)
-    second_part(2)
-    line(1, 0)
     line(0, 1)
     dpre_halves()
     first_parts()
-    wave(2)
-    wave(3)
-    wave(4)
-    wave(5)
+    line(1, 0)
+    line(2, 0)
+    line(0, 2)
+    line(1, 1)
+    line(3, 0)
+    line(2, 1)
+    line(1, 2)
+    write(0)
+    line(4, 0)
+    line(3, 1)
+    line(2, 2)
+    write(1)
+    line(5, 0)
+    line(4, 1)
+    line(3, 2)
+    write(2)
+    line(5, 1)
+    line(4, 2)
+    write(3)
+    write(4)
     grad_volume()
-    for at in range(6, 6 + steps):
-        wave(at)
+    line(5, 2)
+    write(5)
     gain_rows = totals[3][9 * rows : 9 * rows + 2, :rows].astype(F32)
     gain_rows_other = crossed[3][9 * rows : 9 * rows + 2, :rows].astype(F32)
     gain_total = (jnp.sum(gain_rows, axis=0) + jnp.sum(gain_rows_other, axis=0)) * factor

time: 180 us -> 198 us (1.10)
  starting transfers between devices: 66.7 us -> 78 us
  Pallas kernels: 60.5 us -> 67.8 us
    ppermute x10, starting transfers between devices: 16.4 us -> 28.1 us  [to_core(): lax.ppermute(x, 'dp', [(i, i ^ 1) for i in range(lax.axis_size('dp'))])]
    pallas_call x6 -> x8, Pallas kernels: 17.3 us -> 25.7 us  [the longest x3 19.5 us: spread_shares(): pl.pallas_call(functools.partial(share_kernel, n, sign, wanted), in_specs...]
    ppermute x18 -> x17, waiting for transfers between devices: 30.4 us -> 25.3 us  [line_send(): return lax.ppermute(x, 'dp', pairs)]
    ppermute x12, waiting for transfers between devices: 12.9 us -> 17.8 us  [to_partner(): return lax.ppermute(x, 'chan', [(i, i ^ m) for i in range(n)])]
    unnamed x28 -> x40, local copies, waits for them, and re-layouts: 4.63 us -> 2.69 us
    ppermute x18 -> x17, starting transfers between devices: 38.9 us -> 38.3 us  [line_send(): return lax.ppermute(x, 'dp', pairs)]
  transfers between devices with their start and end apart: 40 -> 39, of which waited for: 11 -> 14; matrix products, arithmetic and copies ran while one was open for 0% -> 0% of each run, Pallas kernels for 27% -> 28%
where the time goes in v8:
time: 198 us; the launch traced here: 197 us
  starting transfers between devices  78 us (39%)
  Pallas kernels  67.8 us (34%)
  waiting for transfers between devices  46 us (23%)
  local copies, waits for them, and re-layouts  2.77 us (1%)
    ppermute x17, starting transfers between devices, line_send(): return lax.ppermute(x, 'dp', pairs)  38.3 us
    ppermute x10, starting transfers between devices, to_core(): lax.ppermute(x, 'dp', [(i, i ^ 1) for i in range(lax.axis_size('dp'))])  28.1 us
    ppermute x17, waiting for transfers between devices, line_send(): return lax.ppermute(x, 'dp', pairs)  25.3 us
    pallas_call x3, Pallas kernels, spread_shares(): pl.pallas_call(functools.partial(share_kernel, n, sign, wanted), in_specs...  19.5 us
    ppermute x12, waiting for transfers between devices, to_partner(): return lax.ppermute(x, 'chan', [(i, i ^ m) for i in range(n)])  17.8 us
    pallas_call x2, Pallas kernels, conv_full(): pl.pallas_call(functools.partial(conv_kernel, n, sign, transposed), in_sp...  14.2 us
    pallas_call x6, Pallas kernels, finish(): pl.pallas_call(functools.partial(finish_kernel, n, axis, factor, chunk),...  12.7 us
    ppermute x12, starting transfers between devices, to_partner(): return lax.ppermute(x, 'chan', [(i, i ^ m) for i in range(n)])  11.6 us
  transfers between devices with their start and end apart: 39, of which 14 were waited for; matrix products, arithmetic and copies ran while one was open for 0% of the time, Pallas kernels for 28%

profile of v8, /device:TPU:1, one launch (start us, length us, event | category | flops | bytes accessed | tf_op | source)
XLA Modules:
  0.0 197.4 jit_solution(9207302156316062519)
XLA Ops:
  1.3 6.7 %pre_far.1 = (bf16[1024,128]{1,0:T(8,128)(2,1)}, bf16[1024,128]{1,0:T(8,128)(2,1)}) custom-call(s32[2]{0:T(128)} %pad_add_fusion.idx, bf16[128,1024]{1,0:T(8,128)(2,1)} %bitcast.3.field.vol_own, bf16[3456,512]{1,0:T(8,128)(2,1)} %bitcast.10), custom_call_target="tpu_custom_call" | custom-call | flops 1024 | bytes 1024 | tf_op jit(solution)/shard_map/pre_far/pallas_call | solution.py:118
  8.0 3.1 %collective-permute-start = (bf16[1024,128]{1,0:T(8,128)(2,1)}, bf16[1024,128]{1,0:T(8,128)(2,1)}, u32[]{:S(2)}, u32[]{:S(2)}) collective-permute-start(bf16[1024,128]{1,0:T(8,128)(2,1)} %get-tuple-element.42), channel_id=1, source_target_pairs={{0,3},{1,2},{2,1},{3,0},{4,7},{5,6},{6,5},{7,4},{8,11},{9,10},{10,... | collective-permute-start | bytes 786440 | tf_op jit(solution)/shard_map/ppermute | solution.py:538
  11.1 6.4 %pre_near.1 = (bf16[1024,128]{1,0:T(8,128)(2,1)}, bf16[1024,128]{1,0:T(8,128)(2,1)}) custom-call(s32[2]{0:T(128)} %pad_add_fusion.idx, bf16[128,1024]{1,0:T(8,128)(2,1)} %bitcast.3.field.vol_own, bf16[3456,512]{1,0:T(8,128)(2,1)} %bitcast.11, bf16[1024,128]{1,0:T(8,128)(2,1)} %get-tuple-element.40.refs_0_), custom_call_target="tpu_custom_call" | custom-call | flops 1024 | bytes 1024 | tf_op jit(solution)/shard_map/pre_near/pallas_call | solution.py:118
  21.2 3.6 %collective-permute-done.1.refs_1_ = bf16[1024,128]{1,0:T(8,128)(2,1)} collective-permute-done((bf16[1024,128]{1,0:T(8,128)(2,1)}, bf16[1024,128]{1,0:T(8,128)(2,1)}, u32[]{:S(2)}, u32[]{:S(2)}) %collective-permute-start.1) | collective-permute-done | bytes 262176 | tf_op jit(solution)/shard_map/ppermute | solution.py:538
  28.9 6.3 %dact.1 = (bf16[1024,128]{1,0:T(8,128)(2,1)S(1)}, bf16[1024,128]{1,0:T(8,128)(2,1)S(1)}, bf16[1024,128]{1,0:T(8,128)(2,1)S(1)}, bf16[1024,128]{1,0:T(8,128)(2,1)S(1)}) custom-call(s32[2]{0:T(128)S(1)} %copy-done.19, bf16[128,1024]{1,0:T(8,128)(2,1)} %bitcast.5.own.field, bf16[27,512,128]{2,1,0:T(8,128)(2,1)S(1)} %copy-done.2, ...), custom_call_target="tpu_custom_call" | custom-call | flops 1024 | bytes 1024 | tf_op jit(solution)/shard_map/dact/pallas_call | solution.py:118
  38.7 4.0 %collective-permute-start.8 = (bf16[256,1024]{1,0:T(8,128)(2,1)S(1)}, bf16[256,1024]{1,0:T(8,128)(2,1)S(1)}, u32[]{:S(2)}, u32[]{:S(2)}) collective-permute-start(bf16[256,1024]{1,0:T(8,128)(2,1)S(1)} %get-tuple-element.47), channel_id=1, source_target_pairs={{0,4},{4,0},{8,12},{12,8},{16,20},{20,16},{24,28},{28,24},{1,5},{5... | collective-permute-start | bytes 1572872 | tf_op jit(solution)/shard_map/ppermute | solution.py:541
  45.5 3.4 %collective-permute-start.15 = (bf16[9,256,128]{2,1,0:T(8,128)(2,1)S(1)}, bf16[9,256,128]{2,1,0:T(8,128)(2,1)S(1)}, u32[]{:S(2)}, u32[]{:S(2)}) collective-permute-start(bf16[9,256,128]{2,1,0:T(8,128)(2,1)S(1)} %grad_second.2.refs_0_.x), channel_id=1, source_target_pairs={{0,8},{4,12},{24,16},{28,20},{1,9},{5,13},{25,17},{29,21},{2,10},{... | collective-permute-start | bytes 1769480 | tf_op jit(solution)/shard_map/ppermute | solution.py:511
  51.6 5.5 %collective-permute-done.9.y = bf16[1024,128]{1,0:T(8,128)(2,1)S(1)} collective-permute-done((bf16[1024,128]{1,0:T(8,128)(2,1)S(1)}, bf16[1024,128]{1,0:T(8,128)(2,1)S(1)}, u32[]{:S(2)}, u32[]{:S(2)}) %collective-permute-start.9) | collective-permute-done | bytes 262176 | tf_op jit(solution)/shard_map/ppermute | solution.py:538
  57.1 2.5 %grad_second.3.refs_4_.x = bf16[18,256,128]{2,1,0:T(8,128)(2,1)S(1)} custom-call(bf16[2,3,4,18,16,128]{5,4,3,2,1,0:T(8,128)(2,1)S(1)} %moved_second.1.refs_4_.moved, bf16[256,1024]{1,0:T(8,128)(2,1)S(1)} %get-tuple-element.46.own, bf16[256,1024]{1,0:T(8,128)(2,1)S(1)} %collective-permute-done.8.other, f32[1024,128]{1,0:T(8,128)S(1)} %dact_sum.1.refs_0_), custom_call_target="tpu_custom_call" | custom-call | flops 1024 | bytes 1024 | tf_op jit(solution)/shard_map/grad_second/pallas_call | solution.py:408
  61.4 7.1 %output.1 = (bf16[128,1024]{1,0:T(8,128)(2,1)}, f32[8,128]{1,0:T(8,128)S(1)}) custom-call(s32[2]{0:T(128)S(1)} %copy-done.19, bf16[27,512,128]{2,1,0:T(8,128)(2,1)S(1)} %copy-done.3, bf16[1024,128]{1,0:T(8,128)(2,1)S(1)} %get-tuple-element.44._.refs_0_, bf16[1024,128]{1,0:T(8,128)(2,1)S(1)} %collective-permute-done.3.refs_1_, ...), custom_call_target="tpu_custom_call" | custom-call | flops 1024 | bytes 1024 | tf_op jit(solution)/shard_map/output/pallas_call | solution.py:237
  72.8 2.4 %collective-permute-done.12.refs_1_ = bf16[1024,128]{1,0:T(8,128)(2,1)S(1)} collective-permute-done((bf16[1024,128]{1,0:T(8,128)(2,1)S(1)}, bf16[1024,128]{1,0:T(8,128)(2,1)S(1)}, u32[]{:S(2)}, u32[]{:S(2)}) %collective-permute-start.12) | collective-permute-done | bytes 262176 | tf_op jit(solution)/shard_map/ppermute | solution.py:538
  76.2 4.5 %collective-permute-done.14.refs_3_ = bf16[1024,128]{1,0:T(8,128)(2,1)S(1)} collective-permute-done((bf16[1024,128]{1,0:T(8,128)(2,1)S(1)}, bf16[1024,128]{1,0:T(8,128)(2,1)S(1)}, u32[]{:S(2)}, u32[]{:S(2)}) %collective-permute-start.14) | collective-permute-done | bytes 262176 | tf_op jit(solution)/shard_map/ppermute | solution.py:538
  81.3 4.0 %collective-permute-start.17 = (bf16[2,1024,128]{2,1,0:T(8,128)(2,1)S(1)}, bf16[2,1024,128]{2,1,0:T(8,128)(2,1)S(1)}, u32[]{:S(2)}, u32[]{:S(2)}) collective-permute-start(bf16[2,1024,128]{2,1,0:T(8,128)(2,1)S(1)} %get-tuple-element.57), channel_id=1, source_target_pairs={{0,4},{4,0},{8,12},{12,8},{16,20},{20,16},{24,28},{28,24},{1,5},{5... | collective-permute-start | bytes 1572872 | tf_op jit(solution)/shard_map/ppermute | solution.py:541
  86.9 4.4 %grad_first.1 = (bf16[1168,256]{1,0:T(8,128)(2,1)S(1)}, bf16[1168,256]{1,0:T(8,128)(2,1)S(1)}, bf16[1168,256]{1,0:T(8,128)(2,1)S(1)}) custom-call(bf16[128,1024]{1,0:T(8,128)(2,1)} %bitcast.3.field.vol_own, bf16[128,1024]{1,0:T(8,128)(2,1)} %collective-permute-done.7.refs_5_.vol_other, bf16[2,1024,128]{2,1,0:T(8,128)(2,1)S(1)} %get-tuple-element.56.own.refs_0_, ...), custom_call_target="tpu_custom_call" | custom-call | flops 1024 | bytes 1024 | tf_op jit(solution)/shard_map/grad_first/pallas_call | solution.py:370
  94.6 6.5 %collective-permute-start.25 = (bf16[1168,256]{1,0:T(8,128)(2,1)}, bf16[1168,256]{1,0:T(8,128)(2,1)S(1)}, u32[]{:S(2)}, u32[]{:S(2)}) collective-permute-start(bf16[1168,256]{1,0:T(8,128)(2,1)} %copy-done.4), channel_id=1, source_target_pairs={{0,8},{4,12},{24,16},{28,20},{1,9},{5,13},{25,17},{29,21},{2,10},{... | collective-permute-start | bytes 1794056 | tf_op jit(solution)/shard_map/ppermute | solution.py:511
  108.4 5.3 %collective-permute-done.25.y = bf16[1168,256]{1,0:T(8,128)(2,1)S(1)} collective-permute-done((bf16[1168,256]{1,0:T(8,128)(2,1)}, bf16[1168,256]{1,0:T(8,128)(2,1)S(1)}, u32[]{:S(2)}, u32[]{:S(2)}) %collective-permute-start.25) | collective-permute-done | bytes 598048 | tf_op jit(solution)/shard_map/ppermute | solution.py:511
  114.5 12.3 %collective-permute-start.27 = (bf16[1168,256]{1,0:T(8,128)(2,1)S(1)}, bf16[1168,256]{1,0:T(8,128)(2,1)S(1)}, u32[]{:S(2)}, u32[]{:S(2)}) collective-permute-start(bf16[1168,256]{1,0:T(8,128)(2,1)S(1)} %copy-done.15), channel_id=1, source_target_pairs={{0,8},{4,12},{24,16},{28,20},{1,9},{5,13},{25,17},{29,21},{2,10},{... | collective-permute-start | bytes 1794056 | tf_op jit(solution)/shard_map/ppermute | solution.py:511
  127.6 2.0 %finish_second.3 = (f32[27,512,128]{2,1,0:T(8,128)}, f32[8,128]{1,0:T(8,128)S(1)}) custom-call(s32[2]{0:T(128)S(1)} %copy-done.19, bf16[9,256,128]{2,1,0:T(8,128)(2,1)S(1)} %line_pick.6.refs_0_.own, bf16[9,256,128]{2,1,0:T(8,128)(2,1)S(1)} %collective-permute-done.21.other, bf16[9,256,128]{2,1,0:T(8,128)(2,1)S(1)} %line_pick.7.refs_0_.own), custom_call_target="tpu_custom_call" | custom-call | flops 1024 | bytes 1024 | tf_op jit(solution)/shard_map/finish_second/pallas_call | solution.py:449
  131.8 2.2 %collective-permute-start.28 = (bf16[9,256,128]{2,1,0:T(8,128)(2,1)S(1)}, bf16[9,256,128]{2,1,0:T(8,128)(2,1)S(1)}, u32[]{:S(2)}, u32[]{:S(2)}) collective-permute-start(bf16[9,256,128]{2,1,0:T(8,128)(2,1)S(1)} %line_pick.7.refs_0_.own), channel_id=1, source_target_pairs={{0,4},{4,0},{8,12},{12,8},{16,20},{20,16},{24,28},{28,24},{1,5},{5... | collective-permute-start | bytes 1769480 | tf_op jit(solution)/shard_map/ppermute | solution.py:541
  135.5 9.5 %collective-permute-done.29.y = bf16[9,256,128]{2,1,0:T(8,128)(2,1)S(1)} collective-permute-done((bf16[9,256,128]{2,1,0:T(8,128)(2,1)S(1)}, bf16[9,256,128]{2,1,0:T(8,128)(2,1)S(1)}, u32[]{:S(2)}, u32[]{:S(2)}) %collective-permute-start.29) | collective-permute-done | bytes 589856 | tf_op jit(solution)/shard_map/ppermute | solution.py:511
  145.7 2.0 %finish_second.4 = (f32[27,512,128]{2,1,0:T(8,128)}, f32[8,128]{1,0:T(8,128)S(1)}) custom-call(s32[2]{0:T(128)S(1)} %copy-done.19, bf16[9,256,128]{2,1,0:T(8,128)(2,1)S(1)} %line_pick.7.refs_0_.own, bf16[9,256,128]{2,1,0:T(8,128)(2,1)S(1)} %collective-permute-done.28.other, ...), custom_call_target="tpu_custom_call", output_to_operand_aliasing={{0}: (3, {})} | custom-call | flops 1024 | bytes 1024 | tf_op jit(solution)/shard_map/finish_second/pallas_call | solution.py:449
  150.1 5.9 %collective-permute-start.33 = (bf16[9,256,128]{2,1,0:T(8,128)(2,1)S(1)}, bf16[9,256,128]{2,1,0:T(8,128)(2,1)S(1)}, u32[]{:S(2)}, u32[]{:S(2)}) collective-permute-start(bf16[9,256,128]{2,1,0:T(8,128)(2,1)S(1)} %line_pick.8.refs_1_.own), channel_id=1, source_target_pairs={{0,4},{4,0},{8,12},{12,8},{16,20},{20,16},{24,28},{28,24},{1,5},{5... | collective-permute-start | bytes 1769480 | tf_op jit(solution)/shard_map/ppermute | solution.py:541
  155.9 2.0 %collective-permute-done.34.y = bf16[1168,256]{1,0:T(8,128)(2,1)S(1)} collective-permute-done((bf16[1168,256]{1,0:T(8,128)(2,1)S(1)}, bf16[1168,256]{1,0:T(8,128)(2,1)S(1)}, u32[]{:S(2)}, u32[]{:S(2)}) %collective-permute-start.34) | collective-permute-done | bytes 598048 | tf_op jit(solution)/shard_map/ppermute | solution.py:511
  158.5 5.9 %collective-permute-start.36 = (bf16[1168,256]{1,0:T(8,128)(2,1)S(1)}, bf16[1168,256]{1,0:T(8,128)(2,1)S(1)}, u32[]{:S(2)}, u32[]{:S(2)}) collective-permute-start(bf16[1168,256]{1,0:T(8,128)(2,1)S(1)} %line_pick.9.refs_1_.own), channel_id=1, source_target_pairs={{0,4},{4,0},{8,12},{12,8},{16,20},{20,16},{24,28},{28,24},{1,5},{5... | collective-permute-start | bytes 1794056 | tf_op jit(solution)/shard_map/ppermute | solution.py:541
  164.4 2.0 %finish_second.5 = (f32[27,512,128]{2,1,0:T(8,128)}, f32[8,128]{1,0:T(8,128)S(1)}) custom-call(s32[2]{0:T(128)S(1)} %copy-done.19, bf16[9,256,128]{2,1,0:T(8,128)(2,1)S(1)} %line_pick.8.refs_1_.own, bf16[9,256,128]{2,1,0:T(8,128)(2,1)S(1)} %collective-permute-done.33.other, ...), custom_call_target="tpu_custom_call", output_to_operand_aliasing={{0}: (3, {})} | custom-call | flops 1024 | bytes 1024 | tf_op jit(solution)/shard_map/finish_second/pallas_call | solution.py:449
  166.6 4.1 %collective-permute-done.31.y = bf16[1168,256]{1,0:T(8,128)(2,1)S(1)} collective-permute-done((bf16[1168,256]{1,0:T(8,128)(2,1)S(1)}, bf16[1168,256]{1,0:T(8,128)(2,1)S(1)}, u32[]{:S(2)}, u32[]{:S(2)}) %collective-permute-start.31) | collective-permute-done | bytes 598048 | tf_op jit(solution)/shard_map/ppermute | solution.py:511
  171.3 3.2 %collective-permute-start.35 = (bf16[1168,256]{1,0:T(8,128)(2,1)S(1)}, bf16[1168,256]{1,0:T(8,128)(2,1)S(1)}, u32[]{:S(2)}, u32[]{:S(2)}) collective-permute-start(bf16[1168,256]{1,0:T(8,128)(2,1)S(1)} %line_pick.10.refs_0_.own), channel_id=1, source_target_pairs={{0,4},{4,0},{8,12},{12,8},{16,20},{20,16},{24,28},{28,24},{1,5},{5... | collective-permute-start | bytes 1794056 | tf_op jit(solution)/shard_map/ppermute | solution.py:541
  175.8 2.0 %finish_first.3 = (f32[27,128,512]{2,1,0:T(8,128)}, f32[8,128]{1,0:T(8,128)S(1)}) custom-call(s32[2]{0:T(128)S(1)} %copy-done.19, bf16[1168,256]{1,0:T(8,128)(2,1)S(1)} %line_pick.9.refs_1_.own, bf16[1168,256]{1,0:T(8,128)(2,1)S(1)} %collective-permute-done.36.other, bf16[1168,256]{1,0:T(8,128)(2,1)S(1)} %line_pick.10.refs_0_.own), custom_call_target="tpu_custom_call" | custom-call | flops 1024 | bytes 1024 | tf_op jit(solution)/shard_map/finish_first/pallas_call | solution.py:449
  177.8 2.0 %finish_first.4 = (f32[27,128,512]{2,1,0:T(8,128)}, f32[8,128]{1,0:T(8,128)S(1)}) custom-call(s32[2]{0:T(128)S(1)} %copy-done.19, bf16[1168,256]{1,0:T(8,128)(2,1)S(1)} %line_pick.10.refs_0_.own, bf16[1168,256]{1,0:T(8,128)(2,1)S(1)} %collective-permute-done.35.other, f32[27,128,512]{2,1,0:T(8,128)} %get-tuple-element.67.refs_0_, ...), custom_call_target="tpu_custom_call", output_to_operand_aliasing={{0}: (3, {})} | custom-call | flops 1024 | bytes 1024 | tf_op jit(solution)/shard_map/finish_first/pallas_call | solution.py:449
  179.9 7.2 %grad_volume.1 = (bf16[128,1024]{1,0:T(8,128)(2,1)}, f32[8,128]{1,0:T(8,128)S(1)}) custom-call(s32[2]{0:T(128)S(1)} %copy-done.19, bf16[3456,512]{1,0:T(8,128)(2,1)S(1)} %bitcast.12, bf16[1024,128]{1,0:T(8,128)(2,1)S(1)} %copy-done.7, bf16[1024,128]{1,0:T(8,128)(2,1)S(1)} %copy-done.9, bf16[1024,128]{1,0:T(8,128)(2,1)S(1)} %copy-done.11, ...), custom_call_target="tpu_custom_call" | custom-call | flops 1024 | bytes 1024 | tf_op jit(solution)/shard_map/grad_volume/pallas_call | solution.py:237
  187.1 4.4 %collective-permute-done.37.y = bf16[1168,256]{1,0:T(8,128)(2,1)S(1)} collective-permute-done((bf16[1168,256]{1,0:T(8,128)(2,1)S(1)}, bf16[1168,256]{1,0:T(8,128)(2,1)S(1)}, u32[]{:S(2)}, u32[]{:S(2)}) %collective-permute-start.37) | collective-permute-done | bytes 598048 | tf_op jit(solution)/shard_map/ppermute | solution.py:511
  194.6 2.6 %finish_first.5 = (f32[27,128,512]{2,1,0:T(8,128)}, f32[8,128]{1,0:T(8,128)}) custom-call(s32[2]{0:T(128)S(1)} %copy-done.19, bf16[1168,256]{1,0:T(8,128)(2,1)S(1)} %line_pick.11.own.refs_1_, bf16[1168,256]{1,0:T(8,128)(2,1)S(1)} %collective-permute-done.38.other, f32[27,128,512]{2,1,0:T(8,128)} %get-tuple-element.72.refs_0_, ...), custom_call_target="tpu_custom_call", output_to_operand_aliasing={{0}: (3, {})} | custom-call | flops 1024 | bytes 1024 | tf_op jit(solution)/shard_map/finish_first/pallas_call | solution.py:449
  (131 shorter events, 50.7 us)
Async XLA Ops:
  8.0 11.2 %collective-permute-start = (bf16[1024,128]{1,0:T(8,128)(2,1)}, bf16[1024,128]{1,0:T(8,128)(2,1)}, u32[]{:S(2)}, u32[]{:S(2)}) collective-permute-start(bf16[1024,128]{1,0:T(8,128)(2,1)} %get-tuple-element.42), channel_id=1, source_target_pairs={{0,3},{1,2},{2,1},{3,0},{4,7},{5,6},{6,5},{7,4},{8,11},{9,10},{10,... | collective-permute-start | bytes 786440 | tf_op jit(solution)/shard_map/ppermute | solution.py:538
  17.5 7.2 %collective-permute-start.1 = (bf16[1024,128]{1,0:T(8,128)(2,1)}, bf16[1024,128]{1,0:T(8,128)(2,1)}, u32[]{:S(2)}, u32[]{:S(2)}) collective-permute-start(bf16[1024,128]{1,0:T(8,128)(2,1)} %get-tuple-element.43), channel_id=1, source_target_pairs={{0,1},{1,0},{2,3},{3,2},{4,5},{5,4},{6,7},{7,6},{8,9},{9,8},{10,11... | collective-permute-start | bytes 786440 | tf_op jit(solution)/shard_map/ppermute | solution.py:538
  17.8 6.9 %collective-permute-start.2 = (bf16[1024,128]{1,0:T(8,128)(2,1)}, bf16[1024,128]{1,0:T(8,128)(2,1)}, u32[]{:S(2)}, u32[]{:S(2)}) collective-permute-start(bf16[1024,128]{1,0:T(8,128)(2,1)} %get-tuple-element.40.refs_0_), channel_id=1, source_target_pairs={{0,2},{1,3},{2,0},{3,1},{4,6},{5,7},{6,4},{7,5},{8,10},{9,11},{10,... | collective-permute-start | bytes 786440 | tf_op jit(solution)/shard_map/ppermute | solution.py:538
  17.9 19.1 %collective-permute-start.7 = (bf16[128,1024]{1,0:T(8,128)(2,1)}, bf16[128,1024]{1,0:T(8,128)(2,1)}, u32[]{:S(2)}, u32[]{:S(2)}) collective-permute-start(bf16[128,1024]{1,0:T(8,128)(2,1)} %bitcast.3.field.vol_own), channel_id=1, source_target_pairs={{0,4},{4,0},{8,12},{12,8},{16,20},{20,16},{24,28},{28,24},{1,5},{5... | collective-permute-start | bytes 786440 | tf_op jit(solution)/shard_map/ppermute | solution.py:541
  19.1 16.1 %collective-permute-start.6 = (bf16[128,1024]{1,0:T(8,128)(2,1)}, bf16[128,1024]{1,0:T(8,128)(2,1)}, u32[]{:S(2)}, u32[]{:S(2)}) collective-permute-start(bf16[128,1024]{1,0:T(8,128)(2,1)} %bitcast.5.own.field), channel_id=1, source_target_pairs={{0,4},{4,0},{8,12},{12,8},{16,20},{20,16},{24,28},{28,24},{1,5},{5... | collective-permute-start | bytes 786440 | tf_op jit(solution)/shard_map/ppermute | solution.py:541
  26.2 10.8 %collective-permute-start.3 = (bf16[1024,128]{1,0:T(8,128)(2,1)S(1)}, bf16[1024,128]{1,0:T(8,128)(2,1)S(1)}, u32[]{:S(2)}, u32[]{:S(2)}) collective-permute-start(bf16[1024,128]{1,0:T(8,128)(2,1)S(1)} %get-tuple-element.44._.refs_0_), channel_id=1, source_target_pairs={{0,1},{1,0},{2,3},{3,2},{4,5},{5,4},{6,7},{7,6},{8,9},{9,8},{10,11... | collective-permute-start | bytes 786440 | tf_op jit(solution)/shard_map/ppermute | solution.py:538
  27.4 9.6 %collective-permute-start.4 = (bf16[1024,128]{1,0:T(8,128)(2,1)S(1)}, bf16[1024,128]{1,0:T(8,128)(2,1)S(1)}, u32[]{:S(2)}, u32[]{:S(2)}) collective-permute-start(bf16[1024,128]{1,0:T(8,128)(2,1)S(1)} %get-tuple-element.44._.refs_0_), channel_id=1, source_target_pairs={{0,2},{1,3},{2,0},{3,1},{4,6},{5,7},{6,4},{7,5},{8,10},{9,11},{10,... | collective-permute-start | bytes 786440 | tf_op jit(solution)/shard_map/ppermute | solution.py:538
  27.7 10.2 %collective-permute-start.5 = (bf16[1024,128]{1,0:T(8,128)(2,1)S(1)}, bf16[1024,128]{1,0:T(8,128)(2,1)S(1)}, u32[]{:S(2)}, u32[]{:S(2)}) collective-permute-start(bf16[1024,128]{1,0:T(8,128)(2,1)S(1)} %get-tuple-element.44._.refs_0_), channel_id=1, source_target_pairs={{0,3},{1,2},{2,1},{3,0},{4,7},{5,6},{6,5},{7,4},{8,11},{9,10},{10,... | collective-permute-start | bytes 786440 | tf_op jit(solution)/shard_map/ppermute | solution.py:538
  45.5 23.6 %collective-permute-start.15 = (bf16[9,256,128]{2,1,0:T(8,128)(2,1)S(1)}, bf16[9,256,128]{2,1,0:T(8,128)(2,1)S(1)}, u32[]{:S(2)}, u32[]{:S(2)}) collective-permute-start(bf16[9,256,128]{2,1,0:T(8,128)(2,1)S(1)} %grad_second.2.refs_0_.x), channel_id=1, source_target_pairs={{0,8},{4,12},{24,16},{28,20},{1,9},{5,13},{25,17},{29,21},{2,10},{... | collective-permute-start | bytes 1769480 | tf_op jit(solution)/shard_map/ppermute | solution.py:511
  48.9 8.2 %collective-permute-start.9 = (bf16[1024,128]{1,0:T(8,128)(2,1)S(1)}, bf16[1024,128]{1,0:T(8,128)(2,1)S(1)}, u32[]{:S(2)}, u32[]{:S(2)}) collective-permute-start(bf16[1024,128]{1,0:T(8,128)(2,1)S(1)} %get-tuple-element.48), channel_id=1, source_target_pairs={{0,3},{1,2},{2,1},{3,0},{4,7},{5,6},{6,5},{7,4},{8,11},{9,10},{10,... | collective-permute-start | bytes 786440 | tf_op jit(solution)/shard_map/ppermute | solution.py:538
  49.8 18.6 %collective-permute-start.10 = (bf16[1024,128]{1,0:T(8,128)(2,1)S(1)}, bf16[1024,128]{1,0:T(8,128)(2,1)S(1)}, u32[]{:S(2)}, u32[]{:S(2)}) collective-permute-start(bf16[1024,128]{1,0:T(8,128)(2,1)S(1)} %get-tuple-element.52), channel_id=1, source_target_pairs={{0,1},{1,0},{2,3},{3,2},{4,5},{5,4},{6,7},{7,6},{8,9},{9,8},{10,11... | collective-permute-start | bytes 786440 | tf_op jit(solution)/shard_map/ppermute | solution.py:538
  50.4 18.1 %collective-permute-start.11 = (bf16[1024,128]{1,0:T(8,128)(2,1)S(1)}, bf16[1024,128]{1,0:T(8,128)(2,1)S(1)}, u32[]{:S(2)}, u32[]{:S(2)}) collective-permute-start(bf16[1024,128]{1,0:T(8,128)(2,1)S(1)} %get-tuple-element.53), channel_id=1, source_target_pairs={{0,2},{1,3},{2,0},{3,1},{4,6},{5,7},{6,4},{7,5},{8,10},{9,11},{10,... | collective-permute-start | bytes 786440 | tf_op jit(solution)/shard_map/ppermute | solution.py:538
  59.7 31.6 %collective-permute-start.20 = (bf16[18,256,128]{2,1,0:T(8,128)(2,1)S(1)}, bf16[18,256,128]{2,1,0:T(8,128)(2,1)S(1)}, u32[]{:S(2)}, u32[]{:S(2)}) collective-permute-start(bf16[18,256,128]{2,1,0:T(8,128)(2,1)S(1)} %grad_second.3.refs_4_.x), channel_id=1, source_target_pairs={{0,8},{4,12},{24,16},{28,20},{1,9},{5,13},{25,17},{29,21},{2,10},{... | collective-permute-start | bytes 3538952 | tf_op jit(solution)/shard_map/ppermute | solution.py:511
  71.1 9.6 %collective-permute-start.14 = (bf16[1024,128]{1,0:T(8,128)(2,1)S(1)}, bf16[1024,128]{1,0:T(8,128)(2,1)S(1)}, u32[]{:S(2)}, u32[]{:S(2)}) collective-permute-start(bf16[1024,128]{1,0:T(8,128)(2,1)S(1)} %get-tuple-element.55.refs_0_), channel_id=1, source_target_pairs={{0,3},{1,2},{2,1},{3,0},{4,7},{5,6},{6,5},{7,4},{8,11},{9,10},{10,... | collective-permute-start | bytes 786440 | tf_op jit(solution)/shard_map/ppermute | solution.py:538
  85.3 18.4 %collective-permute-start.19 = (bf16[9,256,128]{2,1,0:T(8,128)(2,1)S(1)}, bf16[9,256,128]{2,1,0:T(8,128)(2,1)}, u32[]{:S(2)}, u32[]{:S(2)}) collective-permute-start(bf16[9,256,128]{2,1,0:T(8,128)(2,1)S(1)} %line_add.13.refs_4_.x), channel_id=1, source_target_pairs={{8,0},{12,4},{16,24},{20,28},{9,1},{13,5},{17,25},{21,29},{10,2},{... | collective-permute-start | bytes 1769480 | tf_op jit(solution)/shard_map/ppermute | solution.py:511
  93.1 11.8 %collective-permute-start.22 = (bf16[9,256,128]{2,1,0:T(8,128)(2,1)S(1)}, bf16[9,256,128]{2,1,0:T(8,128)(2,1)}, u32[]{:S(2)}, u32[]{:S(2)}) collective-permute-start(bf16[9,256,128]{2,1,0:T(8,128)(2,1)S(1)} %line_add.14.refs_0_.x), channel_id=1, source_target_pairs={{8,16},{12,20},{16,8},{20,12},{9,17},{13,21},{17,9},{21,13},{10,18... | collective-permute-start | bytes 1769480 | tf_op jit(solution)/shard_map/ppermute | solution.py:511
  94.6 19.0 %collective-permute-start.25 = (bf16[1168,256]{1,0:T(8,128)(2,1)}, bf16[1168,256]{1,0:T(8,128)(2,1)S(1)}, u32[]{:S(2)}, u32[]{:S(2)}) collective-permute-start(bf16[1168,256]{1,0:T(8,128)(2,1)} %copy-done.4), channel_id=1, source_target_pairs={{0,8},{4,12},{24,16},{28,20},{1,9},{5,13},{25,17},{29,21},{2,10},{... | collective-permute-start | bytes 1794056 | tf_op jit(solution)/shard_map/ppermute | solution.py:511
  101.1 28.6 %collective-permute-start.18 = (bf16[1168,256]{1,0:T(8,128)(2,1)}, bf16[1168,256]{1,0:T(8,128)(2,1)S(1)}, u32[]{:S(2)}, u32[]{:S(2)}) collective-permute-start(bf16[1168,256]{1,0:T(8,128)(2,1)} %copy-done.16), channel_id=1, source_target_pairs={{0,8},{4,12},{24,16},{28,20},{1,9},{5,13},{25,17},{29,21},{2,10},{... | collective-permute-start | bytes 1794056 | tf_op jit(solution)/shard_map/ppermute | solution.py:511
  102.7 11.8 %collective-permute-start.24 = (bf16[9,256,128]{2,1,0:T(8,128)(2,1)S(1)}, bf16[9,256,128]{2,1,0:T(8,128)(2,1)S(1)}, u32[]{:S(2)}, u32[]{:S(2)}) collective-permute-start(bf16[9,256,128]{2,1,0:T(8,128)(2,1)S(1)} %line_add.15.refs_0_.x), channel_id=1, source_target_pairs={{8,16},{12,20},{16,8},{20,12},{9,17},{13,21},{17,9},{21,13},{10,18... | collective-permute-start | bytes 1769480 | tf_op jit(solution)/shard_map/ppermute | solution.py:511
  106.1 20.9 %collective-permute-start.23 = (bf16[9,256,128]{2,1,0:T(8,128)(2,1)S(1)}, bf16[9,256,128]{2,1,0:T(8,128)(2,1)S(1)}, u32[]{:S(2)}, u32[]{:S(2)}) collective-permute-start(bf16[9,256,128]{2,1,0:T(8,128)(2,1)S(1)} %line_add.16.refs_0_.x), channel_id=1, source_target_pairs={{8,0},{12,4},{16,24},{20,28},{9,1},{13,5},{17,25},{21,29},{10,2},{... | collective-permute-start | bytes 1769480 | tf_op jit(solution)/shard_map/ppermute | solution.py:511
  107.4 20.2 %collective-permute-start.21 = (bf16[9,256,128]{2,1,0:T(8,128)(2,1)S(1)}, bf16[9,256,128]{2,1,0:T(8,128)(2,1)S(1)}, u32[]{:S(2)}, u32[]{:S(2)}) collective-permute-start(bf16[9,256,128]{2,1,0:T(8,128)(2,1)S(1)} %line_pick.6.refs_0_.own), channel_id=1, source_target_pairs={{0,4},{4,0},{8,12},{12,8},{16,20},{20,16},{24,28},{28,24},{1,5},{5... | collective-permute-start | bytes 1769480 | tf_op jit(solution)/shard_map/ppermute | solution.py:541
  113.8 20.3 %collective-permute-start.30 = (bf16[1168,256]{1,0:T(8,128)(2,1)S(1)}, bf16[1168,256]{1,0:T(8,128)(2,1)S(1)}, u32[]{:S(2)}, u32[]{:S(2)}) collective-permute-start(bf16[1168,256]{1,0:T(8,128)(2,1)S(1)} %line_add.17.refs_0_.x), channel_id=1, source_target_pairs={{8,16},{12,20},{16,8},{20,12},{9,17},{13,21},{17,9},{21,13},{10,18... | collective-permute-start | bytes 1794056 | tf_op jit(solution)/shard_map/ppermute | solution.py:511
  114.5 33.2 %collective-permute-start.27 = (bf16[1168,256]{1,0:T(8,128)(2,1)S(1)}, bf16[1168,256]{1,0:T(8,128)(2,1)S(1)}, u32[]{:S(2)}, u32[]{:S(2)}) collective-permute-start(bf16[1168,256]{1,0:T(8,128)(2,1)S(1)} %copy-done.15), channel_id=1, source_target_pairs={{0,8},{4,12},{24,16},{28,20},{1,9},{5,13},{25,17},{29,21},{2,10},{... | collective-permute-start | bytes 1794056 | tf_op jit(solution)/shard_map/ppermute | solution.py:511
  129.8 18.8 %collective-permute-start.26 = (bf16[1168,256]{1,0:T(8,128)(2,1)S(1)}, bf16[1168,256]{1,0:T(8,128)(2,1)S(1)}, u32[]{:S(2)}, u32[]{:S(2)}) collective-permute-start(bf16[1168,256]{1,0:T(8,128)(2,1)S(1)} %line_add.19.refs_0_.x), channel_id=1, source_target_pairs={{8,16},{12,20},{16,8},{20,12},{9,17},{13,21},{17,9},{21,13},{10,18... | collective-permute-start | bytes 1794056 | tf_op jit(solution)/shard_map/ppermute | solution.py:511
  130.5 14.5 %collective-permute-start.29 = (bf16[9,256,128]{2,1,0:T(8,128)(2,1)S(1)}, bf16[9,256,128]{2,1,0:T(8,128)(2,1)S(1)}, u32[]{:S(2)}, u32[]{:S(2)}) collective-permute-start(bf16[9,256,128]{2,1,0:T(8,128)(2,1)S(1)} %line_add.18.refs_0_.x), channel_id=1, source_target_pairs={{8,0},{12,4},{16,24},{20,28},{9,1},{13,5},{17,25},{21,29},{10,2},{... | collective-permute-start | bytes 1769480 | tf_op jit(solution)/shard_map/ppermute | solution.py:511
  131.8 13.8 %collective-permute-start.28 = (bf16[9,256,128]{2,1,0:T(8,128)(2,1)S(1)}, bf16[9,256,128]{2,1,0:T(8,128)(2,1)S(1)}, u32[]{:S(2)}, u32[]{:S(2)}) collective-permute-start(bf16[9,256,128]{2,1,0:T(8,128)(2,1)S(1)} %line_pick.7.refs_0_.own), channel_id=1, source_target_pairs={{0,4},{4,0},{8,12},{12,8},{16,20},{20,16},{24,28},{28,24},{1,5},{5... | collective-permute-start | bytes 1769480 | tf_op jit(solution)/shard_map/ppermute | solution.py:541
  134.2 23.7 %collective-permute-start.34 = (bf16[1168,256]{1,0:T(8,128)(2,1)S(1)}, bf16[1168,256]{1,0:T(8,128)(2,1)S(1)}, u32[]{:S(2)}, u32[]{:S(2)}) collective-permute-start(bf16[1168,256]{1,0:T(8,128)(2,1)S(1)} %line_add.20.refs_0_.x), channel_id=1, source_target_pairs={{8,0},{12,4},{16,24},{20,28},{9,1},{13,5},{17,25},{21,29},{10,2},{... | collective-permute-start | bytes 1794056 | tf_op jit(solution)/shard_map/ppermute | solution.py:511
  147.9 18.5 %collective-permute-start.32 = (bf16[1168,256]{1,0:T(8,128)(2,1)S(1)}, bf16[1168,256]{1,0:T(8,128)(2,1)S(1)}, u32[]{:S(2)}, u32[]{:S(2)}) collective-permute-start(bf16[1168,256]{1,0:T(8,128)(2,1)S(1)} %line_add.21.refs_0_.x), channel_id=1, source_target_pairs={{8,16},{12,20},{16,8},{20,12},{9,17},{13,21},{17,9},{21,13},{10,18... | collective-permute-start | bytes 1794056 | tf_op jit(solution)/shard_map/ppermute | solution.py:511
  148.8 21.9 %collective-permute-start.31 = (bf16[1168,256]{1,0:T(8,128)(2,1)S(1)}, bf16[1168,256]{1,0:T(8,128)(2,1)S(1)}, u32[]{:S(2)}, u32[]{:S(2)}) collective-permute-start(bf16[1168,256]{1,0:T(8,128)(2,1)S(1)} %line_add.22.refs_0_.x), channel_id=1, source_target_pairs={{8,0},{12,4},{16,24},{20,28},{9,1},{13,5},{17,25},{21,29},{10,2},{... | collective-permute-start | bytes 1794056 | tf_op jit(solution)/shard_map/ppermute | solution.py:511
  150.1 14.3 %collective-permute-start.33 = (bf16[9,256,128]{2,1,0:T(8,128)(2,1)S(1)}, bf16[9,256,128]{2,1,0:T(8,128)(2,1)S(1)}, u32[]{:S(2)}, u32[]{:S(2)}) collective-permute-start(bf16[9,256,128]{2,1,0:T(8,128)(2,1)S(1)} %line_pick.8.refs_1_.own), channel_id=1, source_target_pairs={{0,4},{4,0},{8,12},{12,8},{16,20},{20,16},{24,28},{28,24},{1,5},{5... | collective-permute-start | bytes 1769480 | tf_op jit(solution)/shard_map/ppermute | solution.py:541
  158.5 17.3 %collective-permute-start.36 = (bf16[1168,256]{1,0:T(8,128)(2,1)S(1)}, bf16[1168,256]{1,0:T(8,128)(2,1)S(1)}, u32[]{:S(2)}, u32[]{:S(2)}) collective-permute-start(bf16[1168,256]{1,0:T(8,128)(2,1)S(1)} %line_pick.9.refs_1_.own), channel_id=1, source_target_pairs={{0,4},{4,0},{8,12},{12,8},{16,20},{20,16},{24,28},{28,24},{1,5},{5... | collective-permute-start | bytes 1794056 | tf_op jit(solution)/shard_map/ppermute | solution.py:541
  174.5 17.0 %collective-permute-start.37 = (bf16[1168,256]{1,0:T(8,128)(2,1)S(1)}, bf16[1168,256]{1,0:T(8,128)(2,1)S(1)}, u32[]{:S(2)}, u32[]{:S(2)}) collective-permute-start(bf16[1168,256]{1,0:T(8,128)(2,1)S(1)} %line_add.23.refs_0_.x), channel_id=1, source_target_pairs={{8,0},{12,4},{16,24},{20,28},{9,1},{13,5},{17,25},{21,29},{10,2},{... | collective-permute-start | bytes 1794056 | tf_op jit(solution)/shard_map/ppermute | solution.py:511
  (27 other events, 316.6 us)

commit v9 on v7

--- a/solution.py
+++ b/solution.py
@@ -550,8 +550,15 @@
     parts, totals, crossed = {}, {}, {}
     last = ()
 
+    reached = [0] * 6
+
     def line(chunk, step):
         nonlocal last
+        if reached[chunk] > step:
+            return
+        if reached[chunk] < step:
+            line(chunk, step - 1)
+        reached[chunk] = step + 1
         before = totals.get(chunk, parts[chunk])
         totals[chunk] = line_step(step, parts[chunk], before, idx, place, last)
         last = (totals[chunk],)
@@ -560,6 +567,7 @@
 
     def write(chunk):
         nonlocal last
+        line(chunk, steps - 1)
         name, axis = ("finish_second", 1) if chunk < 3 else ("finish_first", 2)
         shape = (9, n // 2 * rows, rows) if chunk < 3 else (9, rows, n // 2 * rows)
         written[axis], mark = finish(
@@ -624,31 +632,39 @@
         )
         last = (mark,)
 
-    def wave(at):
-        for step in range(steps):
-            if 0 <= at - step < 6:
-                line(at - step, step)
-        if 0 <= at - steps < 6:
-            write(at - steps)
-
     written, done = {}, {}
     second_part(0)
+    output()
     second_part(1)
-    output()
     norm_back()
     line(0, 0)
     second_part(2)
     line(1, 0)
-    line(0, 1)
     dpre_halves()
     first_parts()
-    wave(2)
-    wave(3)
-    wave(4)
-    wave(5)
+    line(0, 1)
+    line(2, 0)
+    line(1, 1)
+    line(0, 2)
+    line(3, 0)
+    line(2, 1)
+    line(1, 2)
+    line(4, 0)
+    line(3, 1)
+    write(0)
+    line(5, 0)
+    line(2, 2)
+    line(4, 1)
+    write(1)
+    line(3, 2)
+    write(2)
+    line(5, 1)
+    line(4, 2)
+    write(3)
+    write(4)
     grad_volume()
-    for at in range(6, 6 + steps):
-        wave(at)
+    line(5, 2)
+    write(5)
     gain_rows = totals[3][9 * rows : 9 * rows + 2, :rows].astype(F32)
     gain_rows_other = crossed[3][9 * rows : 9 * rows + 2, :rows].astype(F32)
     gain_total = (jnp.sum(gain_rows, axis=0) + jnp.sum(gain_rows_other, axis=0)) * factor

time: 180 us -> 209 us (1.16)
  waiting for transfers between devices: 44.9 us -> 74.9 us
  starting transfers between devices: 66.7 us -> 53.2 us
  local copies, waits for them, and re-layouts: 4.71 us -> 13.4 us
  Pallas kernels: 60.5 us -> 63.9 us
    ppermute x18, waiting for transfers between devices: 30.4 us -> 46.3 us  [line_send(): return lax.ppermute(x, 'dp', pairs)]
    ppermute x12, waiting for transfers between devices: 12.9 us -> 22.9 us  [to_partner(): return lax.ppermute(x, 'chan', [(i, i ^ m) for i in range(n)])]
    ppermute x18, starting transfers between devices: 38.9 us -> 29.8 us  [line_send(): return lax.ppermute(x, 'dp', pairs)]
    unnamed x28 -> x52, local copies, waits for them, and re-layouts: 4.63 us -> 13.3 us
    ppermute x10, starting transfers between devices: 16.4 us -> 11.7 us  [to_core(): lax.ppermute(x, 'dp', [(i, i ^ 1) for i in range(lax.axis_size('dp'))])]
    ppermute x10, waiting for transfers between devices: 1.56 us -> 5.73 us  [to_core(): lax.ppermute(x, 'dp', [(i, i ^ 1) for i in range(lax.axis_size('dp'))])]
  transfers between devices with their start and end apart: 40 -> 40, of which waited for: 11 -> 16; matrix products, arithmetic and copies ran while one was open for 0% -> 0% of each run, Pallas kernels for 27% -> 25%
where the time goes in v9:
time: 209 us; the launch traced here: 208 us
  waiting for transfers between devices  74.9 us (36%)
  Pallas kernels  63.9 us (31%)
  starting transfers between devices  53.2 us (25%)
  local copies, waits for them, and re-layouts  13.4 us (6%)
    ppermute x18, waiting for transfers between devices, line_send(): return lax.ppermute(x, 'dp', pairs)  46.3 us
    ppermute x18, starting transfers between devices, line_send(): return lax.ppermute(x, 'dp', pairs)  29.8 us
    ppermute x12, waiting for transfers between devices, to_partner(): return lax.ppermute(x, 'chan', [(i, i ^ m) for i in range(n)])  22.9 us
    pallas_call x2, Pallas kernels, conv_full(): pl.pallas_call(functools.partial(conv_kernel, n, sign, transposed), in_sp...  14.2 us
    unnamed x52, local copies, waits for them, and re-layouts  13.3 us
    pallas_call x2, Pallas kernels, spread_shares(): pl.pallas_call(functools.partial(share_kernel, n, sign), in_specs=[smem()...  12.8 us
    pallas_call x6, Pallas kernels, finish(): pl.pallas_call(functools.partial(finish_kernel, n, axis, factor, chunk),...  12.7 us
    ppermute x12, starting transfers between devices, to_partner(): return lax.ppermute(x, 'chan', [(i, i ^ m) for i in range(n)])  11.7 us
  transfers between devices with their start and end apart: 40, of which 16 were waited for; matrix products, arithmetic and copies ran while one was open for 0% of the time, Pallas kernels for 25%

profile of v9, /device:TPU:1, one launch (start us, length us, event | category | flops | bytes accessed | tf_op | source)
XLA Modules:
  0.0 208.1 jit_solution(15884368935240808064)
XLA Ops:
  1.3 7.1 %pre.1 = (bf16[1024,128]{1,0:T(8,128)(2,1)}, bf16[1024,128]{1,0:T(8,128)(2,1)}, bf16[1024,128]{1,0:T(8,128)(2,1)}, bf16[1024,128]{1,0:T(8,128)(2,1)}) custom-call(s32[2]{0:T(128)} %pad_add_fusion.idx, bf16[128,1024]{1,0:T(8,128)(2,1)} %bitcast.15, bf16[3456,512]{1,0:T(8,128)(2,1)} %bitcast.10), custom_call_target="tpu_custom_call" | custom-call | flops 1024 | bytes 1024 | tf_op jit(solution)/shard_map/pre/pallas_call | solution.py:105
  8.4 2.1 %collective-permute-start = (bf16[1024,128]{1,0:T(8,128)(2,1)}, bf16[1024,128]{1,0:T(8,128)(2,1)}, u32[]{:S(2)}, u32[]{:S(2)}) collective-permute-start(bf16[1024,128]{1,0:T(8,128)(2,1)} %get-tuple-element.44), channel_id=1, source_target_pairs={{0,1},{1,0},{2,3},{3,2},{4,5},{5,4},{6,7},{7,6},{8,9},{9,8},{10,11... | collective-permute-start | bytes 786440 | tf_op jit(solution)/shard_map/ppermute | solution.py:506
  13.0 2.0 copy-done.1
  16.6 5.7 %dact.1 = (bf16[1024,128]{1,0:T(8,128)(2,1)S(1)}, bf16[1024,128]{1,0:T(8,128)(2,1)S(1)}, bf16[1024,128]{1,0:T(8,128)(2,1)S(1)}, bf16[1024,128]{1,0:T(8,128)(2,1)S(1)}) custom-call(s32[2]{0:T(128)S(1)} %copy-done.24, bf16[128,1024]{1,0:T(8,128)(2,1)S(1)} %bitcast.13, bf16[27,512,128]{2,1,0:T(8,128)(2,1)S(1)} %copy-done.1), custom_call_target="tpu_custom_call" | custom-call | flops 1024 | bytes 1024 | tf_op jit(solution)/shard_map/dact/pallas_call | solution.py:105
  32.6 1.7 collective-permute-start.3
  36.5 1.6 moved_second.1.refs_4_.moved
  38.2 2.3 %collective-permute-done.3.refs_1_ = bf16[1024,128]{1,0:T(8,128)(2,1)S(1)} collective-permute-done((bf16[1024,128]{1,0:T(8,128)(2,1)S(1)}, bf16[1024,128]{1,0:T(8,128)(2,1)S(1)}, u32[]{:S(2)}, u32[]{:S(2)}) %collective-permute-start.3) | collective-permute-done | bytes 262176 | tf_op jit(solution)/shard_map/ppermute | solution.py:506
  41.3 5.7 %collective-permute-done.5.refs_3_ = bf16[1024,128]{1,0:T(8,128)(2,1)S(1)} collective-permute-done((bf16[1024,128]{1,0:T(8,128)(2,1)S(1)}, bf16[1024,128]{1,0:T(8,128)(2,1)S(1)}, u32[]{:S(2)}, u32[]{:S(2)}) %collective-permute-start.5) | collective-permute-done | bytes 262176 | tf_op jit(solution)/shard_map/ppermute | solution.py:506
  48.0 1.6 collective-permute-start.8
  52.3 3.4 %collective-permute-start.16 = (bf16[9,256,128]{2,1,0:T(8,128)(2,1)S(1)}, bf16[9,256,128]{2,1,0:T(8,128)(2,1)S(1)}, u32[]{:S(2)}, u32[]{:S(2)}) collective-permute-start(bf16[9,256,128]{2,1,0:T(8,128)(2,1)S(1)} %grad_second.3.refs_4_.x), channel_id=1, source_target_pairs={{0,8},{4,12},{24,16},{28,20},{1,9},{5,13},{25,17},{29,21},{2,10},{... | collective-permute-start | bytes 1769480 | tf_op jit(solution)/shard_map/ppermute | solution.py:480
  55.8 7.0 %output.1 = (bf16[128,1024]{1,0:T(8,128)(2,1)}, f32[8,128]{1,0:T(8,128)S(1)}) custom-call(s32[2]{0:T(128)S(1)} %copy-done.25, bf16[27,512,128]{2,1,0:T(8,128)(2,1)S(1)} %copy-done.2, bf16[1024,128]{1,0:T(8,128)(2,1)S(1)} %get-tuple-element.50._.refs_0_, bf16[1024,128]{1,0:T(8,128)(2,1)S(1)} %collective-permute-done.3.refs_1_, ...), custom_call_target="tpu_custom_call" | custom-call | flops 1024 | bytes 1024 | tf_op jit(solution)/shard_map/output/pallas_call | solution.py:208
  68.4 10.1 %collective-permute-done.10.refs_2_ = bf16[1024,128]{1,0:T(8,128)(2,1)S(1)} collective-permute-done((bf16[1024,128]{1,0:T(8,128)(2,1)S(1)}, bf16[1024,128]{1,0:T(8,128)(2,1)S(1)}, u32[]{:S(2)}, u32[]{:S(2)}) %collective-permute-start.10) | collective-permute-done | bytes 262176 | tf_op jit(solution)/shard_map/ppermute | solution.py:506
  85.0 4.1 %collective-permute-start.20 = (bf16[9,256,128]{2,1,0:T(8,128)(2,1)S(1)}, bf16[9,256,128]{2,1,0:T(8,128)(2,1)S(1)}, u32[]{:S(2)}, u32[]{:S(2)}) collective-permute-start(bf16[9,256,128]{2,1,0:T(8,128)(2,1)S(1)} %grad_second.5.refs_0_.x), channel_id=1, source_target_pairs={{0,8},{4,12},{24,16},{28,20},{1,9},{5,13},{25,17},{29,21},{2,10},{... | collective-permute-start | bytes 1769480 | tf_op jit(solution)/shard_map/ppermute | solution.py:480
  90.0 2.9 %collective-permute-done.14.refs_3_ = bf16[1024,128]{1,0:T(8,128)(2,1)S(1)} collective-permute-done((bf16[1024,128]{1,0:T(8,128)(2,1)S(1)}, bf16[1024,128]{1,0:T(8,128)(2,1)S(1)}, u32[]{:S(2)}, u32[]{:S(2)}) %collective-permute-start.14) | collective-permute-done | bytes 262176 | tf_op jit(solution)/shard_map/ppermute | solution.py:506
  93.5 2.8 %collective-permute-start.17 = (bf16[2,1024,128]{2,1,0:T(8,128)(2,1)S(1)}, bf16[2,1024,128]{2,1,0:T(8,128)(2,1)S(1)}, u32[]{:S(2)}, u32[]{:S(2)}) collective-permute-start(bf16[2,1024,128]{2,1,0:T(8,128)(2,1)S(1)} %get-tuple-element.63), channel_id=1, source_target_pairs={{0,4},{4,0},{8,12},{12,8},{16,20},{20,16},{24,28},{28,24},{1,5},{5... | collective-permute-start | bytes 1572872 | tf_op jit(solution)/shard_map/ppermute | solution.py:509
  97.8 5.2 %grad_first.1 = (bf16[1168,256]{1,0:T(8,128)(2,1)S(1)}, bf16[1168,256]{1,0:T(8,128)(2,1)}, bf16[1168,256]{1,0:T(8,128)(2,1)S(1)}) custom-call(bf16[128,1024]{1,0:T(8,128)(2,1)S(1)} %bitcast.17, bf16[128,1024]{1,0:T(8,128)(2,1)} %collective-permute-done.7.refs_5_.vol_other, bf16[2,1024,128]{2,1,0:T(8,128)(2,1)S(1)} %get-tuple-element.62.own.refs_0_, ...), custom_call_target="tpu_custom_call" | custom-call | flops 1024 | bytes 1024 | tf_op jit(solution)/shard_map/grad_first/pallas_call | solution.py:341
  103.0 2.3 %collective-permute-start.24 = (bf16[1168,256]{1,0:T(8,128)(2,1)S(1)}, bf16[1168,256]{1,0:T(8,128)(2,1)}, u32[]{:S(2)}, u32[]{:S(2)}) collective-permute-start(bf16[1168,256]{1,0:T(8,128)(2,1)S(1)} %get-tuple-element.66.refs_0_.x), channel_id=1, source_target_pairs={{0,8},{4,12},{24,16},{28,20},{1,9},{5,13},{25,17},{29,21},{2,10},{... | collective-permute-start | bytes 1794056 | tf_op jit(solution)/shard_map/ppermute | solution.py:480
  105.3 2.1 %collective-permute-start.18 = (bf16[1168,256]{1,0:T(8,128)(2,1)}, bf16[1168,256]{1,0:T(8,128)(2,1)}, u32[]{:S(2)}, u32[]{:S(2)}) collective-permute-start(bf16[1168,256]{1,0:T(8,128)(2,1)} %get-tuple-element.65.x), channel_id=1, source_target_pairs={{0,8},{4,12},{24,16},{28,20},{1,9},{5,13},{25,17},{29,21},{2,10},{... | collective-permute-start | bytes 1794056 | tf_op jit(solution)/shard_map/ppermute | solution.py:480
  112.3 11.5 %collective-permute-done.25.y = bf16[9,256,128]{2,1,0:T(8,128)(2,1)} collective-permute-done((bf16[9,256,128]{2,1,0:T(8,128)(2,1)S(1)}, bf16[9,256,128]{2,1,0:T(8,128)(2,1)}, u32[]{:S(2)}, u32[]{:S(2)}) %collective-permute-start.25) | collective-permute-done | bytes 589856 | tf_op jit(solution)/shard_map/ppermute | solution.py:480
  127.0 3.6 %collective-permute-start.28 = (bf16[1168,256]{1,0:T(8,128)(2,1)}, bf16[1168,256]{1,0:T(8,128)(2,1)S(1)}, u32[]{:S(2)}, u32[]{:S(2)}) collective-permute-start(bf16[1168,256]{1,0:T(8,128)(2,1)} %copy-done.7), channel_id=1, source_target_pairs={{0,8},{4,12},{24,16},{28,20},{1,9},{5,13},{25,17},{29,21},{2,10},{... | collective-permute-start | bytes 1794056 | tf_op jit(solution)/shard_map/ppermute | solution.py:480
  131.8 4.7 %collective-permute-done.22.y = bf16[9,256,128]{2,1,0:T(8,128)(2,1)} collective-permute-done((bf16[9,256,128]{2,1,0:T(8,128)(2,1)S(1)}, bf16[9,256,128]{2,1,0:T(8,128)(2,1)}, u32[]{:S(2)}, u32[]{:S(2)}) %collective-permute-start.22) | collective-permute-done | bytes 589856 | tf_op jit(solution)/shard_map/ppermute | solution.py:480
  144.1 2.0 finish_second.3
  147.0 11.1 %collective-permute-done.27.y = bf16[9,256,128]{2,1,0:T(8,128)(2,1)S(1)} collective-permute-done((bf16[9,256,128]{2,1,0:T(8,128)(2,1)S(1)}, bf16[9,256,128]{2,1,0:T(8,128)(2,1)S(1)}, u32[]{:S(2)}, u32[]{:S(2)}) %collective-permute-start.27) | collective-permute-done | bytes 589856 | tf_op jit(solution)/shard_map/ppermute | solution.py:480
  163.1 2.0 finish_second.4
  165.1 5.8 %collective-permute-done.35.y = bf16[1168,256]{1,0:T(8,128)(2,1)S(1)} collective-permute-done((bf16[1168,256]{1,0:T(8,128)(2,1)S(1)}, bf16[1168,256]{1,0:T(8,128)(2,1)S(1)}, u32[]{:S(2)}, u32[]{:S(2)}) %collective-permute-start.35) | collective-permute-done | bytes 598048 | tf_op jit(solution)/shard_map/ppermute | solution.py:480
  172.8 2.0 finish_second.5
  175.0 8.7 %collective-permute-done.31.y = bf16[1168,256]{1,0:T(8,128)(2,1)S(1)} collective-permute-done((bf16[1168,256]{1,0:T(8,128)(2,1)S(1)}, bf16[1168,256]{1,0:T(8,128)(2,1)S(1)}, u32[]{:S(2)}, u32[]{:S(2)}) %collective-permute-start.31) | collective-permute-done | bytes 598048 | tf_op jit(solution)/shard_map/ppermute | solution.py:480
  186.5 2.0 finish_first.3
  188.6 2.0 finish_first.4
  190.6 7.2 %grad_volume.1 = (bf16[128,1024]{1,0:T(8,128)(2,1)}, f32[8,128]{1,0:T(8,128)S(1)}) custom-call(s32[2]{0:T(128)S(1)} %copy-done.25, bf16[3456,512]{1,0:T(8,128)(2,1)S(1)} %bitcast.11, bf16[1024,128]{1,0:T(8,128)(2,1)S(1)} %get-tuple-element.61.refs_0_, bf16[1024,128]{1,0:T(8,128)(2,1)S(1)} %collective-permute-done.12.refs_1_, ...), custom_call_target="tpu_custom_call" | custom-call | flops 1024 | bytes 1024 | tf_op jit(solution)/shard_map/grad_volume/pallas_call | solution.py:208
  197.8 4.4 %collective-permute-done.38.y = bf16[1168,256]{1,0:T(8,128)(2,1)S(1)} collective-permute-done((bf16[1168,256]{1,0:T(8,128)(2,1)S(1)}, bf16[1168,256]{1,0:T(8,128)(2,1)S(1)}, u32[]{:S(2)}, u32[]{:S(2)}) %collective-permute-start.38) | collective-permute-done | bytes 598048 | tf_op jit(solution)/shard_map/ppermute | solution.py:480
  205.3 2.6 %finish_first.5 = (f32[27,128,512]{2,1,0:T(8,128)}, f32[8,128]{1,0:T(8,128)}) custom-call(s32[2]{0:T(128)S(1)} %copy-done.25, bf16[1168,256]{1,0:T(8,128)(2,1)S(1)} %line_pick.11.own.refs_1_, bf16[1168,256]{1,0:T(8,128)(2,1)S(1)} %collective-permute-done.39.other, f32[27,128,512]{2,1,0:T(8,128)} %get-tuple-element.78.refs_0_, ...), custom_call_target="tpu_custom_call", output_to_operand_aliasing={{0}: (3, {})} | custom-call | flops 1024 | bytes 1024 | tf_op jit(solution)/shard_map/finish_first/pallas_call | solution.py:419
  (143 shorter events, 67.0 us)
Async XLA Ops:
  8.4 16.8 %collective-permute-start = (bf16[1024,128]{1,0:T(8,128)(2,1)}, bf16[1024,128]{1,0:T(8,128)(2,1)}, u32[]{:S(2)}, u32[]{:S(2)}) collective-permute-start(bf16[1024,128]{1,0:T(8,128)(2,1)} %get-tuple-element.44), channel_id=1, source_target_pairs={{0,1},{1,0},{2,3},{3,2},{4,5},{5,4},{6,7},{7,6},{8,9},{9,8},{10,11... | collective-permute-start | bytes 786440 | tf_op jit(solution)/shard_map/ppermute | solution.py:506
  10.5 14.7 %collective-permute-start.1 = (bf16[1024,128]{1,0:T(8,128)(2,1)}, bf16[1024,128]{1,0:T(8,128)(2,1)}, u32[]{:S(2)}, u32[]{:S(2)}) collective-permute-start(bf16[1024,128]{1,0:T(8,128)(2,1)} %get-tuple-element.45), channel_id=1, source_target_pairs={{0,2},{1,3},{2,0},{3,1},{4,6},{5,7},{6,4},{7,5},{8,10},{9,11},{10,... | collective-permute-start | bytes 786440 | tf_op jit(solution)/shard_map/ppermute | solution.py:506
  11.7 13.5 %collective-permute-start.2 = (bf16[1024,128]{1,0:T(8,128)(2,1)}, bf16[1024,128]{1,0:T(8,128)(2,1)}, u32[]{:S(2)}, u32[]{:S(2)}) collective-permute-start(bf16[1024,128]{1,0:T(8,128)(2,1)} %get-tuple-element.46), channel_id=1, source_target_pairs={{0,3},{1,2},{2,1},{3,0},{4,7},{5,6},{6,5},{7,4},{8,11},{9,10},{10,... | collective-permute-start | bytes 786440 | tf_op jit(solution)/shard_map/ppermute | solution.py:506
  11.8 26.4 %collective-permute-start.7 = (bf16[128,1024]{1,0:T(8,128)(2,1)}, bf16[128,1024]{1,0:T(8,128)(2,1)}, u32[]{:S(2)}, u32[]{:S(2)}) collective-permute-start(bf16[128,1024]{1,0:T(8,128)(2,1)} %bitcast.16), channel_id=1, source_target_pairs={{0,4},{4,0},{8,12},{12,8},{16,20},{20,16},{24,28},{28,24},{1,5},{5... | collective-permute-start | bytes 786440 | tf_op jit(solution)/shard_map/ppermute | solution.py:509
  13.0 22.5 %collective-permute-start.6 = (bf16[128,1024]{1,0:T(8,128)(2,1)}, bf16[128,1024]{1,0:T(8,128)(2,1)}, u32[]{:S(2)}, u32[]{:S(2)}) collective-permute-start(bf16[128,1024]{1,0:T(8,128)(2,1)} %bitcast.12), channel_id=1, source_target_pairs={{0,4},{4,0},{8,12},{12,8},{16,20},{20,16},{24,28},{28,24},{1,5},{5... | collective-permute-start | bytes 786440 | tf_op jit(solution)/shard_map/ppermute | solution.py:509
  35.5 11.5 %collective-permute-start.5 = (bf16[1024,128]{1,0:T(8,128)(2,1)S(1)}, bf16[1024,128]{1,0:T(8,128)(2,1)S(1)}, u32[]{:S(2)}, u32[]{:S(2)}) collective-permute-start(bf16[1024,128]{1,0:T(8,128)(2,1)S(1)} %get-tuple-element.50._.refs_0_), channel_id=1, source_target_pairs={{0,3},{1,2},{2,1},{3,0},{4,7},{5,6},{6,5},{7,4},{8,11},{9,10},{10,... | collective-permute-start | bytes 786440 | tf_op jit(solution)/shard_map/ppermute | solution.py:506
  52.3 30.6 %collective-permute-start.16 = (bf16[9,256,128]{2,1,0:T(8,128)(2,1)S(1)}, bf16[9,256,128]{2,1,0:T(8,128)(2,1)S(1)}, u32[]{:S(2)}, u32[]{:S(2)}) collective-permute-start(bf16[9,256,128]{2,1,0:T(8,128)(2,1)S(1)} %grad_second.3.refs_4_.x), channel_id=1, source_target_pairs={{0,8},{4,12},{24,16},{28,20},{1,9},{5,13},{25,17},{29,21},{2,10},{... | collective-permute-start | bytes 1769480 | tf_op jit(solution)/shard_map/ppermute | solution.py:480
  64.4 20.6 %collective-permute-start.15 = (bf16[9,256,128]{2,1,0:T(8,128)(2,1)S(1)}, bf16[9,256,128]{2,1,0:T(8,128)(2,1)S(1)}, u32[]{:S(2)}, u32[]{:S(2)}) collective-permute-start(bf16[9,256,128]{2,1,0:T(8,128)(2,1)S(1)} %grad_second.4.refs_4_.x), channel_id=1, source_target_pairs={{0,8},{4,12},{24,16},{28,20},{1,9},{5,13},{25,17},{29,21},{2,10},{... | collective-permute-start | bytes 1769480 | tf_op jit(solution)/shard_map/ppermute | solution.py:480
  65.7 12.9 %collective-permute-start.10 = (bf16[1024,128]{1,0:T(8,128)(2,1)S(1)}, bf16[1024,128]{1,0:T(8,128)(2,1)S(1)}, u32[]{:S(2)}, u32[]{:S(2)}) collective-permute-start(bf16[1024,128]{1,0:T(8,128)(2,1)S(1)} %copy-done.17), channel_id=1, source_target_pairs={{0,2},{1,3},{2,0},{3,1},{4,6},{5,7},{6,4},{7,5},{8,10},{9,11},{10,... | collective-permute-start | bytes 786440 | tf_op jit(solution)/shard_map/ppermute | solution.py:506
  67.0 11.6 %collective-permute-start.11 = (bf16[1024,128]{1,0:T(8,128)(2,1)S(1)}, bf16[1024,128]{1,0:T(8,128)(2,1)S(1)}, u32[]{:S(2)}, u32[]{:S(2)}) collective-permute-start(bf16[1024,128]{1,0:T(8,128)(2,1)S(1)} %copy-done.21), channel_id=1, source_target_pairs={{0,3},{1,2},{2,1},{3,0},{4,7},{5,6},{6,5},{7,4},{8,11},{9,10},{10,... | collective-permute-start | bytes 786440 | tf_op jit(solution)/shard_map/ppermute | solution.py:506
  67.9 11.6 %collective-permute-start.9 = (bf16[1024,128]{1,0:T(8,128)(2,1)S(1)}, bf16[1024,128]{1,0:T(8,128)(2,1)S(1)}, u32[]{:S(2)}, u32[]{:S(2)}) collective-permute-start(bf16[1024,128]{1,0:T(8,128)(2,1)S(1)} %copy-done.13), channel_id=1, source_target_pairs={{0,1},{1,0},{2,3},{3,2},{4,5},{5,4},{6,7},{7,6},{8,9},{9,8},{10,11... | collective-permute-start | bytes 786440 | tf_op jit(solution)/shard_map/ppermute | solution.py:506
  80.2 9.0 %collective-permute-start.12 = (bf16[1024,128]{1,0:T(8,128)(2,1)S(1)}, bf16[1024,128]{1,0:T(8,128)(2,1)S(1)}, u32[]{:S(2)}, u32[]{:S(2)}) collective-permute-start(bf16[1024,128]{1,0:T(8,128)(2,1)S(1)} %get-tuple-element.61.refs_0_), channel_id=1, source_target_pairs={{0,1},{1,0},{2,3},{3,2},{4,5},{5,4},{6,7},{7,6},{8,9},{9,8},{10,11... | collective-permute-start | bytes 786440 | tf_op jit(solution)/shard_map/ppermute | solution.py:506
  81.2 8.7 %collective-permute-start.13 = (bf16[1024,128]{1,0:T(8,128)(2,1)S(1)}, bf16[1024,128]{1,0:T(8,128)(2,1)S(1)}, u32[]{:S(2)}, u32[]{:S(2)}) collective-permute-start(bf16[1024,128]{1,0:T(8,128)(2,1)S(1)} %get-tuple-element.61.refs_0_), channel_id=1, source_target_pairs={{0,2},{1,3},{2,0},{3,1},{4,6},{5,7},{6,4},{7,5},{8,10},{9,11},{10,... | collective-permute-start | bytes 786440 | tf_op jit(solution)/shard_map/ppermute | solution.py:506
  81.8 11.1 %collective-permute-start.14 = (bf16[1024,128]{1,0:T(8,128)(2,1)S(1)}, bf16[1024,128]{1,0:T(8,128)(2,1)S(1)}, u32[]{:S(2)}, u32[]{:S(2)}) collective-permute-start(bf16[1024,128]{1,0:T(8,128)(2,1)S(1)} %get-tuple-element.61.refs_0_), channel_id=1, source_target_pairs={{0,3},{1,2},{2,1},{3,0},{4,7},{5,6},{6,5},{7,4},{8,11},{9,10},{10,... | collective-permute-start | bytes 786440 | tf_op jit(solution)/shard_map/ppermute | solution.py:506
  83.1 24.4 %collective-permute-start.21 = (bf16[9,256,128]{2,1,0:T(8,128)(2,1)S(1)}, bf16[9,256,128]{2,1,0:T(8,128)(2,1)S(1)}, u32[]{:S(2)}, u32[]{:S(2)}) collective-permute-start(bf16[9,256,128]{2,1,0:T(8,128)(2,1)S(1)} %line_add.12.refs_0_.x), channel_id=1, source_target_pairs={{8,16},{12,20},{16,8},{20,12},{9,17},{13,21},{17,9},{21,13},{10,18... | collective-permute-start | bytes 1769480 | tf_op jit(solution)/shard_map/ppermute | solution.py:480
  85.0 24.2 %collective-permute-start.20 = (bf16[9,256,128]{2,1,0:T(8,128)(2,1)S(1)}, bf16[9,256,128]{2,1,0:T(8,128)(2,1)S(1)}, u32[]{:S(2)}, u32[]{:S(2)}) collective-permute-start(bf16[9,256,128]{2,1,0:T(8,128)(2,1)S(1)} %grad_second.5.refs_0_.x), channel_id=1, source_target_pairs={{0,8},{4,12},{24,16},{28,20},{1,9},{5,13},{25,17},{29,21},{2,10},{... | collective-permute-start | bytes 1769480 | tf_op jit(solution)/shard_map/ppermute | solution.py:480
  89.3 21.5 %collective-permute-start.19 = (bf16[9,256,128]{2,1,0:T(8,128)(2,1)S(1)}, bf16[9,256,128]{2,1,0:T(8,128)(2,1)S(1)}, u32[]{:S(2)}, u32[]{:S(2)}) collective-permute-start(bf16[9,256,128]{2,1,0:T(8,128)(2,1)S(1)} %line_add.13.refs_4_.x), channel_id=1, source_target_pairs={{8,16},{12,20},{16,8},{20,12},{9,17},{13,21},{17,9},{21,13},{10,18... | collective-permute-start | bytes 1769480 | tf_op jit(solution)/shard_map/ppermute | solution.py:480
  103.0 22.0 %collective-permute-start.24 = (bf16[1168,256]{1,0:T(8,128)(2,1)S(1)}, bf16[1168,256]{1,0:T(8,128)(2,1)}, u32[]{:S(2)}, u32[]{:S(2)}) collective-permute-start(bf16[1168,256]{1,0:T(8,128)(2,1)S(1)} %get-tuple-element.66.refs_0_.x), channel_id=1, source_target_pairs={{0,8},{4,12},{24,16},{28,20},{1,9},{5,13},{25,17},{29,21},{2,10},{... | collective-permute-start | bytes 1794056 | tf_op jit(solution)/shard_map/ppermute | solution.py:480
  105.3 32.3 %collective-permute-start.18 = (bf16[1168,256]{1,0:T(8,128)(2,1)}, bf16[1168,256]{1,0:T(8,128)(2,1)}, u32[]{:S(2)}, u32[]{:S(2)}) collective-permute-start(bf16[1168,256]{1,0:T(8,128)(2,1)} %get-tuple-element.65.x), channel_id=1, source_target_pairs={{0,8},{4,12},{24,16},{28,20},{1,9},{5,13},{25,17},{29,21},{2,10},{... | collective-permute-start | bytes 1794056 | tf_op jit(solution)/shard_map/ppermute | solution.py:480
  107.6 16.2 %collective-permute-start.25 = (bf16[9,256,128]{2,1,0:T(8,128)(2,1)S(1)}, bf16[9,256,128]{2,1,0:T(8,128)(2,1)}, u32[]{:S(2)}, u32[]{:S(2)}) collective-permute-start(bf16[9,256,128]{2,1,0:T(8,128)(2,1)S(1)} %line_add.14.refs_0_.x), channel_id=1, source_target_pairs={{8,0},{12,4},{16,24},{20,28},{9,1},{13,5},{17,25},{21,29},{10,2},{... | collective-permute-start | bytes 1769480 | tf_op jit(solution)/shard_map/ppermute | solution.py:480
  109.3 21.3 %collective-permute-start.23 = (bf16[9,256,128]{2,1,0:T(8,128)(2,1)S(1)}, bf16[9,256,128]{2,1,0:T(8,128)(2,1)}, u32[]{:S(2)}, u32[]{:S(2)}) collective-permute-start(bf16[9,256,128]{2,1,0:T(8,128)(2,1)S(1)} %line_add.15.refs_0_.x), channel_id=1, source_target_pairs={{8,16},{12,20},{16,8},{20,12},{9,17},{13,21},{17,9},{21,13},{10,18... | collective-permute-start | bytes 1769480 | tf_op jit(solution)/shard_map/ppermute | solution.py:480
  110.9 25.5 %collective-permute-start.22 = (bf16[9,256,128]{2,1,0:T(8,128)(2,1)S(1)}, bf16[9,256,128]{2,1,0:T(8,128)(2,1)}, u32[]{:S(2)}, u32[]{:S(2)}) collective-permute-start(bf16[9,256,128]{2,1,0:T(8,128)(2,1)S(1)} %line_add.16.refs_0_.x), channel_id=1, source_target_pairs={{8,0},{12,4},{16,24},{20,28},{9,1},{13,5},{17,25},{21,29},{10,2},{... | collective-permute-start | bytes 1769480 | tf_op jit(solution)/shard_map/ppermute | solution.py:480
  126.2 16.3 %collective-permute-start.30 = (bf16[1168,256]{1,0:T(8,128)(2,1)S(1)}, bf16[1168,256]{1,0:T(8,128)(2,1)S(1)}, u32[]{:S(2)}, u32[]{:S(2)}) collective-permute-start(bf16[1168,256]{1,0:T(8,128)(2,1)S(1)} %line_add.17.refs_0_.x), channel_id=1, source_target_pairs={{8,16},{12,20},{16,8},{20,12},{9,17},{13,21},{17,9},{21,13},{10,18... | collective-permute-start | bytes 1794056 | tf_op jit(solution)/shard_map/ppermute | solution.py:480
  127.0 19.1 %collective-permute-start.28 = (bf16[1168,256]{1,0:T(8,128)(2,1)}, bf16[1168,256]{1,0:T(8,128)(2,1)S(1)}, u32[]{:S(2)}, u32[]{:S(2)}) collective-permute-start(bf16[1168,256]{1,0:T(8,128)(2,1)} %copy-done.7), channel_id=1, source_target_pairs={{0,8},{4,12},{24,16},{28,20},{1,9},{5,13},{25,17},{29,21},{2,10},{... | collective-permute-start | bytes 1794056 | tf_op jit(solution)/shard_map/ppermute | solution.py:480
  139.0 19.7 %collective-permute-start.26 = (bf16[1168,256]{1,0:T(8,128)(2,1)S(1)}, bf16[1168,256]{1,0:T(8,128)(2,1)S(1)}, u32[]{:S(2)}, u32[]{:S(2)}) collective-permute-start(bf16[1168,256]{1,0:T(8,128)(2,1)S(1)} %line_add.19.refs_0_.x), channel_id=1, source_target_pairs={{8,16},{12,20},{16,8},{20,12},{9,17},{13,21},{17,9},{21,13},{10,18... | collective-permute-start | bytes 1794056 | tf_op jit(solution)/shard_map/ppermute | solution.py:480
  141.3 16.8 %collective-permute-start.27 = (bf16[9,256,128]{2,1,0:T(8,128)(2,1)S(1)}, bf16[9,256,128]{2,1,0:T(8,128)(2,1)S(1)}, u32[]{:S(2)}, u32[]{:S(2)}) collective-permute-start(bf16[9,256,128]{2,1,0:T(8,128)(2,1)S(1)} %line_add.18.refs_0_.x), channel_id=1, source_target_pairs={{8,0},{12,4},{16,24},{20,28},{9,1},{13,5},{17,25},{21,29},{10,2},{... | collective-permute-start | bytes 1769480 | tf_op jit(solution)/shard_map/ppermute | solution.py:480
  142.8 28.2 %collective-permute-start.35 = (bf16[1168,256]{1,0:T(8,128)(2,1)S(1)}, bf16[1168,256]{1,0:T(8,128)(2,1)S(1)}, u32[]{:S(2)}, u32[]{:S(2)}) collective-permute-start(bf16[1168,256]{1,0:T(8,128)(2,1)S(1)} %line_add.20.refs_0_.x), channel_id=1, source_target_pairs={{8,0},{12,4},{16,24},{20,28},{9,1},{13,5},{17,25},{21,29},{10,2},{... | collective-permute-start | bytes 1794056 | tf_op jit(solution)/shard_map/ppermute | solution.py:480
  146.3 28.6 %collective-permute-start.32 = (bf16[1168,256]{1,0:T(8,128)(2,1)S(1)}, bf16[1168,256]{1,0:T(8,128)(2,1)S(1)}, u32[]{:S(2)}, u32[]{:S(2)}) collective-permute-start(bf16[1168,256]{1,0:T(8,128)(2,1)S(1)} %line_add.21.refs_0_.x), channel_id=1, source_target_pairs={{8,16},{12,20},{16,8},{20,12},{9,17},{13,21},{17,9},{21,13},{10,18... | collective-permute-start | bytes 1794056 | tf_op jit(solution)/shard_map/ppermute | solution.py:480
  158.9 24.9 %collective-permute-start.31 = (bf16[1168,256]{1,0:T(8,128)(2,1)S(1)}, bf16[1168,256]{1,0:T(8,128)(2,1)S(1)}, u32[]{:S(2)}, u32[]{:S(2)}) collective-permute-start(bf16[1168,256]{1,0:T(8,128)(2,1)S(1)} %line_add.22.refs_1_.x), channel_id=1, source_target_pairs={{8,0},{12,4},{16,24},{20,28},{9,1},{13,5},{17,25},{21,29},{10,2},{... | collective-permute-start | bytes 1794056 | tf_op jit(solution)/shard_map/ppermute | solution.py:480
  161.5 11.4 %collective-permute-start.33 = (bf16[9,256,128]{2,1,0:T(8,128)(2,1)S(1)}, bf16[9,256,128]{2,1,0:T(8,128)(2,1)S(1)}, u32[]{:S(2)}, u32[]{:S(2)}) collective-permute-start(bf16[9,256,128]{2,1,0:T(8,128)(2,1)S(1)} %line_pick.8.refs_0_.own), channel_id=1, source_target_pairs={{0,4},{4,0},{8,12},{12,8},{16,20},{20,16},{24,28},{28,24},{1,5},{5... | collective-permute-start | bytes 1769480 | tf_op jit(solution)/shard_map/ppermute | solution.py:509
  171.5 15.0 %collective-permute-start.37 = (bf16[1168,256]{1,0:T(8,128)(2,1)S(1)}, bf16[1168,256]{1,0:T(8,128)(2,1)S(1)}, u32[]{:S(2)}, u32[]{:S(2)}) collective-permute-start(bf16[1168,256]{1,0:T(8,128)(2,1)S(1)} %line_pick.9.refs_1_.own), channel_id=1, source_target_pairs={{0,4},{4,0},{8,12},{12,8},{16,20},{20,16},{24,28},{28,24},{1,5},{5... | collective-permute-start | bytes 1794056 | tf_op jit(solution)/shard_map/ppermute | solution.py:509
  185.2 17.0 %collective-permute-start.38 = (bf16[1168,256]{1,0:T(8,128)(2,1)S(1)}, bf16[1168,256]{1,0:T(8,128)(2,1)S(1)}, u32[]{:S(2)}, u32[]{:S(2)}) collective-permute-start(bf16[1168,256]{1,0:T(8,128)(2,1)S(1)} %line_add.23.refs_0_.x), channel_id=1, source_target_pairs={{8,0},{12,4},{16,24},{20,28},{9,1},{13,5},{17,25},{21,29},{10,2},{... | collective-permute-start | bytes 1794056 | tf_op jit(solution)/shard_map/ppermute | solution.py:480
  (34 other events, 366.6 us)

commit v10 on v9

--- a/solution.py
+++ b/solution.py
@@ -634,26 +634,26 @@
 
     written, done = {}, {}
     second_part(0)
+    second_part(1)
     output()
-    second_part(1)
     norm_back()
     line(0, 0)
     second_part(2)
     line(1, 0)
+    line(0, 1)
     dpre_halves()
     first_parts()
-    line(0, 1)
     line(2, 0)
     line(1, 1)
     line(0, 2)
     line(3, 0)
     line(2, 1)
     line(1, 2)
+    write(0)
     line(4, 0)
     line(3, 1)
-    write(0)
+    line(2, 2)
     line(5, 0)
-    line(2, 2)
     line(4, 1)
     write(1)
     line(3, 2)

time: 209 us -> 193 us (0.923)
  waiting for transfers between devices: 74.9 us -> 49 us
  starting transfers between devices: 53.2 us -> 74.5 us
  local copies, waits for them, and re-layouts: 13.4 us -> 4.71 us
  Pallas kernels: 63.9 us -> 60.5 us
    ppermute x10, starting transfers between devices: 11.7 us -> 25.9 us  [to_core(): lax.ppermute(x, 'dp', [(i, i ^ 1) for i in range(lax.axis_size('dp'))])]
    ppermute x18, waiting for transfers between devices: 46.3 us -> 32.1 us  [line_send(): return lax.ppermute(x, 'dp', pairs)]
    ppermute x12, waiting for transfers between devices: 22.9 us -> 12.7 us  [to_partner(): return lax.ppermute(x, 'chan', [(i, i ^ m) for i in range(n)])]
    unnamed x52 -> x28, local copies, waits for them, and re-layouts: 13.3 us -> 4.63 us
    ppermute x18, starting transfers between devices: 29.8 us -> 37.1 us  [line_send(): return lax.ppermute(x, 'dp', pairs)]
  transfers between devices with their start and end apart: 40 -> 40, of which waited for: 16 -> 16; matrix products, arithmetic and copies ran while one was open for 0% -> 0% of each run, Pallas kernels for 25% -> 24%
where the time goes in v10:
time: 193 us; the launch traced here: 191 us
  starting transfers between devices  74.5 us (39%)
  Pallas kernels  60.5 us (31%)
  waiting for transfers between devices  49 us (25%)
  local copies, waits for them, and re-layouts  4.71 us (2%)
    ppermute x18, starting transfers between devices, line_send(): return lax.ppermute(x, 'dp', pairs)  37.1 us
    ppermute x18, waiting for transfers between devices, line_send(): return lax.ppermute(x, 'dp', pairs)  32.1 us
    ppermute x10, starting transfers between devices, to_core(): lax.ppermute(x, 'dp', [(i, i ^ 1) for i in range(lax.axis_size('dp'))])  25.9 us
    pallas_call x2, Pallas kernels, conv_full(): pl.pallas_call(functools.partial(conv_kernel, n, sign, transposed), in_sp...  14.2 us
    pallas_call x2, Pallas kernels, spread_shares(): pl.pallas_call(functools.partial(share_kernel, n, sign), in_specs=[smem()...  12.8 us
    ppermute x12, waiting for transfers between devices, to_partner(): return lax.ppermute(x, 'chan', [(i, i ^ m) for i in range(n)])  12.7 us
    pallas_call x6, Pallas kernels, finish(): pl.pallas_call(functools.partial(finish_kernel, n, axis, factor, chunk),...  12.7 us
    ppermute x12, starting transfers between devices, to_partner(): return lax.ppermute(x, 'chan', [(i, i ^ m) for i in range(n)])  11.5 us
  transfers between devices with their start and end apart: 40, of which 16 were waited for; matrix products, arithmetic and copies ran while one was open for 0% of the time, Pallas kernels for 24%

profile of v10, /device:TPU:1, one launch (start us, length us, event | category | flops | bytes accessed | tf_op | source)
XLA Modules:
  0.0 191.4 jit_solution(4493139699313082518)
XLA Ops:
  1.3 7.1 %pre.1 = (bf16[1024,128]{1,0:T(8,128)(2,1)}, bf16[1024,128]{1,0:T(8,128)(2,1)}, bf16[1024,128]{1,0:T(8,128)(2,1)}, bf16[1024,128]{1,0:T(8,128)(2,1)}) custom-call(s32[2]{0:T(128)} %pad_add_fusion.idx, bf16[128,1024]{1,0:T(8,128)(2,1)} %bitcast.15, bf16[3456,512]{1,0:T(8,128)(2,1)} %bitcast.10), custom_call_target="tpu_custom_call" | custom-call | flops 1024 | bytes 1024 | tf_op jit(solution)/shard_map/pre/pallas_call | solution.py:105
  8.5 2.1 %collective-permute-start = (bf16[1024,128]{1,0:T(8,128)(2,1)}, bf16[1024,128]{1,0:T(8,128)(2,1)S(1)}, u32[]{:S(2)}, u32[]{:S(2)}) collective-permute-start(bf16[1024,128]{1,0:T(8,128)(2,1)} %get-tuple-element.44), channel_id=1, source_target_pairs={{0,1},{1,0},{2,3},{3,2},{4,5},{5,4},{6,7},{7,6},{8,9},{9,8},{10,11... | collective-permute-start | bytes 786440 | tf_op jit(solution)/shard_map/ppermute | solution.py:506
  13.1 2.0 %copy-done.1 = bf16[27,512,128]{2,1,0:T(8,128)(2,1)S(1)} copy-done((bf16[27,512,128]{2,1,0:T(8,128)(2,1)S(1)}, bf16[27,512,128]{2,1,0:T(8,128)(2,1)}, u32[]{:S(2)}) %copy-start.1) | copy-done | bytes 3538968
  16.7 5.7 %dact.1 = (bf16[1024,128]{1,0:T(8,128)(2,1)S(1)}, bf16[1024,128]{1,0:T(8,128)(2,1)S(1)}, bf16[1024,128]{1,0:T(8,128)(2,1)S(1)}, bf16[1024,128]{1,0:T(8,128)(2,1)S(1)}) custom-call(s32[2]{0:T(128)S(1)} %copy-done.12, bf16[128,1024]{1,0:T(8,128)(2,1)S(1)} %bitcast.13, bf16[27,512,128]{2,1,0:T(8,128)(2,1)S(1)} %copy-done.1), custom_call_target="tpu_custom_call" | custom-call | flops 1024 | bytes 1024 | tf_op jit(solution)/shard_map/dact/pallas_call | solution.py:105
  28.3 2.7 %collective-permute-done.3.refs_1_ = bf16[1024,128]{1,0:T(8,128)(2,1)S(1)} collective-permute-done((bf16[1024,128]{1,0:T(8,128)(2,1)S(1)}, bf16[1024,128]{1,0:T(8,128)(2,1)S(1)}, u32[]{:S(2)}, u32[]{:S(2)}) %collective-permute-start.3) | collective-permute-done | bytes 262176 | tf_op jit(solution)/shard_map/ppermute | solution.py:506
  31.0 2.0 %collective-permute-done.4.refs_2_ = bf16[1024,128]{1,0:T(8,128)(2,1)S(1)} collective-permute-done((bf16[1024,128]{1,0:T(8,128)(2,1)S(1)}, bf16[1024,128]{1,0:T(8,128)(2,1)S(1)}, u32[]{:S(2)}, u32[]{:S(2)}) %collective-permute-start.4) | collective-permute-done | bytes 262176 | tf_op jit(solution)/shard_map/ppermute | solution.py:506
  33.0 3.7 %collective-permute-done.5.refs_3_ = bf16[1024,128]{1,0:T(8,128)(2,1)S(1)} collective-permute-done((bf16[1024,128]{1,0:T(8,128)(2,1)S(1)}, bf16[1024,128]{1,0:T(8,128)(2,1)S(1)}, u32[]{:S(2)}, u32[]{:S(2)}) %collective-permute-start.5) | collective-permute-done | bytes 262176 | tf_op jit(solution)/shard_map/ppermute | solution.py:506
  37.6 3.8 %collective-permute-start.8 = (bf16[256,1024]{1,0:T(8,128)(2,1)S(1)}, bf16[256,1024]{1,0:T(8,128)(2,1)S(1)}, u32[]{:S(2)}, u32[]{:S(2)}) collective-permute-start(bf16[256,1024]{1,0:T(8,128)(2,1)S(1)} %get-tuple-element.52), channel_id=1, source_target_pairs={{0,4},{4,0},{8,12},{12,8},{16,20},{20,16},{24,28},{28,24},{1,5},{5... | collective-permute-start | bytes 1572872 | tf_op jit(solution)/shard_map/ppermute | solution.py:509
  44.1 3.2 %collective-permute-start.15 = (bf16[9,256,128]{2,1,0:T(8,128)(2,1)S(1)}, bf16[9,256,128]{2,1,0:T(8,128)(2,1)S(1)}, u32[]{:S(2)}, u32[]{:S(2)}) collective-permute-start(bf16[9,256,128]{2,1,0:T(8,128)(2,1)S(1)} %grad_second.3.refs_0_.x), channel_id=1, source_target_pairs={{0,8},{4,12},{24,16},{28,20},{1,9},{5,13},{25,17},{29,21},{2,10},{... | collective-permute-start | bytes 1769480 | tf_op jit(solution)/shard_map/ppermute | solution.py:480
  53.1 7.0 %output.1 = (bf16[128,1024]{1,0:T(8,128)(2,1)}, f32[8,128]{1,0:T(8,128)S(1)}) custom-call(s32[2]{0:T(128)S(1)} %copy-done.13, bf16[27,512,128]{2,1,0:T(8,128)(2,1)S(1)} %copy-done.2, bf16[1024,128]{1,0:T(8,128)(2,1)S(1)} %get-tuple-element.50._.refs_0_, bf16[1024,128]{1,0:T(8,128)(2,1)S(1)} %collective-permute-done.3.refs_1_, ...), custom_call_target="tpu_custom_call" | custom-call | flops 1024 | bytes 1024 | tf_op jit(solution)/shard_map/output/pallas_call | solution.py:208
  66.6 5.7 %collective-permute-done.17.y = bf16[9,256,128]{2,1,0:T(8,128)(2,1)S(1)} collective-permute-done((bf16[9,256,128]{2,1,0:T(8,128)(2,1)S(1)}, bf16[9,256,128]{2,1,0:T(8,128)(2,1)S(1)}, u32[]{:S(2)}, u32[]{:S(2)}) %collective-permute-start.17) | collective-permute-done | bytes 589856 | tf_op jit(solution)/shard_map/ppermute | solution.py:480
  72.6 2.4 %collective-permute-done.14.refs_3_ = bf16[1024,128]{1,0:T(8,128)(2,1)S(1)} collective-permute-done((bf16[1024,128]{1,0:T(8,128)(2,1)S(1)}, bf16[1024,128]{1,0:T(8,128)(2,1)S(1)}, u32[]{:S(2)}, u32[]{:S(2)}) %collective-permute-start.14) | collective-permute-done | bytes 262176 | tf_op jit(solution)/shard_map/ppermute | solution.py:506
  76.4 2.7 %collective-permute-start.18 = (bf16[2,1024,128]{2,1,0:T(8,128)(2,1)}, bf16[2,1024,128]{2,1,0:T(8,128)(2,1)}, u32[]{:S(2)}, u32[]{:S(2)}) collective-permute-start(bf16[2,1024,128]{2,1,0:T(8,128)(2,1)} %get-tuple-element.63), channel_id=1, source_target_pairs={{0,4},{4,0},{8,12},{12,8},{16,20},{20,16},{24,28},{28,24},{1,5},{5... | collective-permute-start | bytes 1572872 | tf_op jit(solution)/shard_map/ppermute | solution.py:509
  79.2 5.3 %collective-permute-start.22 = (bf16[9,256,128]{2,1,0:T(8,128)(2,1)S(1)}, bf16[9,256,128]{2,1,0:T(8,128)(2,1)}, u32[]{:S(2)}, u32[]{:S(2)}) collective-permute-start(bf16[9,256,128]{2,1,0:T(8,128)(2,1)S(1)} %grad_second.5.refs_0_.x), channel_id=1, source_target_pairs={{0,8},{4,12},{24,16},{28,20},{1,9},{5,13},{25,17},{29,21},{2,10},{... | collective-permute-start | bytes 1769480 | tf_op jit(solution)/shard_map/ppermute | solution.py:480
  87.3 4.4 %grad_first.1 = (bf16[1168,256]{1,0:T(8,128)(2,1)S(1)}, bf16[1168,256]{1,0:T(8,128)(2,1)S(1)}, bf16[1168,256]{1,0:T(8,128)(2,1)S(1)}) custom-call(bf16[128,1024]{1,0:T(8,128)(2,1)S(1)} %bitcast.17, bf16[128,1024]{1,0:T(8,128)(2,1)S(1)} %collective-permute-done.7.refs_5_.vol_other, bf16[2,1024,128]{2,1,0:T(8,128)(2,1)S(1)} %get-tuple-element.62.own.refs_0_, ...), custom_call_target="tpu_custom_call" | custom-call | flops 1024 | bytes 1024 | tf_op jit(solution)/shard_map/grad_first/pallas_call | solution.py:341
  91.7 4.8 %collective-permute-start.26 = (bf16[1168,256]{1,0:T(8,128)(2,1)S(1)}, bf16[1168,256]{1,0:T(8,128)(2,1)S(1)}, u32[]{:S(2)}, u32[]{:S(2)}) collective-permute-start(bf16[1168,256]{1,0:T(8,128)(2,1)S(1)} %get-tuple-element.66.refs_0_.x), channel_id=1, source_target_pairs={{0,8},{4,12},{24,16},{28,20},{1,9},{5,13},{25,17},{29,21},{2,10},{... | collective-permute-start | bytes 1794056 | tf_op jit(solution)/shard_map/ppermute | solution.py:480
  104.9 3.9 %collective-permute-done.26.y = bf16[1168,256]{1,0:T(8,128)(2,1)S(1)} collective-permute-done((bf16[1168,256]{1,0:T(8,128)(2,1)S(1)}, bf16[1168,256]{1,0:T(8,128)(2,1)S(1)}, u32[]{:S(2)}, u32[]{:S(2)}) %collective-permute-start.26) | collective-permute-done | bytes 598048 | tf_op jit(solution)/shard_map/ppermute | solution.py:480
  109.7 8.2 %collective-permute-start.28 = (bf16[1168,256]{1,0:T(8,128)(2,1)S(1)}, bf16[1168,256]{1,0:T(8,128)(2,1)S(1)}, u32[]{:S(2)}, u32[]{:S(2)}) collective-permute-start(bf16[1168,256]{1,0:T(8,128)(2,1)S(1)} %get-tuple-element.68.x), channel_id=1, source_target_pairs={{0,8},{4,12},{24,16},{28,20},{1,9},{5,13},{25,17},{29,21},{2,10},{... | collective-permute-start | bytes 1794056 | tf_op jit(solution)/shard_map/ppermute | solution.py:480
  118.8 2.0 %finish_second.3 = (f32[27,512,128]{2,1,0:T(8,128)}, f32[8,128]{1,0:T(8,128)S(1)}) custom-call(s32[2]{0:T(128)S(1)} %copy-done.13, bf16[9,256,128]{2,1,0:T(8,128)(2,1)S(1)} %line_pick.6.refs_0_.own, bf16[9,256,128]{2,1,0:T(8,128)(2,1)S(1)} %collective-permute-done.23.other, bf16[9,256,128]{2,1,0:T(8,128)(2,1)S(1)} %line_pick.7.refs_0_.own), custom_call_target="tpu_custom_call" | custom-call | flops 1024 | bytes 1024 | tf_op jit(solution)/shard_map/finish_second/pallas_call | solution.py:419
  125.2 13.7 %collective-permute-done.29.y = bf16[9,256,128]{2,1,0:T(8,128)(2,1)S(1)} collective-permute-done((bf16[9,256,128]{2,1,0:T(8,128)(2,1)S(1)}, bf16[9,256,128]{2,1,0:T(8,128)(2,1)S(1)}, u32[]{:S(2)}, u32[]{:S(2)}) %collective-permute-start.29) | collective-permute-done | bytes 589856 | tf_op jit(solution)/shard_map/ppermute | solution.py:480
  141.8 6.4 %collective-permute-start.34 = (bf16[9,256,128]{2,1,0:T(8,128)(2,1)S(1)}, bf16[9,256,128]{2,1,0:T(8,128)(2,1)S(1)}, u32[]{:S(2)}, u32[]{:S(2)}) collective-permute-start(bf16[9,256,128]{2,1,0:T(8,128)(2,1)S(1)} %line_pick.7.refs_0_.own), channel_id=1, source_target_pairs={{0,4},{4,0},{8,12},{12,8},{16,20},{20,16},{24,28},{28,24},{1,5},{5... | collective-permute-start | bytes 1769480 | tf_op jit(solution)/shard_map/ppermute | solution.py:509
  148.3 1.6 collective-permute-done.34.other
  149.8 2.0 %finish_second.4 = (f32[27,512,128]{2,1,0:T(8,128)}, f32[8,128]{1,0:T(8,128)S(1)}) custom-call(s32[2]{0:T(128)S(1)} %copy-done.13, bf16[9,256,128]{2,1,0:T(8,128)(2,1)S(1)} %line_pick.7.refs_0_.own, bf16[9,256,128]{2,1,0:T(8,128)(2,1)S(1)} %collective-permute-done.34.other, ...), custom_call_target="tpu_custom_call", output_to_operand_aliasing={{0}: (3, {})} | custom-call | flops 1024 | bytes 1024 | tf_op jit(solution)/shard_map/finish_second/pallas_call | solution.py:419
  152.5 6.2 %collective-permute-start.37 = (bf16[1168,256]{1,0:T(8,128)(2,1)S(1)}, bf16[1168,256]{1,0:T(8,128)(2,1)S(1)}, u32[]{:S(2)}, u32[]{:S(2)}) collective-permute-start(bf16[1168,256]{1,0:T(8,128)(2,1)S(1)} %line_pick.9.refs_1_.own), channel_id=1, source_target_pairs={{0,4},{4,0},{8,12},{12,8},{16,20},{20,16},{24,28},{28,24},{1,5},{5... | collective-permute-start | bytes 1794056 | tf_op jit(solution)/shard_map/ppermute | solution.py:509
  158.7 2.0 %finish_second.5 = (f32[27,512,128]{2,1,0:T(8,128)}, f32[8,128]{1,0:T(8,128)S(1)}) custom-call(s32[2]{0:T(128)S(1)} %copy-done.13, bf16[9,256,128]{2,1,0:T(8,128)(2,1)S(1)} %line_pick.8.refs_0_.own, bf16[9,256,128]{2,1,0:T(8,128)(2,1)S(1)} %collective-permute-done.33.other, ...), custom_call_target="tpu_custom_call", output_to_operand_aliasing={{0}: (3, {})} | custom-call | flops 1024 | bytes 1024 | tf_op jit(solution)/shard_map/finish_second/pallas_call | solution.py:419
  160.9 3.6 %collective-permute-done.31.y = bf16[1168,256]{1,0:T(8,128)(2,1)S(1)} collective-permute-done((bf16[1168,256]{1,0:T(8,128)(2,1)S(1)}, bf16[1168,256]{1,0:T(8,128)(2,1)S(1)}, u32[]{:S(2)}, u32[]{:S(2)}) %collective-permute-start.31) | collective-permute-done | bytes 598048 | tf_op jit(solution)/shard_map/ppermute | solution.py:480
  165.1 3.4 %collective-permute-start.36 = (bf16[1168,256]{1,0:T(8,128)(2,1)S(1)}, bf16[1168,256]{1,0:T(8,128)(2,1)S(1)}, u32[]{:S(2)}, u32[]{:S(2)}) collective-permute-start(bf16[1168,256]{1,0:T(8,128)(2,1)S(1)} %line_pick.10.refs_0_.own), channel_id=1, source_target_pairs={{0,4},{4,0},{8,12},{12,8},{16,20},{20,16},{24,28},{28,24},{1,5},{5... | collective-permute-start | bytes 1794056 | tf_op jit(solution)/shard_map/ppermute | solution.py:509
  169.8 2.0 %finish_first.3 = (f32[27,128,512]{2,1,0:T(8,128)}, f32[8,128]{1,0:T(8,128)S(1)}) custom-call(s32[2]{0:T(128)S(1)} %copy-done.13, bf16[1168,256]{1,0:T(8,128)(2,1)S(1)} %line_pick.9.refs_1_.own, bf16[1168,256]{1,0:T(8,128)(2,1)S(1)} %collective-permute-done.37.other, bf16[1168,256]{1,0:T(8,128)(2,1)S(1)} %line_pick.10.refs_0_.own), custom_call_target="tpu_custom_call" | custom-call | flops 1024 | bytes 1024 | tf_op jit(solution)/shard_map/finish_first/pallas_call | solution.py:419
  171.9 2.0 %finish_first.4 = (f32[27,128,512]{2,1,0:T(8,128)}, f32[8,128]{1,0:T(8,128)S(1)}) custom-call(s32[2]{0:T(128)S(1)} %copy-done.13, bf16[1168,256]{1,0:T(8,128)(2,1)S(1)} %line_pick.10.refs_0_.own, bf16[1168,256]{1,0:T(8,128)(2,1)S(1)} %collective-permute-done.36.other, f32[27,128,512]{2,1,0:T(8,128)} %get-tuple-element.73.refs_0_, ...), custom_call_target="tpu_custom_call", output_to_operand_aliasing={{0}: (3, {})} | custom-call | flops 1024 | bytes 1024 | tf_op jit(solution)/shard_map/finish_first/pallas_call | solution.py:419
  173.9 7.2 %grad_volume.1 = (bf16[128,1024]{1,0:T(8,128)(2,1)}, f32[8,128]{1,0:T(8,128)S(1)}) custom-call(s32[2]{0:T(128)S(1)} %copy-done.13, bf16[3456,512]{1,0:T(8,128)(2,1)S(1)} %bitcast.11, bf16[1024,128]{1,0:T(8,128)(2,1)S(1)} %get-tuple-element.61.refs_0_, bf16[1024,128]{1,0:T(8,128)(2,1)S(1)} %collective-permute-done.12.refs_1_, ...), custom_call_target="tpu_custom_call" | custom-call | flops 1024 | bytes 1024 | tf_op jit(solution)/shard_map/grad_volume/pallas_call | solution.py:208
  181.1 4.4 %collective-permute-done.38.y = bf16[1168,256]{1,0:T(8,128)(2,1)S(1)} collective-permute-done((bf16[1168,256]{1,0:T(8,128)(2,1)S(1)}, bf16[1168,256]{1,0:T(8,128)(2,1)S(1)}, u32[]{:S(2)}, u32[]{:S(2)}) %collective-permute-start.38) | collective-permute-done | bytes 598048 | tf_op jit(solution)/shard_map/ppermute | solution.py:480
  188.7 2.6 %finish_first.5 = (f32[27,128,512]{2,1,0:T(8,128)}, f32[8,128]{1,0:T(8,128)}) custom-call(s32[2]{0:T(128)S(1)} %copy-done.13, bf16[1168,256]{1,0:T(8,128)(2,1)S(1)} %line_pick.11.own.refs_1_, bf16[1168,256]{1,0:T(8,128)(2,1)S(1)} %collective-permute-done.39.other, f32[27,128,512]{2,1,0:T(8,128)} %get-tuple-element.78.refs_0_, ...), custom_call_target="tpu_custom_call", output_to_operand_aliasing={{0}: (3, {})} | custom-call | flops 1024 | bytes 1024 | tf_op jit(solution)/shard_map/finish_first/pallas_call | solution.py:419
  (119 shorter events, 53.9 us)
Async XLA Ops:
  8.5 14.0 %collective-permute-start = (bf16[1024,128]{1,0:T(8,128)(2,1)}, bf16[1024,128]{1,0:T(8,128)(2,1)S(1)}, u32[]{:S(2)}, u32[]{:S(2)}) collective-permute-start(bf16[1024,128]{1,0:T(8,128)(2,1)} %get-tuple-element.44), channel_id=1, source_target_pairs={{0,1},{1,0},{2,3},{3,2},{4,5},{5,4},{6,7},{7,6},{8,9},{9,8},{10,11... | collective-permute-start | bytes 786440 | tf_op jit(solution)/shard_map/ppermute | solution.py:506
  10.6 11.9 %collective-permute-start.1 = (bf16[1024,128]{1,0:T(8,128)(2,1)}, bf16[1024,128]{1,0:T(8,128)(2,1)S(1)}, u32[]{:S(2)}, u32[]{:S(2)}) collective-permute-start(bf16[1024,128]{1,0:T(8,128)(2,1)} %get-tuple-element.45), channel_id=1, source_target_pairs={{0,2},{1,3},{2,0},{3,1},{4,6},{5,7},{6,4},{7,5},{8,10},{9,11},{10,... | collective-permute-start | bytes 786440 | tf_op jit(solution)/shard_map/ppermute | solution.py:506
  11.8 11.6 %collective-permute-start.2 = (bf16[1024,128]{1,0:T(8,128)(2,1)}, bf16[1024,128]{1,0:T(8,128)(2,1)S(1)}, u32[]{:S(2)}, u32[]{:S(2)}) collective-permute-start(bf16[1024,128]{1,0:T(8,128)(2,1)} %get-tuple-element.46), channel_id=1, source_target_pairs={{0,3},{1,2},{2,1},{3,0},{4,7},{5,6},{6,5},{7,4},{8,11},{9,10},{10,... | collective-permute-start | bytes 786440 | tf_op jit(solution)/shard_map/ppermute | solution.py:506
  11.8 16.4 %collective-permute-start.7 = (bf16[128,1024]{1,0:T(8,128)(2,1)}, bf16[128,1024]{1,0:T(8,128)(2,1)S(1)}, u32[]{:S(2)}, u32[]{:S(2)}) collective-permute-start(bf16[128,1024]{1,0:T(8,128)(2,1)} %bitcast.16), channel_id=1, source_target_pairs={{0,4},{4,0},{8,12},{12,8},{16,20},{20,16},{24,28},{28,24},{1,5},{5... | collective-permute-start | bytes 786440 | tf_op jit(solution)/shard_map/ppermute | solution.py:509
  13.1 14.5 %collective-permute-start.6 = (bf16[128,1024]{1,0:T(8,128)(2,1)}, bf16[128,1024]{1,0:T(8,128)(2,1)S(1)}, u32[]{:S(2)}, u32[]{:S(2)}) collective-permute-start(bf16[128,1024]{1,0:T(8,128)(2,1)} %bitcast.12), channel_id=1, source_target_pairs={{0,4},{4,0},{8,12},{12,8},{16,20},{20,16},{24,28},{28,24},{1,5},{5... | collective-permute-start | bytes 786440 | tf_op jit(solution)/shard_map/ppermute | solution.py:509
  44.1 17.7 %collective-permute-start.15 = (bf16[9,256,128]{2,1,0:T(8,128)(2,1)S(1)}, bf16[9,256,128]{2,1,0:T(8,128)(2,1)S(1)}, u32[]{:S(2)}, u32[]{:S(2)}) collective-permute-start(bf16[9,256,128]{2,1,0:T(8,128)(2,1)S(1)} %grad_second.3.refs_0_.x), channel_id=1, source_target_pairs={{0,8},{4,12},{24,16},{28,20},{1,9},{5,13},{25,17},{29,21},{2,10},{... | collective-permute-start | bytes 1769480 | tf_op jit(solution)/shard_map/ppermute | solution.py:480
  47.4 12.9 %collective-permute-start.10 = (bf16[1024,128]{1,0:T(8,128)(2,1)S(1)}, bf16[1024,128]{1,0:T(8,128)(2,1)S(1)}, u32[]{:S(2)}, u32[]{:S(2)}) collective-permute-start(bf16[1024,128]{1,0:T(8,128)(2,1)S(1)} %get-tuple-element.58), channel_id=1, source_target_pairs={{0,2},{1,3},{2,0},{3,1},{4,6},{5,7},{6,4},{7,5},{8,10},{9,11},{10,... | collective-permute-start | bytes 786440 | tf_op jit(solution)/shard_map/ppermute | solution.py:506
  48.3 11.9 %collective-permute-start.11 = (bf16[1024,128]{1,0:T(8,128)(2,1)S(1)}, bf16[1024,128]{1,0:T(8,128)(2,1)S(1)}, u32[]{:S(2)}, u32[]{:S(2)}) collective-permute-start(bf16[1024,128]{1,0:T(8,128)(2,1)S(1)} %get-tuple-element.59), channel_id=1, source_target_pairs={{0,3},{1,2},{2,1},{3,0},{4,7},{5,6},{6,5},{7,4},{8,11},{9,10},{10,... | collective-permute-start | bytes 786440 | tf_op jit(solution)/shard_map/ppermute | solution.py:506
  49.2 12.0 %collective-permute-start.9 = (bf16[1024,128]{1,0:T(8,128)(2,1)S(1)}, bf16[1024,128]{1,0:T(8,128)(2,1)S(1)}, u32[]{:S(2)}, u32[]{:S(2)}) collective-permute-start(bf16[1024,128]{1,0:T(8,128)(2,1)S(1)} %get-tuple-element.57), channel_id=1, source_target_pairs={{0,1},{1,0},{2,3},{3,2},{4,5},{5,4},{6,7},{7,6},{8,9},{9,8},{10,11... | collective-permute-start | bytes 786440 | tf_op jit(solution)/shard_map/ppermute | solution.py:506
  51.6 20.7 %collective-permute-start.17 = (bf16[9,256,128]{2,1,0:T(8,128)(2,1)S(1)}, bf16[9,256,128]{2,1,0:T(8,128)(2,1)S(1)}, u32[]{:S(2)}, u32[]{:S(2)}) collective-permute-start(bf16[9,256,128]{2,1,0:T(8,128)(2,1)S(1)} %grad_second.4.refs_4_.x), channel_id=1, source_target_pairs={{0,8},{4,12},{24,16},{28,20},{1,9},{5,13},{25,17},{29,21},{2,10},{... | collective-permute-start | bytes 1769480 | tf_op jit(solution)/shard_map/ppermute | solution.py:480
  62.0 10.4 %collective-permute-start.16 = (bf16[9,256,128]{2,1,0:T(8,128)(2,1)S(1)}, bf16[9,256,128]{2,1,0:T(8,128)(2,1)S(1)}, u32[]{:S(2)}, u32[]{:S(2)}) collective-permute-start(bf16[9,256,128]{2,1,0:T(8,128)(2,1)S(1)} %line_add.12.refs_0_.x), channel_id=1, source_target_pairs={{8,16},{12,20},{16,8},{20,12},{9,17},{13,21},{17,9},{21,13},{10,18... | collective-permute-start | bytes 1769480 | tf_op jit(solution)/shard_map/ppermute | solution.py:480
  62.7 9.9 %collective-permute-start.12 = (bf16[1024,128]{1,0:T(8,128)(2,1)S(1)}, bf16[1024,128]{1,0:T(8,128)(2,1)S(1)}, u32[]{:S(2)}, u32[]{:S(2)}) collective-permute-start(bf16[1024,128]{1,0:T(8,128)(2,1)S(1)} %get-tuple-element.61.refs_0_), channel_id=1, source_target_pairs={{0,1},{1,0},{2,3},{3,2},{4,5},{5,4},{6,7},{7,6},{8,9},{9,8},{10,11... | collective-permute-start | bytes 786440 | tf_op jit(solution)/shard_map/ppermute | solution.py:506
  64.0 11.0 %collective-permute-start.14 = (bf16[1024,128]{1,0:T(8,128)(2,1)S(1)}, bf16[1024,128]{1,0:T(8,128)(2,1)S(1)}, u32[]{:S(2)}, u32[]{:S(2)}) collective-permute-start(bf16[1024,128]{1,0:T(8,128)(2,1)S(1)} %get-tuple-element.61.refs_0_), channel_id=1, source_target_pairs={{0,3},{1,2},{2,1},{3,0},{4,7},{5,6},{6,5},{7,4},{8,11},{9,10},{10,... | collective-permute-start | bytes 786440 | tf_op jit(solution)/shard_map/ppermute | solution.py:506
  76.4 10.8 %collective-permute-start.18 = (bf16[2,1024,128]{2,1,0:T(8,128)(2,1)}, bf16[2,1024,128]{2,1,0:T(8,128)(2,1)}, u32[]{:S(2)}, u32[]{:S(2)}) collective-permute-start(bf16[2,1024,128]{2,1,0:T(8,128)(2,1)} %get-tuple-element.63), channel_id=1, source_target_pairs={{0,4},{4,0},{8,12},{12,8},{16,20},{20,16},{24,28},{28,24},{1,5},{5... | collective-permute-start | bytes 1572872 | tf_op jit(solution)/shard_map/ppermute | solution.py:509
  79.2 18.8 %collective-permute-start.22 = (bf16[9,256,128]{2,1,0:T(8,128)(2,1)S(1)}, bf16[9,256,128]{2,1,0:T(8,128)(2,1)}, u32[]{:S(2)}, u32[]{:S(2)}) collective-permute-start(bf16[9,256,128]{2,1,0:T(8,128)(2,1)S(1)} %grad_second.5.refs_0_.x), channel_id=1, source_target_pairs={{0,8},{4,12},{24,16},{28,20},{1,9},{5,13},{25,17},{29,21},{2,10},{... | collective-permute-start | bytes 1769480 | tf_op jit(solution)/shard_map/ppermute | solution.py:480
  84.5 15.5 %collective-permute-start.21 = (bf16[9,256,128]{2,1,0:T(8,128)(2,1)S(1)}, bf16[9,256,128]{2,1,0:T(8,128)(2,1)}, u32[]{:S(2)}, u32[]{:S(2)}) collective-permute-start(bf16[9,256,128]{2,1,0:T(8,128)(2,1)S(1)} %line_add.13.refs_0_.x), channel_id=1, source_target_pairs={{8,16},{12,20},{16,8},{20,12},{9,17},{13,21},{17,9},{21,13},{10,18... | collective-permute-start | bytes 1769480 | tf_op jit(solution)/shard_map/ppermute | solution.py:480
  86.0 16.6 %collective-permute-start.20 = (bf16[9,256,128]{2,1,0:T(8,128)(2,1)S(1)}, bf16[9,256,128]{2,1,0:T(8,128)(2,1)}, u32[]{:S(2)}, u32[]{:S(2)}) collective-permute-start(bf16[9,256,128]{2,1,0:T(8,128)(2,1)S(1)} %line_add.14.refs_4_.x), channel_id=1, source_target_pairs={{8,0},{12,4},{16,24},{20,28},{9,1},{13,5},{17,25},{21,29},{10,2},{... | collective-permute-start | bytes 1769480 | tf_op jit(solution)/shard_map/ppermute | solution.py:480
  91.7 17.1 %collective-permute-start.26 = (bf16[1168,256]{1,0:T(8,128)(2,1)S(1)}, bf16[1168,256]{1,0:T(8,128)(2,1)S(1)}, u32[]{:S(2)}, u32[]{:S(2)}) collective-permute-start(bf16[1168,256]{1,0:T(8,128)(2,1)S(1)} %get-tuple-element.66.refs_0_.x), channel_id=1, source_target_pairs={{0,8},{4,12},{24,16},{28,20},{1,9},{5,13},{25,17},{29,21},{2,10},{... | collective-permute-start | bytes 1794056 | tf_op jit(solution)/shard_map/ppermute | solution.py:480
  96.6 25.1 %collective-permute-start.19 = (bf16[1168,256]{1,0:T(8,128)(2,1)S(1)}, bf16[1168,256]{1,0:T(8,128)(2,1)S(1)}, u32[]{:S(2)}, u32[]{:S(2)}) collective-permute-start(bf16[1168,256]{1,0:T(8,128)(2,1)S(1)} %get-tuple-element.65.x), channel_id=1, source_target_pairs={{0,8},{4,12},{24,16},{28,20},{1,9},{5,13},{25,17},{29,21},{2,10},{... | collective-permute-start | bytes 1794056 | tf_op jit(solution)/shard_map/ppermute | solution.py:480
  99.2 10.4 %collective-permute-start.25 = (bf16[9,256,128]{2,1,0:T(8,128)(2,1)S(1)}, bf16[9,256,128]{2,1,0:T(8,128)(2,1)S(1)}, u32[]{:S(2)}, u32[]{:S(2)}) collective-permute-start(bf16[9,256,128]{2,1,0:T(8,128)(2,1)S(1)} %line_add.15.refs_0_.x), channel_id=1, source_target_pairs={{8,16},{12,20},{16,8},{20,12},{9,17},{13,21},{17,9},{21,13},{10,18... | collective-permute-start | bytes 1769480 | tf_op jit(solution)/shard_map/ppermute | solution.py:480
  101.2 16.8 %collective-permute-start.24 = (bf16[9,256,128]{2,1,0:T(8,128)(2,1)S(1)}, bf16[9,256,128]{2,1,0:T(8,128)(2,1)S(1)}, u32[]{:S(2)}, u32[]{:S(2)}) collective-permute-start(bf16[9,256,128]{2,1,0:T(8,128)(2,1)S(1)} %line_add.16.refs_0_.x), channel_id=1, source_target_pairs={{8,0},{12,4},{16,24},{20,28},{9,1},{13,5},{17,25},{21,29},{10,2},{... | collective-permute-start | bytes 1769480 | tf_op jit(solution)/shard_map/ppermute | solution.py:480
  103.7 15.1 %collective-permute-start.23 = (bf16[9,256,128]{2,1,0:T(8,128)(2,1)S(1)}, bf16[9,256,128]{2,1,0:T(8,128)(2,1)S(1)}, u32[]{:S(2)}, u32[]{:S(2)}) collective-permute-start(bf16[9,256,128]{2,1,0:T(8,128)(2,1)S(1)} %line_pick.6.refs_0_.own), channel_id=1, source_target_pairs={{0,4},{4,0},{8,12},{12,8},{16,20},{20,16},{24,28},{28,24},{1,5},{5... | collective-permute-start | bytes 1769480 | tf_op jit(solution)/shard_map/ppermute | solution.py:509
  108.9 14.8 %collective-permute-start.30 = (bf16[1168,256]{1,0:T(8,128)(2,1)S(1)}, bf16[1168,256]{1,0:T(8,128)(2,1)S(1)}, u32[]{:S(2)}, u32[]{:S(2)}) collective-permute-start(bf16[1168,256]{1,0:T(8,128)(2,1)S(1)} %line_add.17.refs_0_.x), channel_id=1, source_target_pairs={{8,16},{12,20},{16,8},{20,12},{9,17},{13,21},{17,9},{21,13},{10,18... | collective-permute-start | bytes 1794056 | tf_op jit(solution)/shard_map/ppermute | solution.py:480
  109.7 29.8 %collective-permute-start.28 = (bf16[1168,256]{1,0:T(8,128)(2,1)S(1)}, bf16[1168,256]{1,0:T(8,128)(2,1)S(1)}, u32[]{:S(2)}, u32[]{:S(2)}) collective-permute-start(bf16[1168,256]{1,0:T(8,128)(2,1)S(1)} %get-tuple-element.68.x), channel_id=1, source_target_pairs={{0,8},{4,12},{24,16},{28,20},{1,9},{5,13},{25,17},{29,21},{2,10},{... | collective-permute-start | bytes 1794056 | tf_op jit(solution)/shard_map/ppermute | solution.py:480
  121.8 18.6 %collective-permute-start.27 = (bf16[1168,256]{1,0:T(8,128)(2,1)S(1)}, bf16[1168,256]{1,0:T(8,128)(2,1)S(1)}, u32[]{:S(2)}, u32[]{:S(2)}) collective-permute-start(bf16[1168,256]{1,0:T(8,128)(2,1)S(1)} %line_add.19.refs_0_.x), channel_id=1, source_target_pairs={{8,16},{12,20},{16,8},{20,12},{9,17},{13,21},{17,9},{21,13},{10,18... | collective-permute-start | bytes 1794056 | tf_op jit(solution)/shard_map/ppermute | solution.py:480
  122.5 16.4 %collective-permute-start.29 = (bf16[9,256,128]{2,1,0:T(8,128)(2,1)S(1)}, bf16[9,256,128]{2,1,0:T(8,128)(2,1)S(1)}, u32[]{:S(2)}, u32[]{:S(2)}) collective-permute-start(bf16[9,256,128]{2,1,0:T(8,128)(2,1)S(1)} %line_add.18.refs_0_.x), channel_id=1, source_target_pairs={{8,0},{12,4},{16,24},{20,28},{9,1},{13,5},{17,25},{21,29},{10,2},{... | collective-permute-start | bytes 1769480 | tf_op jit(solution)/shard_map/ppermute | solution.py:480
  123.9 27.9 %collective-permute-start.35 = (bf16[1168,256]{1,0:T(8,128)(2,1)S(1)}, bf16[1168,256]{1,0:T(8,128)(2,1)S(1)}, u32[]{:S(2)}, u32[]{:S(2)}) collective-permute-start(bf16[1168,256]{1,0:T(8,128)(2,1)S(1)} %line_add.20.refs_0_.x), channel_id=1, source_target_pairs={{8,0},{12,4},{16,24},{20,28},{9,1},{13,5},{17,25},{21,29},{10,2},{... | collective-permute-start | bytes 1794056 | tf_op jit(solution)/shard_map/ppermute | solution.py:480
  139.7 21.1 %collective-permute-start.32 = (bf16[1168,256]{1,0:T(8,128)(2,1)S(1)}, bf16[1168,256]{1,0:T(8,128)(2,1)S(1)}, u32[]{:S(2)}, u32[]{:S(2)}) collective-permute-start(bf16[1168,256]{1,0:T(8,128)(2,1)S(1)} %line_add.21.refs_0_.x), channel_id=1, source_target_pairs={{8,16},{12,20},{16,8},{20,12},{9,17},{13,21},{17,9},{21,13},{10,18... | collective-permute-start | bytes 1794056 | tf_op jit(solution)/shard_map/ppermute | solution.py:480
  140.5 24.0 %collective-permute-start.31 = (bf16[1168,256]{1,0:T(8,128)(2,1)S(1)}, bf16[1168,256]{1,0:T(8,128)(2,1)S(1)}, u32[]{:S(2)}, u32[]{:S(2)}) collective-permute-start(bf16[1168,256]{1,0:T(8,128)(2,1)S(1)} %line_add.22.refs_1_.x), channel_id=1, source_target_pairs={{8,0},{12,4},{16,24},{20,28},{9,1},{13,5},{17,25},{21,29},{10,2},{... | collective-permute-start | bytes 1794056 | tf_op jit(solution)/shard_map/ppermute | solution.py:480
  148.2 10.5 %collective-permute-start.33 = (bf16[9,256,128]{2,1,0:T(8,128)(2,1)S(1)}, bf16[9,256,128]{2,1,0:T(8,128)(2,1)S(1)}, u32[]{:S(2)}, u32[]{:S(2)}) collective-permute-start(bf16[9,256,128]{2,1,0:T(8,128)(2,1)S(1)} %line_pick.8.refs_0_.own), channel_id=1, source_target_pairs={{0,4},{4,0},{8,12},{12,8},{16,20},{20,16},{24,28},{28,24},{1,5},{5... | collective-permute-start | bytes 1769480 | tf_op jit(solution)/shard_map/ppermute | solution.py:509
  152.5 17.4 %collective-permute-start.37 = (bf16[1168,256]{1,0:T(8,128)(2,1)S(1)}, bf16[1168,256]{1,0:T(8,128)(2,1)S(1)}, u32[]{:S(2)}, u32[]{:S(2)}) collective-permute-start(bf16[1168,256]{1,0:T(8,128)(2,1)S(1)} %line_pick.9.refs_1_.own), channel_id=1, source_target_pairs={{0,4},{4,0},{8,12},{12,8},{16,20},{20,16},{24,28},{28,24},{1,5},{5... | collective-permute-start | bytes 1794056 | tf_op jit(solution)/shard_map/ppermute | solution.py:509
  168.5 17.0 %collective-permute-start.38 = (bf16[1168,256]{1,0:T(8,128)(2,1)S(1)}, bf16[1168,256]{1,0:T(8,128)(2,1)S(1)}, u32[]{:S(2)}, u32[]{:S(2)}) collective-permute-start(bf16[1168,256]{1,0:T(8,128)(2,1)S(1)} %line_add.23.refs_0_.x), channel_id=1, source_target_pairs={{8,0},{12,4},{16,24},{20,28},{9,1},{13,5},{17,25},{21,29},{10,2},{... | collective-permute-start | bytes 1794056 | tf_op jit(solution)/shard_map/ppermute | solution.py:480
  (22 other events, 261.5 us)

commit v11 on v7

--- a/solution.py
+++ b/solution.py
@@ -23,6 +23,42 @@
 IN_HBM = pl.BlockSpec(memory_space=pltpu.HBM)
 PLANE_ORDER = (0, -1, 1)
 LIGHT = pl.CostEstimate(flops=1024, bytes_accessed=1024, transcendentals=0)
+
+
+CHAIN = (
+    ("second", 0),
+    ("second", 1),
+    ("output",),
+    ("norm_back",),
+    ("line", 0, 0),
+    ("second", 2),
+    ("line", 1, 0),
+    ("line", 0, 1),
+    ("halves",),
+    ("first",),
+    ("line", 2, 0),
+    ("line", 1, 1),
+    ("line", 0, 2),
+    ("line", 3, 0),
+    ("line", 2, 1),
+    ("line", 1, 2),
+    ("write", 0),
+    ("line", 4, 0),
+    ("line", 3, 1),
+    ("line", 2, 2),
+    ("write", 1),
+    ("line", 5, 0),
+    ("line", 4, 1),
+    ("line", 3, 2),
+    ("write", 2),
+    ("line", 5, 1),
+    ("line", 4, 2),
+    ("grad_volume",),
+    ("write", 3),
+    ("line", 5, 2),
+    ("write", 4),
+    ("write", 5),
+)
 
 
 def params():
@@ -550,8 +586,15 @@
     parts, totals, crossed = {}, {}, {}
     last = ()
 
+    reached = [0] * 6
+
     def line(chunk, step):
         nonlocal last
+        if reached[chunk] > step:
+            return
+        if reached[chunk] < step:
+            line(chunk, step - 1)
+        reached[chunk] = step + 1
         before = totals.get(chunk, parts[chunk])
         totals[chunk] = line_step(step, parts[chunk], before, idx, place, last)
         last = (totals[chunk],)
@@ -560,6 +603,7 @@
 
     def write(chunk):
         nonlocal last
+        line(chunk, steps - 1)
         name, axis = ("finish_second", 1) if chunk < 3 else ("finish_first", 2)
         shape = (9, n // 2 * rows, rows) if chunk < 3 else (9, rows, n // 2 * rows)
         written[axis], mark = finish(
@@ -624,31 +668,19 @@
         )
         last = (mark,)
 
-    def wave(at):
-        for step in range(steps):
-            if 0 <= at - step < 6:
-                line(at - step, step)
-        if 0 <= at - steps < 6:
-            write(at - steps)
-
     written, done = {}, {}
-    second_part(0)
-    second_part(1)
-    output()
-    norm_back()
-    line(0, 0)
-    second_part(2)
-    line(1, 0)
-    line(0, 1)
-    dpre_halves()
-    first_parts()
-    wave(2)
-    wave(3)
-    wave(4)
-    wave(5)
-    grad_volume()
-    for at in range(6, 6 + steps):
-        wave(at)
+    steps_by_name = {
+        "second": second_part,
+        "first": first_parts,
+        "output": output,
+        "grad_volume": grad_volume,
+        "norm_back": norm_back,
+        "halves": dpre_halves,
+        "line": line,
+        "write": write,
+    }
+    for name, *at in CHAIN:
+        steps_by_name[name](*at)
     gain_rows = totals[3][9 * rows : 9 * rows + 2, :rows].astype(F32)
     gain_rows_other = crossed[3][9 * rows : 9 * rows + 2, :rows].astype(F32)
     gain_total = (jnp.sum(gain_rows, axis=0) + jnp.sum(gain_rows_other, axis=0)) * factor

time: 180 us -> 177 us (0.983)
  waiting for transfers between devices: 44.9 us -> 36.9 us
  starting transfers between devices: 66.7 us -> 70.9 us
    ppermute x18, waiting for transfers between devices: 30.4 us -> 22.4 us  [line_send(): return lax.ppermute(x, 'dp', pairs)]
    ppermute x10, starting transfers between devices: 16.4 us -> 20.7 us  [to_core(): lax.ppermute(x, 'dp', [(i, i ^ 1) for i in range(lax.axis_size('dp'))])]
  transfers between devices with their start and end apart: 40 -> 40, of which waited for: 11 -> 11; matrix products, arithmetic and copies ran while one was open for 0% -> 0% of each run, Pallas kernels for 27% -> 28%
where the time goes in v11:
time: 177 us; the launch traced here: 176 us
  starting transfers between devices  70.9 us (40%)
  Pallas kernels  60.5 us (34%)
  waiting for transfers between devices  36.9 us (21%)
  local copies, waits for them, and re-layouts  4.71 us (3%)
    ppermute x18, starting transfers between devices, line_send(): return lax.ppermute(x, 'dp', pairs)  38.7 us
    ppermute x18, waiting for transfers between devices, line_send(): return lax.ppermute(x, 'dp', pairs)  22.4 us
    ppermute x10, starting transfers between devices, to_core(): lax.ppermute(x, 'dp', [(i, i ^ 1) for i in range(lax.axis_size('dp'))])  20.7 us
    pallas_call x2, Pallas kernels, conv_full(): pl.pallas_call(functools.partial(conv_kernel, n, sign, transposed), in_sp...  14.2 us
    ppermute x12, waiting for transfers between devices, to_partner(): return lax.ppermute(x, 'chan', [(i, i ^ m) for i in range(n)])  12.9 us
    pallas_call x2, Pallas kernels, spread_shares(): pl.pallas_call(functools.partial(share_kernel, n, sign), in_specs=[smem()...  12.8 us
    pallas_call x6, Pallas kernels, finish(): pl.pallas_call(functools.partial(finish_kernel, n, axis, factor, chunk),...  12.7 us
    ppermute x12, starting transfers between devices, to_partner(): return lax.ppermute(x, 'chan', [(i, i ^ m) for i in range(n)])  11.5 us
  transfers between devices with their start and end apart: 40, of which 11 were waited for; matrix products, arithmetic and copies ran while one was open for 0% of the time, Pallas kernels for 28%

profile of v11, /device:TPU:1, one launch (start us, length us, event | category | flops | bytes accessed | tf_op | source)
XLA Modules:
  0.0 175.8 jit_solution(10826031759635493504)
XLA Ops:
  1.3 7.1 %pre.1 = (bf16[1024,128]{1,0:T(8,128)(2,1)}, bf16[1024,128]{1,0:T(8,128)(2,1)}, bf16[1024,128]{1,0:T(8,128)(2,1)}, bf16[1024,128]{1,0:T(8,128)(2,1)}) custom-call(s32[2]{0:T(128)} %pad_add_fusion.idx, bf16[128,1024]{1,0:T(8,128)(2,1)} %bitcast.15, bf16[3456,512]{1,0:T(8,128)(2,1)} %bitcast.10), custom_call_target="tpu_custom_call" | custom-call | flops 1024 | bytes 1024 | tf_op jit(solution)/shard_map/pre/pallas_call | solution.py:141
  8.5 2.1 %collective-permute-start = (bf16[1024,128]{1,0:T(8,128)(2,1)}, bf16[1024,128]{1,0:T(8,128)(2,1)S(1)}, u32[]{:S(2)}, u32[]{:S(2)}) collective-permute-start(bf16[1024,128]{1,0:T(8,128)(2,1)} %get-tuple-element.44), channel_id=1, source_target_pairs={{0,1},{1,0},{2,3},{3,2},{4,5},{5,4},{6,7},{7,6},{8,9},{9,8},{10,11... | collective-permute-start | bytes 786440 | tf_op jit(solution)/shard_map/ppermute | solution.py:542
  13.1 2.0 %copy-done.1 = bf16[27,512,128]{2,1,0:T(8,128)(2,1)S(1)} copy-done((bf16[27,512,128]{2,1,0:T(8,128)(2,1)S(1)}, bf16[27,512,128]{2,1,0:T(8,128)(2,1)}, u32[]{:S(2)}) %copy-start.1) | copy-done | bytes 3538968
  16.7 5.7 %dact.1 = (bf16[1024,128]{1,0:T(8,128)(2,1)S(1)}, bf16[1024,128]{1,0:T(8,128)(2,1)S(1)}, bf16[1024,128]{1,0:T(8,128)(2,1)S(1)}, bf16[1024,128]{1,0:T(8,128)(2,1)S(1)}) custom-call(s32[2]{0:T(128)S(1)} %copy-done.12, bf16[128,1024]{1,0:T(8,128)(2,1)S(1)} %bitcast.13, bf16[27,512,128]{2,1,0:T(8,128)(2,1)S(1)} %copy-done.1), custom_call_target="tpu_custom_call" | custom-call | flops 1024 | bytes 1024 | tf_op jit(solution)/shard_map/dact/pallas_call | solution.py:141
  24.9 1.8 %collective-permute-start.5 = (bf16[1024,128]{1,0:T(8,128)(2,1)S(1)}, bf16[1024,128]{1,0:T(8,128)(2,1)S(1)}, u32[]{:S(2)}, u32[]{:S(2)}) collective-permute-start(bf16[1024,128]{1,0:T(8,128)(2,1)S(1)} %get-tuple-element.50._.refs_0_), channel_id=1, source_target_pairs={{0,3},{1,2},{2,1},{3,0},{4,7},{5,6},{6,5},{7,4},{8,11},{9,10},{10,... | collective-permute-start | bytes 786440 | tf_op jit(solution)/shard_map/ppermute | solution.py:542
  28.3 3.7 %collective-permute-done.5.refs_3_ = bf16[1024,128]{1,0:T(8,128)(2,1)S(1)} collective-permute-done((bf16[1024,128]{1,0:T(8,128)(2,1)S(1)}, bf16[1024,128]{1,0:T(8,128)(2,1)S(1)}, u32[]{:S(2)}, u32[]{:S(2)}) %collective-permute-start.5) | collective-permute-done | bytes 262176 | tf_op jit(solution)/shard_map/ppermute | solution.py:542
  31.9 7.8 %collective-permute-done.4.refs_2_ = bf16[1024,128]{1,0:T(8,128)(2,1)S(1)} collective-permute-done((bf16[1024,128]{1,0:T(8,128)(2,1)S(1)}, bf16[1024,128]{1,0:T(8,128)(2,1)S(1)}, u32[]{:S(2)}, u32[]{:S(2)}) %collective-permute-start.4) | collective-permute-done | bytes 262176 | tf_op jit(solution)/shard_map/ppermute | solution.py:542
  41.2 1.5 collective-permute-done.8.other
  43.9 3.2 %collective-permute-start.15 = (bf16[9,256,128]{2,1,0:T(8,128)(2,1)S(1)}, bf16[9,256,128]{2,1,0:T(8,128)(2,1)S(1)}, u32[]{:S(2)}, u32[]{:S(2)}) collective-permute-start(bf16[9,256,128]{2,1,0:T(8,128)(2,1)S(1)} %grad_second.3.refs_0_.x), channel_id=1, source_target_pairs={{0,8},{4,12},{24,16},{28,20},{1,9},{5,13},{25,17},{29,21},{2,10},{... | collective-permute-start | bytes 1769480 | tf_op jit(solution)/shard_map/ppermute | solution.py:516
  49.9 1.5 grad_second.4.refs_4_.x
  52.9 7.0 %output.1 = (bf16[128,1024]{1,0:T(8,128)(2,1)}, f32[8,128]{1,0:T(8,128)S(1)}) custom-call(s32[2]{0:T(128)S(1)} %copy-done.13, bf16[27,512,128]{2,1,0:T(8,128)(2,1)S(1)} %copy-done.2, bf16[1024,128]{1,0:T(8,128)(2,1)S(1)} %get-tuple-element.50._.refs_0_, bf16[1024,128]{1,0:T(8,128)(2,1)S(1)} %collective-permute-done.3.refs_1_, ...), custom_call_target="tpu_custom_call" | custom-call | flops 1024 | bytes 1024 | tf_op jit(solution)/shard_map/output/pallas_call | solution.py:244
  66.0 6.1 %collective-permute-done.17.y = bf16[9,256,128]{2,1,0:T(8,128)(2,1)S(1)} collective-permute-done((bf16[9,256,128]{2,1,0:T(8,128)(2,1)S(1)}, bf16[9,256,128]{2,1,0:T(8,128)(2,1)S(1)}, u32[]{:S(2)}, u32[]{:S(2)}) %collective-permute-start.17) | collective-permute-done | bytes 589856 | tf_op jit(solution)/shard_map/ppermute | solution.py:516
  72.1 4.9 %collective-permute-start.22 = (bf16[9,256,128]{2,1,0:T(8,128)(2,1)S(1)}, bf16[9,256,128]{2,1,0:T(8,128)(2,1)}, u32[]{:S(2)}, u32[]{:S(2)}) collective-permute-start(bf16[9,256,128]{2,1,0:T(8,128)(2,1)S(1)} %grad_second.5.refs_0_.x), channel_id=1, source_target_pairs={{0,8},{4,12},{24,16},{28,20},{1,9},{5,13},{25,17},{29,21},{2,10},{... | collective-permute-start | bytes 1769480 | tf_op jit(solution)/shard_map/ppermute | solution.py:516
  83.1 4.4 %grad_first.1 = (bf16[1168,256]{1,0:T(8,128)(2,1)S(1)}, bf16[1168,256]{1,0:T(8,128)(2,1)S(1)}, bf16[1168,256]{1,0:T(8,128)(2,1)S(1)}) custom-call(bf16[128,1024]{1,0:T(8,128)(2,1)S(1)} %bitcast.17, bf16[128,1024]{1,0:T(8,128)(2,1)S(1)} %collective-permute-done.7.refs_5_.vol_other, bf16[2,1024,128]{2,1,0:T(8,128)(2,1)S(1)} %get-tuple-element.62.own.refs_0_, ...), custom_call_target="tpu_custom_call" | custom-call | flops 1024 | bytes 1024 | tf_op jit(solution)/shard_map/grad_first/pallas_call | solution.py:377
  87.5 5.2 %collective-permute-start.26 = (bf16[1168,256]{1,0:T(8,128)(2,1)S(1)}, bf16[1168,256]{1,0:T(8,128)(2,1)S(1)}, u32[]{:S(2)}, u32[]{:S(2)}) collective-permute-start(bf16[1168,256]{1,0:T(8,128)(2,1)S(1)} %get-tuple-element.66.refs_0_.x), channel_id=1, source_target_pairs={{0,8},{4,12},{24,16},{28,20},{1,9},{5,13},{25,17},{29,21},{2,10},{... | collective-permute-start | bytes 1794056 | tf_op jit(solution)/shard_map/ppermute | solution.py:516
  97.4 1.7 collective-permute-done.20.y
  101.1 4.5 %collective-permute-start.19 = (bf16[1168,256]{1,0:T(8,128)(2,1)S(1)}, bf16[1168,256]{1,0:T(8,128)(2,1)S(1)}, u32[]{:S(2)}, u32[]{:S(2)}) collective-permute-start(bf16[1168,256]{1,0:T(8,128)(2,1)S(1)} %get-tuple-element.65.x), channel_id=1, source_target_pairs={{0,8},{4,12},{24,16},{28,20},{1,9},{5,13},{25,17},{29,21},{2,10},{... | collective-permute-start | bytes 1794056 | tf_op jit(solution)/shard_map/ppermute | solution.py:516
  106.5 6.7 %collective-permute-start.28 = (bf16[1168,256]{1,0:T(8,128)(2,1)S(1)}, bf16[1168,256]{1,0:T(8,128)(2,1)S(1)}, u32[]{:S(2)}, u32[]{:S(2)}) collective-permute-start(bf16[1168,256]{1,0:T(8,128)(2,1)S(1)} %get-tuple-element.68.x), channel_id=1, source_target_pairs={{0,8},{4,12},{24,16},{28,20},{1,9},{5,13},{25,17},{29,21},{2,10},{... | collective-permute-start | bytes 1794056 | tf_op jit(solution)/shard_map/ppermute | solution.py:516
  115.8 1.9 %collective-permute-start.29 = (bf16[9,256,128]{2,1,0:T(8,128)(2,1)S(1)}, bf16[9,256,128]{2,1,0:T(8,128)(2,1)S(1)}, u32[]{:S(2)}, u32[]{:S(2)}) collective-permute-start(bf16[9,256,128]{2,1,0:T(8,128)(2,1)S(1)} %line_pick.7.refs_0_.own), channel_id=1, source_target_pairs={{0,4},{4,0},{8,12},{12,8},{16,20},{20,16},{24,28},{28,24},{1,5},{5... | collective-permute-start | bytes 1769480 | tf_op jit(solution)/shard_map/ppermute | solution.py:545
  117.6 2.0 %finish_second.3 = (f32[27,512,128]{2,1,0:T(8,128)}, f32[8,128]{1,0:T(8,128)S(1)}) custom-call(s32[2]{0:T(128)S(1)} %copy-done.13, bf16[9,256,128]{2,1,0:T(8,128)(2,1)S(1)} %line_pick.6.refs_0_.own, bf16[9,256,128]{2,1,0:T(8,128)(2,1)S(1)} %collective-permute-done.23.other, bf16[9,256,128]{2,1,0:T(8,128)(2,1)S(1)} %line_pick.7.refs_0_.own), custom_call_target="tpu_custom_call" | custom-call | flops 1024 | bytes 1024 | tf_op jit(solution)/shard_map/finish_second/pallas_call | solution.py:455
  122.0 6.6 %collective-permute-done.30.y = bf16[9,256,128]{2,1,0:T(8,128)(2,1)S(1)} collective-permute-done((bf16[9,256,128]{2,1,0:T(8,128)(2,1)S(1)}, bf16[9,256,128]{2,1,0:T(8,128)(2,1)S(1)}, u32[]{:S(2)}, u32[]{:S(2)}) %collective-permute-start.30) | collective-permute-done | bytes 589856 | tf_op jit(solution)/shard_map/ppermute | solution.py:516
  129.2 2.0 %finish_second.4 = (f32[27,512,128]{2,1,0:T(8,128)}, f32[8,128]{1,0:T(8,128)S(1)}) custom-call(s32[2]{0:T(128)S(1)} %copy-done.13, bf16[9,256,128]{2,1,0:T(8,128)(2,1)S(1)} %line_pick.7.refs_0_.own, bf16[9,256,128]{2,1,0:T(8,128)(2,1)S(1)} %collective-permute-done.29.other, ...), custom_call_target="tpu_custom_call", output_to_operand_aliasing={{0}: (3, {})} | custom-call | flops 1024 | bytes 1024 | tf_op jit(solution)/shard_map/finish_second/pallas_call | solution.py:455
  132.1 5.1 %collective-permute-start.34 = (bf16[9,256,128]{2,1,0:T(8,128)(2,1)S(1)}, bf16[9,256,128]{2,1,0:T(8,128)(2,1)S(1)}, u32[]{:S(2)}, u32[]{:S(2)}) collective-permute-start(bf16[9,256,128]{2,1,0:T(8,128)(2,1)S(1)} %line_pick.8.refs_1_.own), channel_id=1, source_target_pairs={{0,4},{4,0},{8,12},{12,8},{16,20},{20,16},{24,28},{28,24},{1,5},{5... | collective-permute-start | bytes 1769480 | tf_op jit(solution)/shard_map/ppermute | solution.py:545
  138.6 2.8 %collective-permute-done.35.y = bf16[1168,256]{1,0:T(8,128)(2,1)S(1)} collective-permute-done((bf16[1168,256]{1,0:T(8,128)(2,1)S(1)}, bf16[1168,256]{1,0:T(8,128)(2,1)S(1)}, u32[]{:S(2)}, u32[]{:S(2)}) %collective-permute-start.35) | collective-permute-done | bytes 598048 | tf_op jit(solution)/shard_map/ppermute | solution.py:516
  142.0 4.5 %collective-permute-start.37 = (bf16[1168,256]{1,0:T(8,128)(2,1)S(1)}, bf16[1168,256]{1,0:T(8,128)(2,1)S(1)}, u32[]{:S(2)}, u32[]{:S(2)}) collective-permute-start(bf16[1168,256]{1,0:T(8,128)(2,1)S(1)} %line_pick.9.refs_1_.own), channel_id=1, source_target_pairs={{0,4},{4,0},{8,12},{12,8},{16,20},{20,16},{24,28},{28,24},{1,5},{5... | collective-permute-start | bytes 1794056 | tf_op jit(solution)/shard_map/ppermute | solution.py:545
  146.5 2.0 %finish_second.5 = (f32[27,512,128]{2,1,0:T(8,128)}, f32[8,128]{1,0:T(8,128)S(1)}) custom-call(s32[2]{0:T(128)S(1)} %copy-done.13, bf16[9,256,128]{2,1,0:T(8,128)(2,1)S(1)} %line_pick.8.refs_1_.own, bf16[9,256,128]{2,1,0:T(8,128)(2,1)S(1)} %collective-permute-done.34.other, ...), custom_call_target="tpu_custom_call", output_to_operand_aliasing={{0}: (3, {})} | custom-call | flops 1024 | bytes 1024 | tf_op jit(solution)/shard_map/finish_second/pallas_call | solution.py:455
  150.0 4.8 %collective-permute-done.32.y = bf16[1168,256]{1,0:T(8,128)(2,1)S(1)} collective-permute-done((bf16[1168,256]{1,0:T(8,128)(2,1)S(1)}, bf16[1168,256]{1,0:T(8,128)(2,1)S(1)}, u32[]{:S(2)}, u32[]{:S(2)}) %collective-permute-start.32) | collective-permute-done | bytes 598048 | tf_op jit(solution)/shard_map/ppermute | solution.py:516
  155.4 3.9 %collective-permute-start.39 = (bf16[1168,256]{1,0:T(8,128)(2,1)S(1)}, bf16[1168,256]{1,0:T(8,128)(2,1)S(1)}, u32[]{:S(2)}, u32[]{:S(2)}) collective-permute-start(bf16[1168,256]{1,0:T(8,128)(2,1)S(1)} %line_pick.10.refs_4_.own), channel_id=1, source_target_pairs={{0,4},{4,0},{8,12},{12,8},{16,20},{20,16},{24,28},{28,24},{1,5},{5... | collective-permute-start | bytes 1794056 | tf_op jit(solution)/shard_map/ppermute | solution.py:545
  159.3 7.2 %grad_volume.1 = (bf16[128,1024]{1,0:T(8,128)(2,1)}, f32[8,128]{1,0:T(8,128)S(1)}) custom-call(s32[2]{0:T(128)S(1)} %copy-done.13, bf16[3456,512]{1,0:T(8,128)(2,1)S(1)} %bitcast.11, bf16[1024,128]{1,0:T(8,128)(2,1)S(1)} %get-tuple-element.61.refs_0_, bf16[1024,128]{1,0:T(8,128)(2,1)S(1)} %copy-done.10, bf16[1024,128]{1,0:T(8,128)(2,1)S(1)} %copy-done.8, ...), custom_call_target="tpu_custom_call" | custom-call | flops 1024 | bytes 1024 | tf_op jit(solution)/shard_map/grad_volume/pallas_call | solution.py:244
  166.5 2.0 %finish_first.3 = (f32[27,128,512]{2,1,0:T(8,128)}, f32[8,128]{1,0:T(8,128)S(1)}) custom-call(s32[2]{0:T(128)S(1)} %copy-done.13, bf16[1168,256]{1,0:T(8,128)(2,1)S(1)} %line_pick.9.refs_1_.own, bf16[1168,256]{1,0:T(8,128)(2,1)S(1)} %collective-permute-done.37.other, f32[8,128]{1,0:T(8,128)S(1)} %get-tuple-element.74.refs_0_), custom_call_target="tpu_custom_call" | custom-call | flops 1024 | bytes 1024 | tf_op jit(solution)/shard_map/finish_first/pallas_call | solution.py:455
  171.0 2.0 %finish_first.4 = (f32[27,128,512]{2,1,0:T(8,128)}, f32[8,128]{1,0:T(8,128)S(1)}) custom-call(s32[2]{0:T(128)S(1)} %copy-done.13, bf16[1168,256]{1,0:T(8,128)(2,1)S(1)} %line_pick.10.refs_4_.own, bf16[1168,256]{1,0:T(8,128)(2,1)S(1)} %collective-permute-done.39.other, f32[27,128,512]{2,1,0:T(8,128)} %get-tuple-element.76.refs_0_, ...), custom_call_target="tpu_custom_call", output_to_operand_aliasing={{0}: (3, {})} | custom-call | flops 1024 | bytes 1024 | tf_op jit(solution)/shard_map/finish_first/pallas_call | solution.py:455
  173.0 2.6 %finish_first.5 = (f32[27,128,512]{2,1,0:T(8,128)}, f32[8,128]{1,0:T(8,128)}) custom-call(s32[2]{0:T(128)S(1)} %copy-done.13, bf16[1168,256]{1,0:T(8,128)(2,1)S(1)} %line_pick.11.refs_1_.own, bf16[1168,256]{1,0:T(8,128)(2,1)S(1)} %collective-permute-done.38.other, f32[27,128,512]{2,1,0:T(8,128)} %get-tuple-element.77.refs_0_, ...), custom_call_target="tpu_custom_call", output_to_operand_aliasing={{0}: (3, {})} | custom-call | flops 1024 | bytes 1024 | tf_op jit(solution)/shard_map/finish_first/pallas_call | solution.py:455
  (119 shorter events, 47.9 us)
Async XLA Ops:
  8.5 14.0 %collective-permute-start = (bf16[1024,128]{1,0:T(8,128)(2,1)}, bf16[1024,128]{1,0:T(8,128)(2,1)S(1)}, u32[]{:S(2)}, u32[]{:S(2)}) collective-permute-start(bf16[1024,128]{1,0:T(8,128)(2,1)} %get-tuple-element.44), channel_id=1, source_target_pairs={{0,1},{1,0},{2,3},{3,2},{4,5},{5,4},{6,7},{7,6},{8,9},{9,8},{10,11... | collective-permute-start | bytes 786440 | tf_op jit(solution)/shard_map/ppermute | solution.py:542
  11.8 16.4 %collective-permute-start.7 = (bf16[128,1024]{1,0:T(8,128)(2,1)}, bf16[128,1024]{1,0:T(8,128)(2,1)S(1)}, u32[]{:S(2)}, u32[]{:S(2)}) collective-permute-start(bf16[128,1024]{1,0:T(8,128)(2,1)} %bitcast.16), channel_id=1, source_target_pairs={{0,4},{4,0},{8,12},{12,8},{16,20},{20,16},{24,28},{28,24},{1,5},{5... | collective-permute-start | bytes 786440 | tf_op jit(solution)/shard_map/ppermute | solution.py:545
  13.1 14.5 %collective-permute-start.6 = (bf16[128,1024]{1,0:T(8,128)(2,1)}, bf16[128,1024]{1,0:T(8,128)(2,1)S(1)}, u32[]{:S(2)}, u32[]{:S(2)}) collective-permute-start(bf16[128,1024]{1,0:T(8,128)(2,1)} %bitcast.12), channel_id=1, source_target_pairs={{0,4},{4,0},{8,12},{12,8},{16,20},{20,16},{24,28},{28,24},{1,5},{5... | collective-permute-start | bytes 786440 | tf_op jit(solution)/shard_map/ppermute | solution.py:545
  26.7 13.0 %collective-permute-start.4 = (bf16[1024,128]{1,0:T(8,128)(2,1)S(1)}, bf16[1024,128]{1,0:T(8,128)(2,1)S(1)}, u32[]{:S(2)}, u32[]{:S(2)}) collective-permute-start(bf16[1024,128]{1,0:T(8,128)(2,1)S(1)} %get-tuple-element.50._.refs_0_), channel_id=1, source_target_pairs={{0,2},{1,3},{2,0},{3,1},{4,6},{5,7},{6,4},{7,5},{8,10},{9,11},{10,... | collective-permute-start | bytes 786440 | tf_op jit(solution)/shard_map/ppermute | solution.py:542
  27.3 12.4 %collective-permute-start.3 = (bf16[1024,128]{1,0:T(8,128)(2,1)S(1)}, bf16[1024,128]{1,0:T(8,128)(2,1)S(1)}, u32[]{:S(2)}, u32[]{:S(2)}) collective-permute-start(bf16[1024,128]{1,0:T(8,128)(2,1)S(1)} %get-tuple-element.50._.refs_0_), channel_id=1, source_target_pairs={{0,1},{1,0},{2,3},{3,2},{4,5},{5,4},{6,7},{7,6},{8,9},{9,8},{10,11... | collective-permute-start | bytes 786440 | tf_op jit(solution)/shard_map/ppermute | solution.py:542
  43.9 17.4 %collective-permute-start.15 = (bf16[9,256,128]{2,1,0:T(8,128)(2,1)S(1)}, bf16[9,256,128]{2,1,0:T(8,128)(2,1)S(1)}, u32[]{:S(2)}, u32[]{:S(2)}) collective-permute-start(bf16[9,256,128]{2,1,0:T(8,128)(2,1)S(1)} %grad_second.3.refs_0_.x), channel_id=1, source_target_pairs={{0,8},{4,12},{24,16},{28,20},{1,9},{5,13},{25,17},{29,21},{2,10},{... | collective-permute-start | bytes 1769480 | tf_op jit(solution)/shard_map/ppermute | solution.py:516
  47.1 12.8 %collective-permute-start.9 = (bf16[1024,128]{1,0:T(8,128)(2,1)S(1)}, bf16[1024,128]{1,0:T(8,128)(2,1)S(1)}, u32[]{:S(2)}, u32[]{:S(2)}) collective-permute-start(bf16[1024,128]{1,0:T(8,128)(2,1)S(1)} %get-tuple-element.57), channel_id=1, source_target_pairs={{0,1},{1,0},{2,3},{3,2},{4,5},{5,4},{6,7},{7,6},{8,9},{9,8},{10,11... | collective-permute-start | bytes 786440 | tf_op jit(solution)/shard_map/ppermute | solution.py:542
  51.4 20.7 %collective-permute-start.17 = (bf16[9,256,128]{2,1,0:T(8,128)(2,1)S(1)}, bf16[9,256,128]{2,1,0:T(8,128)(2,1)S(1)}, u32[]{:S(2)}, u32[]{:S(2)}) collective-permute-start(bf16[9,256,128]{2,1,0:T(8,128)(2,1)S(1)} %grad_second.4.refs_4_.x), channel_id=1, source_target_pairs={{0,8},{4,12},{24,16},{28,20},{1,9},{5,13},{25,17},{29,21},{2,10},{... | collective-permute-start | bytes 1769480 | tf_op jit(solution)/shard_map/ppermute | solution.py:516
  61.4 15.7 %collective-permute-start.16 = (bf16[9,256,128]{2,1,0:T(8,128)(2,1)S(1)}, bf16[9,256,128]{2,1,0:T(8,128)(2,1)S(1)}, u32[]{:S(2)}, u32[]{:S(2)}) collective-permute-start(bf16[9,256,128]{2,1,0:T(8,128)(2,1)S(1)} %line_add.12.refs_0_.x), channel_id=1, source_target_pairs={{8,16},{12,20},{16,8},{20,12},{9,17},{13,21},{17,9},{21,13},{10,18... | collective-permute-start | bytes 1769480 | tf_op jit(solution)/shard_map/ppermute | solution.py:516
  62.1 15.2 %collective-permute-start.14 = (bf16[1024,128]{1,0:T(8,128)(2,1)S(1)}, bf16[1024,128]{1,0:T(8,128)(2,1)S(1)}, u32[]{:S(2)}, u32[]{:S(2)}) collective-permute-start(bf16[1024,128]{1,0:T(8,128)(2,1)S(1)} %get-tuple-element.61.refs_0_), channel_id=1, source_target_pairs={{0,3},{1,2},{2,1},{3,0},{4,7},{5,6},{6,5},{7,4},{8,11},{9,10},{10,... | collective-permute-start | bytes 786440 | tf_op jit(solution)/shard_map/ppermute | solution.py:542
  63.6 13.7 %collective-permute-start.13 = (bf16[1024,128]{1,0:T(8,128)(2,1)S(1)}, bf16[1024,128]{1,0:T(8,128)(2,1)S(1)}, u32[]{:S(2)}, u32[]{:S(2)}) collective-permute-start(bf16[1024,128]{1,0:T(8,128)(2,1)S(1)} %get-tuple-element.61.refs_0_), channel_id=1, source_target_pairs={{0,2},{1,3},{2,0},{3,1},{4,6},{5,7},{6,4},{7,5},{8,10},{9,11},{10,... | collective-permute-start | bytes 786440 | tf_op jit(solution)/shard_map/ppermute | solution.py:542
  64.2 13.1 %collective-permute-start.12 = (bf16[1024,128]{1,0:T(8,128)(2,1)S(1)}, bf16[1024,128]{1,0:T(8,128)(2,1)S(1)}, u32[]{:S(2)}, u32[]{:S(2)}) collective-permute-start(bf16[1024,128]{1,0:T(8,128)(2,1)S(1)} %get-tuple-element.61.refs_0_), channel_id=1, source_target_pairs={{0,1},{1,0},{2,3},{3,2},{4,5},{5,4},{6,7},{7,6},{8,9},{9,8},{10,11... | collective-permute-start | bytes 786440 | tf_op jit(solution)/shard_map/ppermute | solution.py:542
  72.1 20.7 %collective-permute-start.22 = (bf16[9,256,128]{2,1,0:T(8,128)(2,1)S(1)}, bf16[9,256,128]{2,1,0:T(8,128)(2,1)}, u32[]{:S(2)}, u32[]{:S(2)}) collective-permute-start(bf16[9,256,128]{2,1,0:T(8,128)(2,1)S(1)} %grad_second.5.refs_0_.x), channel_id=1, source_target_pairs={{0,8},{4,12},{24,16},{28,20},{1,9},{5,13},{25,17},{29,21},{2,10},{... | collective-permute-start | bytes 1769480 | tf_op jit(solution)/shard_map/ppermute | solution.py:516
  80.2 14.5 %collective-permute-start.21 = (bf16[9,256,128]{2,1,0:T(8,128)(2,1)S(1)}, bf16[9,256,128]{2,1,0:T(8,128)(2,1)}, u32[]{:S(2)}, u32[]{:S(2)}) collective-permute-start(bf16[9,256,128]{2,1,0:T(8,128)(2,1)S(1)} %line_add.13.refs_0_.x), channel_id=1, source_target_pairs={{8,16},{12,20},{16,8},{20,12},{9,17},{13,21},{17,9},{21,13},{10,18... | collective-permute-start | bytes 1769480 | tf_op jit(solution)/shard_map/ppermute | solution.py:516
  81.7 17.4 %collective-permute-start.20 = (bf16[9,256,128]{2,1,0:T(8,128)(2,1)S(1)}, bf16[9,256,128]{2,1,0:T(8,128)(2,1)}, u32[]{:S(2)}, u32[]{:S(2)}) collective-permute-start(bf16[9,256,128]{2,1,0:T(8,128)(2,1)S(1)} %line_add.14.refs_4_.x), channel_id=1, source_target_pairs={{8,0},{12,4},{16,24},{20,28},{9,1},{13,5},{17,25},{21,29},{10,2},{... | collective-permute-start | bytes 1769480 | tf_op jit(solution)/shard_map/ppermute | solution.py:516
  87.5 18.1 %collective-permute-start.26 = (bf16[1168,256]{1,0:T(8,128)(2,1)S(1)}, bf16[1168,256]{1,0:T(8,128)(2,1)S(1)}, u32[]{:S(2)}, u32[]{:S(2)}) collective-permute-start(bf16[1168,256]{1,0:T(8,128)(2,1)S(1)} %get-tuple-element.66.refs_0_.x), channel_id=1, source_target_pairs={{0,8},{4,12},{24,16},{28,20},{1,9},{5,13},{25,17},{29,21},{2,10},{... | collective-permute-start | bytes 1794056 | tf_op jit(solution)/shard_map/ppermute | solution.py:516
  94.0 12.4 %collective-permute-start.25 = (bf16[9,256,128]{2,1,0:T(8,128)(2,1)S(1)}, bf16[9,256,128]{2,1,0:T(8,128)(2,1)S(1)}, u32[]{:S(2)}, u32[]{:S(2)}) collective-permute-start(bf16[9,256,128]{2,1,0:T(8,128)(2,1)S(1)} %line_add.15.refs_0_.x), channel_id=1, source_target_pairs={{8,16},{12,20},{16,8},{20,12},{9,17},{13,21},{17,9},{21,13},{10,18... | collective-permute-start | bytes 1769480 | tf_op jit(solution)/shard_map/ppermute | solution.py:516
  96.1 17.6 %collective-permute-start.24 = (bf16[9,256,128]{2,1,0:T(8,128)(2,1)S(1)}, bf16[9,256,128]{2,1,0:T(8,128)(2,1)S(1)}, u32[]{:S(2)}, u32[]{:S(2)}) collective-permute-start(bf16[9,256,128]{2,1,0:T(8,128)(2,1)S(1)} %line_add.16.refs_0_.x), channel_id=1, source_target_pairs={{8,0},{12,4},{16,24},{20,28},{9,1},{13,5},{17,25},{21,29},{10,2},{... | collective-permute-start | bytes 1769480 | tf_op jit(solution)/shard_map/ppermute | solution.py:516
  100.2 15.6 %collective-permute-start.23 = (bf16[9,256,128]{2,1,0:T(8,128)(2,1)S(1)}, bf16[9,256,128]{2,1,0:T(8,128)(2,1)S(1)}, u32[]{:S(2)}, u32[]{:S(2)}) collective-permute-start(bf16[9,256,128]{2,1,0:T(8,128)(2,1)S(1)} %line_pick.6.refs_0_.own), channel_id=1, source_target_pairs={{0,4},{4,0},{8,12},{12,8},{16,20},{20,16},{24,28},{28,24},{1,5},{5... | collective-permute-start | bytes 1769480 | tf_op jit(solution)/shard_map/ppermute | solution.py:545
  101.1 18.6 %collective-permute-start.19 = (bf16[1168,256]{1,0:T(8,128)(2,1)S(1)}, bf16[1168,256]{1,0:T(8,128)(2,1)S(1)}, u32[]{:S(2)}, u32[]{:S(2)}) collective-permute-start(bf16[1168,256]{1,0:T(8,128)(2,1)S(1)} %get-tuple-element.65.x), channel_id=1, source_target_pairs={{0,8},{4,12},{24,16},{28,20},{1,9},{5,13},{25,17},{29,21},{2,10},{... | collective-permute-start | bytes 1794056 | tf_op jit(solution)/shard_map/ppermute | solution.py:516
  105.7 14.8 %collective-permute-start.31 = (bf16[1168,256]{1,0:T(8,128)(2,1)S(1)}, bf16[1168,256]{1,0:T(8,128)(2,1)S(1)}, u32[]{:S(2)}, u32[]{:S(2)}) collective-permute-start(bf16[1168,256]{1,0:T(8,128)(2,1)S(1)} %line_add.17.refs_0_.x), channel_id=1, source_target_pairs={{8,16},{12,20},{16,8},{20,12},{9,17},{13,21},{17,9},{21,13},{10,18... | collective-permute-start | bytes 1794056 | tf_op jit(solution)/shard_map/ppermute | solution.py:516
  106.5 24.8 %collective-permute-start.28 = (bf16[1168,256]{1,0:T(8,128)(2,1)S(1)}, bf16[1168,256]{1,0:T(8,128)(2,1)S(1)}, u32[]{:S(2)}, u32[]{:S(2)}) collective-permute-start(bf16[1168,256]{1,0:T(8,128)(2,1)S(1)} %get-tuple-element.68.x), channel_id=1, source_target_pairs={{0,8},{4,12},{24,16},{28,20},{1,9},{5,13},{25,17},{29,21},{2,10},{... | collective-permute-start | bytes 1794056 | tf_op jit(solution)/shard_map/ppermute | solution.py:516
  113.7 14.9 %collective-permute-start.30 = (bf16[9,256,128]{2,1,0:T(8,128)(2,1)S(1)}, bf16[9,256,128]{2,1,0:T(8,128)(2,1)S(1)}, u32[]{:S(2)}, u32[]{:S(2)}) collective-permute-start(bf16[9,256,128]{2,1,0:T(8,128)(2,1)S(1)} %line_add.18.refs_0_.x), channel_id=1, source_target_pairs={{8,0},{12,4},{16,24},{20,28},{9,1},{13,5},{17,25},{21,29},{10,2},{... | collective-permute-start | bytes 1769480 | tf_op jit(solution)/shard_map/ppermute | solution.py:516
  115.8 13.4 %collective-permute-start.29 = (bf16[9,256,128]{2,1,0:T(8,128)(2,1)S(1)}, bf16[9,256,128]{2,1,0:T(8,128)(2,1)S(1)}, u32[]{:S(2)}, u32[]{:S(2)}) collective-permute-start(bf16[9,256,128]{2,1,0:T(8,128)(2,1)S(1)} %line_pick.7.refs_0_.own), channel_id=1, source_target_pairs={{0,4},{4,0},{8,12},{12,8},{16,20},{20,16},{24,28},{28,24},{1,5},{5... | collective-permute-start | bytes 1769480 | tf_op jit(solution)/shard_map/ppermute | solution.py:545
  119.8 17.4 %collective-permute-start.27 = (bf16[1168,256]{1,0:T(8,128)(2,1)S(1)}, bf16[1168,256]{1,0:T(8,128)(2,1)S(1)}, u32[]{:S(2)}, u32[]{:S(2)}) collective-permute-start(bf16[1168,256]{1,0:T(8,128)(2,1)S(1)} %line_add.19.refs_0_.x), channel_id=1, source_target_pairs={{8,16},{12,20},{16,8},{20,12},{9,17},{13,21},{17,9},{21,13},{10,18... | collective-permute-start | bytes 1794056 | tf_op jit(solution)/shard_map/ppermute | solution.py:516
  120.7 20.7 %collective-permute-start.35 = (bf16[1168,256]{1,0:T(8,128)(2,1)S(1)}, bf16[1168,256]{1,0:T(8,128)(2,1)S(1)}, u32[]{:S(2)}, u32[]{:S(2)}) collective-permute-start(bf16[1168,256]{1,0:T(8,128)(2,1)S(1)} %line_add.20.refs_0_.x), channel_id=1, source_target_pairs={{8,0},{12,4},{16,24},{20,28},{9,1},{13,5},{17,25},{21,29},{10,2},{... | collective-permute-start | bytes 1794056 | tf_op jit(solution)/shard_map/ppermute | solution.py:516
  131.4 17.2 %collective-permute-start.33 = (bf16[1168,256]{1,0:T(8,128)(2,1)S(1)}, bf16[1168,256]{1,0:T(8,128)(2,1)S(1)}, u32[]{:S(2)}, u32[]{:S(2)}) collective-permute-start(bf16[1168,256]{1,0:T(8,128)(2,1)S(1)} %line_add.21.refs_0_.x), channel_id=1, source_target_pairs={{8,16},{12,20},{16,8},{20,12},{9,17},{13,21},{17,9},{21,13},{10,18... | collective-permute-start | bytes 1794056 | tf_op jit(solution)/shard_map/ppermute | solution.py:516
  132.1 14.4 %collective-permute-start.34 = (bf16[9,256,128]{2,1,0:T(8,128)(2,1)S(1)}, bf16[9,256,128]{2,1,0:T(8,128)(2,1)S(1)}, u32[]{:S(2)}, u32[]{:S(2)}) collective-permute-start(bf16[9,256,128]{2,1,0:T(8,128)(2,1)S(1)} %line_pick.8.refs_1_.own), channel_id=1, source_target_pairs={{0,4},{4,0},{8,12},{12,8},{16,20},{20,16},{24,28},{28,24},{1,5},{5... | collective-permute-start | bytes 1769480 | tf_op jit(solution)/shard_map/ppermute | solution.py:545
  137.3 17.5 %collective-permute-start.32 = (bf16[1168,256]{1,0:T(8,128)(2,1)S(1)}, bf16[1168,256]{1,0:T(8,128)(2,1)S(1)}, u32[]{:S(2)}, u32[]{:S(2)}) collective-permute-start(bf16[1168,256]{1,0:T(8,128)(2,1)S(1)} %line_add.22.refs_0_.x), channel_id=1, source_target_pairs={{8,0},{12,4},{16,24},{20,28},{9,1},{13,5},{17,25},{21,29},{10,2},{... | collective-permute-start | bytes 1794056 | tf_op jit(solution)/shard_map/ppermute | solution.py:516
  142.0 24.5 %collective-permute-start.37 = (bf16[1168,256]{1,0:T(8,128)(2,1)S(1)}, bf16[1168,256]{1,0:T(8,128)(2,1)S(1)}, u32[]{:S(2)}, u32[]{:S(2)}) collective-permute-start(bf16[1168,256]{1,0:T(8,128)(2,1)S(1)} %line_pick.9.refs_1_.own), channel_id=1, source_target_pairs={{0,4},{4,0},{8,12},{12,8},{16,20},{20,16},{24,28},{28,24},{1,5},{5... | collective-permute-start | bytes 1794056 | tf_op jit(solution)/shard_map/ppermute | solution.py:545
  148.7 19.8 %collective-permute-start.36 = (bf16[1168,256]{1,0:T(8,128)(2,1)S(1)}, bf16[1168,256]{1,0:T(8,128)(2,1)S(1)}, u32[]{:S(2)}, u32[]{:S(2)}) collective-permute-start(bf16[1168,256]{1,0:T(8,128)(2,1)S(1)} %line_add.23.refs_0_.x), channel_id=1, source_target_pairs={{8,0},{12,4},{16,24},{20,28},{9,1},{13,5},{17,25},{21,29},{10,2},{... | collective-permute-start | bytes 1794056 | tf_op jit(solution)/shard_map/ppermute | solution.py:516
  155.4 15.6 %collective-permute-start.39 = (bf16[1168,256]{1,0:T(8,128)(2,1)S(1)}, bf16[1168,256]{1,0:T(8,128)(2,1)S(1)}, u32[]{:S(2)}, u32[]{:S(2)}) collective-permute-start(bf16[1168,256]{1,0:T(8,128)(2,1)S(1)} %line_pick.10.refs_4_.own), channel_id=1, source_target_pairs={{0,4},{4,0},{8,12},{12,8},{16,20},{20,16},{24,28},{28,24},{1,5},{5... | collective-permute-start | bytes 1794056 | tf_op jit(solution)/shard_map/ppermute | solution.py:545
  (22 other events, 266.7 us)

commit v12 on v11

--- a/solution.py
+++ b/solution.py
@@ -13,9 +13,9 @@
 CELLS = DEPTH * PLANE
 TAPS = [(a, b, c) for a in (-1, 0, 1) for b in (-1, 0, 1) for c in (-1, 0, 1)]
 NORM_EPS = 1e-05
-LIMIT = 16 * 1024 * 1024
+LIMIT = 12 * 1024 * 1024
 SMALL = 8 * 1024 * 1024
-LARGE = 59 * 1024 * 1024
+LARGE = 44 * 1024 * 1024
 EXTRA = 16
 F32, BF16 = jnp.float32, jnp.bfloat16
 NT = (((1,), (1,)), ((), ()))

time: 177 us -> 178 us (level)
  local copies, waits for them, and re-layouts: 4.71 us -> 7.41 us
    unnamed x28 -> x26, local copies, waits for them, and re-layouts: 4.63 us -> 7.34 us
  transfers between devices with their start and end apart: 40 -> 40, of which waited for: 11 -> 12; matrix products, arithmetic and copies ran while one was open for 0% -> 0% of each run, Pallas kernels for 28% -> 27%
where the time goes in v12:
time: 178 us
  starting transfers between devices  70.7 us (40%)
  Pallas kernels  60.3 us (34%)
  waiting for transfers between devices  37 us (21%)
  local copies, waits for them, and re-layouts  7.41 us (4%)
    ppermute x18, starting transfers between devices, line_send(): return lax.ppermute(x, 'dp', pairs)  38.8 us
    ppermute x18, waiting for transfers between devices, line_send(): return lax.ppermute(x, 'dp', pairs)  22.6 us
    ppermute x10, starting transfers between devices, to_core(): lax.ppermute(x, 'dp', [(i, i ^ 1) for i in range(lax.axis_size('dp'))])  20.5 us
    pallas_call x2, Pallas kernels, conv_full(): pl.pallas_call(functools.partial(conv_kernel, n, sign, transposed), in_sp...  14.2 us
    ppermute x12, waiting for transfers between devices, to_partner(): return lax.ppermute(x, 'chan', [(i, i ^ m) for i in range(n)])  12.9 us
    pallas_call x6, Pallas kernels, finish(): pl.pallas_call(functools.partial(finish_kernel, n, axis, factor, chunk),...  12.7 us
    pallas_call x2, Pallas kernels, spread_shares(): pl.pallas_call(functools.partial(share_kernel, n, sign), in_specs=[smem()...  12.6 us
    ppermute x12, starting transfers between devices, to_partner(): return lax.ppermute(x, 'chan', [(i, i ^ m) for i in range(n)])  11.4 us
  transfers between devices with their start and end apart: 40, of which 12 were waited for; matrix products, arithmetic and copies ran while one was open for 0% of the time, Pallas kernels for 27%

profile of v12, /device:TPU:1, one launch (start us, length us, event | category | flops | bytes accessed | tf_op | source)
XLA Modules:
  0.0 177.6 jit_solution(12935444452177201259)
XLA Ops:
  0.7 2.0 %copy-done.3 = bf16[27,128,512]{2,1,0:T(8,128)(2,1)S(1)} copy-done((bf16[27,128,512]{2,1,0:T(8,128)(2,1)S(1)}, bf16[27,128,512]{2,1,0:T(8,128)(2,1)}, u32[]{:S(2)}) %copy-start.3) | copy-done | bytes 3538968
  2.7 6.9 %pre.1 = (bf16[1024,128]{1,0:T(8,128)(2,1)S(1)}, bf16[1024,128]{1,0:T(8,128)(2,1)}, bf16[1024,128]{1,0:T(8,128)(2,1)}, bf16[1024,128]{1,0:T(8,128)(2,1)S(1)}) custom-call(s32[2]{0:T(128)S(1)} %pad_add_fusion.idx, bf16[128,1024]{1,0:T(8,128)(2,1)} %bitcast.3.field.vol_own, bf16[3456,512]{1,0:T(8,128)(2,1)S(1)} %bitcast.10), custom_call_target="tpu_custom_call" | custom-call | flops 1024 | bytes 1024 | tf_op jit(solution)/shard_map/pre/pallas_call | solution.py:141
  9.6 2.1 %collective-permute-start = (bf16[1024,128]{1,0:T(8,128)(2,1)}, bf16[1024,128]{1,0:T(8,128)(2,1)S(1)}, u32[]{:S(2)}, u32[]{:S(2)}) collective-permute-start(bf16[1024,128]{1,0:T(8,128)(2,1)} %get-tuple-element.44), channel_id=1, source_target_pairs={{0,1},{1,0},{2,3},{3,2},{4,5},{5,4},{6,7},{7,6},{8,9},{9,8},{10,11... | collective-permute-start | bytes 786440 | tf_op jit(solution)/shard_map/ppermute | solution.py:542
  14.3 2.0 %copy-done.1 = bf16[27,512,128]{2,1,0:T(8,128)(2,1)S(1)} copy-done((bf16[27,512,128]{2,1,0:T(8,128)(2,1)S(1)}, bf16[27,512,128]{2,1,0:T(8,128)(2,1)}, u32[]{:S(2)}) %copy-start.1) | copy-done | bytes 3538968
  17.2 5.7 %dact.1 = (bf16[1024,128]{1,0:T(8,128)(2,1)S(1)}, bf16[1024,128]{1,0:T(8,128)(2,1)S(1)}, bf16[1024,128]{1,0:T(8,128)(2,1)S(1)}, bf16[1024,128]{1,0:T(8,128)(2,1)S(1)}) custom-call(s32[2]{0:T(128)S(1)} %pad_add_fusion.idx, bf16[128,1024]{1,0:T(8,128)(2,1)S(1)} %bitcast.13, bf16[27,512,128]{2,1,0:T(8,128)(2,1)S(1)} %copy-done.1), custom_call_target="tpu_custom_call" | custom-call | flops 1024 | bytes 1024 | tf_op jit(solution)/shard_map/dact/pallas_call | solution.py:141
  26.8 1.8 %collective-permute-start.5 = (bf16[1024,128]{1,0:T(8,128)(2,1)S(1)}, bf16[1024,128]{1,0:T(8,128)(2,1)S(1)}, u32[]{:S(2)}, u32[]{:S(2)}) collective-permute-start(bf16[1024,128]{1,0:T(8,128)(2,1)S(1)} %get-tuple-element.50._.refs_0_), channel_id=1, source_target_pairs={{0,3},{1,2},{2,1},{3,0},{4,7},{5,6},{6,5},{7,4},{8,11},{9,10},{10,... | collective-permute-start | bytes 786440 | tf_op jit(solution)/shard_map/ppermute | solution.py:542
  30.1 3.7 %collective-permute-done.5.refs_3_ = bf16[1024,128]{1,0:T(8,128)(2,1)S(1)} collective-permute-done((bf16[1024,128]{1,0:T(8,128)(2,1)S(1)}, bf16[1024,128]{1,0:T(8,128)(2,1)S(1)}, u32[]{:S(2)}, u32[]{:S(2)}) %collective-permute-start.5) | collective-permute-done | bytes 262176 | tf_op jit(solution)/shard_map/ppermute | solution.py:542
  33.7 7.8 %collective-permute-done.4.refs_2_ = bf16[1024,128]{1,0:T(8,128)(2,1)S(1)} collective-permute-done((bf16[1024,128]{1,0:T(8,128)(2,1)S(1)}, bf16[1024,128]{1,0:T(8,128)(2,1)S(1)}, u32[]{:S(2)}, u32[]{:S(2)}) %collective-permute-start.4) | collective-permute-done | bytes 262176 | tf_op jit(solution)/shard_map/ppermute | solution.py:542
  43.0 1.5 collective-permute-done.8.other
  45.7 3.2 %collective-permute-start.15 = (bf16[9,256,128]{2,1,0:T(8,128)(2,1)S(1)}, bf16[9,256,128]{2,1,0:T(8,128)(2,1)S(1)}, u32[]{:S(2)}, u32[]{:S(2)}) collective-permute-start(bf16[9,256,128]{2,1,0:T(8,128)(2,1)S(1)} %grad_second.3.refs_0_.x), channel_id=1, source_target_pairs={{0,8},{4,12},{24,16},{28,20},{1,9},{5,13},{25,17},{29,21},{2,10},{... | collective-permute-start | bytes 1769480 | tf_op jit(solution)/shard_map/ppermute | solution.py:516
  54.7 7.0 %output.1 = (bf16[128,1024]{1,0:T(8,128)(2,1)}, f32[8,128]{1,0:T(8,128)S(1)}) custom-call(s32[2]{0:T(128)S(1)} %pad_add_fusion.idx, bf16[27,512,128]{2,1,0:T(8,128)(2,1)S(1)} %copy-done.2, bf16[1024,128]{1,0:T(8,128)(2,1)S(1)} %get-tuple-element.50._.refs_0_, bf16[1024,128]{1,0:T(8,128)(2,1)S(1)} %collective-permute-done.3.refs_1_, ...), custom_call_target="tpu_custom_call" | custom-call | flops 1024 | bytes 1024 | tf_op jit(solution)/shard_map/output/pallas_call | solution.py:244
  67.9 6.0 %collective-permute-done.17.y = bf16[9,256,128]{2,1,0:T(8,128)(2,1)S(1)} collective-permute-done((bf16[9,256,128]{2,1,0:T(8,128)(2,1)S(1)}, bf16[9,256,128]{2,1,0:T(8,128)(2,1)S(1)}, u32[]{:S(2)}, u32[]{:S(2)}) %collective-permute-start.17) | collective-permute-done | bytes 589856 | tf_op jit(solution)/shard_map/ppermute | solution.py:516
  73.9 4.9 %collective-permute-start.22 = (bf16[9,256,128]{2,1,0:T(8,128)(2,1)S(1)}, bf16[9,256,128]{2,1,0:T(8,128)(2,1)}, u32[]{:S(2)}, u32[]{:S(2)}) collective-permute-start(bf16[9,256,128]{2,1,0:T(8,128)(2,1)S(1)} %grad_second.5.refs_0_.x), channel_id=1, source_target_pairs={{0,8},{4,12},{24,16},{28,20},{1,9},{5,13},{25,17},{29,21},{2,10},{... | collective-permute-start | bytes 1769480 | tf_op jit(solution)/shard_map/ppermute | solution.py:516
  84.9 4.5 %grad_first.1 = (bf16[1168,256]{1,0:T(8,128)(2,1)S(1)}, bf16[1168,256]{1,0:T(8,128)(2,1)S(1)}, bf16[1168,256]{1,0:T(8,128)(2,1)S(1)}) custom-call(bf16[128,1024]{1,0:T(8,128)(2,1)} %bitcast.3.field.vol_own, bf16[128,1024]{1,0:T(8,128)(2,1)S(1)} %collective-permute-done.7.refs_5_.vol_other, bf16[2,1024,128]{2,1,0:T(8,128)(2,1)S(1)} %get-tuple-element.62.own.refs_0_, ...), custom_call_target="tpu_custom_call" | custom-call | flops 1024 | bytes 1024 | tf_op jit(solution)/shard_map/grad_first/pallas_call | solution.py:377
  89.4 5.2 %collective-permute-start.26 = (bf16[1168,256]{1,0:T(8,128)(2,1)S(1)}, bf16[1168,256]{1,0:T(8,128)(2,1)S(1)}, u32[]{:S(2)}, u32[]{:S(2)}) collective-permute-start(bf16[1168,256]{1,0:T(8,128)(2,1)S(1)} %get-tuple-element.66.refs_0_.x), channel_id=1, source_target_pairs={{0,8},{4,12},{24,16},{28,20},{1,9},{5,13},{25,17},{29,21},{2,10},{... | collective-permute-start | bytes 1794056 | tf_op jit(solution)/shard_map/ppermute | solution.py:516
  99.1 1.8 %collective-permute-done.20.y = bf16[9,256,128]{2,1,0:T(8,128)(2,1)} collective-permute-done((bf16[9,256,128]{2,1,0:T(8,128)(2,1)S(1)}, bf16[9,256,128]{2,1,0:T(8,128)(2,1)}, u32[]{:S(2)}, u32[]{:S(2)}) %collective-permute-start.20) | collective-permute-done | bytes 589856 | tf_op jit(solution)/shard_map/ppermute | solution.py:516
  102.9 4.4 %collective-permute-start.19 = (bf16[1168,256]{1,0:T(8,128)(2,1)S(1)}, bf16[1168,256]{1,0:T(8,128)(2,1)S(1)}, u32[]{:S(2)}, u32[]{:S(2)}) collective-permute-start(bf16[1168,256]{1,0:T(8,128)(2,1)S(1)} %get-tuple-element.65.x), channel_id=1, source_target_pairs={{0,8},{4,12},{24,16},{28,20},{1,9},{5,13},{25,17},{29,21},{2,10},{... | collective-permute-start | bytes 1794056 | tf_op jit(solution)/shard_map/ppermute | solution.py:516
  108.2 6.7 %collective-permute-start.28 = (bf16[1168,256]{1,0:T(8,128)(2,1)S(1)}, bf16[1168,256]{1,0:T(8,128)(2,1)S(1)}, u32[]{:S(2)}, u32[]{:S(2)}) collective-permute-start(bf16[1168,256]{1,0:T(8,128)(2,1)S(1)} %get-tuple-element.68.x), channel_id=1, source_target_pairs={{0,8},{4,12},{24,16},{28,20},{1,9},{5,13},{25,17},{29,21},{2,10},{... | collective-permute-start | bytes 1794056 | tf_op jit(solution)/shard_map/ppermute | solution.py:516
  117.6 1.9 %collective-permute-start.29 = (bf16[9,256,128]{2,1,0:T(8,128)(2,1)S(1)}, bf16[9,256,128]{2,1,0:T(8,128)(2,1)S(1)}, u32[]{:S(2)}, u32[]{:S(2)}) collective-permute-start(bf16[9,256,128]{2,1,0:T(8,128)(2,1)S(1)} %line_pick.7.refs_0_.own), channel_id=1, source_target_pairs={{0,4},{4,0},{8,12},{12,8},{16,20},{20,16},{24,28},{28,24},{1,5},{5... | collective-permute-start | bytes 1769480 | tf_op jit(solution)/shard_map/ppermute | solution.py:545
  119.4 2.0 %finish_second.3 = (f32[27,512,128]{2,1,0:T(8,128)}, f32[8,128]{1,0:T(8,128)S(1)}) custom-call(s32[2]{0:T(128)S(1)} %pad_add_fusion.idx, bf16[9,256,128]{2,1,0:T(8,128)(2,1)S(1)} %line_pick.6.refs_0_.own, bf16[9,256,128]{2,1,0:T(8,128)(2,1)S(1)} %collective-permute-done.23.other, bf16[9,256,128]{2,1,0:T(8,128)(2,1)S(1)} %line_pick.7.refs_0_.own), custom_call_target="tpu_custom_call" | custom-call | flops 1024 | bytes 1024 | tf_op jit(solution)/shard_map/finish_second/pallas_call | solution.py:455
  123.8 6.6 %collective-permute-done.30.y = bf16[9,256,128]{2,1,0:T(8,128)(2,1)S(1)} collective-permute-done((bf16[9,256,128]{2,1,0:T(8,128)(2,1)S(1)}, bf16[9,256,128]{2,1,0:T(8,128)(2,1)S(1)}, u32[]{:S(2)}, u32[]{:S(2)}) %collective-permute-start.30) | collective-permute-done | bytes 589856 | tf_op jit(solution)/shard_map/ppermute | solution.py:516
  131.0 2.0 %finish_second.4 = (f32[27,512,128]{2,1,0:T(8,128)}, f32[8,128]{1,0:T(8,128)S(1)}) custom-call(s32[2]{0:T(128)S(1)} %pad_add_fusion.idx, bf16[9,256,128]{2,1,0:T(8,128)(2,1)S(1)} %line_pick.7.refs_0_.own, bf16[9,256,128]{2,1,0:T(8,128)(2,1)S(1)} %collective-permute-done.29.other, ...), custom_call_target="tpu_custom_call", output_to_operand_aliasing={{0}: (3, {})} | custom-call | flops 1024 | bytes 1024 | tf_op jit(solution)/shard_map/finish_second/pallas_call | solution.py:455
  134.1 4.8 %collective-permute-start.34 = (bf16[9,256,128]{2,1,0:T(8,128)(2,1)S(1)}, bf16[9,256,128]{2,1,0:T(8,128)(2,1)S(1)}, u32[]{:S(2)}, u32[]{:S(2)}) collective-permute-start(bf16[9,256,128]{2,1,0:T(8,128)(2,1)S(1)} %line_pick.8.refs_1_.own), channel_id=1, source_target_pairs={{0,4},{4,0},{8,12},{12,8},{16,20},{20,16},{24,28},{28,24},{1,5},{5... | collective-permute-start | bytes 1769480 | tf_op jit(solution)/shard_map/ppermute | solution.py:545
  140.4 2.8 %collective-permute-done.35.y = bf16[1168,256]{1,0:T(8,128)(2,1)S(1)} collective-permute-done((bf16[1168,256]{1,0:T(8,128)(2,1)S(1)}, bf16[1168,256]{1,0:T(8,128)(2,1)S(1)}, u32[]{:S(2)}, u32[]{:S(2)}) %collective-permute-start.35) | collective-permute-done | bytes 598048 | tf_op jit(solution)/shard_map/ppermute | solution.py:516
  143.8 4.5 %collective-permute-start.37 = (bf16[1168,256]{1,0:T(8,128)(2,1)S(1)}, bf16[1168,256]{1,0:T(8,128)(2,1)S(1)}, u32[]{:S(2)}, u32[]{:S(2)}) collective-permute-start(bf16[1168,256]{1,0:T(8,128)(2,1)S(1)} %line_pick.9.refs_1_.own), channel_id=1, source_target_pairs={{0,4},{4,0},{8,12},{12,8},{16,20},{20,16},{24,28},{28,24},{1,5},{5... | collective-permute-start | bytes 1794056 | tf_op jit(solution)/shard_map/ppermute | solution.py:545
  148.3 2.0 %finish_second.5 = (f32[27,512,128]{2,1,0:T(8,128)}, f32[8,128]{1,0:T(8,128)S(1)}) custom-call(s32[2]{0:T(128)S(1)} %pad_add_fusion.idx, bf16[9,256,128]{2,1,0:T(8,128)(2,1)S(1)} %line_pick.8.refs_1_.own, bf16[9,256,128]{2,1,0:T(8,128)(2,1)S(1)} %collective-permute-done.34.other, ...), custom_call_target="tpu_custom_call", output_to_operand_aliasing={{0}: (3, {})} | custom-call | flops 1024 | bytes 1024 | tf_op jit(solution)/shard_map/finish_second/pallas_call | solution.py:455
  151.8 4.8 %collective-permute-done.32.y = bf16[1168,256]{1,0:T(8,128)(2,1)S(1)} collective-permute-done((bf16[1168,256]{1,0:T(8,128)(2,1)S(1)}, bf16[1168,256]{1,0:T(8,128)(2,1)S(1)}, u32[]{:S(2)}, u32[]{:S(2)}) %collective-permute-start.32) | collective-permute-done | bytes 598048 | tf_op jit(solution)/shard_map/ppermute | solution.py:516
  157.2 3.9 %collective-permute-start.39 = (bf16[1168,256]{1,0:T(8,128)(2,1)S(1)}, bf16[1168,256]{1,0:T(8,128)(2,1)S(1)}, u32[]{:S(2)}, u32[]{:S(2)}) collective-permute-start(bf16[1168,256]{1,0:T(8,128)(2,1)S(1)} %line_pick.10.refs_4_.own), channel_id=1, source_target_pairs={{0,4},{4,0},{8,12},{12,8},{16,20},{20,16},{24,28},{28,24},{1,5},{5... | collective-permute-start | bytes 1794056 | tf_op jit(solution)/shard_map/ppermute | solution.py:545
  161.1 7.2 %grad_volume.1 = (bf16[128,1024]{1,0:T(8,128)(2,1)}, f32[8,128]{1,0:T(8,128)S(1)}) custom-call(s32[2]{0:T(128)S(1)} %pad_add_fusion.idx, bf16[3456,512]{1,0:T(8,128)(2,1)S(1)} %bitcast.11, bf16[1024,128]{1,0:T(8,128)(2,1)S(1)} %get-tuple-element.61.refs_0_, bf16[1024,128]{1,0:T(8,128)(2,1)S(1)} %copy-done.8, ...), custom_call_target="tpu_custom_call" | custom-call | flops 1024 | bytes 1024 | tf_op jit(solution)/shard_map/grad_volume/pallas_call | solution.py:244
  168.3 2.0 %finish_first.3 = (f32[27,128,512]{2,1,0:T(8,128)}, f32[8,128]{1,0:T(8,128)S(1)}) custom-call(s32[2]{0:T(128)S(1)} %pad_add_fusion.idx, bf16[1168,256]{1,0:T(8,128)(2,1)S(1)} %line_pick.9.refs_1_.own, bf16[1168,256]{1,0:T(8,128)(2,1)S(1)} %collective-permute-done.37.other, f32[8,128]{1,0:T(8,128)S(1)} %get-tuple-element.74.refs_0_), custom_call_target="tpu_custom_call" | custom-call | flops 1024 | bytes 1024 | tf_op jit(solution)/shard_map/finish_first/pallas_call | solution.py:455
  172.7 2.0 %finish_first.4 = (f32[27,128,512]{2,1,0:T(8,128)}, f32[8,128]{1,0:T(8,128)S(1)}) custom-call(s32[2]{0:T(128)S(1)} %pad_add_fusion.idx, bf16[1168,256]{1,0:T(8,128)(2,1)S(1)} %line_pick.10.refs_4_.own, bf16[1168,256]{1,0:T(8,128)(2,1)S(1)} %collective-permute-done.39.other, ...), custom_call_target="tpu_custom_call", output_to_operand_aliasing={{0}: (3, {})} | custom-call | flops 1024 | bytes 1024 | tf_op jit(solution)/shard_map/finish_first/pallas_call | solution.py:455
  174.8 2.6 %finish_first.5 = (f32[27,128,512]{2,1,0:T(8,128)}, f32[8,128]{1,0:T(8,128)}) custom-call(s32[2]{0:T(128)S(1)} %pad_add_fusion.idx, bf16[1168,256]{1,0:T(8,128)(2,1)S(1)} %line_pick.11.refs_1_.own, bf16[1168,256]{1,0:T(8,128)(2,1)S(1)} %collective-permute-done.38.other, f32[27,128,512]{2,1,0:T(8,128)} %get-tuple-element.77.refs_0_, ...), custom_call_target="tpu_custom_call", output_to_operand_aliasing={{0}: (3, {})} | custom-call | flops 1024 | bytes 1024 | tf_op jit(solution)/shard_map/finish_first/pallas_call | solution.py:455
  (117 shorter events, 49.7 us)
Async XLA Ops:
  9.6 14.0 %collective-permute-start = (bf16[1024,128]{1,0:T(8,128)(2,1)}, bf16[1024,128]{1,0:T(8,128)(2,1)S(1)}, u32[]{:S(2)}, u32[]{:S(2)}) collective-permute-start(bf16[1024,128]{1,0:T(8,128)(2,1)} %get-tuple-element.44), channel_id=1, source_target_pairs={{0,1},{1,0},{2,3},{3,2},{4,5},{5,4},{6,7},{7,6},{8,9},{9,8},{10,11... | collective-permute-start | bytes 786440 | tf_op jit(solution)/shard_map/ppermute | solution.py:542
  13.0 17.1 %collective-permute-start.7 = (bf16[128,1024]{1,0:T(8,128)(2,1)}, bf16[128,1024]{1,0:T(8,128)(2,1)S(1)}, u32[]{:S(2)}, u32[]{:S(2)}) collective-permute-start(bf16[128,1024]{1,0:T(8,128)(2,1)} %bitcast.3.field.vol_own), channel_id=1, source_target_pairs={{0,4},{4,0},{8,12},{12,8},{16,20},{20,16},{24,28},{28,24},{1,5},{5... | collective-permute-start | bytes 786440 | tf_op jit(solution)/shard_map/ppermute | solution.py:545
  14.2 15.2 %collective-permute-start.6 = (bf16[128,1024]{1,0:T(8,128)(2,1)}, bf16[128,1024]{1,0:T(8,128)(2,1)S(1)}, u32[]{:S(2)}, u32[]{:S(2)}) collective-permute-start(bf16[128,1024]{1,0:T(8,128)(2,1)} %bitcast.12), channel_id=1, source_target_pairs={{0,4},{4,0},{8,12},{12,8},{16,20},{20,16},{24,28},{28,24},{1,5},{5... | collective-permute-start | bytes 786440 | tf_op jit(solution)/shard_map/ppermute | solution.py:545
  28.5 13.0 %collective-permute-start.4 = (bf16[1024,128]{1,0:T(8,128)(2,1)S(1)}, bf16[1024,128]{1,0:T(8,128)(2,1)S(1)}, u32[]{:S(2)}, u32[]{:S(2)}) collective-permute-start(bf16[1024,128]{1,0:T(8,128)(2,1)S(1)} %get-tuple-element.50._.refs_0_), channel_id=1, source_target_pairs={{0,2},{1,3},{2,0},{3,1},{4,6},{5,7},{6,4},{7,5},{8,10},{9,11},{10,... | collective-permute-start | bytes 786440 | tf_op jit(solution)/shard_map/ppermute | solution.py:542
  29.1 12.4 %collective-permute-start.3 = (bf16[1024,128]{1,0:T(8,128)(2,1)S(1)}, bf16[1024,128]{1,0:T(8,128)(2,1)S(1)}, u32[]{:S(2)}, u32[]{:S(2)}) collective-permute-start(bf16[1024,128]{1,0:T(8,128)(2,1)S(1)} %get-tuple-element.50._.refs_0_), channel_id=1, source_target_pairs={{0,1},{1,0},{2,3},{3,2},{4,5},{5,4},{6,7},{7,6},{8,9},{9,8},{10,11... | collective-permute-start | bytes 786440 | tf_op jit(solution)/shard_map/ppermute | solution.py:542
  45.7 17.4 %collective-permute-start.15 = (bf16[9,256,128]{2,1,0:T(8,128)(2,1)S(1)}, bf16[9,256,128]{2,1,0:T(8,128)(2,1)S(1)}, u32[]{:S(2)}, u32[]{:S(2)}) collective-permute-start(bf16[9,256,128]{2,1,0:T(8,128)(2,1)S(1)} %grad_second.3.refs_0_.x), channel_id=1, source_target_pairs={{0,8},{4,12},{24,16},{28,20},{1,9},{5,13},{25,17},{29,21},{2,10},{... | collective-permute-start | bytes 1769480 | tf_op jit(solution)/shard_map/ppermute | solution.py:516
  48.9 12.8 %collective-permute-start.9 = (bf16[1024,128]{1,0:T(8,128)(2,1)S(1)}, bf16[1024,128]{1,0:T(8,128)(2,1)S(1)}, u32[]{:S(2)}, u32[]{:S(2)}) collective-permute-start(bf16[1024,128]{1,0:T(8,128)(2,1)S(1)} %get-tuple-element.57), channel_id=1, source_target_pairs={{0,1},{1,0},{2,3},{3,2},{4,5},{5,4},{6,7},{7,6},{8,9},{9,8},{10,11... | collective-permute-start | bytes 786440 | tf_op jit(solution)/shard_map/ppermute | solution.py:542
  53.2 20.7 %collective-permute-start.17 = (bf16[9,256,128]{2,1,0:T(8,128)(2,1)S(1)}, bf16[9,256,128]{2,1,0:T(8,128)(2,1)S(1)}, u32[]{:S(2)}, u32[]{:S(2)}) collective-permute-start(bf16[9,256,128]{2,1,0:T(8,128)(2,1)S(1)} %grad_second.4.refs_4_.x), channel_id=1, source_target_pairs={{0,8},{4,12},{24,16},{28,20},{1,9},{5,13},{25,17},{29,21},{2,10},{... | collective-permute-start | bytes 1769480 | tf_op jit(solution)/shard_map/ppermute | solution.py:516
  63.2 15.7 %collective-permute-start.16 = (bf16[9,256,128]{2,1,0:T(8,128)(2,1)S(1)}, bf16[9,256,128]{2,1,0:T(8,128)(2,1)S(1)}, u32[]{:S(2)}, u32[]{:S(2)}) collective-permute-start(bf16[9,256,128]{2,1,0:T(8,128)(2,1)S(1)} %line_add.12.refs_0_.x), channel_id=1, source_target_pairs={{8,16},{12,20},{16,8},{20,12},{9,17},{13,21},{17,9},{21,13},{10,18... | collective-permute-start | bytes 1769480 | tf_op jit(solution)/shard_map/ppermute | solution.py:516
  64.0 15.2 %collective-permute-start.14 = (bf16[1024,128]{1,0:T(8,128)(2,1)S(1)}, bf16[1024,128]{1,0:T(8,128)(2,1)S(1)}, u32[]{:S(2)}, u32[]{:S(2)}) collective-permute-start(bf16[1024,128]{1,0:T(8,128)(2,1)S(1)} %get-tuple-element.61.refs_0_), channel_id=1, source_target_pairs={{0,3},{1,2},{2,1},{3,0},{4,7},{5,6},{6,5},{7,4},{8,11},{9,10},{10,... | collective-permute-start | bytes 786440 | tf_op jit(solution)/shard_map/ppermute | solution.py:542
  65.4 13.7 %collective-permute-start.13 = (bf16[1024,128]{1,0:T(8,128)(2,1)S(1)}, bf16[1024,128]{1,0:T(8,128)(2,1)S(1)}, u32[]{:S(2)}, u32[]{:S(2)}) collective-permute-start(bf16[1024,128]{1,0:T(8,128)(2,1)S(1)} %get-tuple-element.61.refs_0_), channel_id=1, source_target_pairs={{0,2},{1,3},{2,0},{3,1},{4,6},{5,7},{6,4},{7,5},{8,10},{9,11},{10,... | collective-permute-start | bytes 786440 | tf_op jit(solution)/shard_map/ppermute | solution.py:542
  66.1 13.1 %collective-permute-start.12 = (bf16[1024,128]{1,0:T(8,128)(2,1)S(1)}, bf16[1024,128]{1,0:T(8,128)(2,1)S(1)}, u32[]{:S(2)}, u32[]{:S(2)}) collective-permute-start(bf16[1024,128]{1,0:T(8,128)(2,1)S(1)} %get-tuple-element.61.refs_0_), channel_id=1, source_target_pairs={{0,1},{1,0},{2,3},{3,2},{4,5},{5,4},{6,7},{7,6},{8,9},{9,8},{10,11... | collective-permute-start | bytes 786440 | tf_op jit(solution)/shard_map/ppermute | solution.py:542
  73.9 20.8 %collective-permute-start.22 = (bf16[9,256,128]{2,1,0:T(8,128)(2,1)S(1)}, bf16[9,256,128]{2,1,0:T(8,128)(2,1)}, u32[]{:S(2)}, u32[]{:S(2)}) collective-permute-start(bf16[9,256,128]{2,1,0:T(8,128)(2,1)S(1)} %grad_second.5.refs_0_.x), channel_id=1, source_target_pairs={{0,8},{4,12},{24,16},{28,20},{1,9},{5,13},{25,17},{29,21},{2,10},{... | collective-permute-start | bytes 1769480 | tf_op jit(solution)/shard_map/ppermute | solution.py:516
  82.1 14.6 %collective-permute-start.21 = (bf16[9,256,128]{2,1,0:T(8,128)(2,1)S(1)}, bf16[9,256,128]{2,1,0:T(8,128)(2,1)}, u32[]{:S(2)}, u32[]{:S(2)}) collective-permute-start(bf16[9,256,128]{2,1,0:T(8,128)(2,1)S(1)} %line_add.13.refs_0_.x), channel_id=1, source_target_pairs={{8,16},{12,20},{16,8},{20,12},{9,17},{13,21},{17,9},{21,13},{10,18... | collective-permute-start | bytes 1769480 | tf_op jit(solution)/shard_map/ppermute | solution.py:516
  83.6 17.4 %collective-permute-start.20 = (bf16[9,256,128]{2,1,0:T(8,128)(2,1)S(1)}, bf16[9,256,128]{2,1,0:T(8,128)(2,1)}, u32[]{:S(2)}, u32[]{:S(2)}) collective-permute-start(bf16[9,256,128]{2,1,0:T(8,128)(2,1)S(1)} %line_add.14.refs_4_.x), channel_id=1, source_target_pairs={{8,0},{12,4},{16,24},{20,28},{9,1},{13,5},{17,25},{21,29},{10,2},{... | collective-permute-start | bytes 1769480 | tf_op jit(solution)/shard_map/ppermute | solution.py:516
  89.4 17.9 %collective-permute-start.26 = (bf16[1168,256]{1,0:T(8,128)(2,1)S(1)}, bf16[1168,256]{1,0:T(8,128)(2,1)S(1)}, u32[]{:S(2)}, u32[]{:S(2)}) collective-permute-start(bf16[1168,256]{1,0:T(8,128)(2,1)S(1)} %get-tuple-element.66.refs_0_.x), channel_id=1, source_target_pairs={{0,8},{4,12},{24,16},{28,20},{1,9},{5,13},{25,17},{29,21},{2,10},{... | collective-permute-start | bytes 1794056 | tf_op jit(solution)/shard_map/ppermute | solution.py:516
  95.8 12.3 %collective-permute-start.25 = (bf16[9,256,128]{2,1,0:T(8,128)(2,1)S(1)}, bf16[9,256,128]{2,1,0:T(8,128)(2,1)S(1)}, u32[]{:S(2)}, u32[]{:S(2)}) collective-permute-start(bf16[9,256,128]{2,1,0:T(8,128)(2,1)S(1)} %line_add.15.refs_0_.x), channel_id=1, source_target_pairs={{8,16},{12,20},{16,8},{20,12},{9,17},{13,21},{17,9},{21,13},{10,18... | collective-permute-start | bytes 1769480 | tf_op jit(solution)/shard_map/ppermute | solution.py:516
  97.8 17.6 %collective-permute-start.24 = (bf16[9,256,128]{2,1,0:T(8,128)(2,1)S(1)}, bf16[9,256,128]{2,1,0:T(8,128)(2,1)S(1)}, u32[]{:S(2)}, u32[]{:S(2)}) collective-permute-start(bf16[9,256,128]{2,1,0:T(8,128)(2,1)S(1)} %line_add.16.refs_0_.x), channel_id=1, source_target_pairs={{8,0},{12,4},{16,24},{20,28},{9,1},{13,5},{17,25},{21,29},{10,2},{... | collective-permute-start | bytes 1769480 | tf_op jit(solution)/shard_map/ppermute | solution.py:516
  102.0 15.5 %collective-permute-start.23 = (bf16[9,256,128]{2,1,0:T(8,128)(2,1)S(1)}, bf16[9,256,128]{2,1,0:T(8,128)(2,1)S(1)}, u32[]{:S(2)}, u32[]{:S(2)}) collective-permute-start(bf16[9,256,128]{2,1,0:T(8,128)(2,1)S(1)} %line_pick.6.refs_0_.own), channel_id=1, source_target_pairs={{0,4},{4,0},{8,12},{12,8},{16,20},{20,16},{24,28},{28,24},{1,5},{5... | collective-permute-start | bytes 1769480 | tf_op jit(solution)/shard_map/ppermute | solution.py:545
  102.9 18.5 %collective-permute-start.19 = (bf16[1168,256]{1,0:T(8,128)(2,1)S(1)}, bf16[1168,256]{1,0:T(8,128)(2,1)S(1)}, u32[]{:S(2)}, u32[]{:S(2)}) collective-permute-start(bf16[1168,256]{1,0:T(8,128)(2,1)S(1)} %get-tuple-element.65.x), channel_id=1, source_target_pairs={{0,8},{4,12},{24,16},{28,20},{1,9},{5,13},{25,17},{29,21},{2,10},{... | collective-permute-start | bytes 1794056 | tf_op jit(solution)/shard_map/ppermute | solution.py:516
  107.5 14.8 %collective-permute-start.31 = (bf16[1168,256]{1,0:T(8,128)(2,1)S(1)}, bf16[1168,256]{1,0:T(8,128)(2,1)S(1)}, u32[]{:S(2)}, u32[]{:S(2)}) collective-permute-start(bf16[1168,256]{1,0:T(8,128)(2,1)S(1)} %line_add.17.refs_0_.x), channel_id=1, source_target_pairs={{8,16},{12,20},{16,8},{20,12},{9,17},{13,21},{17,9},{21,13},{10,18... | collective-permute-start | bytes 1794056 | tf_op jit(solution)/shard_map/ppermute | solution.py:516
  108.2 25.0 %collective-permute-start.28 = (bf16[1168,256]{1,0:T(8,128)(2,1)S(1)}, bf16[1168,256]{1,0:T(8,128)(2,1)S(1)}, u32[]{:S(2)}, u32[]{:S(2)}) collective-permute-start(bf16[1168,256]{1,0:T(8,128)(2,1)S(1)} %get-tuple-element.68.x), channel_id=1, source_target_pairs={{0,8},{4,12},{24,16},{28,20},{1,9},{5,13},{25,17},{29,21},{2,10},{... | collective-permute-start | bytes 1794056 | tf_op jit(solution)/shard_map/ppermute | solution.py:516
  115.4 14.9 %collective-permute-start.30 = (bf16[9,256,128]{2,1,0:T(8,128)(2,1)S(1)}, bf16[9,256,128]{2,1,0:T(8,128)(2,1)S(1)}, u32[]{:S(2)}, u32[]{:S(2)}) collective-permute-start(bf16[9,256,128]{2,1,0:T(8,128)(2,1)S(1)} %line_add.18.refs_0_.x), channel_id=1, source_target_pairs={{8,0},{12,4},{16,24},{20,28},{9,1},{13,5},{17,25},{21,29},{10,2},{... | collective-permute-start | bytes 1769480 | tf_op jit(solution)/shard_map/ppermute | solution.py:516
  117.6 13.4 %collective-permute-start.29 = (bf16[9,256,128]{2,1,0:T(8,128)(2,1)S(1)}, bf16[9,256,128]{2,1,0:T(8,128)(2,1)S(1)}, u32[]{:S(2)}, u32[]{:S(2)}) collective-permute-start(bf16[9,256,128]{2,1,0:T(8,128)(2,1)S(1)} %line_pick.7.refs_0_.own), channel_id=1, source_target_pairs={{0,4},{4,0},{8,12},{12,8},{16,20},{20,16},{24,28},{28,24},{1,5},{5... | collective-permute-start | bytes 1769480 | tf_op jit(solution)/shard_map/ppermute | solution.py:545
  121.6 17.3 %collective-permute-start.27 = (bf16[1168,256]{1,0:T(8,128)(2,1)S(1)}, bf16[1168,256]{1,0:T(8,128)(2,1)S(1)}, u32[]{:S(2)}, u32[]{:S(2)}) collective-permute-start(bf16[1168,256]{1,0:T(8,128)(2,1)S(1)} %line_add.19.refs_0_.x), channel_id=1, source_target_pairs={{8,16},{12,20},{16,8},{20,12},{9,17},{13,21},{17,9},{21,13},{10,18... | collective-permute-start | bytes 1794056 | tf_op jit(solution)/shard_map/ppermute | solution.py:516
  122.5 20.7 %collective-permute-start.35 = (bf16[1168,256]{1,0:T(8,128)(2,1)S(1)}, bf16[1168,256]{1,0:T(8,128)(2,1)S(1)}, u32[]{:S(2)}, u32[]{:S(2)}) collective-permute-start(bf16[1168,256]{1,0:T(8,128)(2,1)S(1)} %line_add.20.refs_0_.x), channel_id=1, source_target_pairs={{8,0},{12,4},{16,24},{20,28},{9,1},{13,5},{17,25},{21,29},{10,2},{... | collective-permute-start | bytes 1794056 | tf_op jit(solution)/shard_map/ppermute | solution.py:516
  133.4 16.9 %collective-permute-start.33 = (bf16[1168,256]{1,0:T(8,128)(2,1)S(1)}, bf16[1168,256]{1,0:T(8,128)(2,1)S(1)}, u32[]{:S(2)}, u32[]{:S(2)}) collective-permute-start(bf16[1168,256]{1,0:T(8,128)(2,1)S(1)} %line_add.21.refs_0_.x), channel_id=1, source_target_pairs={{8,16},{12,20},{16,8},{20,12},{9,17},{13,21},{17,9},{21,13},{10,18... | collective-permute-start | bytes 1794056 | tf_op jit(solution)/shard_map/ppermute | solution.py:516
  134.1 14.2 %collective-permute-start.34 = (bf16[9,256,128]{2,1,0:T(8,128)(2,1)S(1)}, bf16[9,256,128]{2,1,0:T(8,128)(2,1)S(1)}, u32[]{:S(2)}, u32[]{:S(2)}) collective-permute-start(bf16[9,256,128]{2,1,0:T(8,128)(2,1)S(1)} %line_pick.8.refs_1_.own), channel_id=1, source_target_pairs={{0,4},{4,0},{8,12},{12,8},{16,20},{20,16},{24,28},{28,24},{1,5},{5... | collective-permute-start | bytes 1769480 | tf_op jit(solution)/shard_map/ppermute | solution.py:545
  139.1 17.5 %collective-permute-start.32 = (bf16[1168,256]{1,0:T(8,128)(2,1)S(1)}, bf16[1168,256]{1,0:T(8,128)(2,1)S(1)}, u32[]{:S(2)}, u32[]{:S(2)}) collective-permute-start(bf16[1168,256]{1,0:T(8,128)(2,1)S(1)} %line_add.22.refs_0_.x), channel_id=1, source_target_pairs={{8,0},{12,4},{16,24},{20,28},{9,1},{13,5},{17,25},{21,29},{10,2},{... | collective-permute-start | bytes 1794056 | tf_op jit(solution)/shard_map/ppermute | solution.py:516
  143.8 24.5 %collective-permute-start.37 = (bf16[1168,256]{1,0:T(8,128)(2,1)S(1)}, bf16[1168,256]{1,0:T(8,128)(2,1)S(1)}, u32[]{:S(2)}, u32[]{:S(2)}) collective-permute-start(bf16[1168,256]{1,0:T(8,128)(2,1)S(1)} %line_pick.9.refs_1_.own), channel_id=1, source_target_pairs={{0,4},{4,0},{8,12},{12,8},{16,20},{20,16},{24,28},{28,24},{1,5},{5... | collective-permute-start | bytes 1794056 | tf_op jit(solution)/shard_map/ppermute | solution.py:545
  150.5 19.8 %collective-permute-start.36 = (bf16[1168,256]{1,0:T(8,128)(2,1)S(1)}, bf16[1168,256]{1,0:T(8,128)(2,1)S(1)}, u32[]{:S(2)}, u32[]{:S(2)}) collective-permute-start(bf16[1168,256]{1,0:T(8,128)(2,1)S(1)} %line_add.23.refs_0_.x), channel_id=1, source_target_pairs={{8,0},{12,4},{16,24},{20,28},{9,1},{13,5},{17,25},{21,29},{10,2},{... | collective-permute-start | bytes 1794056 | tf_op jit(solution)/shard_map/ppermute | solution.py:516
  157.2 15.6 %collective-permute-start.39 = (bf16[1168,256]{1,0:T(8,128)(2,1)S(1)}, bf16[1168,256]{1,0:T(8,128)(2,1)S(1)}, u32[]{:S(2)}, u32[]{:S(2)}) collective-permute-start(bf16[1168,256]{1,0:T(8,128)(2,1)S(1)} %line_pick.10.refs_4_.own), channel_id=1, source_target_pairs={{0,4},{4,0},{8,12},{12,8},{16,20},{20,16},{24,28},{28,24},{1,5},{5... | collective-permute-start | bytes 1794056 | tf_op jit(solution)/shard_map/ppermute | solution.py:545
  (21 other events, 211.8 us)

commit v13 on v11

--- a/solution.py
+++ b/solution.py
@@ -21,7 +21,7 @@
 NT = (((1,), (1,)), ((), ()))
 UNREAD = pl.BlockSpec(memory_space=pl.ANY)
 IN_HBM = pl.BlockSpec(memory_space=pltpu.HBM)
-PLANE_ORDER = (0, -1, 1)
+PLANE_ORDER = (0, 1, -1)
 LIGHT = pl.CostEstimate(flops=1024, bytes_accessed=1024, transcendentals=0)
 
 
@@ -109,29 +109,46 @@
     rows = field.shape[0]
     copies = start_parts(w, buffer, sems)
     fill_padded(padded, field[...], sign)
-    for a in PLANE_ORDER:
-        begin, planes = span_of(a, sign)
-        pieces = []
-        for b in (-1, 0, 1):
-            for c in (-1, 0, 1):
-                low, first = 1 + sign * b, 1 + begin + sign * a
-                piece = padded[1 + c, first : first + planes, low : low + HEIGHT]
-                pieces.append(piece.reshape(planes * PLANE, rows))
-        lhs = jnp.concatenate(pieces, axis=1)
-        copies[a].wait()
-        if sign == 1:
-            rhs = buffer[(a + 1) * 9 * rows : (a + 2) * 9 * rows]
-            part = jnp.dot(lhs, rhs, preferred_element_type=F32)
-        else:
+    if sign == 1:
+        for plane in range(DEPTH):
+            near = [a for a in (-1, 0, 1) if 0 <= plane + a < DEPTH]
+            if plane == 0:
+                copies[0].wait()
+                copies[1].wait()
+            if plane == 1:
+                copies[-1].wait()
+            pieces = []
+            for a in near:
+                for b in (-1, 0, 1):
+                    for c in (-1, 0, 1):
+                        piece = padded[1 + c, 1 + plane + a, 1 + b : 1 + b + HEIGHT]
+                        pieces.append(piece.reshape(PLANE, rows))
+            lhs = jnp.concatenate(pieces, axis=1)
+            rhs = buffer[(near[0] + 1) * 9 * rows : (near[-1] + 2) * 9 * rows]
+            part = jnp.dot(lhs, rhs, preferred_element_type=F32).astype(BF16)
+            for j in range(n):
+                span = slice(plane * PLANE, (plane + 1) * PLANE)
+                shares[j, span] = part[:, j * rows : (j + 1) * rows]
+    else:
+        for a in PLANE_ORDER:
+            begin, planes = span_of(a, sign)
+            pieces = []
+            for b in (-1, 0, 1):
+                for c in (-1, 0, 1):
+                    low, first = 1 + sign * b, 1 + begin + sign * a
+                    piece = padded[1 + c, first : first + planes, low : low + HEIGHT]
+                    pieces.append(piece.reshape(planes * PLANE, rows))
+            lhs = jnp.concatenate(pieces, axis=1)
+            copies[a].wait()
             rhs = jnp.concatenate([buffer[(a + 1) * 9 + k] for k in range(9)], axis=1)
             part = lax.dot_general(lhs, rhs, NT, preferred_element_type=F32)
-        span = slice(begin * PLANE, (begin + planes) * PLANE)
-        if a == 0:
-            sums[...] = part
-        else:
-            sums[span] += part
-    for j in range(n):
-        shares[j] = sums[:, j * rows : (j + 1) * rows].astype(BF16)
+            span = slice(begin * PLANE, (begin + planes) * PLANE)
+            if a == 0:
+                sums[...] = part
+            else:
+                sums[span] += part
+        for j in range(n):
+            shares[j] = sums[:, j * rows : (j + 1) * rows].astype(BF16)
     for m in range(n):
         outs[m][...] = shares[idx[0] ^ m]
 

time: 177 us -> 176 us (level)
  no operation moved by 1% of the time
where the time goes in v13:
time: 176 us
  starting transfers between devices  71 us (40%)
  Pallas kernels  60.4 us (34%)
  waiting for transfers between devices  36.8 us (21%)
  local copies, waits for them, and re-layouts  4.71 us (3%)
    ppermute x18, starting transfers between devices, line_send(): return lax.ppermute(x, 'dp', pairs)  38.8 us
    ppermute x18, waiting for transfers between devices, line_send(): return lax.ppermute(x, 'dp', pairs)  22.2 us
    ppermute x10, starting transfers between devices, to_core(): lax.ppermute(x, 'dp', [(i, i ^ 1) for i in range(lax.axis_size('dp'))])  20.7 us
    pallas_call x2, Pallas kernels, conv_full(): pl.pallas_call(functools.partial(conv_kernel, n, sign, transposed), in_sp...  14.1 us
    ppermute x12, waiting for transfers between devices, to_partner(): return lax.ppermute(x, 'chan', [(i, i ^ m) for i in range(n)])  13 us
    pallas_call x2, Pallas kernels, spread_shares(): pl.pallas_call(functools.partial(share_kernel, n, sign), in_specs=[smem()...  12.8 us
    pallas_call x6, Pallas kernels, finish(): pl.pallas_call(functools.partial(finish_kernel, n, axis, factor, chunk),...  12.7 us
    ppermute x12, starting transfers between devices, to_partner(): return lax.ppermute(x, 'chan', [(i, i ^ m) for i in range(n)])  11.5 us
  transfers between devices with their start and end apart: 40, of which 11 were waited for; matrix products, arithmetic and copies ran while one was open for 0% of the time, Pallas kernels for 28%

profile of v13, /device:TPU:1, one launch (start us, length us, event | category | flops | bytes accessed | tf_op | source)
XLA Modules:
  0.0 175.7 jit_solution(13733182817054199979)
XLA Ops:
  1.3 7.0 %pre.1 = (bf16[1024,128]{1,0:T(8,128)(2,1)}, bf16[1024,128]{1,0:T(8,128)(2,1)}, bf16[1024,128]{1,0:T(8,128)(2,1)}, bf16[1024,128]{1,0:T(8,128)(2,1)}) custom-call(s32[2]{0:T(128)} %pad_add_fusion.idx, bf16[128,1024]{1,0:T(8,128)(2,1)} %bitcast.15, bf16[3456,512]{1,0:T(8,128)(2,1)} %bitcast.10), custom_call_target="tpu_custom_call" | custom-call | flops 1024 | bytes 1024 | tf_op jit(solution)/shard_map/pre/pallas_call | solution.py:158
  8.4 2.1 %collective-permute-start = (bf16[1024,128]{1,0:T(8,128)(2,1)}, bf16[1024,128]{1,0:T(8,128)(2,1)S(1)}, u32[]{:S(2)}, u32[]{:S(2)}) collective-permute-start(bf16[1024,128]{1,0:T(8,128)(2,1)} %get-tuple-element.44), channel_id=1, source_target_pairs={{0,1},{1,0},{2,3},{3,2},{4,5},{5,4},{6,7},{7,6},{8,9},{9,8},{10,11... | collective-permute-start | bytes 786440 | tf_op jit(solution)/shard_map/ppermute | solution.py:559
  13.0 2.0 %copy-done.1 = bf16[27,512,128]{2,1,0:T(8,128)(2,1)S(1)} copy-done((bf16[27,512,128]{2,1,0:T(8,128)(2,1)S(1)}, bf16[27,512,128]{2,1,0:T(8,128)(2,1)}, u32[]{:S(2)}) %copy-start.1) | copy-done | bytes 3538968
  16.6 5.8 %dact.1 = (bf16[1024,128]{1,0:T(8,128)(2,1)S(1)}, bf16[1024,128]{1,0:T(8,128)(2,1)S(1)}, bf16[1024,128]{1,0:T(8,128)(2,1)S(1)}, bf16[1024,128]{1,0:T(8,128)(2,1)S(1)}) custom-call(s32[2]{0:T(128)S(1)} %copy-done.12, bf16[128,1024]{1,0:T(8,128)(2,1)S(1)} %bitcast.13, bf16[27,512,128]{2,1,0:T(8,128)(2,1)S(1)} %copy-done.1), custom_call_target="tpu_custom_call" | custom-call | flops 1024 | bytes 1024 | tf_op jit(solution)/shard_map/dact/pallas_call | solution.py:158
  24.8 2.0 %collective-permute-start.5 = (bf16[1024,128]{1,0:T(8,128)(2,1)S(1)}, bf16[1024,128]{1,0:T(8,128)(2,1)S(1)}, u32[]{:S(2)}, u32[]{:S(2)}) collective-permute-start(bf16[1024,128]{1,0:T(8,128)(2,1)S(1)} %get-tuple-element.50._.refs_0_), channel_id=1, source_target_pairs={{0,3},{1,2},{2,1},{3,0},{4,7},{5,6},{6,5},{7,4},{8,11},{9,10},{10,... | collective-permute-start | bytes 786440 | tf_op jit(solution)/shard_map/ppermute | solution.py:559
  28.2 3.7 %collective-permute-done.5.refs_3_ = bf16[1024,128]{1,0:T(8,128)(2,1)S(1)} collective-permute-done((bf16[1024,128]{1,0:T(8,128)(2,1)S(1)}, bf16[1024,128]{1,0:T(8,128)(2,1)S(1)}, u32[]{:S(2)}, u32[]{:S(2)}) %collective-permute-start.5) | collective-permute-done | bytes 262176 | tf_op jit(solution)/shard_map/ppermute | solution.py:559
  31.8 7.8 %collective-permute-done.4.refs_2_ = bf16[1024,128]{1,0:T(8,128)(2,1)S(1)} collective-permute-done((bf16[1024,128]{1,0:T(8,128)(2,1)S(1)}, bf16[1024,128]{1,0:T(8,128)(2,1)S(1)}, u32[]{:S(2)}, u32[]{:S(2)}) %collective-permute-start.4) | collective-permute-done | bytes 262176 | tf_op jit(solution)/shard_map/ppermute | solution.py:559
  41.0 1.5 collective-permute-done.8.other
  43.8 3.2 %collective-permute-start.15 = (bf16[9,256,128]{2,1,0:T(8,128)(2,1)S(1)}, bf16[9,256,128]{2,1,0:T(8,128)(2,1)S(1)}, u32[]{:S(2)}, u32[]{:S(2)}) collective-permute-start(bf16[9,256,128]{2,1,0:T(8,128)(2,1)S(1)} %grad_second.3.refs_0_.x), channel_id=1, source_target_pairs={{0,8},{4,12},{24,16},{28,20},{1,9},{5,13},{25,17},{29,21},{2,10},{... | collective-permute-start | bytes 1769480 | tf_op jit(solution)/shard_map/ppermute | solution.py:533
  49.7 1.5 grad_second.4.refs_4_.x
  52.8 7.0 %output.1 = (bf16[128,1024]{1,0:T(8,128)(2,1)}, f32[8,128]{1,0:T(8,128)S(1)}) custom-call(s32[2]{0:T(128)S(1)} %copy-done.13, bf16[27,512,128]{2,1,0:T(8,128)(2,1)S(1)} %copy-done.2, bf16[1024,128]{1,0:T(8,128)(2,1)S(1)} %get-tuple-element.50._.refs_0_, bf16[1024,128]{1,0:T(8,128)(2,1)S(1)} %collective-permute-done.3.refs_1_, ...), custom_call_target="tpu_custom_call" | custom-call | flops 1024 | bytes 1024 | tf_op jit(solution)/shard_map/output/pallas_call | solution.py:261
  66.0 5.9 %collective-permute-done.17.y = bf16[9,256,128]{2,1,0:T(8,128)(2,1)S(1)} collective-permute-done((bf16[9,256,128]{2,1,0:T(8,128)(2,1)S(1)}, bf16[9,256,128]{2,1,0:T(8,128)(2,1)S(1)}, u32[]{:S(2)}, u32[]{:S(2)}) %collective-permute-start.17) | collective-permute-done | bytes 589856 | tf_op jit(solution)/shard_map/ppermute | solution.py:533
  71.9 4.9 %collective-permute-start.22 = (bf16[9,256,128]{2,1,0:T(8,128)(2,1)S(1)}, bf16[9,256,128]{2,1,0:T(8,128)(2,1)}, u32[]{:S(2)}, u32[]{:S(2)}) collective-permute-start(bf16[9,256,128]{2,1,0:T(8,128)(2,1)S(1)} %grad_second.5.refs_0_.x), channel_id=1, source_target_pairs={{0,8},{4,12},{24,16},{28,20},{1,9},{5,13},{25,17},{29,21},{2,10},{... | collective-permute-start | bytes 1769480 | tf_op jit(solution)/shard_map/ppermute | solution.py:533
  82.9 4.4 %grad_first.1 = (bf16[1168,256]{1,0:T(8,128)(2,1)S(1)}, bf16[1168,256]{1,0:T(8,128)(2,1)S(1)}, bf16[1168,256]{1,0:T(8,128)(2,1)S(1)}) custom-call(bf16[128,1024]{1,0:T(8,128)(2,1)S(1)} %bitcast.17, bf16[128,1024]{1,0:T(8,128)(2,1)S(1)} %collective-permute-done.7.refs_5_.vol_other, bf16[2,1024,128]{2,1,0:T(8,128)(2,1)S(1)} %get-tuple-element.62.own.refs_0_, ...), custom_call_target="tpu_custom_call" | custom-call | flops 1024 | bytes 1024 | tf_op jit(solution)/shard_map/grad_first/pallas_call | solution.py:394
  87.4 5.2 %collective-permute-start.26 = (bf16[1168,256]{1,0:T(8,128)(2,1)S(1)}, bf16[1168,256]{1,0:T(8,128)(2,1)S(1)}, u32[]{:S(2)}, u32[]{:S(2)}) collective-permute-start(bf16[1168,256]{1,0:T(8,128)(2,1)S(1)} %get-tuple-element.66.refs_0_.x), channel_id=1, source_target_pairs={{0,8},{4,12},{24,16},{28,20},{1,9},{5,13},{25,17},{29,21},{2,10},{... | collective-permute-start | bytes 1794056 | tf_op jit(solution)/shard_map/ppermute | solution.py:533
  97.3 1.7 collective-permute-done.20.y
  101.0 4.5 %collective-permute-start.19 = (bf16[1168,256]{1,0:T(8,128)(2,1)S(1)}, bf16[1168,256]{1,0:T(8,128)(2,1)S(1)}, u32[]{:S(2)}, u32[]{:S(2)}) collective-permute-start(bf16[1168,256]{1,0:T(8,128)(2,1)S(1)} %get-tuple-element.65.x), channel_id=1, source_target_pairs={{0,8},{4,12},{24,16},{28,20},{1,9},{5,13},{25,17},{29,21},{2,10},{... | collective-permute-start | bytes 1794056 | tf_op jit(solution)/shard_map/ppermute | solution.py:533
  106.3 6.7 %collective-permute-start.28 = (bf16[1168,256]{1,0:T(8,128)(2,1)S(1)}, bf16[1168,256]{1,0:T(8,128)(2,1)S(1)}, u32[]{:S(2)}, u32[]{:S(2)}) collective-permute-start(bf16[1168,256]{1,0:T(8,128)(2,1)S(1)} %get-tuple-element.68.x), channel_id=1, source_target_pairs={{0,8},{4,12},{24,16},{28,20},{1,9},{5,13},{25,17},{29,21},{2,10},{... | collective-permute-start | bytes 1794056 | tf_op jit(solution)/shard_map/ppermute | solution.py:533
  115.7 1.9 %collective-permute-start.29 = (bf16[9,256,128]{2,1,0:T(8,128)(2,1)S(1)}, bf16[9,256,128]{2,1,0:T(8,128)(2,1)S(1)}, u32[]{:S(2)}, u32[]{:S(2)}) collective-permute-start(bf16[9,256,128]{2,1,0:T(8,128)(2,1)S(1)} %line_pick.7.refs_0_.own), channel_id=1, source_target_pairs={{0,4},{4,0},{8,12},{12,8},{16,20},{20,16},{24,28},{28,24},{1,5},{5... | collective-permute-start | bytes 1769480 | tf_op jit(solution)/shard_map/ppermute | solution.py:562
  117.5 2.0 %finish_second.3 = (f32[27,512,128]{2,1,0:T(8,128)}, f32[8,128]{1,0:T(8,128)S(1)}) custom-call(s32[2]{0:T(128)S(1)} %copy-done.13, bf16[9,256,128]{2,1,0:T(8,128)(2,1)S(1)} %line_pick.6.refs_0_.own, bf16[9,256,128]{2,1,0:T(8,128)(2,1)S(1)} %collective-permute-done.23.other, bf16[9,256,128]{2,1,0:T(8,128)(2,1)S(1)} %line_pick.7.refs_0_.own), custom_call_target="tpu_custom_call" | custom-call | flops 1024 | bytes 1024 | tf_op jit(solution)/shard_map/finish_second/pallas_call | solution.py:472
  121.9 6.6 %collective-permute-done.30.y = bf16[9,256,128]{2,1,0:T(8,128)(2,1)S(1)} collective-permute-done((bf16[9,256,128]{2,1,0:T(8,128)(2,1)S(1)}, bf16[9,256,128]{2,1,0:T(8,128)(2,1)S(1)}, u32[]{:S(2)}, u32[]{:S(2)}) %collective-permute-start.30) | collective-permute-done | bytes 589856 | tf_op jit(solution)/shard_map/ppermute | solution.py:533
  129.1 2.0 %finish_second.4 = (f32[27,512,128]{2,1,0:T(8,128)}, f32[8,128]{1,0:T(8,128)S(1)}) custom-call(s32[2]{0:T(128)S(1)} %copy-done.13, bf16[9,256,128]{2,1,0:T(8,128)(2,1)S(1)} %line_pick.7.refs_0_.own, bf16[9,256,128]{2,1,0:T(8,128)(2,1)S(1)} %collective-permute-done.29.other, ...), custom_call_target="tpu_custom_call", output_to_operand_aliasing={{0}: (3, {})} | custom-call | flops 1024 | bytes 1024 | tf_op jit(solution)/shard_map/finish_second/pallas_call | solution.py:472
  132.0 5.1 %collective-permute-start.34 = (bf16[9,256,128]{2,1,0:T(8,128)(2,1)S(1)}, bf16[9,256,128]{2,1,0:T(8,128)(2,1)S(1)}, u32[]{:S(2)}, u32[]{:S(2)}) collective-permute-start(bf16[9,256,128]{2,1,0:T(8,128)(2,1)S(1)} %line_pick.8.refs_1_.own), channel_id=1, source_target_pairs={{0,4},{4,0},{8,12},{12,8},{16,20},{20,16},{24,28},{28,24},{1,5},{5... | collective-permute-start | bytes 1769480 | tf_op jit(solution)/shard_map/ppermute | solution.py:562
  138.5 2.8 %collective-permute-done.35.y = bf16[1168,256]{1,0:T(8,128)(2,1)S(1)} collective-permute-done((bf16[1168,256]{1,0:T(8,128)(2,1)S(1)}, bf16[1168,256]{1,0:T(8,128)(2,1)S(1)}, u32[]{:S(2)}, u32[]{:S(2)}) %collective-permute-start.35) | collective-permute-done | bytes 598048 | tf_op jit(solution)/shard_map/ppermute | solution.py:533
  141.9 4.5 %collective-permute-start.37 = (bf16[1168,256]{1,0:T(8,128)(2,1)S(1)}, bf16[1168,256]{1,0:T(8,128)(2,1)S(1)}, u32[]{:S(2)}, u32[]{:S(2)}) collective-permute-start(bf16[1168,256]{1,0:T(8,128)(2,1)S(1)} %line_pick.9.refs_1_.own), channel_id=1, source_target_pairs={{0,4},{4,0},{8,12},{12,8},{16,20},{20,16},{24,28},{28,24},{1,5},{5... | collective-permute-start | bytes 1794056 | tf_op jit(solution)/shard_map/ppermute | solution.py:562
  146.4 2.0 %finish_second.5 = (f32[27,512,128]{2,1,0:T(8,128)}, f32[8,128]{1,0:T(8,128)S(1)}) custom-call(s32[2]{0:T(128)S(1)} %copy-done.13, bf16[9,256,128]{2,1,0:T(8,128)(2,1)S(1)} %line_pick.8.refs_1_.own, bf16[9,256,128]{2,1,0:T(8,128)(2,1)S(1)} %collective-permute-done.34.other, ...), custom_call_target="tpu_custom_call", output_to_operand_aliasing={{0}: (3, {})} | custom-call | flops 1024 | bytes 1024 | tf_op jit(solution)/shard_map/finish_second/pallas_call | solution.py:472
  149.9 4.8 %collective-permute-done.32.y = bf16[1168,256]{1,0:T(8,128)(2,1)S(1)} collective-permute-done((bf16[1168,256]{1,0:T(8,128)(2,1)S(1)}, bf16[1168,256]{1,0:T(8,128)(2,1)S(1)}, u32[]{:S(2)}, u32[]{:S(2)}) %collective-permute-start.32) | collective-permute-done | bytes 598048 | tf_op jit(solution)/shard_map/ppermute | solution.py:533
  155.3 3.9 %collective-permute-start.39 = (bf16[1168,256]{1,0:T(8,128)(2,1)S(1)}, bf16[1168,256]{1,0:T(8,128)(2,1)S(1)}, u32[]{:S(2)}, u32[]{:S(2)}) collective-permute-start(bf16[1168,256]{1,0:T(8,128)(2,1)S(1)} %line_pick.10.refs_4_.own), channel_id=1, source_target_pairs={{0,4},{4,0},{8,12},{12,8},{16,20},{20,16},{24,28},{28,24},{1,5},{5... | collective-permute-start | bytes 1794056 | tf_op jit(solution)/shard_map/ppermute | solution.py:562
  159.2 7.2 %grad_volume.1 = (bf16[128,1024]{1,0:T(8,128)(2,1)}, f32[8,128]{1,0:T(8,128)S(1)}) custom-call(s32[2]{0:T(128)S(1)} %copy-done.13, bf16[3456,512]{1,0:T(8,128)(2,1)S(1)} %bitcast.11, bf16[1024,128]{1,0:T(8,128)(2,1)S(1)} %get-tuple-element.61.refs_0_, bf16[1024,128]{1,0:T(8,128)(2,1)S(1)} %copy-done.10, bf16[1024,128]{1,0:T(8,128)(2,1)S(1)} %copy-done.8, ...), custom_call_target="tpu_custom_call" | custom-call | flops 1024 | bytes 1024 | tf_op jit(solution)/shard_map/grad_volume/pallas_call | solution.py:261
  166.4 2.0 %finish_first.3 = (f32[27,128,512]{2,1,0:T(8,128)}, f32[8,128]{1,0:T(8,128)S(1)}) custom-call(s32[2]{0:T(128)S(1)} %copy-done.13, bf16[1168,256]{1,0:T(8,128)(2,1)S(1)} %line_pick.9.refs_1_.own, bf16[1168,256]{1,0:T(8,128)(2,1)S(1)} %collective-permute-done.37.other, f32[8,128]{1,0:T(8,128)S(1)} %get-tuple-element.74.refs_0_), custom_call_target="tpu_custom_call" | custom-call | flops 1024 | bytes 1024 | tf_op jit(solution)/shard_map/finish_first/pallas_call | solution.py:472
  170.9 2.0 %finish_first.4 = (f32[27,128,512]{2,1,0:T(8,128)}, f32[8,128]{1,0:T(8,128)S(1)}) custom-call(s32[2]{0:T(128)S(1)} %copy-done.13, bf16[1168,256]{1,0:T(8,128)(2,1)S(1)} %line_pick.10.refs_4_.own, bf16[1168,256]{1,0:T(8,128)(2,1)S(1)} %collective-permute-done.39.other, f32[27,128,512]{2,1,0:T(8,128)} %get-tuple-element.76.refs_0_, ...), custom_call_target="tpu_custom_call", output_to_operand_aliasing={{0}: (3, {})} | custom-call | flops 1024 | bytes 1024 | tf_op jit(solution)/shard_map/finish_first/pallas_call | solution.py:472
  172.9 2.6 %finish_first.5 = (f32[27,128,512]{2,1,0:T(8,128)}, f32[8,128]{1,0:T(8,128)}) custom-call(s32[2]{0:T(128)S(1)} %copy-done.13, bf16[1168,256]{1,0:T(8,128)(2,1)S(1)} %line_pick.11.refs_1_.own, bf16[1168,256]{1,0:T(8,128)(2,1)S(1)} %collective-permute-done.38.other, f32[27,128,512]{2,1,0:T(8,128)} %get-tuple-element.77.refs_0_, ...), custom_call_target="tpu_custom_call", output_to_operand_aliasing={{0}: (3, {})} | custom-call | flops 1024 | bytes 1024 | tf_op jit(solution)/shard_map/finish_first/pallas_call | solution.py:472
  (119 shorter events, 47.9 us)
Async XLA Ops:
  8.4 14.1 %collective-permute-start = (bf16[1024,128]{1,0:T(8,128)(2,1)}, bf16[1024,128]{1,0:T(8,128)(2,1)S(1)}, u32[]{:S(2)}, u32[]{:S(2)}) collective-permute-start(bf16[1024,128]{1,0:T(8,128)(2,1)} %get-tuple-element.44), channel_id=1, source_target_pairs={{0,1},{1,0},{2,3},{3,2},{4,5},{5,4},{6,7},{7,6},{8,9},{9,8},{10,11... | collective-permute-start | bytes 786440 | tf_op jit(solution)/shard_map/ppermute | solution.py:559
  11.7 16.4 %collective-permute-start.7 = (bf16[128,1024]{1,0:T(8,128)(2,1)}, bf16[128,1024]{1,0:T(8,128)(2,1)S(1)}, u32[]{:S(2)}, u32[]{:S(2)}) collective-permute-start(bf16[128,1024]{1,0:T(8,128)(2,1)} %bitcast.16), channel_id=1, source_target_pairs={{0,4},{4,0},{8,12},{12,8},{16,20},{20,16},{24,28},{28,24},{1,5},{5... | collective-permute-start | bytes 786440 | tf_op jit(solution)/shard_map/ppermute | solution.py:562
  13.0 14.5 %collective-permute-start.6 = (bf16[128,1024]{1,0:T(8,128)(2,1)}, bf16[128,1024]{1,0:T(8,128)(2,1)S(1)}, u32[]{:S(2)}, u32[]{:S(2)}) collective-permute-start(bf16[128,1024]{1,0:T(8,128)(2,1)} %bitcast.12), channel_id=1, source_target_pairs={{0,4},{4,0},{8,12},{12,8},{16,20},{20,16},{24,28},{28,24},{1,5},{5... | collective-permute-start | bytes 786440 | tf_op jit(solution)/shard_map/ppermute | solution.py:562
  26.7 12.9 %collective-permute-start.4 = (bf16[1024,128]{1,0:T(8,128)(2,1)S(1)}, bf16[1024,128]{1,0:T(8,128)(2,1)S(1)}, u32[]{:S(2)}, u32[]{:S(2)}) collective-permute-start(bf16[1024,128]{1,0:T(8,128)(2,1)S(1)} %get-tuple-element.50._.refs_0_), channel_id=1, source_target_pairs={{0,2},{1,3},{2,0},{3,1},{4,6},{5,7},{6,4},{7,5},{8,10},{9,11},{10,... | collective-permute-start | bytes 786440 | tf_op jit(solution)/shard_map/ppermute | solution.py:559
  27.2 12.4 %collective-permute-start.3 = (bf16[1024,128]{1,0:T(8,128)(2,1)S(1)}, bf16[1024,128]{1,0:T(8,128)(2,1)S(1)}, u32[]{:S(2)}, u32[]{:S(2)}) collective-permute-start(bf16[1024,128]{1,0:T(8,128)(2,1)S(1)} %get-tuple-element.50._.refs_0_), channel_id=1, source_target_pairs={{0,1},{1,0},{2,3},{3,2},{4,5},{5,4},{6,7},{7,6},{8,9},{9,8},{10,11... | collective-permute-start | bytes 786440 | tf_op jit(solution)/shard_map/ppermute | solution.py:559
  43.8 17.5 %collective-permute-start.15 = (bf16[9,256,128]{2,1,0:T(8,128)(2,1)S(1)}, bf16[9,256,128]{2,1,0:T(8,128)(2,1)S(1)}, u32[]{:S(2)}, u32[]{:S(2)}) collective-permute-start(bf16[9,256,128]{2,1,0:T(8,128)(2,1)S(1)} %grad_second.3.refs_0_.x), channel_id=1, source_target_pairs={{0,8},{4,12},{24,16},{28,20},{1,9},{5,13},{25,17},{29,21},{2,10},{... | collective-permute-start | bytes 1769480 | tf_op jit(solution)/shard_map/ppermute | solution.py:533
  47.0 12.8 %collective-permute-start.9 = (bf16[1024,128]{1,0:T(8,128)(2,1)S(1)}, bf16[1024,128]{1,0:T(8,128)(2,1)S(1)}, u32[]{:S(2)}, u32[]{:S(2)}) collective-permute-start(bf16[1024,128]{1,0:T(8,128)(2,1)S(1)} %get-tuple-element.57), channel_id=1, source_target_pairs={{0,1},{1,0},{2,3},{3,2},{4,5},{5,4},{6,7},{7,6},{8,9},{9,8},{10,11... | collective-permute-start | bytes 786440 | tf_op jit(solution)/shard_map/ppermute | solution.py:559
  51.3 20.7 %collective-permute-start.17 = (bf16[9,256,128]{2,1,0:T(8,128)(2,1)S(1)}, bf16[9,256,128]{2,1,0:T(8,128)(2,1)S(1)}, u32[]{:S(2)}, u32[]{:S(2)}) collective-permute-start(bf16[9,256,128]{2,1,0:T(8,128)(2,1)S(1)} %grad_second.4.refs_4_.x), channel_id=1, source_target_pairs={{0,8},{4,12},{24,16},{28,20},{1,9},{5,13},{25,17},{29,21},{2,10},{... | collective-permute-start | bytes 1769480 | tf_op jit(solution)/shard_map/ppermute | solution.py:533
  61.4 15.6 %collective-permute-start.16 = (bf16[9,256,128]{2,1,0:T(8,128)(2,1)S(1)}, bf16[9,256,128]{2,1,0:T(8,128)(2,1)S(1)}, u32[]{:S(2)}, u32[]{:S(2)}) collective-permute-start(bf16[9,256,128]{2,1,0:T(8,128)(2,1)S(1)} %line_add.12.refs_0_.x), channel_id=1, source_target_pairs={{8,16},{12,20},{16,8},{20,12},{9,17},{13,21},{17,9},{21,13},{10,18... | collective-permute-start | bytes 1769480 | tf_op jit(solution)/shard_map/ppermute | solution.py:533
  62.1 15.1 %collective-permute-start.14 = (bf16[1024,128]{1,0:T(8,128)(2,1)S(1)}, bf16[1024,128]{1,0:T(8,128)(2,1)S(1)}, u32[]{:S(2)}, u32[]{:S(2)}) collective-permute-start(bf16[1024,128]{1,0:T(8,128)(2,1)S(1)} %get-tuple-element.61.refs_0_), channel_id=1, source_target_pairs={{0,3},{1,2},{2,1},{3,0},{4,7},{5,6},{6,5},{7,4},{8,11},{9,10},{10,... | collective-permute-start | bytes 786440 | tf_op jit(solution)/shard_map/ppermute | solution.py:559
  63.5 13.6 %collective-permute-start.13 = (bf16[1024,128]{1,0:T(8,128)(2,1)S(1)}, bf16[1024,128]{1,0:T(8,128)(2,1)S(1)}, u32[]{:S(2)}, u32[]{:S(2)}) collective-permute-start(bf16[1024,128]{1,0:T(8,128)(2,1)S(1)} %get-tuple-element.61.refs_0_), channel_id=1, source_target_pairs={{0,2},{1,3},{2,0},{3,1},{4,6},{5,7},{6,4},{7,5},{8,10},{9,11},{10,... | collective-permute-start | bytes 786440 | tf_op jit(solution)/shard_map/ppermute | solution.py:559
  64.1 13.1 %collective-permute-start.12 = (bf16[1024,128]{1,0:T(8,128)(2,1)S(1)}, bf16[1024,128]{1,0:T(8,128)(2,1)S(1)}, u32[]{:S(2)}, u32[]{:S(2)}) collective-permute-start(bf16[1024,128]{1,0:T(8,128)(2,1)S(1)} %get-tuple-element.61.refs_0_), channel_id=1, source_target_pairs={{0,1},{1,0},{2,3},{3,2},{4,5},{5,4},{6,7},{7,6},{8,9},{9,8},{10,11... | collective-permute-start | bytes 786440 | tf_op jit(solution)/shard_map/ppermute | solution.py:559
  71.9 20.7 %collective-permute-start.22 = (bf16[9,256,128]{2,1,0:T(8,128)(2,1)S(1)}, bf16[9,256,128]{2,1,0:T(8,128)(2,1)}, u32[]{:S(2)}, u32[]{:S(2)}) collective-permute-start(bf16[9,256,128]{2,1,0:T(8,128)(2,1)S(1)} %grad_second.5.refs_0_.x), channel_id=1, source_target_pairs={{0,8},{4,12},{24,16},{28,20},{1,9},{5,13},{25,17},{29,21},{2,10},{... | collective-permute-start | bytes 1769480 | tf_op jit(solution)/shard_map/ppermute | solution.py:533
  80.1 14.6 %collective-permute-start.21 = (bf16[9,256,128]{2,1,0:T(8,128)(2,1)S(1)}, bf16[9,256,128]{2,1,0:T(8,128)(2,1)}, u32[]{:S(2)}, u32[]{:S(2)}) collective-permute-start(bf16[9,256,128]{2,1,0:T(8,128)(2,1)S(1)} %line_add.13.refs_0_.x), channel_id=1, source_target_pairs={{8,16},{12,20},{16,8},{20,12},{9,17},{13,21},{17,9},{21,13},{10,18... | collective-permute-start | bytes 1769480 | tf_op jit(solution)/shard_map/ppermute | solution.py:533
  81.6 17.4 %collective-permute-start.20 = (bf16[9,256,128]{2,1,0:T(8,128)(2,1)S(1)}, bf16[9,256,128]{2,1,0:T(8,128)(2,1)}, u32[]{:S(2)}, u32[]{:S(2)}) collective-permute-start(bf16[9,256,128]{2,1,0:T(8,128)(2,1)S(1)} %line_add.14.refs_4_.x), channel_id=1, source_target_pairs={{8,0},{12,4},{16,24},{20,28},{9,1},{13,5},{17,25},{21,29},{10,2},{... | collective-permute-start | bytes 1769480 | tf_op jit(solution)/shard_map/ppermute | solution.py:533
  87.4 18.1 %collective-permute-start.26 = (bf16[1168,256]{1,0:T(8,128)(2,1)S(1)}, bf16[1168,256]{1,0:T(8,128)(2,1)S(1)}, u32[]{:S(2)}, u32[]{:S(2)}) collective-permute-start(bf16[1168,256]{1,0:T(8,128)(2,1)S(1)} %get-tuple-element.66.refs_0_.x), channel_id=1, source_target_pairs={{0,8},{4,12},{24,16},{28,20},{1,9},{5,13},{25,17},{29,21},{2,10},{... | collective-permute-start | bytes 1794056 | tf_op jit(solution)/shard_map/ppermute | solution.py:533
  93.9 12.4 %collective-permute-start.25 = (bf16[9,256,128]{2,1,0:T(8,128)(2,1)S(1)}, bf16[9,256,128]{2,1,0:T(8,128)(2,1)S(1)}, u32[]{:S(2)}, u32[]{:S(2)}) collective-permute-start(bf16[9,256,128]{2,1,0:T(8,128)(2,1)S(1)} %line_add.15.refs_0_.x), channel_id=1, source_target_pairs={{8,16},{12,20},{16,8},{20,12},{9,17},{13,21},{17,9},{21,13},{10,18... | collective-permute-start | bytes 1769480 | tf_op jit(solution)/shard_map/ppermute | solution.py:533
  96.0 17.6 %collective-permute-start.24 = (bf16[9,256,128]{2,1,0:T(8,128)(2,1)S(1)}, bf16[9,256,128]{2,1,0:T(8,128)(2,1)S(1)}, u32[]{:S(2)}, u32[]{:S(2)}) collective-permute-start(bf16[9,256,128]{2,1,0:T(8,128)(2,1)S(1)} %line_add.16.refs_0_.x), channel_id=1, source_target_pairs={{8,0},{12,4},{16,24},{20,28},{9,1},{13,5},{17,25},{21,29},{10,2},{... | collective-permute-start | bytes 1769480 | tf_op jit(solution)/shard_map/ppermute | solution.py:533
  100.1 15.6 %collective-permute-start.23 = (bf16[9,256,128]{2,1,0:T(8,128)(2,1)S(1)}, bf16[9,256,128]{2,1,0:T(8,128)(2,1)S(1)}, u32[]{:S(2)}, u32[]{:S(2)}) collective-permute-start(bf16[9,256,128]{2,1,0:T(8,128)(2,1)S(1)} %line_pick.6.refs_0_.own), channel_id=1, source_target_pairs={{0,4},{4,0},{8,12},{12,8},{16,20},{20,16},{24,28},{28,24},{1,5},{5... | collective-permute-start | bytes 1769480 | tf_op jit(solution)/shard_map/ppermute | solution.py:562
  101.0 18.6 %collective-permute-start.19 = (bf16[1168,256]{1,0:T(8,128)(2,1)S(1)}, bf16[1168,256]{1,0:T(8,128)(2,1)S(1)}, u32[]{:S(2)}, u32[]{:S(2)}) collective-permute-start(bf16[1168,256]{1,0:T(8,128)(2,1)S(1)} %get-tuple-element.65.x), channel_id=1, source_target_pairs={{0,8},{4,12},{24,16},{28,20},{1,9},{5,13},{25,17},{29,21},{2,10},{... | collective-permute-start | bytes 1794056 | tf_op jit(solution)/shard_map/ppermute | solution.py:533
  105.6 14.8 %collective-permute-start.31 = (bf16[1168,256]{1,0:T(8,128)(2,1)S(1)}, bf16[1168,256]{1,0:T(8,128)(2,1)S(1)}, u32[]{:S(2)}, u32[]{:S(2)}) collective-permute-start(bf16[1168,256]{1,0:T(8,128)(2,1)S(1)} %line_add.17.refs_0_.x), channel_id=1, source_target_pairs={{8,16},{12,20},{16,8},{20,12},{9,17},{13,21},{17,9},{21,13},{10,18... | collective-permute-start | bytes 1794056 | tf_op jit(solution)/shard_map/ppermute | solution.py:533
  106.3 24.8 %collective-permute-start.28 = (bf16[1168,256]{1,0:T(8,128)(2,1)S(1)}, bf16[1168,256]{1,0:T(8,128)(2,1)S(1)}, u32[]{:S(2)}, u32[]{:S(2)}) collective-permute-start(bf16[1168,256]{1,0:T(8,128)(2,1)S(1)} %get-tuple-element.68.x), channel_id=1, source_target_pairs={{0,8},{4,12},{24,16},{28,20},{1,9},{5,13},{25,17},{29,21},{2,10},{... | collective-permute-start | bytes 1794056 | tf_op jit(solution)/shard_map/ppermute | solution.py:533
  113.6 14.9 %collective-permute-start.30 = (bf16[9,256,128]{2,1,0:T(8,128)(2,1)S(1)}, bf16[9,256,128]{2,1,0:T(8,128)(2,1)S(1)}, u32[]{:S(2)}, u32[]{:S(2)}) collective-permute-start(bf16[9,256,128]{2,1,0:T(8,128)(2,1)S(1)} %line_add.18.refs_0_.x), channel_id=1, source_target_pairs={{8,0},{12,4},{16,24},{20,28},{9,1},{13,5},{17,25},{21,29},{10,2},{... | collective-permute-start | bytes 1769480 | tf_op jit(solution)/shard_map/ppermute | solution.py:533
  115.7 13.4 %collective-permute-start.29 = (bf16[9,256,128]{2,1,0:T(8,128)(2,1)S(1)}, bf16[9,256,128]{2,1,0:T(8,128)(2,1)S(1)}, u32[]{:S(2)}, u32[]{:S(2)}) collective-permute-start(bf16[9,256,128]{2,1,0:T(8,128)(2,1)S(1)} %line_pick.7.refs_0_.own), channel_id=1, source_target_pairs={{0,4},{4,0},{8,12},{12,8},{16,20},{20,16},{24,28},{28,24},{1,5},{5... | collective-permute-start | bytes 1769480 | tf_op jit(solution)/shard_map/ppermute | solution.py:562
  119.7 17.4 %collective-permute-start.27 = (bf16[1168,256]{1,0:T(8,128)(2,1)S(1)}, bf16[1168,256]{1,0:T(8,128)(2,1)S(1)}, u32[]{:S(2)}, u32[]{:S(2)}) collective-permute-start(bf16[1168,256]{1,0:T(8,128)(2,1)S(1)} %line_add.19.refs_0_.x), channel_id=1, source_target_pairs={{8,16},{12,20},{16,8},{20,12},{9,17},{13,21},{17,9},{21,13},{10,18... | collective-permute-start | bytes 1794056 | tf_op jit(solution)/shard_map/ppermute | solution.py:533
  120.6 20.7 %collective-permute-start.35 = (bf16[1168,256]{1,0:T(8,128)(2,1)S(1)}, bf16[1168,256]{1,0:T(8,128)(2,1)S(1)}, u32[]{:S(2)}, u32[]{:S(2)}) collective-permute-start(bf16[1168,256]{1,0:T(8,128)(2,1)S(1)} %line_add.20.refs_0_.x), channel_id=1, source_target_pairs={{8,0},{12,4},{16,24},{20,28},{9,1},{13,5},{17,25},{21,29},{10,2},{... | collective-permute-start | bytes 1794056 | tf_op jit(solution)/shard_map/ppermute | solution.py:533
  131.3 17.2 %collective-permute-start.33 = (bf16[1168,256]{1,0:T(8,128)(2,1)S(1)}, bf16[1168,256]{1,0:T(8,128)(2,1)S(1)}, u32[]{:S(2)}, u32[]{:S(2)}) collective-permute-start(bf16[1168,256]{1,0:T(8,128)(2,1)S(1)} %line_add.21.refs_0_.x), channel_id=1, source_target_pairs={{8,16},{12,20},{16,8},{20,12},{9,17},{13,21},{17,9},{21,13},{10,18... | collective-permute-start | bytes 1794056 | tf_op jit(solution)/shard_map/ppermute | solution.py:533
  132.0 14.4 %collective-permute-start.34 = (bf16[9,256,128]{2,1,0:T(8,128)(2,1)S(1)}, bf16[9,256,128]{2,1,0:T(8,128)(2,1)S(1)}, u32[]{:S(2)}, u32[]{:S(2)}) collective-permute-start(bf16[9,256,128]{2,1,0:T(8,128)(2,1)S(1)} %line_pick.8.refs_1_.own), channel_id=1, source_target_pairs={{0,4},{4,0},{8,12},{12,8},{16,20},{20,16},{24,28},{28,24},{1,5},{5... | collective-permute-start | bytes 1769480 | tf_op jit(solution)/shard_map/ppermute | solution.py:562
  137.2 17.5 %collective-permute-start.32 = (bf16[1168,256]{1,0:T(8,128)(2,1)S(1)}, bf16[1168,256]{1,0:T(8,128)(2,1)S(1)}, u32[]{:S(2)}, u32[]{:S(2)}) collective-permute-start(bf16[1168,256]{1,0:T(8,128)(2,1)S(1)} %line_add.22.refs_0_.x), channel_id=1, source_target_pairs={{8,0},{12,4},{16,24},{20,28},{9,1},{13,5},{17,25},{21,29},{10,2},{... | collective-permute-start | bytes 1794056 | tf_op jit(solution)/shard_map/ppermute | solution.py:533
  141.9 24.4 %collective-permute-start.37 = (bf16[1168,256]{1,0:T(8,128)(2,1)S(1)}, bf16[1168,256]{1,0:T(8,128)(2,1)S(1)}, u32[]{:S(2)}, u32[]{:S(2)}) collective-permute-start(bf16[1168,256]{1,0:T(8,128)(2,1)S(1)} %line_pick.9.refs_1_.own), channel_id=1, source_target_pairs={{0,4},{4,0},{8,12},{12,8},{16,20},{20,16},{24,28},{28,24},{1,5},{5... | collective-permute-start | bytes 1794056 | tf_op jit(solution)/shard_map/ppermute | solution.py:562
  148.6 19.8 %collective-permute-start.36 = (bf16[1168,256]{1,0:T(8,128)(2,1)S(1)}, bf16[1168,256]{1,0:T(8,128)(2,1)S(1)}, u32[]{:S(2)}, u32[]{:S(2)}) collective-permute-start(bf16[1168,256]{1,0:T(8,128)(2,1)S(1)} %line_add.23.refs_0_.x), channel_id=1, source_target_pairs={{8,0},{12,4},{16,24},{20,28},{9,1},{13,5},{17,25},{21,29},{10,2},{... | collective-permute-start | bytes 1794056 | tf_op jit(solution)/shard_map/ppermute | solution.py:533
  155.3 15.6 %collective-permute-start.39 = (bf16[1168,256]{1,0:T(8,128)(2,1)S(1)}, bf16[1168,256]{1,0:T(8,128)(2,1)S(1)}, u32[]{:S(2)}, u32[]{:S(2)}) collective-permute-start(bf16[1168,256]{1,0:T(8,128)(2,1)S(1)} %line_pick.10.refs_4_.own), channel_id=1, source_target_pairs={{0,4},{4,0},{8,12},{12,8},{16,20},{20,16},{24,28},{28,24},{1,5},{5... | collective-permute-start | bytes 1794056 | tf_op jit(solution)/shard_map/ppermute | solution.py:562
  (22 other events, 266.6 us)

commit v14 on v13

--- a/solution.py
+++ b/solution.py
@@ -33,10 +33,11 @@
     ("line", 0, 0),
     ("second", 2),
     ("line", 1, 0),
+    ("halves",),
     ("line", 0, 1),
-    ("halves",),
-    ("first",),
+    ("first", -1),
     ("line", 2, 0),
+    ("first", 0, 1),
     ("line", 1, 1),
     ("line", 0, 2),
     ("line", 3, 0),
@@ -365,8 +366,8 @@
     return jnp.where(inside, pltpu.roll(cells, (-off) % CELLS, 1), 0.0).astype(BF16)
 
 
-def grad_first_kernel(vol_own, vol_other, own, other, gain_part, *refs):
-    outs, moved = refs[-4:-1], refs[-1]
+def grad_first_kernel(offsets, vol_own, vol_other, own, other, gain_part, *refs):
+    outs, moved = refs[-1 - len(offsets) : -1], refs[-1]
     half, rows = own.shape[0], own.shape[2]
     fields = [ref[...].astype(F32) for ref in (vol_own, vol_other)]
     rhs = [jnp.concatenate([ref[j] for j in range(half)], axis=1) for ref in (own, other)]
@@ -374,7 +375,7 @@
         for which in range(2):
             for c in range(3):
                 moved[which, c * rows : (c + 1) * rows] = moved_lanes(fields[which], b - 1, c - 1)
-        for a in (-1, 0, 1):
+        for out, a in zip(outs, offsets):
             begin, count = max(0, -a) * PLANE, (DEPTH - abs(a)) * PLANE
             shift = begin + a * PLANE
             grads = None
@@ -382,20 +383,24 @@
                 lhs = moved[which, :, shift : shift + count]
                 part = jnp.dot(lhs, rhs[which][begin : begin + count], preferred_element_type=F32)
                 grads = part if grads is None else grads + part
-            outs[a + 1][3 * rows * b : 3 * rows * (b + 1)] = grads.astype(BF16)
+            out[3 * rows * b : 3 * rows * (b + 1)] = grads.astype(BF16)
     filler = jnp.zeros((1, half * rows - rows), F32)
-    outs[0][9 * rows :] = split_rows(jnp.concatenate([gain_part[...], filler], axis=1))
-    for out in outs[1:]:
-        out[9 * rows :] = jnp.zeros((EXTRA, half * rows), BF16)
-
-
-def grad_first(vol_own, vol_other, own, other, gain_part, after):
+    for out, a in zip(outs, offsets):
+        if a == -1:
+            extra = split_rows(jnp.concatenate([gain_part[...], filler], axis=1))
+        else:
+            extra = jnp.zeros((EXTRA, half * rows), BF16)
+        out[9 * rows :] = extra
+
+
+def grad_first(offsets, vol_own, vol_other, own, other, gain_part, after):
     half, cells, rows = own.shape
+    count = len(offsets)
     return pl.pallas_call(
-        grad_first_kernel,
+        functools.partial(grad_first_kernel, offsets),
         in_specs=[pl.BlockSpec(memory_space=pltpu.VMEM)] * 5 + [UNREAD] * len(after),
-        out_specs=[pl.BlockSpec(memory_space=pltpu.VMEM)] * 3,
-        out_shape=[jax.ShapeDtypeStruct((9 * rows + EXTRA, half * rows), BF16)] * 3,
+        out_specs=[pl.BlockSpec(memory_space=pltpu.VMEM)] * count,
+        out_shape=[jax.ShapeDtypeStruct((9 * rows + EXTRA, half * rows), BF16)] * count,
         scratch_shapes=[pltpu.VMEM((2, 3 * rows, CELLS), BF16)],
         compiler_params=pltpu.CompilerParams(vmem_limit_bytes=LIMIT),
         cost_estimate=LIGHT,
@@ -643,13 +648,13 @@
         parts[chunk] = grad_second(chunk - 1, moved_cot, act_keep, act_other, last)
         last = (parts[chunk],)
 
-    def first_parts():
+    def first_parts(*offsets):
         nonlocal last
         own, other = done["dpre_halves"]
-        parts[3], parts[4], parts[5] = grad_first(
-            vol, vol_other, own, other, done["gain"], last
-        )
-        last = (parts[3],)
+        made = grad_first(offsets, vol, vol_other, own, other, done["gain"], last)
+        for a, part in zip(offsets, made):
+            parts[4 + a] = part
+        last = (made[0],)
 
     def norm_back():
         nonlocal last

time: 176 us -> 176 us (level)
    pallas_call x1 -> x2, Pallas kernels: 4.44 us -> 5.99 us  [grad_first(): pl.pallas_call(functools.partial(grad_first_kernel, offsets), in_specs=[p...]
where the time goes in v14:
time: 176 us
  starting transfers between devices  70.8 us (40%)
  Pallas kernels  61.6 us (35%)
  waiting for transfers between devices  35.6 us (20%)
  local copies, waits for them, and re-layouts  4.71 us (3%)
    ppermute x18, starting transfers between devices, line_send(): return lax.ppermute(x, 'dp', pairs)  39 us
    ppermute x18, waiting for transfers between devices, line_send(): return lax.ppermute(x, 'dp', pairs)  21.1 us
    ppermute x10, starting transfers between devices, to_core(): lax.ppermute(x, 'dp', [(i, i ^ 1) for i in range(lax.axis_size('dp'))])  20.3 us
    pallas_call x2, Pallas kernels, conv_full(): pl.pallas_call(functools.partial(conv_kernel, n, sign, transposed), in_sp...  14.1 us
    ppermute x12, waiting for transfers between devices, to_partner(): return lax.ppermute(x, 'chan', [(i, i ^ m) for i in range(n)])  13 us
    pallas_call x2, Pallas kernels, spread_shares(): pl.pallas_call(functools.partial(share_kernel, n, sign), in_specs=[smem()...  12.8 us
    pallas_call x6, Pallas kernels, finish(): pl.pallas_call(functools.partial(finish_kernel, n, axis, factor, chunk),...  12.7 us
    ppermute x12, starting transfers between devices, to_partner(): return lax.ppermute(x, 'chan', [(i, i ^ m) for i in range(n)])  11.5 us
  transfers between devices with their start and end apart: 40, of which 11 were waited for; matrix products, arithmetic and copies ran while one was open for 0% of the time, Pallas kernels for 28%

profile of v14, /device:TPU:1, one launch (start us, length us, event | category | flops | bytes accessed | tf_op | source)
XLA Modules:
  0.0 175.5 jit_solution(881771377488385957)
XLA Ops:
  1.3 7.0 %pre.1 = (bf16[1024,128]{1,0:T(8,128)(2,1)}, bf16[1024,128]{1,0:T(8,128)(2,1)}, bf16[1024,128]{1,0:T(8,128)(2,1)}, bf16[1024,128]{1,0:T(8,128)(2,1)}) custom-call(s32[2]{0:T(128)} %pad_add_fusion.idx, bf16[128,1024]{1,0:T(8,128)(2,1)} %bitcast.12, bf16[3456,512]{1,0:T(8,128)(2,1)} %bitcast.10), custom_call_target="tpu_custom_call" | custom-call | flops 1024 | bytes 1024 | tf_op jit(solution)/shard_map/pre/pallas_call | solution.py:159
  8.4 2.1 %collective-permute-start = (bf16[1024,128]{1,0:T(8,128)(2,1)}, bf16[1024,128]{1,0:T(8,128)(2,1)S(1)}, u32[]{:S(2)}, u32[]{:S(2)}) collective-permute-start(bf16[1024,128]{1,0:T(8,128)(2,1)} %get-tuple-element.43), channel_id=1, source_target_pairs={{0,1},{1,0},{2,3},{3,2},{4,5},{5,4},{6,7},{7,6},{8,9},{9,8},{10,11... | collective-permute-start | bytes 786440 | tf_op jit(solution)/shard_map/ppermute | solution.py:564
  13.0 2.0 %copy-done.1 = bf16[27,512,128]{2,1,0:T(8,128)(2,1)S(1)} copy-done((bf16[27,512,128]{2,1,0:T(8,128)(2,1)S(1)}, bf16[27,512,128]{2,1,0:T(8,128)(2,1)}, u32[]{:S(2)}) %copy-start.1) | copy-done | bytes 3538968
  16.6 5.8 %dact.1 = (bf16[1024,128]{1,0:T(8,128)(2,1)S(1)}, bf16[1024,128]{1,0:T(8,128)(2,1)S(1)}, bf16[1024,128]{1,0:T(8,128)(2,1)S(1)}, bf16[1024,128]{1,0:T(8,128)(2,1)S(1)}) custom-call(s32[2]{0:T(128)S(1)} %copy-done.12, bf16[128,1024]{1,0:T(8,128)(2,1)S(1)} %bitcast.17, bf16[27,512,128]{2,1,0:T(8,128)(2,1)S(1)} %copy-done.1), custom_call_target="tpu_custom_call" | custom-call | flops 1024 | bytes 1024 | tf_op jit(solution)/shard_map/dact/pallas_call | solution.py:159
  24.8 2.0 %collective-permute-start.5 = (bf16[1024,128]{1,0:T(8,128)(2,1)S(1)}, bf16[1024,128]{1,0:T(8,128)(2,1)S(1)}, u32[]{:S(2)}, u32[]{:S(2)}) collective-permute-start(bf16[1024,128]{1,0:T(8,128)(2,1)S(1)} %get-tuple-element.49._.refs_0_), channel_id=1, source_target_pairs={{0,3},{1,2},{2,1},{3,0},{4,7},{5,6},{6,5},{7,4},{8,11},{9,10},{10,... | collective-permute-start | bytes 786440 | tf_op jit(solution)/shard_map/ppermute | solution.py:564
  28.2 3.7 %collective-permute-done.5.refs_3_ = bf16[1024,128]{1,0:T(8,128)(2,1)S(1)} collective-permute-done((bf16[1024,128]{1,0:T(8,128)(2,1)S(1)}, bf16[1024,128]{1,0:T(8,128)(2,1)S(1)}, u32[]{:S(2)}, u32[]{:S(2)}) %collective-permute-start.5) | collective-permute-done | bytes 262176 | tf_op jit(solution)/shard_map/ppermute | solution.py:564
  31.8 7.8 %collective-permute-done.4.refs_2_ = bf16[1024,128]{1,0:T(8,128)(2,1)S(1)} collective-permute-done((bf16[1024,128]{1,0:T(8,128)(2,1)S(1)}, bf16[1024,128]{1,0:T(8,128)(2,1)S(1)}, u32[]{:S(2)}, u32[]{:S(2)}) %collective-permute-start.4) | collective-permute-done | bytes 262176 | tf_op jit(solution)/shard_map/ppermute | solution.py:564
  41.0 1.5 collective-permute-done.8.other
  43.8 3.2 %collective-permute-start.16 = (bf16[9,256,128]{2,1,0:T(8,128)(2,1)S(1)}, bf16[9,256,128]{2,1,0:T(8,128)(2,1)S(1)}, u32[]{:S(2)}, u32[]{:S(2)}) collective-permute-start(bf16[9,256,128]{2,1,0:T(8,128)(2,1)S(1)} %grad_second.3.refs_0_.x), channel_id=1, source_target_pairs={{0,8},{4,12},{24,16},{28,20},{1,9},{5,13},{25,17},{29,21},{2,10},{... | collective-permute-start | bytes 1769480 | tf_op jit(solution)/shard_map/ppermute | solution.py:538
  49.7 1.5 grad_second.4.refs_4_.x
  52.8 7.0 %output.1 = (bf16[128,1024]{1,0:T(8,128)(2,1)}, f32[8,128]{1,0:T(8,128)S(1)}) custom-call(s32[2]{0:T(128)S(1)} %copy-done.13, bf16[27,512,128]{2,1,0:T(8,128)(2,1)S(1)} %copy-done.2, bf16[1024,128]{1,0:T(8,128)(2,1)S(1)} %get-tuple-element.49._.refs_0_, bf16[1024,128]{1,0:T(8,128)(2,1)S(1)} %collective-permute-done.3.refs_1_, ...), custom_call_target="tpu_custom_call" | custom-call | flops 1024 | bytes 1024 | tf_op jit(solution)/shard_map/output/pallas_call | solution.py:262
  66.0 5.9 %collective-permute-done.15.y = bf16[9,256,128]{2,1,0:T(8,128)(2,1)S(1)} collective-permute-done((bf16[9,256,128]{2,1,0:T(8,128)(2,1)S(1)}, bf16[9,256,128]{2,1,0:T(8,128)(2,1)S(1)}, u32[]{:S(2)}, u32[]{:S(2)}) %collective-permute-start.15) | collective-permute-done | bytes 589856 | tf_op jit(solution)/shard_map/ppermute | solution.py:538
  72.0 4.9 %collective-permute-start.18 = (bf16[9,256,128]{2,1,0:T(8,128)(2,1)S(1)}, bf16[9,256,128]{2,1,0:T(8,128)(2,1)}, u32[]{:S(2)}, u32[]{:S(2)}) collective-permute-start(bf16[9,256,128]{2,1,0:T(8,128)(2,1)S(1)} %grad_second.5.refs_0_.x), channel_id=1, source_target_pairs={{0,8},{4,12},{24,16},{28,20},{1,9},{5,13},{25,17},{29,21},{2,10},{... | collective-permute-start | bytes 1769480 | tf_op jit(solution)/shard_map/ppermute | solution.py:538
  83.0 2.5 %grad_first.2.refs_0_.x = bf16[1168,256]{1,0:T(8,128)(2,1)S(1)} custom-call(bf16[128,1024]{1,0:T(8,128)(2,1)S(1)} %bitcast.14, bf16[128,1024]{1,0:T(8,128)(2,1)S(1)} %collective-permute-done.7.refs_5_.vol_other, bf16[2,1024,128]{2,1,0:T(8,128)(2,1)S(1)} %get-tuple-element.61.refs_0_.own, bf16[2,1024,128]{2,1,0:T(8,128)(2,1)} %collective-permute-done.17.other, ...), custom_call_target="tpu_custom_call" | custom-call | flops 1024 | bytes 1024 | tf_op jit(solution)/shard_map/grad_first/pallas_call | solution.py:399
  85.5 5.0 %collective-permute-start.26 = (bf16[1168,256]{1,0:T(8,128)(2,1)S(1)}, bf16[1168,256]{1,0:T(8,128)(2,1)S(1)}, u32[]{:S(2)}, u32[]{:S(2)}) collective-permute-start(bf16[1168,256]{1,0:T(8,128)(2,1)S(1)} %grad_first.2.refs_0_.x), channel_id=1, source_target_pairs={{0,8},{4,12},{24,16},{28,20},{1,9},{5,13},{25,17},{29,21},{2,10},{... | collective-permute-start | bytes 1794056 | tf_op jit(solution)/shard_map/ppermute | solution.py:538
  92.4 3.5 %grad_first.3 = (bf16[1168,256]{1,0:T(8,128)(2,1)S(1)}, bf16[1168,256]{1,0:T(8,128)(2,1)S(1)}) custom-call(bf16[128,1024]{1,0:T(8,128)(2,1)S(1)} %bitcast.15, bf16[128,1024]{1,0:T(8,128)(2,1)S(1)} %collective-permute-done.7.refs_5_.vol_other, bf16[2,1024,128]{2,1,0:T(8,128)(2,1)S(1)} %get-tuple-element.61.refs_0_.own, ...), custom_call_target="tpu_custom_call" | custom-call | flops 1024 | bytes 1024 | tf_op jit(solution)/shard_map/grad_first/pallas_call | solution.py:399
  100.7 5.1 %collective-permute-start.20 = (bf16[1168,256]{1,0:T(8,128)(2,1)S(1)}, bf16[1168,256]{1,0:T(8,128)(2,1)S(1)}, u32[]{:S(2)}, u32[]{:S(2)}) collective-permute-start(bf16[1168,256]{1,0:T(8,128)(2,1)S(1)} %get-tuple-element.64.refs_0_.x), channel_id=1, source_target_pairs={{0,8},{4,12},{24,16},{28,20},{1,9},{5,13},{25,17},{29,21},{2,10},{... | collective-permute-start | bytes 1794056 | tf_op jit(solution)/shard_map/ppermute | solution.py:538
  106.7 6.5 %collective-permute-start.28 = (bf16[1168,256]{1,0:T(8,128)(2,1)S(1)}, bf16[1168,256]{1,0:T(8,128)(2,1)S(1)}, u32[]{:S(2)}, u32[]{:S(2)}) collective-permute-start(bf16[1168,256]{1,0:T(8,128)(2,1)S(1)} %get-tuple-element.66.x), channel_id=1, source_target_pairs={{0,8},{4,12},{24,16},{28,20},{1,9},{5,13},{25,17},{29,21},{2,10},{... | collective-permute-start | bytes 1794056 | tf_op jit(solution)/shard_map/ppermute | solution.py:538
  115.3 2.0 %collective-permute-start.29 = (bf16[9,256,128]{2,1,0:T(8,128)(2,1)S(1)}, bf16[9,256,128]{2,1,0:T(8,128)(2,1)S(1)}, u32[]{:S(2)}, u32[]{:S(2)}) collective-permute-start(bf16[9,256,128]{2,1,0:T(8,128)(2,1)S(1)} %line_pick.7.refs_0_.own), channel_id=1, source_target_pairs={{0,4},{4,0},{8,12},{12,8},{16,20},{20,16},{24,28},{28,24},{1,5},{5... | collective-permute-start | bytes 1769480 | tf_op jit(solution)/shard_map/ppermute | solution.py:567
  117.3 2.0 %finish_second.3 = (f32[27,512,128]{2,1,0:T(8,128)}, f32[8,128]{1,0:T(8,128)S(1)}) custom-call(s32[2]{0:T(128)S(1)} %copy-done.13, bf16[9,256,128]{2,1,0:T(8,128)(2,1)S(1)} %line_pick.6.refs_0_.own, bf16[9,256,128]{2,1,0:T(8,128)(2,1)S(1)} %collective-permute-done.23.other, bf16[9,256,128]{2,1,0:T(8,128)(2,1)S(1)} %line_pick.7.refs_0_.own), custom_call_target="tpu_custom_call" | custom-call | flops 1024 | bytes 1024 | tf_op jit(solution)/shard_map/finish_second/pallas_call | solution.py:477
  121.6 6.6 %collective-permute-done.30.y = bf16[9,256,128]{2,1,0:T(8,128)(2,1)S(1)} collective-permute-done((bf16[9,256,128]{2,1,0:T(8,128)(2,1)S(1)}, bf16[9,256,128]{2,1,0:T(8,128)(2,1)S(1)}, u32[]{:S(2)}, u32[]{:S(2)}) %collective-permute-start.30) | collective-permute-done | bytes 589856 | tf_op jit(solution)/shard_map/ppermute | solution.py:538
  128.8 2.0 %finish_second.4 = (f32[27,512,128]{2,1,0:T(8,128)}, f32[8,128]{1,0:T(8,128)S(1)}) custom-call(s32[2]{0:T(128)S(1)} %copy-done.13, bf16[9,256,128]{2,1,0:T(8,128)(2,1)S(1)} %line_pick.7.refs_0_.own, bf16[9,256,128]{2,1,0:T(8,128)(2,1)S(1)} %collective-permute-done.29.other, ...), custom_call_target="tpu_custom_call", output_to_operand_aliasing={{0}: (3, {})} | custom-call | flops 1024 | bytes 1024 | tf_op jit(solution)/shard_map/finish_second/pallas_call | solution.py:477
  132.4 4.7 %collective-permute-start.34 = (bf16[9,256,128]{2,1,0:T(8,128)(2,1)S(1)}, bf16[9,256,128]{2,1,0:T(8,128)(2,1)S(1)}, u32[]{:S(2)}, u32[]{:S(2)}) collective-permute-start(bf16[9,256,128]{2,1,0:T(8,128)(2,1)S(1)} %line_pick.8.refs_1_.own), channel_id=1, source_target_pairs={{0,4},{4,0},{8,12},{12,8},{16,20},{20,16},{24,28},{28,24},{1,5},{5... | collective-permute-start | bytes 1769480 | tf_op jit(solution)/shard_map/ppermute | solution.py:567
  138.5 2.5 %collective-permute-done.35.y = bf16[1168,256]{1,0:T(8,128)(2,1)S(1)} collective-permute-done((bf16[1168,256]{1,0:T(8,128)(2,1)S(1)}, bf16[1168,256]{1,0:T(8,128)(2,1)S(1)}, u32[]{:S(2)}, u32[]{:S(2)}) %collective-permute-start.35) | collective-permute-done | bytes 598048 | tf_op jit(solution)/shard_map/ppermute | solution.py:538
  141.7 4.5 %collective-permute-start.37 = (bf16[1168,256]{1,0:T(8,128)(2,1)S(1)}, bf16[1168,256]{1,0:T(8,128)(2,1)S(1)}, u32[]{:S(2)}, u32[]{:S(2)}) collective-permute-start(bf16[1168,256]{1,0:T(8,128)(2,1)S(1)} %line_pick.9.refs_1_.own), channel_id=1, source_target_pairs={{0,4},{4,0},{8,12},{12,8},{16,20},{20,16},{24,28},{28,24},{1,5},{5... | collective-permute-start | bytes 1794056 | tf_op jit(solution)/shard_map/ppermute | solution.py:567
  146.1 2.0 %finish_second.5 = (f32[27,512,128]{2,1,0:T(8,128)}, f32[8,128]{1,0:T(8,128)S(1)}) custom-call(s32[2]{0:T(128)S(1)} %copy-done.13, bf16[9,256,128]{2,1,0:T(8,128)(2,1)S(1)} %line_pick.8.refs_1_.own, bf16[9,256,128]{2,1,0:T(8,128)(2,1)S(1)} %collective-permute-done.34.other, ...), custom_call_target="tpu_custom_call", output_to_operand_aliasing={{0}: (3, {})} | custom-call | flops 1024 | bytes 1024 | tf_op jit(solution)/shard_map/finish_second/pallas_call | solution.py:477
  149.6 5.0 %collective-permute-done.32.y = bf16[1168,256]{1,0:T(8,128)(2,1)S(1)} collective-permute-done((bf16[1168,256]{1,0:T(8,128)(2,1)S(1)}, bf16[1168,256]{1,0:T(8,128)(2,1)S(1)}, u32[]{:S(2)}, u32[]{:S(2)}) %collective-permute-start.32) | collective-permute-done | bytes 598048 | tf_op jit(solution)/shard_map/ppermute | solution.py:538
  155.3 3.7 %collective-permute-start.39 = (bf16[1168,256]{1,0:T(8,128)(2,1)S(1)}, bf16[1168,256]{1,0:T(8,128)(2,1)S(1)}, u32[]{:S(2)}, u32[]{:S(2)}) collective-permute-start(bf16[1168,256]{1,0:T(8,128)(2,1)S(1)} %line_pick.10.refs_4_.own), channel_id=1, source_target_pairs={{0,4},{4,0},{8,12},{12,8},{16,20},{20,16},{24,28},{28,24},{1,5},{5... | collective-permute-start | bytes 1794056 | tf_op jit(solution)/shard_map/ppermute | solution.py:567
  158.9 7.2 %grad_volume.1 = (bf16[128,1024]{1,0:T(8,128)(2,1)}, f32[8,128]{1,0:T(8,128)S(1)}) custom-call(s32[2]{0:T(128)S(1)} %copy-done.13, bf16[3456,512]{1,0:T(8,128)(2,1)S(1)} %bitcast.11, bf16[1024,128]{1,0:T(8,128)(2,1)S(1)} %get-tuple-element.60.refs_0_, bf16[1024,128]{1,0:T(8,128)(2,1)S(1)} %copy-done.10, bf16[1024,128]{1,0:T(8,128)(2,1)S(1)} %copy-done.8, ...), custom_call_target="tpu_custom_call" | custom-call | flops 1024 | bytes 1024 | tf_op jit(solution)/shard_map/grad_volume/pallas_call | solution.py:262
  166.1 2.0 %finish_first.3 = (f32[27,128,512]{2,1,0:T(8,128)}, f32[8,128]{1,0:T(8,128)S(1)}) custom-call(s32[2]{0:T(128)S(1)} %copy-done.13, bf16[1168,256]{1,0:T(8,128)(2,1)S(1)} %line_pick.9.refs_1_.own, bf16[1168,256]{1,0:T(8,128)(2,1)S(1)} %collective-permute-done.37.other, f32[8,128]{1,0:T(8,128)S(1)} %get-tuple-element.72.refs_0_), custom_call_target="tpu_custom_call" | custom-call | flops 1024 | bytes 1024 | tf_op jit(solution)/shard_map/finish_first/pallas_call | solution.py:477
  170.7 2.0 %finish_first.4 = (f32[27,128,512]{2,1,0:T(8,128)}, f32[8,128]{1,0:T(8,128)S(1)}) custom-call(s32[2]{0:T(128)S(1)} %copy-done.13, bf16[1168,256]{1,0:T(8,128)(2,1)S(1)} %line_pick.10.refs_4_.own, bf16[1168,256]{1,0:T(8,128)(2,1)S(1)} %collective-permute-done.39.other, f32[27,128,512]{2,1,0:T(8,128)} %get-tuple-element.74.refs_0_, ...), custom_call_target="tpu_custom_call", output_to_operand_aliasing={{0}: (3, {})} | custom-call | flops 1024 | bytes 1024 | tf_op jit(solution)/shard_map/finish_first/pallas_call | solution.py:477
  172.7 2.6 %finish_first.5 = (f32[27,128,512]{2,1,0:T(8,128)}, f32[8,128]{1,0:T(8,128)}) custom-call(s32[2]{0:T(128)S(1)} %copy-done.13, bf16[1168,256]{1,0:T(8,128)(2,1)S(1)} %line_pick.11.refs_1_.own, bf16[1168,256]{1,0:T(8,128)(2,1)S(1)} %collective-permute-done.38.other, f32[27,128,512]{2,1,0:T(8,128)} %get-tuple-element.75.refs_0_, ...), custom_call_target="tpu_custom_call", output_to_operand_aliasing={{0}: (3, {})} | custom-call | flops 1024 | bytes 1024 | tf_op jit(solution)/shard_map/finish_first/pallas_call | solution.py:477
  (120 shorter events, 48.2 us)
Async XLA Ops:
  8.4 14.1 %collective-permute-start = (bf16[1024,128]{1,0:T(8,128)(2,1)}, bf16[1024,128]{1,0:T(8,128)(2,1)S(1)}, u32[]{:S(2)}, u32[]{:S(2)}) collective-permute-start(bf16[1024,128]{1,0:T(8,128)(2,1)} %get-tuple-element.43), channel_id=1, source_target_pairs={{0,1},{1,0},{2,3},{3,2},{4,5},{5,4},{6,7},{7,6},{8,9},{9,8},{10,11... | collective-permute-start | bytes 786440 | tf_op jit(solution)/shard_map/ppermute | solution.py:564
  11.7 16.4 %collective-permute-start.7 = (bf16[128,1024]{1,0:T(8,128)(2,1)}, bf16[128,1024]{1,0:T(8,128)(2,1)S(1)}, u32[]{:S(2)}, u32[]{:S(2)}) collective-permute-start(bf16[128,1024]{1,0:T(8,128)(2,1)} %bitcast.13), channel_id=1, source_target_pairs={{0,4},{4,0},{8,12},{12,8},{16,20},{20,16},{24,28},{28,24},{1,5},{5... | collective-permute-start | bytes 786440 | tf_op jit(solution)/shard_map/ppermute | solution.py:567
  13.0 14.5 %collective-permute-start.6 = (bf16[128,1024]{1,0:T(8,128)(2,1)}, bf16[128,1024]{1,0:T(8,128)(2,1)S(1)}, u32[]{:S(2)}, u32[]{:S(2)}) collective-permute-start(bf16[128,1024]{1,0:T(8,128)(2,1)} %bitcast.16), channel_id=1, source_target_pairs={{0,4},{4,0},{8,12},{12,8},{16,20},{20,16},{24,28},{28,24},{1,5},{5... | collective-permute-start | bytes 786440 | tf_op jit(solution)/shard_map/ppermute | solution.py:567
  26.7 12.9 %collective-permute-start.4 = (bf16[1024,128]{1,0:T(8,128)(2,1)S(1)}, bf16[1024,128]{1,0:T(8,128)(2,1)S(1)}, u32[]{:S(2)}, u32[]{:S(2)}) collective-permute-start(bf16[1024,128]{1,0:T(8,128)(2,1)S(1)} %get-tuple-element.49._.refs_0_), channel_id=1, source_target_pairs={{0,2},{1,3},{2,0},{3,1},{4,6},{5,7},{6,4},{7,5},{8,10},{9,11},{10,... | collective-permute-start | bytes 786440 | tf_op jit(solution)/shard_map/ppermute | solution.py:564
  27.2 12.4 %collective-permute-start.3 = (bf16[1024,128]{1,0:T(8,128)(2,1)S(1)}, bf16[1024,128]{1,0:T(8,128)(2,1)S(1)}, u32[]{:S(2)}, u32[]{:S(2)}) collective-permute-start(bf16[1024,128]{1,0:T(8,128)(2,1)S(1)} %get-tuple-element.49._.refs_0_), channel_id=1, source_target_pairs={{0,1},{1,0},{2,3},{3,2},{4,5},{5,4},{6,7},{7,6},{8,9},{9,8},{10,11... | collective-permute-start | bytes 786440 | tf_op jit(solution)/shard_map/ppermute | solution.py:564
  43.8 17.5 %collective-permute-start.16 = (bf16[9,256,128]{2,1,0:T(8,128)(2,1)S(1)}, bf16[9,256,128]{2,1,0:T(8,128)(2,1)S(1)}, u32[]{:S(2)}, u32[]{:S(2)}) collective-permute-start(bf16[9,256,128]{2,1,0:T(8,128)(2,1)S(1)} %grad_second.3.refs_0_.x), channel_id=1, source_target_pairs={{0,8},{4,12},{24,16},{28,20},{1,9},{5,13},{25,17},{29,21},{2,10},{... | collective-permute-start | bytes 1769480 | tf_op jit(solution)/shard_map/ppermute | solution.py:538
  47.0 12.8 %collective-permute-start.9 = (bf16[1024,128]{1,0:T(8,128)(2,1)S(1)}, bf16[1024,128]{1,0:T(8,128)(2,1)S(1)}, u32[]{:S(2)}, u32[]{:S(2)}) collective-permute-start(bf16[1024,128]{1,0:T(8,128)(2,1)S(1)} %get-tuple-element.56), channel_id=1, source_target_pairs={{0,1},{1,0},{2,3},{3,2},{4,5},{5,4},{6,7},{7,6},{8,9},{9,8},{10,11... | collective-permute-start | bytes 786440 | tf_op jit(solution)/shard_map/ppermute | solution.py:564
  51.3 20.7 %collective-permute-start.15 = (bf16[9,256,128]{2,1,0:T(8,128)(2,1)S(1)}, bf16[9,256,128]{2,1,0:T(8,128)(2,1)S(1)}, u32[]{:S(2)}, u32[]{:S(2)}) collective-permute-start(bf16[9,256,128]{2,1,0:T(8,128)(2,1)S(1)} %grad_second.4.refs_4_.x), channel_id=1, source_target_pairs={{0,8},{4,12},{24,16},{28,20},{1,9},{5,13},{25,17},{29,21},{2,10},{... | collective-permute-start | bytes 1769480 | tf_op jit(solution)/shard_map/ppermute | solution.py:538
  61.4 20.1 %collective-permute-start.19 = (bf16[9,256,128]{2,1,0:T(8,128)(2,1)S(1)}, bf16[9,256,128]{2,1,0:T(8,128)(2,1)S(1)}, u32[]{:S(2)}, u32[]{:S(2)}) collective-permute-start(bf16[9,256,128]{2,1,0:T(8,128)(2,1)S(1)} %line_add.12.refs_0_.x), channel_id=1, source_target_pairs={{8,16},{12,20},{16,8},{20,12},{9,17},{13,21},{17,9},{21,13},{10,18... | collective-permute-start | bytes 1769480 | tf_op jit(solution)/shard_map/ppermute | solution.py:538
  62.1 14.9 %collective-permute-start.14 = (bf16[1024,128]{1,0:T(8,128)(2,1)S(1)}, bf16[1024,128]{1,0:T(8,128)(2,1)S(1)}, u32[]{:S(2)}, u32[]{:S(2)}) collective-permute-start(bf16[1024,128]{1,0:T(8,128)(2,1)S(1)} %get-tuple-element.60.refs_0_), channel_id=1, source_target_pairs={{0,3},{1,2},{2,1},{3,0},{4,7},{5,6},{6,5},{7,4},{8,11},{9,10},{10,... | collective-permute-start | bytes 786440 | tf_op jit(solution)/shard_map/ppermute | solution.py:564
  63.5 13.5 %collective-permute-start.13 = (bf16[1024,128]{1,0:T(8,128)(2,1)S(1)}, bf16[1024,128]{1,0:T(8,128)(2,1)S(1)}, u32[]{:S(2)}, u32[]{:S(2)}) collective-permute-start(bf16[1024,128]{1,0:T(8,128)(2,1)S(1)} %get-tuple-element.60.refs_0_), channel_id=1, source_target_pairs={{0,2},{1,3},{2,0},{3,1},{4,6},{5,7},{6,4},{7,5},{8,10},{9,11},{10,... | collective-permute-start | bytes 786440 | tf_op jit(solution)/shard_map/ppermute | solution.py:564
  64.1 13.0 %collective-permute-start.12 = (bf16[1024,128]{1,0:T(8,128)(2,1)S(1)}, bf16[1024,128]{1,0:T(8,128)(2,1)S(1)}, u32[]{:S(2)}, u32[]{:S(2)}) collective-permute-start(bf16[1024,128]{1,0:T(8,128)(2,1)S(1)} %get-tuple-element.60.refs_0_), channel_id=1, source_target_pairs={{0,1},{1,0},{2,3},{3,2},{4,5},{5,4},{6,7},{7,6},{8,9},{9,8},{10,11... | collective-permute-start | bytes 786440 | tf_op jit(solution)/shard_map/ppermute | solution.py:564
  72.0 18.5 %collective-permute-start.18 = (bf16[9,256,128]{2,1,0:T(8,128)(2,1)S(1)}, bf16[9,256,128]{2,1,0:T(8,128)(2,1)}, u32[]{:S(2)}, u32[]{:S(2)}) collective-permute-start(bf16[9,256,128]{2,1,0:T(8,128)(2,1)S(1)} %grad_second.5.refs_0_.x), channel_id=1, source_target_pairs={{0,8},{4,12},{24,16},{28,20},{1,9},{5,13},{25,17},{29,21},{2,10},{... | collective-permute-start | bytes 1769480 | tf_op jit(solution)/shard_map/ppermute | solution.py:538
  80.0 15.9 %collective-permute-start.22 = (bf16[9,256,128]{2,1,0:T(8,128)(2,1)S(1)}, bf16[9,256,128]{2,1,0:T(8,128)(2,1)}, u32[]{:S(2)}, u32[]{:S(2)}) collective-permute-start(bf16[9,256,128]{2,1,0:T(8,128)(2,1)S(1)} %line_add.13.refs_4_.x), channel_id=1, source_target_pairs={{8,16},{12,20},{16,8},{20,12},{9,17},{13,21},{17,9},{21,13},{10,18... | collective-permute-start | bytes 1769480 | tf_op jit(solution)/shard_map/ppermute | solution.py:538
  81.6 17.1 %collective-permute-start.21 = (bf16[9,256,128]{2,1,0:T(8,128)(2,1)S(1)}, bf16[9,256,128]{2,1,0:T(8,128)(2,1)}, u32[]{:S(2)}, u32[]{:S(2)}) collective-permute-start(bf16[9,256,128]{2,1,0:T(8,128)(2,1)S(1)} %line_add.14.refs_0_.x), channel_id=1, source_target_pairs={{8,0},{12,4},{16,24},{20,28},{9,1},{13,5},{17,25},{21,29},{10,2},{... | collective-permute-start | bytes 1769480 | tf_op jit(solution)/shard_map/ppermute | solution.py:538
  85.5 20.4 %collective-permute-start.26 = (bf16[1168,256]{1,0:T(8,128)(2,1)S(1)}, bf16[1168,256]{1,0:T(8,128)(2,1)S(1)}, u32[]{:S(2)}, u32[]{:S(2)}) collective-permute-start(bf16[1168,256]{1,0:T(8,128)(2,1)S(1)} %grad_first.2.refs_0_.x), channel_id=1, source_target_pairs={{0,8},{4,12},{24,16},{28,20},{1,9},{5,13},{25,17},{29,21},{2,10},{... | collective-permute-start | bytes 1794056 | tf_op jit(solution)/shard_map/ppermute | solution.py:538
  91.7 15.1 %collective-permute-start.25 = (bf16[9,256,128]{2,1,0:T(8,128)(2,1)S(1)}, bf16[9,256,128]{2,1,0:T(8,128)(2,1)S(1)}, u32[]{:S(2)}, u32[]{:S(2)}) collective-permute-start(bf16[9,256,128]{2,1,0:T(8,128)(2,1)S(1)} %line_add.15.refs_0_.x), channel_id=1, source_target_pairs={{8,16},{12,20},{16,8},{20,12},{9,17},{13,21},{17,9},{21,13},{10,18... | collective-permute-start | bytes 1769480 | tf_op jit(solution)/shard_map/ppermute | solution.py:538
  97.1 16.2 %collective-permute-start.24 = (bf16[9,256,128]{2,1,0:T(8,128)(2,1)S(1)}, bf16[9,256,128]{2,1,0:T(8,128)(2,1)S(1)}, u32[]{:S(2)}, u32[]{:S(2)}) collective-permute-start(bf16[9,256,128]{2,1,0:T(8,128)(2,1)S(1)} %line_add.16.refs_0_.x), channel_id=1, source_target_pairs={{8,0},{12,4},{16,24},{20,28},{9,1},{13,5},{17,25},{21,29},{10,2},{... | collective-permute-start | bytes 1769480 | tf_op jit(solution)/shard_map/ppermute | solution.py:538
  99.9 15.4 %collective-permute-start.23 = (bf16[9,256,128]{2,1,0:T(8,128)(2,1)S(1)}, bf16[9,256,128]{2,1,0:T(8,128)(2,1)S(1)}, u32[]{:S(2)}, u32[]{:S(2)}) collective-permute-start(bf16[9,256,128]{2,1,0:T(8,128)(2,1)S(1)} %line_pick.6.refs_0_.own), channel_id=1, source_target_pairs={{0,4},{4,0},{8,12},{12,8},{16,20},{20,16},{24,28},{28,24},{1,5},{5... | collective-permute-start | bytes 1769480 | tf_op jit(solution)/shard_map/ppermute | solution.py:567
  100.7 18.6 %collective-permute-start.20 = (bf16[1168,256]{1,0:T(8,128)(2,1)S(1)}, bf16[1168,256]{1,0:T(8,128)(2,1)S(1)}, u32[]{:S(2)}, u32[]{:S(2)}) collective-permute-start(bf16[1168,256]{1,0:T(8,128)(2,1)S(1)} %get-tuple-element.64.refs_0_.x), channel_id=1, source_target_pairs={{0,8},{4,12},{24,16},{28,20},{1,9},{5,13},{25,17},{29,21},{2,10},{... | collective-permute-start | bytes 1794056 | tf_op jit(solution)/shard_map/ppermute | solution.py:538
  106.0 14.2 %collective-permute-start.31 = (bf16[1168,256]{1,0:T(8,128)(2,1)S(1)}, bf16[1168,256]{1,0:T(8,128)(2,1)S(1)}, u32[]{:S(2)}, u32[]{:S(2)}) collective-permute-start(bf16[1168,256]{1,0:T(8,128)(2,1)S(1)} %line_add.17.refs_0_.x), channel_id=1, source_target_pairs={{8,16},{12,20},{16,8},{20,12},{9,17},{13,21},{17,9},{21,13},{10,18... | collective-permute-start | bytes 1794056 | tf_op jit(solution)/shard_map/ppermute | solution.py:538
  106.7 24.8 %collective-permute-start.28 = (bf16[1168,256]{1,0:T(8,128)(2,1)S(1)}, bf16[1168,256]{1,0:T(8,128)(2,1)S(1)}, u32[]{:S(2)}, u32[]{:S(2)}) collective-permute-start(bf16[1168,256]{1,0:T(8,128)(2,1)S(1)} %get-tuple-element.66.x), channel_id=1, source_target_pairs={{0,8},{4,12},{24,16},{28,20},{1,9},{5,13},{25,17},{29,21},{2,10},{... | collective-permute-start | bytes 1794056 | tf_op jit(solution)/shard_map/ppermute | solution.py:538
  113.4 14.8 %collective-permute-start.30 = (bf16[9,256,128]{2,1,0:T(8,128)(2,1)S(1)}, bf16[9,256,128]{2,1,0:T(8,128)(2,1)S(1)}, u32[]{:S(2)}, u32[]{:S(2)}) collective-permute-start(bf16[9,256,128]{2,1,0:T(8,128)(2,1)S(1)} %line_add.18.refs_0_.x), channel_id=1, source_target_pairs={{8,0},{12,4},{16,24},{20,28},{9,1},{13,5},{17,25},{21,29},{10,2},{... | collective-permute-start | bytes 1769480 | tf_op jit(solution)/shard_map/ppermute | solution.py:538
  115.3 13.5 %collective-permute-start.29 = (bf16[9,256,128]{2,1,0:T(8,128)(2,1)S(1)}, bf16[9,256,128]{2,1,0:T(8,128)(2,1)S(1)}, u32[]{:S(2)}, u32[]{:S(2)}) collective-permute-start(bf16[9,256,128]{2,1,0:T(8,128)(2,1)S(1)} %line_pick.7.refs_0_.own), channel_id=1, source_target_pairs={{0,4},{4,0},{8,12},{12,8},{16,20},{20,16},{24,28},{28,24},{1,5},{5... | collective-permute-start | bytes 1769480 | tf_op jit(solution)/shard_map/ppermute | solution.py:567
  119.5 17.6 %collective-permute-start.27 = (bf16[1168,256]{1,0:T(8,128)(2,1)S(1)}, bf16[1168,256]{1,0:T(8,128)(2,1)S(1)}, u32[]{:S(2)}, u32[]{:S(2)}) collective-permute-start(bf16[1168,256]{1,0:T(8,128)(2,1)S(1)} %line_add.19.refs_0_.x), channel_id=1, source_target_pairs={{8,16},{12,20},{16,8},{20,12},{9,17},{13,21},{17,9},{21,13},{10,18... | collective-permute-start | bytes 1794056 | tf_op jit(solution)/shard_map/ppermute | solution.py:538
  120.3 20.7 %collective-permute-start.35 = (bf16[1168,256]{1,0:T(8,128)(2,1)S(1)}, bf16[1168,256]{1,0:T(8,128)(2,1)S(1)}, u32[]{:S(2)}, u32[]{:S(2)}) collective-permute-start(bf16[1168,256]{1,0:T(8,128)(2,1)S(1)} %line_add.20.refs_0_.x), channel_id=1, source_target_pairs={{8,0},{12,4},{16,24},{20,28},{9,1},{13,5},{17,25},{21,29},{10,2},{... | collective-permute-start | bytes 1794056 | tf_op jit(solution)/shard_map/ppermute | solution.py:538
  131.7 16.5 %collective-permute-start.33 = (bf16[1168,256]{1,0:T(8,128)(2,1)S(1)}, bf16[1168,256]{1,0:T(8,128)(2,1)S(1)}, u32[]{:S(2)}, u32[]{:S(2)}) collective-permute-start(bf16[1168,256]{1,0:T(8,128)(2,1)S(1)} %line_add.21.refs_0_.x), channel_id=1, source_target_pairs={{8,16},{12,20},{16,8},{20,12},{9,17},{13,21},{17,9},{21,13},{10,18... | collective-permute-start | bytes 1794056 | tf_op jit(solution)/shard_map/ppermute | solution.py:538
  132.4 13.8 %collective-permute-start.34 = (bf16[9,256,128]{2,1,0:T(8,128)(2,1)S(1)}, bf16[9,256,128]{2,1,0:T(8,128)(2,1)S(1)}, u32[]{:S(2)}, u32[]{:S(2)}) collective-permute-start(bf16[9,256,128]{2,1,0:T(8,128)(2,1)S(1)} %line_pick.8.refs_1_.own), channel_id=1, source_target_pairs={{0,4},{4,0},{8,12},{12,8},{16,20},{20,16},{24,28},{28,24},{1,5},{5... | collective-permute-start | bytes 1769480 | tf_op jit(solution)/shard_map/ppermute | solution.py:567
  137.2 17.5 %collective-permute-start.32 = (bf16[1168,256]{1,0:T(8,128)(2,1)S(1)}, bf16[1168,256]{1,0:T(8,128)(2,1)S(1)}, u32[]{:S(2)}, u32[]{:S(2)}) collective-permute-start(bf16[1168,256]{1,0:T(8,128)(2,1)S(1)} %line_add.22.refs_0_.x), channel_id=1, source_target_pairs={{8,0},{12,4},{16,24},{20,28},{9,1},{13,5},{17,25},{21,29},{10,2},{... | collective-permute-start | bytes 1794056 | tf_op jit(solution)/shard_map/ppermute | solution.py:538
  141.7 24.4 %collective-permute-start.37 = (bf16[1168,256]{1,0:T(8,128)(2,1)S(1)}, bf16[1168,256]{1,0:T(8,128)(2,1)S(1)}, u32[]{:S(2)}, u32[]{:S(2)}) collective-permute-start(bf16[1168,256]{1,0:T(8,128)(2,1)S(1)} %line_pick.9.refs_1_.own), channel_id=1, source_target_pairs={{0,4},{4,0},{8,12},{12,8},{16,20},{20,16},{24,28},{28,24},{1,5},{5... | collective-permute-start | bytes 1794056 | tf_op jit(solution)/shard_map/ppermute | solution.py:567
  148.3 19.8 %collective-permute-start.36 = (bf16[1168,256]{1,0:T(8,128)(2,1)S(1)}, bf16[1168,256]{1,0:T(8,128)(2,1)S(1)}, u32[]{:S(2)}, u32[]{:S(2)}) collective-permute-start(bf16[1168,256]{1,0:T(8,128)(2,1)S(1)} %line_add.23.refs_0_.x), channel_id=1, source_target_pairs={{8,0},{12,4},{16,24},{20,28},{9,1},{13,5},{17,25},{21,29},{10,2},{... | collective-permute-start | bytes 1794056 | tf_op jit(solution)/shard_map/ppermute | solution.py:538
  155.3 15.4 %collective-permute-start.39 = (bf16[1168,256]{1,0:T(8,128)(2,1)S(1)}, bf16[1168,256]{1,0:T(8,128)(2,1)S(1)}, u32[]{:S(2)}, u32[]{:S(2)}) collective-permute-start(bf16[1168,256]{1,0:T(8,128)(2,1)S(1)} %line_pick.10.refs_4_.own), channel_id=1, source_target_pairs={{0,4},{4,0},{8,12},{12,8},{16,20},{20,16},{24,28},{28,24},{1,5},{5... | collective-permute-start | bytes 1794056 | tf_op jit(solution)/shard_map/ppermute | solution.py:567
  (22 other events, 268.7 us)

commit v15 on v14

--- a/solution.py
+++ b/solution.py
@@ -571,7 +571,7 @@
         return [parts[0]] + [got[m] for m in range(1, n)]
 
     first_flat = w_first.reshape(27 * rows, n * rows)
-    pre_shares = swap(spread_shares(1, "pre", idx, n, vol, first_flat, LARGE))
+    pre_shares = swap(spread_shares(1, "pre", chan.astype(jnp.int32).reshape(1), n, vol, first_flat, LARGE))
     dact_parts = spread_shares(-1, "dact", idx, n, cot, w_second, LIMIT)
     held = dact_parts[1:]
     act, normed, inverse, *held = pl.pallas_call(

time: 176 us -> 176 us (level)
    unnamed x28 -> x24, local copies, waits for them, and re-layouts: 4.63 us -> 3.95 us
  transfers between devices with their start and end apart: 40 -> 40, of which waited for: 11 -> 11; matrix products, arithmetic and copies ran while one was open for 0% -> 0% of each run, Pallas kernels for 28% -> 29%
where the time goes in v15:
time: 176 us; the launch traced here: 175 us
  starting transfers between devices  70.8 us (40%)
  Pallas kernels  61.7 us (35%)
  waiting for transfers between devices  36.2 us (21%)
  local copies, waits for them, and re-layouts  4.03 us (2%)
    ppermute x18, starting transfers between devices, line_send(): return lax.ppermute(x, 'dp', pairs)  39 us
    ppermute x18, waiting for transfers between devices, line_send(): return lax.ppermute(x, 'dp', pairs)  21.7 us
    ppermute x10, starting transfers between devices, to_core(): lax.ppermute(x, 'dp', [(i, i ^ 1) for i in range(lax.axis_size('dp'))])  20.3 us
    pallas_call x2, Pallas kernels, conv_full(): pl.pallas_call(functools.partial(conv_kernel, n, sign, transposed), in_sp...  14.1 us
    ppermute x12, waiting for transfers between devices, to_partner(): return lax.ppermute(x, 'chan', [(i, i ^ m) for i in range(n)])  13 us
    pallas_call x2, Pallas kernels, spread_shares(): pl.pallas_call(functools.partial(share_kernel, n, sign), in_specs=[smem()...  12.9 us
    pallas_call x6, Pallas kernels, finish(): pl.pallas_call(functools.partial(finish_kernel, n, axis, factor, chunk),...  12.7 us
    ppermute x12, starting transfers between devices, to_partner(): return lax.ppermute(x, 'chan', [(i, i ^ m) for i in range(n)])  11.5 us
  transfers between devices with their start and end apart: 40, of which 11 were waited for; matrix products, arithmetic and copies ran while one was open for 0% of the time, Pallas kernels for 29%

profile of v15, /device:TPU:1, one launch (start us, length us, event | category | flops | bytes accessed | tf_op | source)
XLA Modules:
  0.0 174.9 jit_solution(5950856790378273328)
XLA Ops:
  0.7 7.1 %pre.1 = (bf16[1024,128]{1,0:T(8,128)(2,1)}, bf16[1024,128]{1,0:T(8,128)(2,1)}, bf16[1024,128]{1,0:T(8,128)(2,1)}, bf16[1024,128]{1,0:T(8,128)(2,1)}) custom-call(s32[1]{0:T(128)} %bitcast.idx, bf16[128,1024]{1,0:T(8,128)(2,1)} %bitcast.12, bf16[3456,512]{1,0:T(8,128)(2,1)} %bitcast.10), custom_call_target="tpu_custom_call" | custom-call | flops 1024 | bytes 1024 | tf_op jit(solution)/shard_map/pre/pallas_call | solution.py:159
  7.7 2.1 %collective-permute-start = (bf16[1024,128]{1,0:T(8,128)(2,1)}, bf16[1024,128]{1,0:T(8,128)(2,1)S(1)}, u32[]{:S(2)}, u32[]{:S(2)}) collective-permute-start(bf16[1024,128]{1,0:T(8,128)(2,1)} %get-tuple-element.43), channel_id=1, source_target_pairs={{0,1},{1,0},{2,3},{3,2},{4,5},{5,4},{6,7},{7,6},{8,9},{9,8},{10,11... | collective-permute-start | bytes 786440 | tf_op jit(solution)/shard_map/ppermute | solution.py:564
  12.4 2.0 %copy-done.1 = bf16[27,512,128]{2,1,0:T(8,128)(2,1)S(1)} copy-done((bf16[27,512,128]{2,1,0:T(8,128)(2,1)S(1)}, bf16[27,512,128]{2,1,0:T(8,128)(2,1)}, u32[]{:S(2)}) %copy-start.1) | copy-done | bytes 3538968
  15.4 5.8 %dact.1 = (bf16[1024,128]{1,0:T(8,128)(2,1)S(1)}, bf16[1024,128]{1,0:T(8,128)(2,1)S(1)}, bf16[1024,128]{1,0:T(8,128)(2,1)S(1)}, bf16[1024,128]{1,0:T(8,128)(2,1)S(1)}) custom-call(s32[2]{0:T(128)S(1)} %pad_add_fusion.idx, bf16[128,1024]{1,0:T(8,128)(2,1)S(1)} %bitcast.17, bf16[27,512,128]{2,1,0:T(8,128)(2,1)S(1)} %copy-done.1), custom_call_target="tpu_custom_call" | custom-call | flops 1024 | bytes 1024 | tf_op jit(solution)/shard_map/dact/pallas_call | solution.py:159
  27.5 3.7 %collective-permute-done.5.refs_3_ = bf16[1024,128]{1,0:T(8,128)(2,1)S(1)} collective-permute-done((bf16[1024,128]{1,0:T(8,128)(2,1)S(1)}, bf16[1024,128]{1,0:T(8,128)(2,1)S(1)}, u32[]{:S(2)}, u32[]{:S(2)}) %collective-permute-start.5) | collective-permute-done | bytes 262176 | tf_op jit(solution)/shard_map/ppermute | solution.py:564
  31.2 7.7 %collective-permute-done.4.refs_2_ = bf16[1024,128]{1,0:T(8,128)(2,1)S(1)} collective-permute-done((bf16[1024,128]{1,0:T(8,128)(2,1)S(1)}, bf16[1024,128]{1,0:T(8,128)(2,1)S(1)}, u32[]{:S(2)}, u32[]{:S(2)}) %collective-permute-start.4) | collective-permute-done | bytes 262176 | tf_op jit(solution)/shard_map/ppermute | solution.py:564
  40.4 1.5 collective-permute-done.8.other
  43.2 3.2 %collective-permute-start.16 = (bf16[9,256,128]{2,1,0:T(8,128)(2,1)S(1)}, bf16[9,256,128]{2,1,0:T(8,128)(2,1)S(1)}, u32[]{:S(2)}, u32[]{:S(2)}) collective-permute-start(bf16[9,256,128]{2,1,0:T(8,128)(2,1)S(1)} %grad_second.3.refs_0_.x), channel_id=1, source_target_pairs={{0,8},{4,12},{24,16},{28,20},{1,9},{5,13},{25,17},{29,21},{2,10},{... | collective-permute-start | bytes 1769480 | tf_op jit(solution)/shard_map/ppermute | solution.py:538
  49.1 1.5 grad_second.4.refs_4_.x
  50.7 1.5 collective-permute-start.15
  52.2 7.0 %output.1 = (bf16[128,1024]{1,0:T(8,128)(2,1)}, f32[8,128]{1,0:T(8,128)S(1)}) custom-call(s32[2]{0:T(128)S(1)} %pad_add_fusion.idx, bf16[27,512,128]{2,1,0:T(8,128)(2,1)S(1)} %copy-done.2, bf16[1024,128]{1,0:T(8,128)(2,1)S(1)} %get-tuple-element.49._.refs_0_, bf16[1024,128]{1,0:T(8,128)(2,1)S(1)} %collective-permute-done.3.refs_1_, ...), custom_call_target="tpu_custom_call" | custom-call | flops 1024 | bytes 1024 | tf_op jit(solution)/shard_map/output/pallas_call | solution.py:262
  64.8 6.5 %collective-permute-done.15.y = bf16[9,256,128]{2,1,0:T(8,128)(2,1)S(1)} collective-permute-done((bf16[9,256,128]{2,1,0:T(8,128)(2,1)S(1)}, bf16[9,256,128]{2,1,0:T(8,128)(2,1)S(1)}, u32[]{:S(2)}, u32[]{:S(2)}) %collective-permute-start.15) | collective-permute-done | bytes 589856 | tf_op jit(solution)/shard_map/ppermute | solution.py:538
  71.3 4.9 %collective-permute-start.18 = (bf16[9,256,128]{2,1,0:T(8,128)(2,1)S(1)}, bf16[9,256,128]{2,1,0:T(8,128)(2,1)}, u32[]{:S(2)}, u32[]{:S(2)}) collective-permute-start(bf16[9,256,128]{2,1,0:T(8,128)(2,1)S(1)} %grad_second.5.refs_0_.x), channel_id=1, source_target_pairs={{0,8},{4,12},{24,16},{28,20},{1,9},{5,13},{25,17},{29,21},{2,10},{... | collective-permute-start | bytes 1769480 | tf_op jit(solution)/shard_map/ppermute | solution.py:538
  82.3 2.5 %grad_first.2.refs_0_.x = bf16[1168,256]{1,0:T(8,128)(2,1)S(1)} custom-call(bf16[128,1024]{1,0:T(8,128)(2,1)S(1)} %bitcast.14, bf16[128,1024]{1,0:T(8,128)(2,1)S(1)} %collective-permute-done.7.refs_5_.vol_other, bf16[2,1024,128]{2,1,0:T(8,128)(2,1)S(1)} %get-tuple-element.61.refs_0_.own, bf16[2,1024,128]{2,1,0:T(8,128)(2,1)} %collective-permute-done.17.other, ...), custom_call_target="tpu_custom_call" | custom-call | flops 1024 | bytes 1024 | tf_op jit(solution)/shard_map/grad_first/pallas_call | solution.py:399
  84.9 4.9 %collective-permute-start.26 = (bf16[1168,256]{1,0:T(8,128)(2,1)S(1)}, bf16[1168,256]{1,0:T(8,128)(2,1)S(1)}, u32[]{:S(2)}, u32[]{:S(2)}) collective-permute-start(bf16[1168,256]{1,0:T(8,128)(2,1)S(1)} %grad_first.2.refs_0_.x), channel_id=1, source_target_pairs={{0,8},{4,12},{24,16},{28,20},{1,9},{5,13},{25,17},{29,21},{2,10},{... | collective-permute-start | bytes 1794056 | tf_op jit(solution)/shard_map/ppermute | solution.py:538
  91.8 3.5 %grad_first.3 = (bf16[1168,256]{1,0:T(8,128)(2,1)S(1)}, bf16[1168,256]{1,0:T(8,128)(2,1)S(1)}) custom-call(bf16[128,1024]{1,0:T(8,128)(2,1)S(1)} %bitcast.15, bf16[128,1024]{1,0:T(8,128)(2,1)S(1)} %collective-permute-done.7.refs_5_.vol_other, bf16[2,1024,128]{2,1,0:T(8,128)(2,1)S(1)} %get-tuple-element.61.refs_0_.own, ...), custom_call_target="tpu_custom_call" | custom-call | flops 1024 | bytes 1024 | tf_op jit(solution)/shard_map/grad_first/pallas_call | solution.py:399
  100.1 5.1 %collective-permute-start.20 = (bf16[1168,256]{1,0:T(8,128)(2,1)S(1)}, bf16[1168,256]{1,0:T(8,128)(2,1)S(1)}, u32[]{:S(2)}, u32[]{:S(2)}) collective-permute-start(bf16[1168,256]{1,0:T(8,128)(2,1)S(1)} %get-tuple-element.64.refs_0_.x), channel_id=1, source_target_pairs={{0,8},{4,12},{24,16},{28,20},{1,9},{5,13},{25,17},{29,21},{2,10},{... | collective-permute-start | bytes 1794056 | tf_op jit(solution)/shard_map/ppermute | solution.py:538
  106.1 6.5 %collective-permute-start.28 = (bf16[1168,256]{1,0:T(8,128)(2,1)S(1)}, bf16[1168,256]{1,0:T(8,128)(2,1)S(1)}, u32[]{:S(2)}, u32[]{:S(2)}) collective-permute-start(bf16[1168,256]{1,0:T(8,128)(2,1)S(1)} %get-tuple-element.66.x), channel_id=1, source_target_pairs={{0,8},{4,12},{24,16},{28,20},{1,9},{5,13},{25,17},{29,21},{2,10},{... | collective-permute-start | bytes 1794056 | tf_op jit(solution)/shard_map/ppermute | solution.py:538
  114.7 2.0 %collective-permute-start.29 = (bf16[9,256,128]{2,1,0:T(8,128)(2,1)S(1)}, bf16[9,256,128]{2,1,0:T(8,128)(2,1)S(1)}, u32[]{:S(2)}, u32[]{:S(2)}) collective-permute-start(bf16[9,256,128]{2,1,0:T(8,128)(2,1)S(1)} %line_pick.7.refs_0_.own), channel_id=1, source_target_pairs={{0,4},{4,0},{8,12},{12,8},{16,20},{20,16},{24,28},{28,24},{1,5},{5... | collective-permute-start | bytes 1769480 | tf_op jit(solution)/shard_map/ppermute | solution.py:567
  116.6 2.0 %finish_second.3 = (f32[27,512,128]{2,1,0:T(8,128)}, f32[8,128]{1,0:T(8,128)S(1)}) custom-call(s32[2]{0:T(128)S(1)} %pad_add_fusion.idx, bf16[9,256,128]{2,1,0:T(8,128)(2,1)S(1)} %line_pick.6.refs_0_.own, bf16[9,256,128]{2,1,0:T(8,128)(2,1)S(1)} %collective-permute-done.23.other, bf16[9,256,128]{2,1,0:T(8,128)(2,1)S(1)} %line_pick.7.refs_0_.own), custom_call_target="tpu_custom_call" | custom-call | flops 1024 | bytes 1024 | tf_op jit(solution)/shard_map/finish_second/pallas_call | solution.py:477
  121.0 6.6 %collective-permute-done.30.y = bf16[9,256,128]{2,1,0:T(8,128)(2,1)S(1)} collective-permute-done((bf16[9,256,128]{2,1,0:T(8,128)(2,1)S(1)}, bf16[9,256,128]{2,1,0:T(8,128)(2,1)S(1)}, u32[]{:S(2)}, u32[]{:S(2)}) %collective-permute-start.30) | collective-permute-done | bytes 589856 | tf_op jit(solution)/shard_map/ppermute | solution.py:538
  128.2 2.0 %finish_second.4 = (f32[27,512,128]{2,1,0:T(8,128)}, f32[8,128]{1,0:T(8,128)S(1)}) custom-call(s32[2]{0:T(128)S(1)} %pad_add_fusion.idx, bf16[9,256,128]{2,1,0:T(8,128)(2,1)S(1)} %line_pick.7.refs_0_.own, bf16[9,256,128]{2,1,0:T(8,128)(2,1)S(1)} %collective-permute-done.29.other, ...), custom_call_target="tpu_custom_call", output_to_operand_aliasing={{0}: (3, {})} | custom-call | flops 1024 | bytes 1024 | tf_op jit(solution)/shard_map/finish_second/pallas_call | solution.py:477
  131.7 4.7 %collective-permute-start.34 = (bf16[9,256,128]{2,1,0:T(8,128)(2,1)S(1)}, bf16[9,256,128]{2,1,0:T(8,128)(2,1)S(1)}, u32[]{:S(2)}, u32[]{:S(2)}) collective-permute-start(bf16[9,256,128]{2,1,0:T(8,128)(2,1)S(1)} %line_pick.8.refs_1_.own), channel_id=1, source_target_pairs={{0,4},{4,0},{8,12},{12,8},{16,20},{20,16},{24,28},{28,24},{1,5},{5... | collective-permute-start | bytes 1769480 | tf_op jit(solution)/shard_map/ppermute | solution.py:567
  137.9 2.5 %collective-permute-done.35.y = bf16[1168,256]{1,0:T(8,128)(2,1)S(1)} collective-permute-done((bf16[1168,256]{1,0:T(8,128)(2,1)S(1)}, bf16[1168,256]{1,0:T(8,128)(2,1)S(1)}, u32[]{:S(2)}, u32[]{:S(2)}) %collective-permute-start.35) | collective-permute-done | bytes 598048 | tf_op jit(solution)/shard_map/ppermute | solution.py:538
  141.0 4.5 %collective-permute-start.37 = (bf16[1168,256]{1,0:T(8,128)(2,1)S(1)}, bf16[1168,256]{1,0:T(8,128)(2,1)S(1)}, u32[]{:S(2)}, u32[]{:S(2)}) collective-permute-start(bf16[1168,256]{1,0:T(8,128)(2,1)S(1)} %line_pick.9.refs_1_.own), channel_id=1, source_target_pairs={{0,4},{4,0},{8,12},{12,8},{16,20},{20,16},{24,28},{28,24},{1,5},{5... | collective-permute-start | bytes 1794056 | tf_op jit(solution)/shard_map/ppermute | solution.py:567
  145.5 2.0 %finish_second.5 = (f32[27,512,128]{2,1,0:T(8,128)}, f32[8,128]{1,0:T(8,128)S(1)}) custom-call(s32[2]{0:T(128)S(1)} %pad_add_fusion.idx, bf16[9,256,128]{2,1,0:T(8,128)(2,1)S(1)} %line_pick.8.refs_1_.own, bf16[9,256,128]{2,1,0:T(8,128)(2,1)S(1)} %collective-permute-done.34.other, ...), custom_call_target="tpu_custom_call", output_to_operand_aliasing={{0}: (3, {})} | custom-call | flops 1024 | bytes 1024 | tf_op jit(solution)/shard_map/finish_second/pallas_call | solution.py:477
  149.0 5.0 %collective-permute-done.32.y = bf16[1168,256]{1,0:T(8,128)(2,1)S(1)} collective-permute-done((bf16[1168,256]{1,0:T(8,128)(2,1)S(1)}, bf16[1168,256]{1,0:T(8,128)(2,1)S(1)}, u32[]{:S(2)}, u32[]{:S(2)}) %collective-permute-start.32) | collective-permute-done | bytes 598048 | tf_op jit(solution)/shard_map/ppermute | solution.py:538
  154.6 3.7 %collective-permute-start.39 = (bf16[1168,256]{1,0:T(8,128)(2,1)S(1)}, bf16[1168,256]{1,0:T(8,128)(2,1)S(1)}, u32[]{:S(2)}, u32[]{:S(2)}) collective-permute-start(bf16[1168,256]{1,0:T(8,128)(2,1)S(1)} %line_pick.10.refs_4_.own), channel_id=1, source_target_pairs={{0,4},{4,0},{8,12},{12,8},{16,20},{20,16},{24,28},{28,24},{1,5},{5... | collective-permute-start | bytes 1794056 | tf_op jit(solution)/shard_map/ppermute | solution.py:567
  158.3 7.2 %grad_volume.1 = (bf16[128,1024]{1,0:T(8,128)(2,1)}, f32[8,128]{1,0:T(8,128)S(1)}) custom-call(s32[2]{0:T(128)S(1)} %pad_add_fusion.idx, bf16[3456,512]{1,0:T(8,128)(2,1)S(1)} %bitcast.11, bf16[1024,128]{1,0:T(8,128)(2,1)S(1)} %get-tuple-element.60.refs_0_, bf16[1024,128]{1,0:T(8,128)(2,1)S(1)} %copy-done.10, bf16[1024,128]{1,0:T(8,128)(2,1)S(1)} %copy-done.8, ...), custom_call_target="tpu_custom_call" | custom-call | flops 1024 | bytes 1024 | tf_op jit(solution)/shard_map/grad_volume/pallas_call | solution.py:262
  165.5 2.0 %finish_first.3 = (f32[27,128,512]{2,1,0:T(8,128)}, f32[8,128]{1,0:T(8,128)S(1)}) custom-call(s32[2]{0:T(128)S(1)} %pad_add_fusion.idx, bf16[1168,256]{1,0:T(8,128)(2,1)S(1)} %line_pick.9.refs_1_.own, bf16[1168,256]{1,0:T(8,128)(2,1)S(1)} %collective-permute-done.37.other, f32[8,128]{1,0:T(8,128)S(1)} %get-tuple-element.72.refs_0_), custom_call_target="tpu_custom_call" | custom-call | flops 1024 | bytes 1024 | tf_op jit(solution)/shard_map/finish_first/pallas_call | solution.py:477
  170.1 2.0 %finish_first.4 = (f32[27,128,512]{2,1,0:T(8,128)}, f32[8,128]{1,0:T(8,128)S(1)}) custom-call(s32[2]{0:T(128)S(1)} %pad_add_fusion.idx, bf16[1168,256]{1,0:T(8,128)(2,1)S(1)} %line_pick.10.refs_4_.own, bf16[1168,256]{1,0:T(8,128)(2,1)S(1)} %collective-permute-done.39.other, ...), custom_call_target="tpu_custom_call", output_to_operand_aliasing={{0}: (3, {})} | custom-call | flops 1024 | bytes 1024 | tf_op jit(solution)/shard_map/finish_first/pallas_call | solution.py:477
  172.1 2.6 %finish_first.5 = (f32[27,128,512]{2,1,0:T(8,128)}, f32[8,128]{1,0:T(8,128)}) custom-call(s32[2]{0:T(128)S(1)} %pad_add_fusion.idx, bf16[1168,256]{1,0:T(8,128)(2,1)S(1)} %line_pick.11.refs_1_.own, bf16[1168,256]{1,0:T(8,128)(2,1)S(1)} %collective-permute-done.38.other, f32[27,128,512]{2,1,0:T(8,128)} %get-tuple-element.75.refs_0_, ...), custom_call_target="tpu_custom_call", output_to_operand_aliasing={{0}: (3, {})} | custom-call | flops 1024 | bytes 1024 | tf_op jit(solution)/shard_map/finish_first/pallas_call | solution.py:477
  (116 shorter events, 47.4 us)
Async XLA Ops:
  7.7 13.6 %collective-permute-start = (bf16[1024,128]{1,0:T(8,128)(2,1)}, bf16[1024,128]{1,0:T(8,128)(2,1)S(1)}, u32[]{:S(2)}, u32[]{:S(2)}) collective-permute-start(bf16[1024,128]{1,0:T(8,128)(2,1)} %get-tuple-element.43), channel_id=1, source_target_pairs={{0,1},{1,0},{2,3},{3,2},{4,5},{5,4},{6,7},{7,6},{8,9},{9,8},{10,11... | collective-permute-start | bytes 786440 | tf_op jit(solution)/shard_map/ppermute | solution.py:564
  11.1 16.4 %collective-permute-start.7 = (bf16[128,1024]{1,0:T(8,128)(2,1)}, bf16[128,1024]{1,0:T(8,128)(2,1)S(1)}, u32[]{:S(2)}, u32[]{:S(2)}) collective-permute-start(bf16[128,1024]{1,0:T(8,128)(2,1)} %bitcast.13), channel_id=1, source_target_pairs={{0,4},{4,0},{8,12},{12,8},{16,20},{20,16},{24,28},{28,24},{1,5},{5... | collective-permute-start | bytes 786440 | tf_op jit(solution)/shard_map/ppermute | solution.py:567
  12.3 14.5 %collective-permute-start.6 = (bf16[128,1024]{1,0:T(8,128)(2,1)}, bf16[128,1024]{1,0:T(8,128)(2,1)S(1)}, u32[]{:S(2)}, u32[]{:S(2)}) collective-permute-start(bf16[128,1024]{1,0:T(8,128)(2,1)} %bitcast.16), channel_id=1, source_target_pairs={{0,4},{4,0},{8,12},{12,8},{16,20},{20,16},{24,28},{28,24},{1,5},{5... | collective-permute-start | bytes 786440 | tf_op jit(solution)/shard_map/ppermute | solution.py:567
  25.5 13.5 %collective-permute-start.4 = (bf16[1024,128]{1,0:T(8,128)(2,1)S(1)}, bf16[1024,128]{1,0:T(8,128)(2,1)S(1)}, u32[]{:S(2)}, u32[]{:S(2)}) collective-permute-start(bf16[1024,128]{1,0:T(8,128)(2,1)S(1)} %get-tuple-element.49._.refs_0_), channel_id=1, source_target_pairs={{0,2},{1,3},{2,0},{3,1},{4,6},{5,7},{6,4},{7,5},{8,10},{9,11},{10,... | collective-permute-start | bytes 786440 | tf_op jit(solution)/shard_map/ppermute | solution.py:564
  26.6 12.4 %collective-permute-start.3 = (bf16[1024,128]{1,0:T(8,128)(2,1)S(1)}, bf16[1024,128]{1,0:T(8,128)(2,1)S(1)}, u32[]{:S(2)}, u32[]{:S(2)}) collective-permute-start(bf16[1024,128]{1,0:T(8,128)(2,1)S(1)} %get-tuple-element.49._.refs_0_), channel_id=1, source_target_pairs={{0,1},{1,0},{2,3},{3,2},{4,5},{5,4},{6,7},{7,6},{8,9},{9,8},{10,11... | collective-permute-start | bytes 786440 | tf_op jit(solution)/shard_map/ppermute | solution.py:564
  43.2 16.9 %collective-permute-start.16 = (bf16[9,256,128]{2,1,0:T(8,128)(2,1)S(1)}, bf16[9,256,128]{2,1,0:T(8,128)(2,1)S(1)}, u32[]{:S(2)}, u32[]{:S(2)}) collective-permute-start(bf16[9,256,128]{2,1,0:T(8,128)(2,1)S(1)} %grad_second.3.refs_0_.x), channel_id=1, source_target_pairs={{0,8},{4,12},{24,16},{28,20},{1,9},{5,13},{25,17},{29,21},{2,10},{... | collective-permute-start | bytes 1769480 | tf_op jit(solution)/shard_map/ppermute | solution.py:538
  46.4 12.8 %collective-permute-start.9 = (bf16[1024,128]{1,0:T(8,128)(2,1)S(1)}, bf16[1024,128]{1,0:T(8,128)(2,1)S(1)}, u32[]{:S(2)}, u32[]{:S(2)}) collective-permute-start(bf16[1024,128]{1,0:T(8,128)(2,1)S(1)} %get-tuple-element.56), channel_id=1, source_target_pairs={{0,1},{1,0},{2,3},{3,2},{4,5},{5,4},{6,7},{7,6},{8,9},{9,8},{10,11... | collective-permute-start | bytes 786440 | tf_op jit(solution)/shard_map/ppermute | solution.py:564
  50.7 20.7 %collective-permute-start.15 = (bf16[9,256,128]{2,1,0:T(8,128)(2,1)S(1)}, bf16[9,256,128]{2,1,0:T(8,128)(2,1)S(1)}, u32[]{:S(2)}, u32[]{:S(2)}) collective-permute-start(bf16[9,256,128]{2,1,0:T(8,128)(2,1)S(1)} %grad_second.4.refs_4_.x), channel_id=1, source_target_pairs={{0,8},{4,12},{24,16},{28,20},{1,9},{5,13},{25,17},{29,21},{2,10},{... | collective-permute-start | bytes 1769480 | tf_op jit(solution)/shard_map/ppermute | solution.py:538
  60.2 20.7 %collective-permute-start.19 = (bf16[9,256,128]{2,1,0:T(8,128)(2,1)S(1)}, bf16[9,256,128]{2,1,0:T(8,128)(2,1)S(1)}, u32[]{:S(2)}, u32[]{:S(2)}) collective-permute-start(bf16[9,256,128]{2,1,0:T(8,128)(2,1)S(1)} %line_add.12.refs_0_.x), channel_id=1, source_target_pairs={{8,16},{12,20},{16,8},{20,12},{9,17},{13,21},{17,9},{21,13},{10,18... | collective-permute-start | bytes 1769480 | tf_op jit(solution)/shard_map/ppermute | solution.py:538
  60.9 15.5 %collective-permute-start.14 = (bf16[1024,128]{1,0:T(8,128)(2,1)S(1)}, bf16[1024,128]{1,0:T(8,128)(2,1)S(1)}, u32[]{:S(2)}, u32[]{:S(2)}) collective-permute-start(bf16[1024,128]{1,0:T(8,128)(2,1)S(1)} %get-tuple-element.60.refs_0_), channel_id=1, source_target_pairs={{0,3},{1,2},{2,1},{3,0},{4,7},{5,6},{6,5},{7,4},{8,11},{9,10},{10,... | collective-permute-start | bytes 786440 | tf_op jit(solution)/shard_map/ppermute | solution.py:564
  62.4 14.0 %collective-permute-start.13 = (bf16[1024,128]{1,0:T(8,128)(2,1)S(1)}, bf16[1024,128]{1,0:T(8,128)(2,1)S(1)}, u32[]{:S(2)}, u32[]{:S(2)}) collective-permute-start(bf16[1024,128]{1,0:T(8,128)(2,1)S(1)} %get-tuple-element.60.refs_0_), channel_id=1, source_target_pairs={{0,2},{1,3},{2,0},{3,1},{4,6},{5,7},{6,4},{7,5},{8,10},{9,11},{10,... | collective-permute-start | bytes 786440 | tf_op jit(solution)/shard_map/ppermute | solution.py:564
  63.3 13.1 %collective-permute-start.12 = (bf16[1024,128]{1,0:T(8,128)(2,1)S(1)}, bf16[1024,128]{1,0:T(8,128)(2,1)S(1)}, u32[]{:S(2)}, u32[]{:S(2)}) collective-permute-start(bf16[1024,128]{1,0:T(8,128)(2,1)S(1)} %get-tuple-element.60.refs_0_), channel_id=1, source_target_pairs={{0,1},{1,0},{2,3},{3,2},{4,5},{5,4},{6,7},{7,6},{8,9},{9,8},{10,11... | collective-permute-start | bytes 786440 | tf_op jit(solution)/shard_map/ppermute | solution.py:564
  71.3 18.5 %collective-permute-start.18 = (bf16[9,256,128]{2,1,0:T(8,128)(2,1)S(1)}, bf16[9,256,128]{2,1,0:T(8,128)(2,1)}, u32[]{:S(2)}, u32[]{:S(2)}) collective-permute-start(bf16[9,256,128]{2,1,0:T(8,128)(2,1)S(1)} %grad_second.5.refs_0_.x), channel_id=1, source_target_pairs={{0,8},{4,12},{24,16},{28,20},{1,9},{5,13},{25,17},{29,21},{2,10},{... | collective-permute-start | bytes 1769480 | tf_op jit(solution)/shard_map/ppermute | solution.py:538
  79.4 15.9 %collective-permute-start.22 = (bf16[9,256,128]{2,1,0:T(8,128)(2,1)S(1)}, bf16[9,256,128]{2,1,0:T(8,128)(2,1)}, u32[]{:S(2)}, u32[]{:S(2)}) collective-permute-start(bf16[9,256,128]{2,1,0:T(8,128)(2,1)S(1)} %line_add.13.refs_4_.x), channel_id=1, source_target_pairs={{8,16},{12,20},{16,8},{20,12},{9,17},{13,21},{17,9},{21,13},{10,18... | collective-permute-start | bytes 1769480 | tf_op jit(solution)/shard_map/ppermute | solution.py:538
  81.0 17.1 %collective-permute-start.21 = (bf16[9,256,128]{2,1,0:T(8,128)(2,1)S(1)}, bf16[9,256,128]{2,1,0:T(8,128)(2,1)}, u32[]{:S(2)}, u32[]{:S(2)}) collective-permute-start(bf16[9,256,128]{2,1,0:T(8,128)(2,1)S(1)} %line_add.14.refs_0_.x), channel_id=1, source_target_pairs={{8,0},{12,4},{16,24},{20,28},{9,1},{13,5},{17,25},{21,29},{10,2},{... | collective-permute-start | bytes 1769480 | tf_op jit(solution)/shard_map/ppermute | solution.py:538
  84.9 20.4 %collective-permute-start.26 = (bf16[1168,256]{1,0:T(8,128)(2,1)S(1)}, bf16[1168,256]{1,0:T(8,128)(2,1)S(1)}, u32[]{:S(2)}, u32[]{:S(2)}) collective-permute-start(bf16[1168,256]{1,0:T(8,128)(2,1)S(1)} %grad_first.2.refs_0_.x), channel_id=1, source_target_pairs={{0,8},{4,12},{24,16},{28,20},{1,9},{5,13},{25,17},{29,21},{2,10},{... | collective-permute-start | bytes 1794056 | tf_op jit(solution)/shard_map/ppermute | solution.py:538
  91.0 15.1 %collective-permute-start.25 = (bf16[9,256,128]{2,1,0:T(8,128)(2,1)S(1)}, bf16[9,256,128]{2,1,0:T(8,128)(2,1)S(1)}, u32[]{:S(2)}, u32[]{:S(2)}) collective-permute-start(bf16[9,256,128]{2,1,0:T(8,128)(2,1)S(1)} %line_add.15.refs_0_.x), channel_id=1, source_target_pairs={{8,16},{12,20},{16,8},{20,12},{9,17},{13,21},{17,9},{21,13},{10,18... | collective-permute-start | bytes 1769480 | tf_op jit(solution)/shard_map/ppermute | solution.py:538
  96.5 16.3 %collective-permute-start.24 = (bf16[9,256,128]{2,1,0:T(8,128)(2,1)S(1)}, bf16[9,256,128]{2,1,0:T(8,128)(2,1)S(1)}, u32[]{:S(2)}, u32[]{:S(2)}) collective-permute-start(bf16[9,256,128]{2,1,0:T(8,128)(2,1)S(1)} %line_add.16.refs_0_.x), channel_id=1, source_target_pairs={{8,0},{12,4},{16,24},{20,28},{9,1},{13,5},{17,25},{21,29},{10,2},{... | collective-permute-start | bytes 1769480 | tf_op jit(solution)/shard_map/ppermute | solution.py:538
  99.2 15.4 %collective-permute-start.23 = (bf16[9,256,128]{2,1,0:T(8,128)(2,1)S(1)}, bf16[9,256,128]{2,1,0:T(8,128)(2,1)S(1)}, u32[]{:S(2)}, u32[]{:S(2)}) collective-permute-start(bf16[9,256,128]{2,1,0:T(8,128)(2,1)S(1)} %line_pick.6.refs_0_.own), channel_id=1, source_target_pairs={{0,4},{4,0},{8,12},{12,8},{16,20},{20,16},{24,28},{28,24},{1,5},{5... | collective-permute-start | bytes 1769480 | tf_op jit(solution)/shard_map/ppermute | solution.py:567
  100.1 18.6 %collective-permute-start.20 = (bf16[1168,256]{1,0:T(8,128)(2,1)S(1)}, bf16[1168,256]{1,0:T(8,128)(2,1)S(1)}, u32[]{:S(2)}, u32[]{:S(2)}) collective-permute-start(bf16[1168,256]{1,0:T(8,128)(2,1)S(1)} %get-tuple-element.64.refs_0_.x), channel_id=1, source_target_pairs={{0,8},{4,12},{24,16},{28,20},{1,9},{5,13},{25,17},{29,21},{2,10},{... | collective-permute-start | bytes 1794056 | tf_op jit(solution)/shard_map/ppermute | solution.py:538
  105.4 14.2 %collective-permute-start.31 = (bf16[1168,256]{1,0:T(8,128)(2,1)S(1)}, bf16[1168,256]{1,0:T(8,128)(2,1)S(1)}, u32[]{:S(2)}, u32[]{:S(2)}) collective-permute-start(bf16[1168,256]{1,0:T(8,128)(2,1)S(1)} %line_add.17.refs_0_.x), channel_id=1, source_target_pairs={{8,16},{12,20},{16,8},{20,12},{9,17},{13,21},{17,9},{21,13},{10,18... | collective-permute-start | bytes 1794056 | tf_op jit(solution)/shard_map/ppermute | solution.py:538
  106.1 24.8 %collective-permute-start.28 = (bf16[1168,256]{1,0:T(8,128)(2,1)S(1)}, bf16[1168,256]{1,0:T(8,128)(2,1)S(1)}, u32[]{:S(2)}, u32[]{:S(2)}) collective-permute-start(bf16[1168,256]{1,0:T(8,128)(2,1)S(1)} %get-tuple-element.66.x), channel_id=1, source_target_pairs={{0,8},{4,12},{24,16},{28,20},{1,9},{5,13},{25,17},{29,21},{2,10},{... | collective-permute-start | bytes 1794056 | tf_op jit(solution)/shard_map/ppermute | solution.py:538
  112.8 14.8 %collective-permute-start.30 = (bf16[9,256,128]{2,1,0:T(8,128)(2,1)S(1)}, bf16[9,256,128]{2,1,0:T(8,128)(2,1)S(1)}, u32[]{:S(2)}, u32[]{:S(2)}) collective-permute-start(bf16[9,256,128]{2,1,0:T(8,128)(2,1)S(1)} %line_add.18.refs_0_.x), channel_id=1, source_target_pairs={{8,0},{12,4},{16,24},{20,28},{9,1},{13,5},{17,25},{21,29},{10,2},{... | collective-permute-start | bytes 1769480 | tf_op jit(solution)/shard_map/ppermute | solution.py:538
  114.7 13.5 %collective-permute-start.29 = (bf16[9,256,128]{2,1,0:T(8,128)(2,1)S(1)}, bf16[9,256,128]{2,1,0:T(8,128)(2,1)S(1)}, u32[]{:S(2)}, u32[]{:S(2)}) collective-permute-start(bf16[9,256,128]{2,1,0:T(8,128)(2,1)S(1)} %line_pick.7.refs_0_.own), channel_id=1, source_target_pairs={{0,4},{4,0},{8,12},{12,8},{16,20},{20,16},{24,28},{28,24},{1,5},{5... | collective-permute-start | bytes 1769480 | tf_op jit(solution)/shard_map/ppermute | solution.py:567
  118.8 17.6 %collective-permute-start.27 = (bf16[1168,256]{1,0:T(8,128)(2,1)S(1)}, bf16[1168,256]{1,0:T(8,128)(2,1)S(1)}, u32[]{:S(2)}, u32[]{:S(2)}) collective-permute-start(bf16[1168,256]{1,0:T(8,128)(2,1)S(1)} %line_add.19.refs_0_.x), channel_id=1, source_target_pairs={{8,16},{12,20},{16,8},{20,12},{9,17},{13,21},{17,9},{21,13},{10,18... | collective-permute-start | bytes 1794056 | tf_op jit(solution)/shard_map/ppermute | solution.py:538
  119.7 20.7 %collective-permute-start.35 = (bf16[1168,256]{1,0:T(8,128)(2,1)S(1)}, bf16[1168,256]{1,0:T(8,128)(2,1)S(1)}, u32[]{:S(2)}, u32[]{:S(2)}) collective-permute-start(bf16[1168,256]{1,0:T(8,128)(2,1)S(1)} %line_add.20.refs_0_.x), channel_id=1, source_target_pairs={{8,0},{12,4},{16,24},{20,28},{9,1},{13,5},{17,25},{21,29},{10,2},{... | collective-permute-start | bytes 1794056 | tf_op jit(solution)/shard_map/ppermute | solution.py:538
  131.0 16.5 %collective-permute-start.33 = (bf16[1168,256]{1,0:T(8,128)(2,1)S(1)}, bf16[1168,256]{1,0:T(8,128)(2,1)S(1)}, u32[]{:S(2)}, u32[]{:S(2)}) collective-permute-start(bf16[1168,256]{1,0:T(8,128)(2,1)S(1)} %line_add.21.refs_0_.x), channel_id=1, source_target_pairs={{8,16},{12,20},{16,8},{20,12},{9,17},{13,21},{17,9},{21,13},{10,18... | collective-permute-start | bytes 1794056 | tf_op jit(solution)/shard_map/ppermute | solution.py:538
  131.7 13.8 %collective-permute-start.34 = (bf16[9,256,128]{2,1,0:T(8,128)(2,1)S(1)}, bf16[9,256,128]{2,1,0:T(8,128)(2,1)S(1)}, u32[]{:S(2)}, u32[]{:S(2)}) collective-permute-start(bf16[9,256,128]{2,1,0:T(8,128)(2,1)S(1)} %line_pick.8.refs_1_.own), channel_id=1, source_target_pairs={{0,4},{4,0},{8,12},{12,8},{16,20},{20,16},{24,28},{28,24},{1,5},{5... | collective-permute-start | bytes 1769480 | tf_op jit(solution)/shard_map/ppermute | solution.py:567
  136.6 17.5 %collective-permute-start.32 = (bf16[1168,256]{1,0:T(8,128)(2,1)S(1)}, bf16[1168,256]{1,0:T(8,128)(2,1)S(1)}, u32[]{:S(2)}, u32[]{:S(2)}) collective-permute-start(bf16[1168,256]{1,0:T(8,128)(2,1)S(1)} %line_add.22.refs_0_.x), channel_id=1, source_target_pairs={{8,0},{12,4},{16,24},{20,28},{9,1},{13,5},{17,25},{21,29},{10,2},{... | collective-permute-start | bytes 1794056 | tf_op jit(solution)/shard_map/ppermute | solution.py:538
  141.0 24.4 %collective-permute-start.37 = (bf16[1168,256]{1,0:T(8,128)(2,1)S(1)}, bf16[1168,256]{1,0:T(8,128)(2,1)S(1)}, u32[]{:S(2)}, u32[]{:S(2)}) collective-permute-start(bf16[1168,256]{1,0:T(8,128)(2,1)S(1)} %line_pick.9.refs_1_.own), channel_id=1, source_target_pairs={{0,4},{4,0},{8,12},{12,8},{16,20},{20,16},{24,28},{28,24},{1,5},{5... | collective-permute-start | bytes 1794056 | tf_op jit(solution)/shard_map/ppermute | solution.py:567
  147.7 19.8 %collective-permute-start.36 = (bf16[1168,256]{1,0:T(8,128)(2,1)S(1)}, bf16[1168,256]{1,0:T(8,128)(2,1)S(1)}, u32[]{:S(2)}, u32[]{:S(2)}) collective-permute-start(bf16[1168,256]{1,0:T(8,128)(2,1)S(1)} %line_add.23.refs_0_.x), channel_id=1, source_target_pairs={{8,0},{12,4},{16,24},{20,28},{9,1},{13,5},{17,25},{21,29},{10,2},{... | collective-permute-start | bytes 1794056 | tf_op jit(solution)/shard_map/ppermute | solution.py:538
  154.6 15.4 %collective-permute-start.39 = (bf16[1168,256]{1,0:T(8,128)(2,1)S(1)}, bf16[1168,256]{1,0:T(8,128)(2,1)S(1)}, u32[]{:S(2)}, u32[]{:S(2)}) collective-permute-start(bf16[1168,256]{1,0:T(8,128)(2,1)S(1)} %line_pick.10.refs_4_.own), channel_id=1, source_target_pairs={{0,4},{4,0},{8,12},{12,8},{16,20},{20,16},{24,28},{28,24},{1,5},{5... | collective-permute-start | bytes 1794056 | tf_op jit(solution)/shard_map/ppermute | solution.py:567
  (20 other events, 227.5 us)
